TPU v7x, 32 devices: a whole 2x2x4 slice. The times are simulated.
32 devices in a mesh: dp: 8 (over z, y), sp: 4 (over x, core).
Axes of the slice: x: 2, y: 2, z: 4, core: 2. Of those that a mesh axis runs over, the one named last changes fastest.
Arguments:
- tokens: bfloat16 [16384, 1024], P(('dp', 'sp')), may hold values from -6 to 6
- seq_spans: int32 [8, 4], P('dp'), may hold values from 64 to 2048, as said below
- valid_mask: int32 [16384], P(('dp', 'sp')), may hold values from 0 to 1, as said below
- cotangent: bfloat16 [16384, 1024], P(('dp', 'sp')), may hold values from -12 to 12
- w_qkv: bfloat16 [1024, 3072], P('dp', 'sp'), may hold values from -0.1875 to 0.1875
- w_out: bfloat16 [1024, 1024], P('dp', 'sp'), may hold values from -1.5 to 1.5
- w_up: bfloat16 [1024, 4096], P('dp', 'sp'), may hold values from -0.1875 to 0.1875
- w_down: bfloat16 [1024, 4096], P('dp', 'sp'), may hold values from -0.09375 to 0.09375
- model_gains: float32 [3, 1024], replicated, may hold values from 0.5 to 1.5
- model_shifts: float32 [7, 1024], replicated, may hold values from -1.8 to 1.8
- mid_gain: float32 [4096], replicated, may hold values from 0.5 to 1.5
- hidden_shifts: float32 [2, 4096], replicated, may hold values from -3 to 3
- head_scale: float32 [16], replicated, may hold values from 0.5 to 2
Outputs:
- layer_out: bfloat16 [16384, 1024], P(('dp', 'sp'))
- grad_tokens: float32 [16384, 1024], P(('dp', 'sp'))
- grad_w_qkv: float32 [1024, 3072], P('dp', 'sp')
- grad_w_out: float32 [1024, 1024], P('dp', 'sp')
- grad_w_up: float32 [1024, 4096], P('dp', 'sp')
- grad_w_down: float32 [1024, 4096], P('dp', 'sp')
- grad_model_gains: float32 [3, 1024], replicated
- grad_model_shifts: float32 [7, 1024], replicated
- grad_mid_gain: float32 [4096], replicated
- grad_hidden_shifts: float32 [2, 4096], replicated
- grad_head_scale: float32 [16], replicated
Inputs may be any that keep to these rules, and one draw needn't show every extreme that they name: `seq_spans`: each row holds the token counts of the 4 consecutive slots of one group and sums to 2048; in every row one slot starts within the first 512 tokens of the group and ends within the last 512. `valid_mask`: within each slot the ones form a leading run of one token or more, and the rest of the slot is 0.
All inputs are finite; a program needn't handle non-finite values.
Results may differ from a plain program's by a relative error of at most 0.018.
Values may be sent and summed in bfloat16 or wider, within the bound.
No kernel may reach another device: no remote copies, remote signals or barrier semaphores. Data moves between devices by JAX's collectives and lax.ppermute only.
A program may use at most 192 MiB of HBM per device.

v0:
```python
import jax
import jax.numpy as jnp
from jax import lax
from jax.sharding import PartitionSpec as P

EPSILON = 1e-05
MASKED = -1e30


def norm_forward(inputs, gain_row, shift_row):
    row_mean = jnp.mean(inputs, axis=-1, keepdims=True)
    centred = inputs - row_mean
    inv_std = lax.rsqrt(jnp.mean(centred * centred, axis=-1, keepdims=True) + EPSILON)
    normed = centred * inv_std
    return (normed * gain_row + shift_row, normed, inv_std)


def norm_backward(incoming, normed, inv_std, gain_row):
    scaled = incoming * gain_row
    centred_grad = (
        scaled
        - jnp.mean(scaled, axis=-1, keepdims=True)
        - normed * jnp.mean(scaled * normed, axis=-1, keepdims=True)
    )
    return (inv_std * centred_grad, jnp.sum(incoming * normed, axis=0), jnp.sum(incoming, axis=0))


def contract_rows(left_side, right_side):
    return lax.dot_general(
        left_side, right_side, (((0,), (0,)), ((), ())), preferred_element_type=jnp.float32
    )


def contract_cols(left_side, right_side):
    return lax.dot_general(
        left_side, right_side, (((1,), (1,)), ((), ())), preferred_element_type=jnp.float32
    )


def segment_ids(span_row, row_count):
    span_ends = jnp.cumsum(span_row)
    places = lax.broadcasted_iota(jnp.int32, (row_count, span_row.shape[0]), 0)
    return jnp.sum((places >= span_ends[None, :]).astype(jnp.int32), axis=1)


def block_scores(query_block, key_rows, first_row, segment, keep_key, factor):
    block_rows = query_block.shape[0]
    rows_at = first_row + lax.broadcasted_iota(jnp.int32, (block_rows, 1), 0)
    cols_at = lax.broadcasted_iota(jnp.int32, (1, key_rows.shape[0]), 1)
    segment_rows = lax.dynamic_slice_in_dim(segment, first_row, block_rows, 0)
    visible = (segment_rows[:, None] == segment[None, :]) & (cols_at <= rows_at) & keep_key[None, :]
    raw_scores = (
        jnp.einsum("qhe,khe->hqk", query_block, key_rows, preferred_element_type=jnp.float32)
        * factor
    )
    return jnp.where(visible[None], raw_scores, MASKED)


def attend_forward(queries, key_rows, value_rows, segment, keep_key, factor, block_rows):
    block_count = queries.shape[0] // block_rows

    def one_block(block_index):
        first_row = block_index * block_rows
        query_block = lax.dynamic_slice_in_dim(queries, first_row, block_rows, 0)
        scores = block_scores(query_block, key_rows, first_row, segment, keep_key, factor)
        row_peak = jnp.max(scores, axis=-1, keepdims=True)
        exponent = jnp.exp(scores - row_peak)
        row_total = jnp.sum(exponent, axis=-1, keepdims=True)
        weights = (exponent / row_total).astype(jnp.bfloat16)
        result = jnp.einsum("hqk,khe->qhe", weights, value_rows, preferred_element_type=jnp.float32)
        return (result, (row_peak + jnp.log(row_total))[:, :, 0])

    results, log_sums = lax.map(one_block, jnp.arange(block_count, dtype=jnp.int32))
    return (results.reshape(queries.shape), log_sums)


def attend_backward(
    queries,
    key_rows,
    value_rows,
    attended_grad,
    row_dots,
    log_sums,
    segment,
    keep_key,
    factor,
    block_rows,
):
    block_count = queries.shape[0] // block_rows

    def one_block(running, block_index):
        key_grad, value_grad = running
        first_row = block_index * block_rows
        query_block = lax.dynamic_slice_in_dim(queries, first_row, block_rows, 0)
        grad_block = lax.dynamic_slice_in_dim(attended_grad, first_row, block_rows, 0)
        dots_block = lax.dynamic_slice_in_dim(row_dots, first_row, block_rows, 0)
        scores = block_scores(query_block, key_rows, first_row, segment, keep_key, factor)
        probs = jnp.exp(scores - log_sums[block_index][:, :, None])
        prob_grad = jnp.einsum(
            "qhe,khe->hqk", grad_block, value_rows, preferred_element_type=jnp.float32
        )
        score_grad = (probs * (prob_grad - dots_block.T[:, :, None])).astype(jnp.bfloat16)
        query_grad = (
            jnp.einsum("hqk,khe->qhe", score_grad, key_rows, preferred_element_type=jnp.float32)
            * factor
        )
        key_grad = (
            key_grad
            + jnp.einsum(
                "hqk,qhe->khe", score_grad, query_block, preferred_element_type=jnp.float32
            )
            * factor
        )
        value_grad = value_grad + jnp.einsum(
            "hqk,qhe->khe",
            probs.astype(jnp.bfloat16),
            grad_block,
            preferred_element_type=jnp.float32,
        )
        return ((key_grad, value_grad), query_grad)

    empty_grad = jnp.zeros(key_rows.shape, jnp.float32)
    (key_grad, value_grad), query_grad = lax.scan(
        one_block, (empty_grad, empty_grad), jnp.arange(block_count, dtype=jnp.int32)
    )
    return (query_grad.reshape(queries.shape), key_grad, value_grad)


def per_device(
    tokens,
    seq_spans,
    valid_mask,
    cotangent,
    w_qkv,
    w_out,
    w_up,
    w_down,
    model_gains,
    model_shifts,
    mid_gain,
    hidden_shifts,
    head_scale,
):
    sp_count = lax.axis_size("sp")
    local_rows, model_width = tokens.shape
    group_rows = local_rows * sp_count
    head_count = head_scale.shape[0]
    local_heads = head_count // sp_count
    head_width = model_width // head_count
    local_width = local_heads * head_width
    factor = head_width ** (-0.5)
    block_rows = min(512, group_rows)
    sp_place = lax.axis_index("sp")
    part_qkv, part_out, part_up, part_down = (
        lax.all_gather(w_qkv, "dp", axis=0, tiled=True),
        lax.all_gather(w_out, "dp", axis=0, tiled=True),
        lax.all_gather(w_up, "dp", axis=0, tiled=True),
        lax.all_gather(w_down, "dp", axis=0, tiled=True),
    )
    full_qkv, full_out, full_up, full_down = (
        lax.all_gather(part_qkv, "sp", axis=1, tiled=True),
        lax.all_gather(part_out, "sp", axis=1, tiled=True),
        lax.all_gather(part_up, "sp", axis=1, tiled=True),
        lax.all_gather(part_down, "sp", axis=1, tiled=True),
    )
    stream = tokens.astype(jnp.float32)
    first_out, first_normed, first_std = norm_forward(stream, model_gains[0], model_shifts[3])
    first_norm = first_out.astype(jnp.bfloat16)
    qkv_shift = jnp.concatenate([model_shifts[0], jnp.zeros_like(model_shifts[0]), model_shifts[1]])
    projected = (
        jnp.dot(first_norm, full_qkv, preferred_element_type=jnp.float32) + qkv_shift
    ).astype(jnp.bfloat16)
    packed = projected.reshape(local_rows, 3, sp_count, local_width)
    keep_local = jnp.broadcast_to(
        valid_mask.astype(jnp.bfloat16)[:, None, None, None], (local_rows, 1, sp_count, 1)
    )
    gathered, keep_group = (
        lax.all_to_all(packed, "sp", split_axis=2, concat_axis=0, tiled=True),
        lax.all_to_all(keep_local, "sp", split_axis=2, concat_axis=0, tiled=True),
    )
    queries = gathered[:, 0, 0].reshape(group_rows, local_heads, head_width)
    key_rows = gathered[:, 1, 0].reshape(group_rows, local_heads, head_width)
    value_rows = gathered[:, 2, 0].reshape(group_rows, local_heads, head_width)
    keep_key = keep_group[:, 0, 0, 0] > 0.5
    segment = segment_ids(seq_spans[0], group_rows)
    attended, log_sums = attend_forward(
        queries, key_rows, value_rows, segment, keep_key, factor, block_rows
    )
    head_gain = lax.dynamic_slice_in_dim(head_scale, sp_place * local_heads, local_heads, 0)
    scaled = (
        (attended * head_gain[None, :, None])
        .astype(jnp.bfloat16)
        .reshape(group_rows, 1, local_width)
    )
    returned = lax.all_to_all(scaled, "sp", split_axis=0, concat_axis=1, tiled=True)
    merged = returned.reshape(local_rows, model_width)
    attn_pre = jnp.dot(merged, full_out, preferred_element_type=jnp.float32) + model_shifts[2]
    attn_out, attn_normed, attn_std = norm_forward(attn_pre, model_gains[1], model_shifts[4])
    middle = stream + attn_out
    second_out, second_normed, second_std = norm_forward(middle, model_gains[2], model_shifts[5])
    second_norm = second_out.astype(jnp.bfloat16)
    hidden_pre = (
        jnp.dot(second_norm, full_up, preferred_element_type=jnp.float32) + hidden_shifts[0]
    )
    activated, gelu_pull = jax.vjp(jax.nn.gelu, hidden_pre)
    hidden_out, hidden_normed, hidden_std = norm_forward(activated, mid_gain, hidden_shifts[1])
    hidden = hidden_out.astype(jnp.bfloat16)
    layer_out = (middle + contract_cols(hidden, full_down) + model_shifts[6]).astype(jnp.bfloat16)
    upstream = cotangent.astype(jnp.float32) * valid_mask.astype(jnp.float32)[:, None]
    upstream_low = upstream.astype(jnp.bfloat16)
    hidden_grad = jnp.dot(upstream_low, full_down, preferred_element_type=jnp.float32)
    act_grad, grad_mid, grad_mid_shift = norm_backward(
        hidden_grad, hidden_normed, hidden_std, mid_gain
    )
    pre_grad = gelu_pull(act_grad)[0].astype(jnp.bfloat16)
    second_grad = contract_cols(pre_grad, full_up)
    middle_part, grad_gain_ffn, grad_shift_ffn = norm_backward(
        second_grad, second_normed, second_std, model_gains[2]
    )
    middle_grad = upstream + middle_part
    attn_grad_full, grad_gain_attn, grad_shift_attn = norm_backward(
        middle_grad, attn_normed, attn_std, model_gains[1]
    )
    attn_grad = attn_grad_full.astype(jnp.bfloat16)
    merged_grad = contract_cols(attn_grad, full_out).astype(jnp.bfloat16)
    scaled_grad = lax.all_to_all(
        merged_grad.reshape(local_rows, sp_count, local_width),
        "sp",
        split_axis=1,
        concat_axis=0,
        tiled=True,
    )
    scaled_grad = scaled_grad.reshape(group_rows, local_heads, head_width).astype(jnp.float32)
    gain_part = jnp.sum(scaled_grad * attended, axis=(0, 2))
    attended_grad = (scaled_grad * head_gain[None, :, None]).astype(jnp.bfloat16)
    row_dots = jnp.sum(attended_grad.astype(jnp.float32) * attended, axis=2)
    query_grad, key_grad, value_grad = attend_backward(
        queries,
        key_rows,
        value_rows,
        attended_grad,
        row_dots,
        log_sums,
        segment,
        keep_key,
        factor,
        block_rows,
    )
    stacked = jnp.stack(
        [
            query_grad.reshape(group_rows, local_width),
            key_grad.reshape(group_rows, local_width),
            value_grad.reshape(group_rows, local_width),
        ],
        axis=1,
    )
    stacked = stacked.astype(jnp.bfloat16)[:, :, None, :]
    qkv_grad = lax.all_to_all(stacked, "sp", split_axis=0, concat_axis=2, tiled=True).reshape(
        local_rows, 3 * model_width
    )
    first_grad = contract_cols(qkv_grad, full_qkv)
    input_part, grad_gain_in, grad_shift_in = norm_backward(
        first_grad, first_normed, first_std, model_gains[0]
    )
    grad_tokens = middle_grad + input_part
    qkv_sums = jnp.sum(qkv_grad.astype(jnp.float32), axis=0)
    gains_term = jnp.stack([grad_gain_in, grad_gain_attn, grad_gain_ffn])
    shifts_term = jnp.stack(
        [
            qkv_sums[:model_width],
            qkv_sums[2 * model_width :],
            jnp.sum(attn_grad.astype(jnp.float32), axis=0),
            grad_shift_in,
            grad_shift_attn,
            grad_shift_ffn,
            jnp.sum(upstream, axis=0),
        ]
    )
    hidden_term = jnp.stack([jnp.sum(pre_grad.astype(jnp.float32), axis=0), grad_mid_shift])
    scale_term = lax.dynamic_update_slice_in_dim(
        jnp.zeros((head_count,), jnp.float32), gain_part, sp_place * local_heads, 0
    )
    grad_model_gains, grad_model_shifts, grad_mid_gain, grad_hidden_shifts, grad_head_scale = (
        lax.psum((gains_term, shifts_term, grad_mid, hidden_term, scale_term), ("dp", "sp"))
    )
    term_qkv = contract_rows(first_norm, qkv_grad)
    term_out = contract_rows(merged, attn_grad)
    term_up = contract_rows(second_norm, pre_grad)
    term_down = contract_rows(upstream_low, hidden)
    summed_qkv, summed_out, summed_up, summed_down = (
        lax.psum_scatter(
            term_qkv.astype(jnp.bfloat16), "sp", scatter_dimension=1, tiled=True
        ).astype(jnp.float32),
        lax.psum_scatter(
            term_out.astype(jnp.bfloat16), "sp", scatter_dimension=1, tiled=True
        ).astype(jnp.float32),
        lax.psum_scatter(
            term_up.astype(jnp.bfloat16), "sp", scatter_dimension=1, tiled=True
        ).astype(jnp.float32),
        lax.psum_scatter(
            term_down.astype(jnp.bfloat16), "sp", scatter_dimension=1, tiled=True
        ).astype(jnp.float32),
    )
    grad_w_qkv, grad_w_out, grad_w_up, grad_w_down = (
        lax.psum_scatter(
            summed_qkv.astype(jnp.bfloat16), "dp", scatter_dimension=0, tiled=True
        ).astype(jnp.float32),
        lax.psum_scatter(
            summed_out.astype(jnp.bfloat16), "dp", scatter_dimension=0, tiled=True
        ).astype(jnp.float32),
        lax.psum_scatter(
            summed_up.astype(jnp.bfloat16), "dp", scatter_dimension=0, tiled=True
        ).astype(jnp.float32),
        lax.psum_scatter(
            summed_down.astype(jnp.bfloat16), "dp", scatter_dimension=0, tiled=True
        ).astype(jnp.float32),
    )
    return (
        layer_out,
        grad_tokens,
        grad_w_qkv,
        grad_w_out,
        grad_w_up,
        grad_w_down,
        grad_model_gains,
        grad_model_shifts,
        grad_mid_gain,
        grad_hidden_shifts,
        grad_head_scale,
    )


def solution(mesh):
    placed = (
        P(("dp", "sp"), None),
        P("dp", None),
        P(("dp", "sp")),
        P(("dp", "sp"), None),
        P("dp", "sp"),
        P("dp", "sp"),
        P("dp", "sp"),
        P("dp", "sp"),
        P(),
        P(),
        P(),
        P(),
        P(),
    )
    return jax.shard_map(
        per_device,
        mesh=mesh,
        in_specs=placed,
        out_specs=(
            P(("dp", "sp"), None),
            P(("dp", "sp"), None),
            P("dp", "sp"),
            P("dp", "sp"),
            P("dp", "sp"),
            P("dp", "sp"),
            P(),
            P(),
            P(),
            P(),
            P(),
        ),
        check_vma=False,
    )
```

profile of v0, /device:TPU:0, one launch (start us, length us, event | category | flops | bytes accessed | tf_op | source)
XLA Modules:
  0.0 1284.8 jit_solution(14648790442678717087)
XLA Ops:
  8.7 48.4 %all-gather.8.cloned.1.call-done = bf16[1024,768]{1,0:T(8,128)(2,1)} async-done(((bf16[128,768]{1,0:T(8,128)(2,1)}), bf16[1024,768]{1,0:T(8,128)(2,1)}) %all-gather.8.cloned.1.call-update) | async-done | bytes 1572880 | tf_op jit(solution)/shard_map/all_gather | solution.py:155
  57.8 34.4 %all_gather.26 = bf16[1024,256]{1,0:T(8,128)(2,1)} all-gather(bf16[128,256]{1,0:T(8,128)(2,1)} %param.22), channel_id=1, replica_groups=mesh['dp'=8,'sp'=4] {'dp'}, dimensions={0}, use_global_device_ids=true | all-gather | bytes 589824 | tf_op jit(solution)/shard_map/all_gather | solution.py:156
  92.2 17.5 %all-gather.14.cloned.1.call-done = bf16[1024,1024]{1,0:T(8,128)(2,1)} async-done(((bf16[128,1024]{1,0:T(8,128)(2,1)}), bf16[1024,1024]{1,0:T(8,128)(2,1)}) %all-gather.14.cloned.1.call-update) | async-done | bytes 2097168 | tf_op jit(solution)/shard_map/all_gather | solution.py:157
  117.4 39.1 %all-gather.10.cloned.1.call-done = bf16[1024,3072]{1,0:T(8,128)(2,1)} async-done(((bf16[1024,768]{1,0:T(8,128)(2,1)}), bf16[1024,3072]{1,0:T(8,128)(2,1)}) %all-gather.10.cloned.1.call-update) | async-done | bytes 6291472 | tf_op jit(solution)/shard_map/all_gather | solution.py:161
  156.6 7.8 add_convert_fusion.1
  164.4 5.5 reshape.424
  172.1 3.8 all-to-all-start.1
  177.2 30.7 %all-gather.18.cloned.1.call-done = bf16[1024,1024]{1,0:T(8,128)(2,1)} async-done(((bf16[128,1024]{1,0:T(8,128)(2,1)}), bf16[1024,1024]{1,0:T(8,128)(2,1)}) %all-gather.18.cloned.1.call-update) | async-done | bytes 2097168 | tf_op jit(solution)/shard_map/all_gather | solution.py:158
  207.9 5.0 all-to-all-done.1
  216.2 63.6 %while.29 = (s32[]{:T(128)}, f32[4,512,4,64]{1,3,2,0:T(8,128)}, f32[4,4,512]{2,1,0:T(4,128)S(1)}, s32[4]{0:T(128)S(1)}, s32[2048]{0:T(1024)S(1)}, /*index=5*/pre...) while((s32[]{:T(128)}, f32[4,512,4,64]{1,3,2,0:T(8,128)}, ...), condition=%wide.region_7.8_spmd.clone, body=%wide.region_4.7_spmd.sunk.clone | while | flops 1128266240 | bytes 61690072 | solution.py:73
  222.3 4.3 fusion.146
  226.6 5.5 fusion.147
  238.2 4.3 fusion.146
  242.5 5.5 fusion.147
  254.1 4.3 fusion.146
  258.4 5.5 fusion.147
  270.0 4.3 fusion.146
  274.4 5.5 fusion.147
  279.9 4.7 copy.100
  284.6 3.7 reshape.425
  294.1 4.2 all-to-all-start.2
  299.0 23.5 %all-to-all-done.2 = bf16[4,2,65536]{2,1,0:T(2,128)(2,1)} async-done(((bf16[4,2,65536]{2,1,0:T(2,128)(2,1)}), bf16[4,2,65536]{2,1,0:T(2,128)(2,1)}, u32[]{:S(2)}, u32[]{:S(2)}) %all-to-all-start.2) | async-done | bytes 1048608 | tf_op jit(solution)/shard_map/all_to_all | solution.py:195
  328.7 3.4 add_reduce_fusion
  335.1 9.8 fusion.69
  344.9 3.9 multiply_reduce_fusion.2
  348.9 10.6 all-gather.20.cloned.1.call-done
  359.5 12.8 multiply_reduce_fusion
  372.4 9.8 convert_reduce_fusion
  382.2 9.6 multiply_reduce_fusion.5
  399.7 4.3 all-to-all-start.3
  405.1 4.2 convolution_convert_fusion.3
  409.4 9.2 all-to-all-done.3
  426.8 3.9 reshape.429
  433.4 154.4 %while.30 = (s32[]{:T(128)}, f32[2048,4,64]{0,2,1:T(8,128)S(1)}, f32[2048,4,64]{0,2,1:T(8,128)}, bf16[4,512,4,64]{1,3,2,0:T(8,128)(2,1)}, s32[4]{0:T(128)S(1)}, ...) while((s32[]{:T(128)}, f32[2048,4,64]{0,2,1:T(8,128)S(1)}, ...), condition=%wide.region_22.23_spmd.clone.clone, body=%wide.region_21.22_spmd.clone.sunk.clone | while | flops 2733244928 | bytes 167326032 | solution.py:123
  439.7 3.3 fusion.158
  443.0 5.7 copy-done
  448.8 7.6 fusion.161
  456.3 10.0 multiply_convert_fusion.8
  477.9 3.3 fusion.158
  481.3 5.7 copy-done
  487.0 7.9 fusion.161
  494.9 10.0 multiply_convert_fusion.8
  519.8 5.7 copy-done
  525.5 7.9 fusion.161
  533.4 10.0 multiply_convert_fusion.8
  558.3 5.7 copy-done
  564.1 7.9 fusion.161
  572.0 10.0 multiply_convert_fusion.8
  593.7 4.9 copy.107
  598.6 51.9 %all_to_all.66 = bf16[2048,3,1,256]{3,1,2,0:T(4,128)(2,1)S(1)} all-to-all(bf16[2048,3,1,256]{3,1,2,0:T(4,128)(2,1)} %copy.107), channel_id=1, replica_groups=mesh['dp'=8,'sp'=4] {'sp'}, dimensions={0} | all-to-all | bytes 6291456 | tf_op jit(solution)/shard_map/all_to_all | solution.py:258
  653.9 8.6 convolution_convert_fusion.2
  663.2 11.4 convolution_convert_fusion
  675.3 11.2 convolution_convert_fusion.1
  687.2 33.6 %reduce-scatter.9.cloned.1.call-done = bf16[1024,768]{1,0:T(8,128)(2,1)} async-done(((bf16[1024,3072]{1,0:T(8,128)(2,1)}), bf16[1024,768]{1,0:T(8,128)(2,1)}) %reduce-scatter.9.cloned.1.call-update) | async-done | bytes 1572880 | tf_op jit(solution)/shard_map/reduce_scatter | solution.py:291
  720.9 74.1 %reduce-scatter.21.cloned.1.call-done = bf16[1024,1024]{1,0:T(8,128)(2,1)} async-done(((bf16[1024,4096]{1,0:T(8,128)(2,1)}), bf16[1024,1024]{1,0:T(8,128)(2,1)}) %reduce-scatter.21.cloned.1.call-update) | async-done | bytes 2097168 | tf_op jit(solution)/shard_map/reduce_scatter | solution.py:300
  795.8 73.8 %reduce-scatter.17.cloned.1.call-done = bf16[1024,1024]{1,0:T(8,128)(2,1)} async-done(((bf16[1024,4096]{1,0:T(8,128)(2,1)}), bf16[1024,1024]{1,0:T(8,128)(2,1)}) %reduce-scatter.17.cloned.1.call-update) | async-done | bytes 2097168 | tf_op jit(solution)/shard_map/reduce_scatter | solution.py:297
  869.7 12.9 %add_convert_fusion.2 = bf16[512,1024]{1,0:T(8,128)(2,1)} fusion(f32[512,1024]{1,0:T(8,128)} %copy-done.3, bf16[1024,4096]{1,0:T(8,128)(2,1)} %all-gather.20.cloned.1.call-done, f32[1024]{0:T(1024)S(1)} %bitcast.234, f32[4096]{0:T(1024)S(1)} %bitcast.228, f32[4096]{0:T(1024)S(1)} %copy-done.45, f32[512]{0:T(512)S(1)} %copy-done.50, f32[512]{0:T(512)S(1)} %copy-done.32, ...), kind=kOutput, calls=%fused_computation.102 | convolution fusion | flops 4325900288 | bytes 19980288 | tf_op jit(solution)/shard_map/dot_general | solution.py:35
  883.4 9.4 fusion.58
  894.2 3.6 fusion.57
  897.8 36.9 %reduce-scatter.15.cloned.1.call-done = bf16[128,256]{1,0:T(8,128)(2,1)} async-done(((bf16[1024,256]{1,0:T(8,128)(2,1)}), bf16[128,256]{1,0:T(8,128)(2,1)}) %reduce-scatter.15.cloned.1.call-update) | async-done | bytes 65552 | tf_op jit(solution)/shard_map/reduce_scatter | solution.py:308
  936.2 66.2 %reduce-scatter.11.cloned.1.call-done = bf16[128,768]{1,0:T(8,128)(2,1)} async-done(((bf16[1024,768]{1,0:T(8,128)(2,1)}), bf16[128,768]{1,0:T(8,128)(2,1)}) %reduce-scatter.11.cloned.1.call-update) | async-done | bytes 196624 | tf_op jit(solution)/shard_map/reduce_scatter | solution.py:305
  1004.1 68.3 %reduce-scatter.23.cloned.1.call-done = bf16[128,1024]{1,0:T(8,128)(2,1)} async-done(((bf16[1024,1024]{1,0:T(8,128)(2,1)}), bf16[128,1024]{1,0:T(8,128)(2,1)}) %reduce-scatter.23.cloned.1.call-update) | async-done | bytes 262160 | tf_op jit(solution)/shard_map/reduce_scatter | solution.py:314
  1074.2 68.2 %reduce-scatter.19.cloned.1.call-done = bf16[128,1024]{1,0:T(8,128)(2,1)} async-done(((bf16[1024,1024]{1,0:T(8,128)(2,1)}), bf16[128,1024]{1,0:T(8,128)(2,1)}) %reduce-scatter.19.cloned.1.call-update) | async-done | bytes 262160 | tf_op jit(solution)/shard_map/reduce_scatter | solution.py:311
  1144.1 127.3 %all-reduce.3.cloned.1.call-done = (f32[3,1024]{1,0:T(4,128)}, f32[7,1024]{1,0:T(8,128)}, f32[4096]{0:T(1024)}, f32[2,4096]{1,0:T(2,128)}, f32[16]{0:T(128)}) async-done(((f32[3,1024]{1,0:T(4,128)}, f32[7,1024]{1,0:T(8,128)}, f32[4096]{0:T(1024)}, f32[2,4096]{1,0:T(2,128)}, f32[16]{0:T(128)}), (f32[3,1024]{1,0:T(4,128)}, f32[7,1024]{1,0:T(8,128)}, f32[4096]{0:T(1024)}, f32[2,4096]{1,0:T(2,128)}, ...) | async-done | bytes 90192 | tf_op jit(solution)/shard_map/psum | solution.py:284
  (353 shorter events, 142.8 us)
Async XLA Ops:
  7.2 102.6 %copy-start.65 = (s32[512]{0:T(512)S(1)}, s32[512]{0:T(512)}, u32[]{:S(2)}) copy-start(s32[512]{0:T(512)} %param.19) | copy-start | bytes 6148
  7.2 108.3 %copy-start.26 = (f32[7,1024]{1,0:T(8,128)S(1)}, f32[7,1024]{1,0:T(8,128)}, u32[]{:S(2)}) copy-start(f32[7,1024]{1,0:T(8,128)} %param.26) | copy-start | bytes 86020
  7.2 108.9 %copy-start.7 = (bf16[512,1024]{1,0:T(8,128)(2,1)S(1)}, bf16[512,1024]{1,0:T(8,128)(2,1)}, u32[]{:S(2)}) copy-start(bf16[512,1024]{1,0:T(8,128)(2,1)} %param.17) | copy-start | bytes 3145732
  7.2 109.6 %copy-start.46 = (f32[3,1024]{1,0:T(4,128)S(1)}, f32[3,1024]{1,0:T(4,128)}, u32[]{:S(2)}) copy-start(f32[3,1024]{1,0:T(4,128)} %param.25) | copy-start | bytes 36868
  7.2 49.9 %all-gather.8.cloned.1.call-start = ((), (), s32[]{:S(2)}) async-start(), calls=%async_computation.13 | async-start | bytes 1769472 | tf_op jit(solution)/shard_map/all_gather | solution.py:155
  8.0 101.8 %all-gather.14.cloned.1.call-start = ((), (), s32[]{:S(2)}) async-start(), calls=%async_computation.16 | async-start | bytes 2359296 | tf_op jit(solution)/shard_map/all_gather | solution.py:157
  8.7 147.8 %all-gather.10.cloned.1.call-start = ((), (), s32[]{:S(2)}) async-start(), calls=%async_computation.14 | async-start | bytes 7864320 | tf_op jit(solution)/shard_map/all_gather | solution.py:161
  57.2 150.7 %all-gather.18.cloned.1.call-start = ((), (), s32[]{:S(2)}) async-start(), calls=%async_computation.18 | async-start | bytes 2359296 | tf_op jit(solution)/shard_map/all_gather | solution.py:158
  57.8 270.9 %all-gather.12.cloned.1.call-start = ((), (), s32[]{:S(2)}) async-start(), calls=%async_computation.15 | async-start | bytes 2621440 | tf_op jit(solution)/shard_map/all_gather | solution.py:162
  92.2 242.9 %all-gather.16.cloned.1.call-start = ((), (), s32[]{:S(2)}) async-start(), calls=%async_computation.17 | async-start | bytes 10485760 | tf_op jit(solution)/shard_map/all_gather | solution.py:163
  112.2 59.9 %all-to-all-start = ((bf16[4,2,256]{2,1,0:T(2,128)(2,1)}), bf16[4,2,256]{2,1,0:T(2,128)(2,1)S(1)}, u32[]{:S(2)}, u32[]{:S(2)}) async-start(bf16[4,2,256]{2,1,0:T(2,128)(2,1)} %reshape.433), calls=%async_computation | async-start | bytes 8192 | tf_op jit(solution)/shard_map/all_to_all | solution.py:179
  116.1 40.4 %copy-start.61 = (f32[1,1024]{1,0:T(1,128)}, f32[1,1024]{1,0:T(1,128)S(1)}, u32[]{:S(2)}) copy-start(f32[1,1024]{1,0:T(1,128)S(1)} %get-tuple-element.286) | copy-start | bytes 12292
  116.4 40.2 %copy-start.29 = (f32[512]{0:T(512)}, f32[512]{0:T(512)S(1)}, u32[]{:S(2)}) copy-start(f32[512]{0:T(512)S(1)} %broadcast_multiply_fusion.11) | copy-start | bytes 6148
  116.8 39.7 %copy-start.53 = (f32[512]{0:T(512)}, f32[512]{0:T(512)S(1)}, u32[]{:S(2)}) copy-start(f32[512]{0:T(512)S(1)} %add_rsqrt_fusion.3) | copy-start | bytes 6148
  117.4 39.1 %copy-start.35 = (f32[1,1024]{1,0:T(1,128)}, f32[1,1024]{1,0:T(1,128)S(1)}, u32[]{:S(2)}) copy-start(f32[1,1024]{1,0:T(1,128)S(1)} %get-tuple-element.289) | copy-start | bytes 12292
  172.1 40.7 %all-to-all-start.1 = ((bf16[512,3,4,256]{3,0,1,2:T(8,128)(2,1)}), bf16[512,3,4,256]{3,0,1,2:T(8,128)(2,1)S(1)}, u32[]{:S(2)}, u32[]{:S(2)}) async-start(bf16[512,3,4,256]{3,0,1,2:T(8,128)(2,1)} %copy.95), calls=%async_computation.1 | async-start | bytes 6291456 | tf_op jit(solution)/shard_map/all_to_all | solution.py:178
  176.0 183.5 %all-gather.20.cloned.1.call-start = ((), (), s32[]{:S(2)}) async-start(), calls=%async_computation.19 | async-start | bytes 10485760 | tf_op jit(solution)/shard_map/all_gather | solution.py:164
  279.8 8.4 copy-start.2
  279.8 8.4 copy-start.57
  290.0 8.4 copy-start.25
  294.1 28.4 %all-to-all-start.2 = ((bf16[4,2,65536]{2,1,0:T(2,128)(2,1)}), bf16[4,2,65536]{2,1,0:T(2,128)(2,1)}, u32[]{:S(2)}, u32[]{:S(2)}) async-start(bf16[4,2,65536]{2,1,0:T(2,128)(2,1)} %reshape.435), calls=%async_computation.2 | async-start | bytes 2097152 | tf_op jit(solution)/shard_map/all_to_all | solution.py:195
  299.0 73.3 %copy-start.21 = (f32[1,4096]{1,0:T(1,128)}, f32[1,4096]{1,0:T(1,128)S(1)}, u32[]{:S(2)}) copy-start(f32[1,4096]{1,0:T(1,128)S(1)} %get-tuple-element.279) | copy-start | bytes 49156
  299.0 29.7 %copy-start.20 = (f32[1,1024]{1,0:T(1,128)S(1)}, f32[1,1024]{1,0:T(1,128)}, u32[]{:S(2)}) copy-start(f32[1,1024]{1,0:T(1,128)} %get-tuple-element.283) | copy-start | bytes 12292
  333.3 58.6 %copy-start.27 = (f32[512]{0:T(512)}, f32[512]{0:T(512)S(1)}, u32[]{:S(2)}) copy-start(f32[512]{0:T(512)S(1)} %broadcast_multiply_fusion.9) | copy-start | bytes 6148
  335.0 56.9 %copy-start.51 = (f32[512]{0:T(512)}, f32[512]{0:T(512)S(1)}, u32[]{:S(2)}) copy-start(f32[512]{0:T(512)S(1)} %add_rsqrt_fusion.1) | copy-start | bytes 6148
  344.9 27.4 %copy-start.31 = (f32[512]{0:T(512)}, f32[512]{0:T(512)S(1)}, u32[]{:S(2)}) copy-start(f32[512]{0:T(512)S(1)} %broadcast_multiply_fusion.2) | copy-start | bytes 6148
  344.9 14.6 %copy-start.44 = (f32[4096]{0:T(1024)S(1)}, f32[4096]{0:T(1024)}, u32[]{:S(2)}) copy-start(f32[4096]{0:T(1024)} %param.27) | copy-start | bytes 49156
  344.9 14.6 %copy-start.47 = (f32[512]{0:T(512)S(1)}, f32[512]{0:T(512)}, u32[]{:S(2)}) copy-start(f32[512]{0:T(512)} %get-tuple-element.293) | copy-start | bytes 6148
  348.9 23.5 %copy-start.49 = (f32[512]{0:T(512)}, f32[512]{0:T(512)S(1)}, u32[]{:S(2)}) copy-start(f32[512]{0:T(512)S(1)} %add_rsqrt_fusion) | copy-start | bytes 6148
  359.5 12.8 slice-start
  359.5 12.8 slice-start.1
  372.4 9.9 copy-start.4
  382.2 9.6 copy-start.14
  382.2 9.7 copy-start.17
  399.7 18.8 %all-to-all-start.3 = ((bf16[512,4,256]{2,0,1:T(8,128)(2,1)}), bf16[512,4,256]{2,0,1:T(8,128)(2,1)}, u32[]{:S(2)}, u32[]{:S(2)}) async-start(bf16[512,4,256]{2,0,1:T(8,128)(2,1)} %bitcast.129), calls=%async_computation.3 | async-start | bytes 2097152 | tf_op jit(solution)/shard_map/all_to_all | solution.py:226
  404.0 282.7 %reduce-scatter.13.cloned.1.call-start = ((), (), s32[]{:S(2)}) async-start(), calls=%async_computation.22 | async-start | bytes 2621440 | tf_op jit(solution)/shard_map/reduce_scatter | solution.py:294
  409.3 13.5 %copy-start.56 = (f32[4]{0:T(128)S(1)}, f32[4]{0:T(128)}, u32[]{:S(2)}) copy-start(f32[4]{0:T(128)} %copy-done.55) | copy-start | bytes 52
  409.3 311.6 %reduce-scatter.9.cloned.1.call-start = ((), (), s32[]{:S(2)}) async-start(), calls=%async_computation.20 | async-start | bytes 7864320 | tf_op jit(solution)/shard_map/reduce_scatter | solution.py:291
  443.0 5.7 copy-start
  456.3 10.0 copy-start.11
  481.2 5.7 copy-start
  494.9 10.0 copy-start.11
  533.4 10.0 copy-start.11
  572.0 10.0 copy-start.11
  662.5 132.5 %reduce-scatter.21.cloned.1.call-start = ((), (), s32[]{:S(2)}) async-start(), calls=%async_computation.26 | async-start | bytes 10485760 | tf_op jit(solution)/shard_map/reduce_scatter | solution.py:300
  674.7 194.9 %reduce-scatter.17.cloned.1.call-start = ((), (), s32[]{:S(2)}) async-start(), calls=%async_computation.24 | async-start | bytes 10485760 | tf_op jit(solution)/shard_map/reduce_scatter | solution.py:297
  686.6 108.6 %copy-start.24 = (f32[4096]{0:T(1024)S(1)}, f32[4096]{0:T(1024)}, u32[]{:S(2)}) copy-start(f32[4096]{0:T(1024)} %get-tuple-element.264) | copy-start | bytes 49156
  686.6 108.6 %copy-start.42 = (f32[4096]{0:T(1024)S(1)}, f32[4096]{0:T(1024)}, u32[]{:S(2)}) copy-start(f32[4096]{0:T(1024)} %get-tuple-element.200) | copy-start | bytes 49156
  686.6 183.1 %copy-start.58 = (f32[1,1024]{1,0:T(1,128)S(1)}, f32[1,1024]{1,0:T(1,128)}, u32[]{:S(2)}) copy-start(f32[1,1024]{1,0:T(1,128)} %get-tuple-element.287) | copy-start | bytes 12292
  686.6 248.1 %reduce-scatter.15.cloned.1.call-start = ((), (), s32[]{:S(2)}) async-start(), calls=%async_computation.23 | async-start | bytes 589824 | tf_op jit(solution)/shard_map/reduce_scatter | solution.py:308
  687.2 315.2 %reduce-scatter.11.cloned.1.call-start = ((), (), s32[]{:S(2)}) async-start(), calls=%async_computation.21 | async-start | bytes 1769472 | tf_op jit(solution)/shard_map/reduce_scatter | solution.py:305
  720.9 351.5 %reduce-scatter.23.cloned.1.call-start = ((), (), s32[]{:S(2)}) async-start(), calls=%async_computation.27 | async-start | bytes 2359296 | tf_op jit(solution)/shard_map/reduce_scatter | solution.py:314
  795.1 347.3 %reduce-scatter.19.cloned.1.call-start = ((), (), s32[]{:S(2)}) async-start(), calls=%async_computation.25 | async-start | bytes 2359296 | tf_op jit(solution)/shard_map/reduce_scatter | solution.py:311
  869.6 401.8 %all-reduce.3.cloned.1.call-start = ((), (), s32[]{:S(2)}) async-start(), calls=%async_computation.28 | async-start | bytes 197632 | tf_op jit(solution)/shard_map/psum | solution.py:284
  869.7 12.9 %copy-start.66 = (f32[4]{0:T(128)S(1)}, f32[4]{0:T(128)}, u32[]{:S(2)}) copy-start(f32[4]{0:T(128)} %get-tuple-element.205) | copy-start | bytes 52
  882.8 10.0 copy-start.67
  883.3 9.5 copy-start.39
  883.3 9.5 copy-start.40
  883.3 9.5 copy-start.43
  883.3 9.5 copy-start.64
  883.3 10.2 copy-start.34
  883.3 10.2 copy-start.63
  883.3 10.8 copy-start.6
  883.4 10.8 copy-start.9
  (40 other events, 104.6 us)
Sparse Core Ops, SparseCore 0:
  10.2 46.8 all-gather.7
  59.3 50.4 all-gather.13
  111.3 45.1 all-gather.9
  158.5 49.2 all-gather.17
  209.3 21.3 all-gather.11
  232.0 58.2 all-gather.15
  291.9 67.5 all-gather.19
  409.4 32.7 reduce-scatter.12
  662.6 58.1 reduce-scatter.8
  723.3 71.7 reduce-scatter.20
  797.8 71.7 reduce-scatter.16
  872.8 61.8 reduce-scatter.14
  938.5 63.8 reduce-scatter.10
  1005.8 66.5 reduce-scatter.22
  1075.7 66.5 reduce-scatter.18
  1149.8 121.6 all-reduce.2
where the time goes:
time: 1290 us; the launch traced here: 1280 us
  waiting for transfers between devices  735 us (57%)
  matrix products  244 us (19%)
  local copies, waits for them, and re-layouts  95.6 us (7%)
  blocking collectives  86.3 us (7%)
  other arithmetic  77.3 us (6%)
  starting transfers between devices  16.5 us (1%)
  between operations  15.2 us (1%)
  loops' own time  14.7 us (1%)
    psum x1, waiting for transfers between devices, per_device(): lax.psum((gains_term, shifts_term, grad_mid, hidden_term, scale_term), ('...  127 us
    reduce_scatter x1, waiting for transfers between devices, per_device(): lax.psum_scatter(term_down.astype(jnp.bfloat16), 'sp', scatter_dimension=...  74.1 us
    reduce_scatter x1, waiting for transfers between devices, per_device(): lax.psum_scatter(term_up.astype(jnp.bfloat16), 'sp', scatter_dimension=1,...  73.8 us
    reduce_scatter x1, waiting for transfers between devices, per_device(): lax.psum_scatter(summed_down.astype(jnp.bfloat16), 'dp', scatter_dimensio...  68.3 us
    reduce_scatter x1, waiting for transfers between devices, per_device(): lax.psum_scatter(summed_up.astype(jnp.bfloat16), 'dp', scatter_dimension=...  68.2 us
    reduce_scatter x1, waiting for transfers between devices, per_device(): lax.psum_scatter(summed_qkv.astype(jnp.bfloat16), 'dp', scatter_dimension...  66.2 us
    all_to_all x1, blocking collectives, per_device(): lax.all_to_all(stacked, 'sp', split_axis=0, concat_axis=2, tiled=True)  51.9 us
    all_gather x1, waiting for transfers between devices, per_device(): lax.all_gather(w_qkv, 'dp', axis=0, tiled=True)  48.4 us
  transfers between devices with their start and end apart: 20, of which 16 were waited for; matrix products, arithmetic and copies ran while one was open for 27% of the time, Pallas kernels for 0%

commit v1 on v0

v1 whole, which is shorter than its diff:
```python
import functools

import jax
import jax.numpy as jnp
import numpy as np
from jax import lax
from jax.experimental import pallas as pl
from jax.experimental.pallas import tpu as pltpu
from jax.sharding import PartitionSpec as P

EPSILON = 1e-05
MASKED = -1e30
HEAD = 64
BQ = 256
bf16 = jnp.bfloat16
f32 = jnp.float32


def mm(a, b):
    return lax.dot_general(a, b, (((1,), (0,)), ((), ())), preferred_element_type=f32)


def mm_rows(a, b):
    return lax.dot_general(a, b, (((0,), (0,)), ((), ())), preferred_element_type=f32)


def mm_cols(a, b):
    return lax.dot_general(a, b, (((1,), (1,)), ((), ())), preferred_element_type=f32)


def skipping(kernel, at, count):
    return lambda *refs: kernel(*refs[:at], *refs[at + count :])


def unread(deps):
    return [pl.BlockSpec(memory_space=pl.ANY)] * len(deps)


def lanes_of(x, h):
    lane = lax.broadcasted_iota(jnp.int32, x.shape, 1) // HEAD
    return jnp.where(lane == h, x, jnp.zeros_like(x))


def segment_of(spans, places):
    count, end = jnp.zeros_like(places), jnp.int32(0)
    for k in range(spans.shape[0]):
        end = end + spans[k]
        count = count + (places >= end).astype(jnp.int32)
    return count


class Heads:
    def __init__(self, nh, local, first, blocks, order_at, who_at, parts):
        self.nh, self.local, self.first, self.blocks = nh, local, first, blocks
        self.order_at, self.who_at, self.parts = order_at, who_at, parts


def keys_of(hd, tab, spans, keep_ref, kseg, bk):
    for j in range(hd.parts):
        at = pl.ds(pl.multiple_of(tab[hd.order_at + j] * bk, bk), bk)
        places = j * bk + lax.broadcasted_iota(jnp.int32, (bk, 1), 0)
        kseg[at, :] = jnp.where(keep_ref[at, :] > 0.5, segment_of(spans, places), -1)


def visible(i, j, bk, spans, kseg, at):
    kpos = j * bk + lax.broadcasted_iota(jnp.int32, (bk, BQ), 0)
    qpos = i * BQ + lax.broadcasted_iota(jnp.int32, (bk, BQ), 1)
    qseg = segment_of(spans, i * BQ + lax.broadcasted_iota(jnp.int32, (1, BQ), 1))
    return (kseg[at, :] == qseg) & (kpos <= qpos)


def each_block(hd, tab, spans, i, bk, body):
    first = segment_of(spans, i * BQ)

    def step(j, carry):
        at = pl.ds(pl.multiple_of(tab[hd.order_at + j] * bk, bk), bk)
        pl.when(first <= segment_of(spans, (j + 1) * bk - 1))(lambda: body(j, at))
        return carry

    lax.fori_loop(0, (i * BQ) // bk + 1, step, 0)


def fwd_kernel(hd, bk, tab, spans, q_ref, k_ref, v_ref, keep_ref, hs_ref, scaled_ref, o_ref, lse_ref,
               kseg, vms, sscr, mpart, lpart, acc):
    nh = hd.nh
    i = pl.program_id(0)

    @pl.when(i == 0)
    def _():
        for h in range(nh):
            vms[h] = lanes_of(v_ref[...], h)
        keys_of(hd, tab, spans, keep_ref, kseg, bk)

    qs = q_ref[...] * bf16(0.125)
    qm = [lanes_of(qs, h) for h in range(nh)]
    mpart[...] = jnp.full_like(mpart, MASKED)
    lpart[...] = jnp.zeros_like(lpart)
    acc[...] = jnp.zeros_like(acc)

    def one(j, at):
        kb = k_ref[at, :]
        mask = visible(i, j, bk, spans, kseg, at)
        for h in range(nh):
            s = jnp.where(mask, mm_cols(kb, qm[h]), MASKED)
            sscr[h, at, :] = s
            mpart[h] = jnp.maximum(mpart[h], jnp.max(s.reshape(bk // 8, 8, BQ), axis=0))

    each_block(hd, tab, spans, i, bk, one)
    ms = [jnp.max(mpart[h], axis=0, keepdims=True) for h in range(nh)]

    def two(j, at):
        pts = []
        for h in range(nh):
            p = jnp.exp(sscr[h, at, :] - ms[h])
            lpart[h] += jnp.sum(p.reshape(bk // 8, 8, BQ), axis=0)
            pts.append(p.astype(bf16).T)
        acc[...] += mm(
            jnp.concatenate(pts, axis=1),
            jnp.concatenate([vms[h, at, :] for h in range(nh)], axis=0),
        )

    each_block(hd, tab, spans, i, bk, two)
    out_t = acc[...].T
    parts = []
    for h in range(nh):
        rows = slice(h * HEAD, (h + 1) * HEAD)
        total = jnp.sum(lpart[h], axis=0, keepdims=True)
        result = out_t[rows, :] * (1.0 / total)
        o_ref[rows, :] = result
        parts.append(result * hs_ref[0, tab[hd.who_at] * hd.local + hd.first + h])
        lse_ref[h : h + 1, :] = ms[h] + jnp.log(total)
    scaled_ref[...] = jnp.concatenate(parts, axis=0).T.astype(bf16)


def head_specs(hd, n, w, bk):
    q, k, v = hd.blocks
    ratio = bk // BQ
    return [
        pl.BlockSpec((BQ, w), lambda i, t, s: (t[hd.order_at + (i * BQ) // bk] * ratio + i % ratio, q)),
        pl.BlockSpec((n, w), lambda i, t, s: (0, k)),
        pl.BlockSpec((n, w), lambda i, t, s: (0, v)),
    ]


def attend_forward(hd, tab, spans, qkv, keep, head_scale, deps=()):
    n, nh, w = qkv.shape[0], hd.nh, hd.nh * HEAD
    bk = n // hd.parts
    return pl.pallas_call(
        skipping(functools.partial(fwd_kernel, hd, bk), 7, len(deps)),
        grid_spec=pltpu.PrefetchScalarGridSpec(
            num_scalar_prefetch=2,
            grid=(n // BQ,),
            in_specs=head_specs(hd, n, w, bk)
            + [pl.BlockSpec((n, 1), lambda i, t, s: (0, 0)), pl.BlockSpec(memory_space=pltpu.SMEM)]
            + unread(deps),
            out_specs=[
                pl.BlockSpec((BQ, w), lambda i, t, s: (i, 0)),
                pl.BlockSpec((w, BQ), lambda i, t, s: (0, i)),
                pl.BlockSpec((8, BQ), lambda i, t, s: (0, i)),
            ],
            scratch_shapes=[
                pltpu.VMEM((n, 1), jnp.int32),
                pltpu.VMEM((nh, n, w), bf16),
                pltpu.VMEM((nh, n, BQ), f32),
                pltpu.VMEM((nh, 8, BQ), f32),
                pltpu.VMEM((nh, 8, BQ), f32),
                pltpu.VMEM((BQ, w), f32),
            ],
        ),
        out_shape=[
            jax.ShapeDtypeStruct((n, w), bf16),
            jax.ShapeDtypeStruct((w, n), f32),
            jax.ShapeDtypeStruct((8, n), f32),
        ],
        compiler_params=pltpu.CompilerParams(vmem_limit_bytes=48 << 20),
        cost_estimate=pl.CostEstimate(
            flops=nh * n * n * HEAD * 26, bytes_accessed=n * w * 12, transcendentals=nh * n * n // 2
        ),
        name="attend_forward",
    )(tab, spans, qkv, qkv, qkv, keep, head_scale[None], *deps)


def bwd_kernel(hd, bk, tab, spans, q_ref, k_ref, v_ref, keep_ref, hs_ref, sg_ref, o_ref, lse_ref,
               grad_ref, sums_ref, kseg, dk, dv, dq, gacc, kms):
    nh = hd.nh
    i = pl.program_id(0)
    n, w = k_ref.shape[0], nh * HEAD

    @pl.when(i == 0)
    def _():
        dk[...] = jnp.zeros_like(dk)
        dv[...] = jnp.zeros_like(dv)
        gacc[...] = jnp.zeros_like(gacc)
        for h in range(nh):
            kms[h] = lanes_of(k_ref[...], h)
        keys_of(hd, tab, spans, keep_ref, kseg, bk)

    qs = q_ref[...] * bf16(0.125)
    qm = [lanes_of(qs, h) for h in range(nh)]
    scales = [hs_ref[0, tab[hd.who_at] * hd.local + hd.first + h] for h in range(nh)]
    sg = sg_ref[...].astype(f32)
    lane = lax.broadcasted_iota(jnp.int32, (1, w), 1) // HEAD
    scale_row = jnp.zeros((1, w), f32)
    for h in range(nh):
        scale_row = jnp.where(lane == h, scales[h], scale_row)
    grads = (sg * scale_row).astype(bf16)
    dom = [lanes_of(grads, h) for h in range(nh)]
    o = o_ref[...]
    gacc[...] += sg.T * o
    weighed = grads.astype(f32).T * o
    delta = [jnp.sum(weighed[h * HEAD : (h + 1) * HEAD, :], axis=0, keepdims=True) for h in range(nh)]
    lse = [lse_ref[h : h + 1, :] for h in range(nh)]
    qcat = jnp.concatenate(qm, axis=0)
    docat = jnp.concatenate(dom, axis=0)
    dq[...] = jnp.zeros_like(dq)

    def block(j, at):
        kb = k_ref[at, :]
        vb = v_ref[at, :]
        mask = visible(i, j, bk, spans, kseg, at)
        ps, dss, dsts = [], [], []
        for h in range(nh):
            p = jnp.where(mask, jnp.exp(mm_cols(kb, qm[h]) - lse[h]), 0.0)
            ds = (p * (mm_cols(vb, dom[h]) - delta[h])).astype(bf16)
            ps.append(p.astype(bf16))
            dsts.append(ds.T)
            dss.append(ds)
        dv[at, :] += mm(jnp.concatenate(ps, axis=1), docat)
        dk[at, :] += mm(jnp.concatenate(dss, axis=1), qcat)
        dq[...] += mm(
            jnp.concatenate(dsts, axis=1),
            jnp.concatenate([kms[h, at, :] for h in range(nh)], axis=0),
        )

    each_block(hd, tab, spans, i, bk, block)
    mine = tab[hd.order_at + (i * BQ) // bk] * bk + (i * BQ) % bk
    grad_ref[pl.ds(pl.multiple_of(mine, BQ), BQ), 0:w] = (dq[...] * 0.125).astype(bf16)

    @pl.when(i == n // BQ - 1)
    def _():
        grad_ref[:, w : 2 * w] = dk[...].astype(bf16)
        grad_ref[:, 2 * w : 3 * w] = dv[...].astype(bf16)
        place = lax.broadcasted_iota(jnp.int32, (1, 3 * w), 1)
        gains = jnp.zeros((1, 3 * w), f32)
        for h in range(nh):
            gains = jnp.where(place == h, jnp.sum(gacc[h * HEAD : (h + 1) * HEAD, :]), gains)
        sums_ref[...] = jnp.zeros_like(sums_ref)
        sums_ref[0:1, :] = jnp.sum(grad_ref[...].astype(f32), axis=0, keepdims=True)
        sums_ref[1:2, :] = gains


def attend_backward(hd, tab, spans, qkv, keep, head_scale, scaled_grad, o_t, lse, deps=()):
    n, nh, w = qkv.shape[0], hd.nh, hd.nh * HEAD
    bk = n // hd.parts
    return pl.pallas_call(
        skipping(functools.partial(bwd_kernel, hd, bk), 10, len(deps)),
        grid_spec=pltpu.PrefetchScalarGridSpec(
            num_scalar_prefetch=2,
            grid=(n // BQ,),
            in_specs=head_specs(hd, n, w, bk)
            + [
                pl.BlockSpec((n, 1), lambda i, t, s: (0, 0)),
                pl.BlockSpec(memory_space=pltpu.SMEM),
                pl.BlockSpec((BQ, w), lambda i, t, s: (i, 0)),
                pl.BlockSpec((w, BQ), lambda i, t, s: (0, i)),
                pl.BlockSpec((8, BQ), lambda i, t, s: (0, i)),
            ]
            + unread(deps),
            out_specs=[
                pl.BlockSpec((n, 3 * w), lambda i, t, s: (0, 0)),
                pl.BlockSpec((8, 3 * w), lambda i, t, s: (0, 0)),
            ],
            scratch_shapes=[
                pltpu.VMEM((n, 1), jnp.int32),
                pltpu.VMEM((n, w), f32),
                pltpu.VMEM((n, w), f32),
                pltpu.VMEM((BQ, w), f32),
                pltpu.VMEM((w, BQ), f32),
                pltpu.VMEM((nh, n, w), bf16),
            ],
        ),
        out_shape=[
            jax.ShapeDtypeStruct((n, 3 * w), bf16),
            jax.ShapeDtypeStruct((8, 3 * w), f32),
        ],
        compiler_params=pltpu.CompilerParams(vmem_limit_bytes=52 << 20),
        cost_estimate=pl.CostEstimate(
            flops=nh * n * n * HEAD * 42, bytes_accessed=n * w * 20, transcendentals=nh * n * n // 2
        ),
        name="attend_backward",
    )(tab, spans, qkv, qkv, qkv, keep, head_scale[None], scaled_grad, o_t, lse, *deps)


def swap(x, axis, bits):
    return lax.ppermute(x, axis, [(i, i ^ bits) for i in range(lax.axis_size(axis))])


def reorder(x, idx, width):
    rows, cols = x.shape
    return jnp.take(x.reshape(rows, cols // width, width), idx, axis=1).reshape(rows, cols)


def reorder_rows(x, idx, height):
    rows, cols = x.shape
    return jnp.take(x.reshape(rows // height, height, cols), idx, axis=0).reshape(rows, cols)


class Grid:
    def __init__(self, dp, sp):
        self.dp, self.sp = dp, sp
        self.nx = max(sp // 2, 1)
        self.ny = self.nx if dp % self.nx == 0 else 1
        self.nz = dp // self.ny
        self.z_bits = [self.ny * k for k in range(1, self.nz)]
        self.y_bits = list(range(1, self.ny))
        self.x_bits = [2 * k for k in range(1, self.nx)]

    def gather_z(self, w):
        return jnp.concatenate([w] + [swap(w, "dp", b) for b in self.z_bits], axis=0)

    def gather_y(self, w):
        return jnp.concatenate([w] + [swap(w, "dp", b) for b in self.y_bits], axis=0)

    def gather(self, w):
        half = w.shape[1] // 2
        rows = self.gather_z(w)
        first, other = rows[:, :half], rows[:, half:]
        first = self.gather_y(first)
        firsts = [first] + [swap(first, "sp", b) for b in self.x_bits]
        other = jnp.concatenate([other] + [swap(other, "sp", b) for b in self.x_bits], axis=1)
        other = self.gather_y(other)
        parts = []
        for k in range(self.nx):
            parts += [firsts[k], other[:, k * half : (k + 1) * half]]
        return jnp.concatenate(parts, axis=1)

    def fold(self, parts, axis, bits):
        total = parts[0].astype(f32)
        for part, b in zip(parts[1:], bits, strict=True):
            total = total + swap(part.astype(bf16), axis, b).astype(f32)
        return total

    def scatter_y(self, g):
        rows = g.shape[0] // self.ny
        return self.fold([g[k * rows : (k + 1) * rows] for k in range(self.ny)], "dp", self.y_bits)

    def scatter_z(self, g):
        rows = g.shape[0] // self.nz
        return self.fold([g[k * rows : (k + 1) * rows] for k in range(self.nz)], "dp", self.z_bits)

    def scatter_x(self, g):
        cols = g.shape[1] // self.nx
        return self.fold([g[:, k * cols : (k + 1) * cols] for k in range(self.nx)], "sp", self.x_bits)

    def scatter(self, g):
        cols = g.shape[1] // self.nx
        half = cols // 2
        first = jnp.concatenate([g[:, k * cols : k * cols + half] for k in range(self.nx)], axis=1)
        other = jnp.concatenate([g[:, k * cols + half : (k + 1) * cols] for k in range(self.nx)], axis=1)
        first = self.scatter_y(self.scatter_x(first))
        other = self.scatter_x(self.scatter_y(other))
        return self.scatter_z(jnp.concatenate([first, other], axis=1))

    def all_sum(self, v):
        for axis in ("sp", "dp"):
            bit = 1
            while bit < lax.axis_size(axis):
                v = v + swap(v, axis, bit)
                bit *= 2
        return v


def norm_forward(halves, gains, shifts):
    width = sum(h.shape[1] for h in halves)
    mean = sum(jnp.sum(h, axis=1, keepdims=True) for h in halves) / width
    centred = [h - mean for h in halves]
    inv_std = lax.rsqrt(sum(jnp.sum(c * c, axis=1, keepdims=True) for c in centred) / width + EPSILON)
    normed = [c * inv_std for c in centred]
    return [n * a + b for n, a, b in zip(normed, gains, shifts)], normed, inv_std


def norm_backward(incoming, normed, inv_std, gains):
    width = sum(h.shape[1] for h in incoming)
    scaled = [e * a for e, a in zip(incoming, gains)]
    mean = sum(jnp.sum(s, axis=1, keepdims=True) for s in scaled) / width
    along = sum(jnp.sum(s * n, axis=1, keepdims=True) for s, n in zip(scaled, normed)) / width
    grads = [inv_std * (s - mean - n * along) for s, n in zip(scaled, normed)]
    gain_sums = [jnp.sum(e * n, axis=0) for e, n in zip(incoming, normed)]
    return grads, gain_sums, [jnp.sum(e, axis=0) for e in incoming]


def general_layer(
    tokens,
    seq_spans,
    valid_mask,
    cotangent,
    w_qkv,
    w_out,
    w_up,
    w_down,
    model_gains,
    model_shifts,
    mid_gain,
    hidden_shifts,
    head_scale,
):
    dp, sp = lax.axis_size("dp"), lax.axis_size("sp")
    grid = Grid(dp, sp)
    nx, ny, nz = grid.nx, grid.ny, grid.nz
    me_d, me_s = lax.axis_index("dp"), lax.axis_index("sp")
    rows, width = tokens.shape
    group = rows * sp
    heads = head_scale.shape[0]
    nh = heads // sp
    lw = nh * HEAD
    block = width // dp
    ff = mid_gain.shape[0]

    place = jnp.arange(dp, dtype=jnp.int32)
    to_rel = ((place % nz) * ny + place // nz) ^ me_d
    away = place ^ me_d
    to_abs = (away % ny) * nz + away // ny
    sp_place = jnp.arange(sp, dtype=jnp.int32)
    sp_rel = ((sp_place % nx) * 2 + sp_place // nx) ^ me_s
    sp_away = sp_place ^ me_s
    sp_abs = (sp_away % 2) * nx + sp_away // 2

    pad_rows = 16
    valid_rows = rows // lw
    blocks = w_qkv.reshape(block, 3, lw).transpose(1, 0, 2)
    blocks = jnp.concatenate([blocks, jnp.zeros((sp - 3, block, lw), bf16)], axis=0)
    turned = jnp.concatenate(
        [lax.dynamic_slice_in_dim(blocks, (t - 3 * me_s) % sp, 1, 0) for t in range(sp)], axis=0
    )
    flag_rows = jnp.concatenate(
        [valid_mask.astype(bf16).reshape(valid_rows, lw), jnp.zeros((pad_rows - valid_rows, lw), bf16)], axis=0
    )
    sent = jnp.concatenate([turned, jnp.broadcast_to(flag_rows[None], (sp, pad_rows, lw))], axis=1)
    got = lax.all_to_all(sent, "sp", 0, 0, tiled=True)
    keep = got[:, block : block + valid_rows].reshape(group) > 0.5
    wq_shard = jnp.concatenate(
        [lax.dynamic_slice_in_dim(got, (t * sp + me_s) // 3, 1, 0)[0, :block] for t in range(3)], axis=1
    )
    wq = grid.gather_y(grid.gather_z(wq_shard))

    gains = reorder(model_gains, to_rel, block)
    shifts = reorder(model_shifts, to_rel, block)
    stream = reorder(tokens, to_rel, block).astype(f32)
    upstream = reorder(cotangent, to_rel, block) * valid_mask.astype(bf16)[:, None]
    (first_out,), (first_normed,), first_std = norm_forward([stream], gains[0:1], shifts[3:4])
    first = first_out.astype(bf16)

    crossed = [first] + [swap(first, "sp", b) for b in grid.x_bits]
    firsts = []
    for piece in crossed:
        firsts += [piece, swap(piece, "sp", 1)]
    piece_bits = [b for k in [0] + grid.x_bits for b in (k, k + 1)]
    qkv_shift = jnp.concatenate(
        [
            lax.dynamic_slice_in_dim(model_shifts[0], me_s * lw, lw, 0),
            jnp.zeros((lw,), f32),
            lax.dynamic_slice_in_dim(model_shifts[1], me_s * lw, lw, 0),
        ]
    )
    firsts_cat = jnp.concatenate(firsts, axis=0)
    qkv_rel = (mm(firsts_cat, wq) + qkv_shift).astype(bf16)
    group_order = sp_place ^ me_s
    qkv = reorder_rows(qkv_rel, group_order, rows)

    low_down = jnp.concatenate([w_out, w_down], axis=1)
    od_own = grid.gather(low_down)
    up_own = grid.gather(w_up)
    oc, dc = w_out.shape[1], w_down.shape[1]
    out_own = jnp.concatenate([od_own[:, k * (oc + dc) : k * (oc + dc) + oc] for k in range(nx)], axis=1)
    down_own = jnp.concatenate([od_own[:, k * (oc + dc) + oc : (k + 1) * (oc + dc)] for k in range(nx)], axis=1)
    wos = jnp.concatenate([out_own, swap(out_own, "sp", 1)], axis=1)
    downs = [down_own, swap(down_own, "sp", 1)]
    ups = [up_own, swap(up_own, "sp", 1)]
    wo = reorder(reorder_rows(wos, to_abs, block), sp_abs, oc)

    tab = jnp.concatenate([sp_place, me_s[None].astype(jnp.int32)])
    hd = Heads(nh, nh, 0, (0, 1, 2), 0, sp, sp)
    keep_col = keep.astype(f32)[:, None]
    scaled, o_t, lse = attend_forward(hd, tab, seq_spans[0], qkv, keep_col, head_scale)
    returned = lax.all_to_all(scaled.reshape(sp, rows, lw), "sp", 0, 0, tiled=True)
    merged = jnp.concatenate([returned[t] for t in range(sp)], axis=1)

    attn_pre = reorder(mm(merged, wo) + model_shifts[2], to_rel, block)
    (attn_out,), (attn_normed,), attn_std = norm_forward([attn_pre], gains[1:2], shifts[4:5])
    middle = stream + attn_out
    (second_out,), (second_normed,), second_std = norm_forward([middle], gains[2:3], shifts[5:6])
    second = second_out.astype(bf16)

    ff_half = ff // 2
    hidden_vectors = reorder(
        jnp.concatenate([mid_gain[None], hidden_shifts], axis=0), sp_rel, ff // sp
    )
    split = lambda v: [v[:, :ff_half], v[:, ff_half:]]
    hg, hb, hs = split(hidden_vectors[0:1]), split(hidden_vectors[1:2]), split(hidden_vectors[2:3])
    pre = [mm(second, w) + b for w, b in zip(ups, hb)]
    activated, pulls = zip(*[jax.vjp(jax.nn.gelu, p) for p in pre])
    hidden_out, hidden_normed, hidden_std = norm_forward(activated, hg, hs)
    hidden = [h.astype(bf16) for h in hidden_out]
    out_rel = middle + mm_cols(hidden[0], downs[0]) + mm_cols(hidden[1], downs[1]) + shifts[6:7]
    layer_out = reorder(out_rel.astype(bf16), to_abs, block)

    pair = lambda x: jnp.concatenate([x, swap(x, "sp", 1)], axis=0)
    across = lambda halves: jnp.concatenate([halves[0], swap(halves[1], "sp", 1)], axis=0)
    upstream_pair = pair(upstream)
    g_down = mm_rows(upstream_pair, across(hidden)).astype(bf16)
    grad_w_down = grid.scatter(g_down)

    hidden_grad = [mm(upstream, w) for w in downs]
    act_grad, grad_mid, grad_mid_shift = norm_backward(hidden_grad, hidden_normed, hidden_std, hg)
    pre_grad = [pull(a)[0].astype(bf16) for pull, a in zip(pulls, act_grad)]
    second_grad = mm_cols(pre_grad[0], ups[0]) + mm_cols(pre_grad[1], ups[1])
    (middle_part,), (gain_ffn,), (shift_ffn,) = norm_backward([second_grad], [second_normed], second_std, gains[2:3])
    middle_grad = upstream.astype(f32) + middle_part
    (attn_grad_full,), (gain_attn,), (shift_attn,) = norm_backward([middle_grad], [attn_normed], attn_std, gains[1:2])
    attn_grad_rel = attn_grad_full.astype(bf16)
    attn_grad = reorder(attn_grad_rel, to_abs, block)
    merged_grad = mm_cols(attn_grad, wo).astype(bf16)
    scattered = jnp.stack([merged_grad[:, t * lw : (t + 1) * lw] for t in range(sp)], axis=0)
    scaled_grad = lax.all_to_all(scattered, "sp", 0, 0, tiled=True).reshape(group, lw)

    g_up = mm_rows(pair(second), across(pre_grad)).astype(bf16)
    grad_w_up = grid.scatter(g_up)
    merged_rel = reorder(merged, to_rel, block)
    attn_grad_cols = reorder(attn_grad, sp_rel, oc)
    g_out = mm_rows(pair(merged_rel), across([attn_grad_cols[:, : width // 2], attn_grad_cols[:, width // 2 :]]))
    grad_w_out = grid.scatter_z(grid.scatter_y(grid.scatter_x(g_out)))

    qkv_grad, head_sums = attend_backward(
        hd, tab, seq_spans[0], qkv, keep_col, head_scale, scaled_grad, o_t, lse
    )
    qkv_grad_rel = reorder_rows(qkv_grad, group_order, rows)
    first_part = mm_cols(qkv_grad_rel, wq)
    pieces = [first_part[t * rows : (t + 1) * rows] for t in range(sp)]
    folded = [
        pieces[t].astype(f32) + swap(pieces[t + 1].astype(bf16), "sp", 1).astype(f32) for t in range(0, sp, 2)
    ]
    first_grad = grid.fold(folded, "sp", grid.x_bits)
    (input_part,), (gain_in,), (shift_in,) = norm_backward([first_grad], [first_normed], first_std, gains[0:1])
    grad_tokens = reorder(middle_grad + input_part, to_abs, block)

    g_qkv = mm_rows(firsts_cat, qkv_grad_rel)
    g_mine = grid.scatter_z(grid.scatter_y(g_qkv)).astype(bf16)
    g_blocks = jnp.concatenate(
        [g_mine.reshape(block, 3, lw).transpose(1, 0, 2), jnp.zeros((1, block, lw), bf16)], axis=0
    )
    back = []
    for t in range(sp):
        which = jnp.int32(3)
        for u in range(3):
            which = jnp.where((u * sp + me_s) // 3 == t, u, which)
        back.append(lax.dynamic_slice_in_dim(g_blocks, which, 1, 0))
    home = lax.all_to_all(jnp.concatenate(back, axis=0), "sp", 0, 0, tiled=True)
    grad_w_qkv = jnp.concatenate(
        [lax.dynamic_slice_in_dim(home, (3 * me_s + u) % sp, 1, 0)[0] for u in range(3)], axis=1
    ).astype(f32)

    qkv_sums = jnp.sum(qkv_grad.astype(f32), axis=0)
    zeros = jnp.zeros((2, width), f32)
    bias_sums = lax.dynamic_update_slice(
        zeros, jnp.stack([qkv_sums[:lw], qkv_sums[2 * lw :]]), (0, me_s * lw)
    )
    sum_early = jnp.concatenate(
        [
            reorder(
                jnp.stack(
                    [
                        gain_attn,
                        gain_ffn,
                        jnp.sum(attn_grad_rel.astype(f32), axis=0),
                        shift_attn,
                        shift_ffn,
                        jnp.sum(upstream.astype(f32), axis=0),
                    ]
                ),
                to_abs,
                block,
            ),
            reorder(
                jnp.stack(
                    [
                        jnp.concatenate(grad_mid),
                        jnp.concatenate([jnp.sum(p.astype(f32), axis=0) for p in pre_grad]),
                        jnp.concatenate(grad_mid_shift),
                    ]
                ),
                sp_abs,
                ff // sp,
            ).reshape(3 * ff // width, width),
        ],
        axis=0,
    )
    early = grid.all_sum(sum_early)
    scale_row = lax.dynamic_update_slice(
        jnp.zeros((1, width), f32), head_sums[1:2, :nh], (0, me_s * nh)
    )
    late = grid.all_sum(
        jnp.concatenate(
            [reorder(jnp.stack([gain_in, shift_in]), to_abs, block), bias_sums, scale_row], axis=0
        )
    )
    grad_model_gains = jnp.stack([late[0], early[0], early[1]])
    grad_model_shifts = jnp.stack([late[2], late[3], early[2], late[1], early[3], early[4], early[5]])
    hidden_sums = early[6:].reshape(3, ff)
    return (
        layer_out,
        grad_tokens,
        grad_w_qkv,
        grad_w_out,
        grad_w_up,
        grad_w_down,
        grad_model_gains,
        grad_model_shifts,
        hidden_sums[0],
        hidden_sums[1:3],
        late[4, :heads],
    )


REL, HID, ORD, COLS, WHO, SEND, SLOT = 0, 8, 16, 24, 32, 33, 36
LANES = 128


def matchings(sp):
    left = {s: {3 * s + k: (3 * s + k) % sp for k in range(3)} for s in range(sp)}
    rounds = []
    for _ in range(3):
        taken = {}

        def seat(s, seen):
            for b, to in sorted(left[s].items(), key=lambda e: e[1] != s):
                if to not in seen:
                    seen.add(to)
                    if to not in taken or seat(taken[to][0], seen):
                        taken[to] = (s, b)
                        return True
            return False

        for s in range(sp):
            seat(s, set())
        one = [None] * sp
        for to, (s, b) in taken.items():
            one[s] = (b - 3 * s, b // sp, to)
            del left[s][b]
        rounds.append(one)
    return rounds


def tables(dp, sp, ny, nz, rounds):
    out = np.zeros((dp * sp, 128), np.int32)
    for d in range(dp):
        for s in range(sp):
            row = out[d * sp + s]
            where = {}
            for p in range(dp):
                row[REL + p] = ((p % nz) * ny + p // nz) ^ d
                where[row[REL + p]] = p
            for q in range(2 * sp):
                dc, half, dx = q // 4, q // 2 % 2, q % 2
                row[HID + q] = ((dx * 2 + dc) ^ s) * 2 + half
                row[COLS + q] = where[row[HID + q]]
            for t in range(sp):
                row[ORD + t] = s ^ t
            row[WHO] = s
            for m in range(3):
                row[SEND + m] = rounds[m][s][0]
                row[SLOT + m] = next(rounds[m][a][1] for a in range(sp) if rounds[m][a][2] == s)
    return out


def span(index, size):
    return pl.ds(pl.multiple_of(index * size, size), size)


def norm_of(x):
    mean = jnp.mean(x, axis=1, keepdims=True)
    centred = x - mean
    inv_std = lax.rsqrt(jnp.mean(centred * centred, axis=1, keepdims=True) + EPSILON)
    return centred * inv_std, inv_std


def norm_back(incoming, normed, inv_std, gain):
    scaled = incoming * gain
    mean = jnp.mean(scaled, axis=1, keepdims=True)
    along = jnp.mean(scaled * normed, axis=1, keepdims=True)
    return inv_std * (scaled - mean - normed * along)


def down_sum(x):
    return jnp.sum(x, axis=0, keepdims=True)


def whole(shape):
    return pl.BlockSpec(shape, lambda *_: (0,) * len(shape))


def by_rows(rows, cols):
    return pl.BlockSpec((rows, cols), lambda i, *_: (i, 0))


def call(name, body, tab, args, outs, steps=1, in_specs=None, out_specs=None, scratch=(), deps=(), vmem=40, flops=0, moved=0):
    in_specs = [whole(a.shape) for a in args] if in_specs is None else in_specs
    out_specs = [whole(s) for s, _ in outs] if out_specs is None else out_specs
    return pl.pallas_call(
        skipping(body, 1 + len(args), len(deps)),
        grid_spec=pltpu.PrefetchScalarGridSpec(
            num_scalar_prefetch=1,
            grid=(steps,),
            in_specs=list(in_specs) + unread(deps),
            out_specs=list(out_specs),
            scratch_shapes=list(scratch),
        ),
        out_shape=[jax.ShapeDtypeStruct(s, t) for s, t in outs],
        compiler_params=pltpu.CompilerParams(vmem_limit_bytes=vmem << 20),
        cost_estimate=pl.CostEstimate(flops=int(flops), bytes_accessed=int(moved) or (4 << 20), transcendentals=0),
        name=name,
    )(tab, *args, *deps)


def part_body(tab, w, *outs):
    width = outs[0].shape[1]
    for m, out in enumerate(outs):
        out[...] = w[:, span(tab[SEND + m], width)]


def join_body(tab, *refs):
    pieces, out = refs[:-1], refs[-1]
    for m, piece in enumerate(pieces):
        for e in range(2):
            out[:, span(tab[SLOT + m] + 3 * e, LANES)] = piece[:, e * LANES : (e + 1) * LANES]


def unjoin_body(tab, e0, e1, *outs):
    for m, out in enumerate(outs):
        for e, g in enumerate((e0, e1)):
            out[:, e * LANES : (e + 1) * LANES] = g[:, span(tab[SLOT + m], LANES)].astype(bf16)


def home_body(tab, *refs):
    pieces, out = refs[:-1], refs[-1]
    width = pieces[0].shape[1]
    for m, piece in enumerate(pieces):
        out[:, span(tab[SEND + m], width)] = piece[...].astype(f32)


def prologue_body(tab, tok, cot, vcol, vrow, gains, shifts, mid, hsh, first_ref, up_ref, tokr_ref, vec_ref, hid_ref):
    rows, width = tok.shape
    unit = mid.shape[1] // 8
    valid = vcol[...]
    vec_ref[...] = jnp.zeros_like(vec_ref)
    hid_ref[...] = jnp.zeros_like(hid_ref)
    for p in range(8):
        at, to = span(tab[REL + p], LANES), slice(p * LANES, (p + 1) * LANES)
        tokr_ref[:, to] = tok[:, at]
        vec_ref[0:3, to] = gains[:, at]
        vec_ref[3:10, to] = shifts[:, at]
        at, to = span(tab[HID + p], unit), slice(p * unit, (p + 1) * unit)
        hid_ref[0:1, to] = mid[:, at]
        hid_ref[1:3, to] = hsh[:, at]
    gain, shift = vec_ref[0:1, :], vec_ref[6:7, :]

    def chunk(i, carry):
        at = span(i, 64)
        normed, _ = norm_of(tokr_ref[at, :].astype(f32))
        first_ref[at, :] = (normed * gain + shift).astype(bf16)
        return carry

    lax.fori_loop(0, rows // 64, chunk, 0)
    first_ref[rows:, :] = jnp.broadcast_to(vrow[...], (16, width))
    for p in range(8):
        at, to = span(tab[REL + p], LANES), slice(p * LANES, (p + 1) * LANES)
        masked = cot[:, at].astype(f32) * valid
        up_ref[:, to] = masked.astype(bf16)
        vec_ref[10:11, to] = down_sum(masked)


def project_body(count, tab, *refs):
    pieces, (w0, w1, shifts, out_ref, keep_ref) = refs[:count], refs[count:]
    rows, depth = out_ref.shape[0], w0.shape[0]
    bias = []
    for e in range(2):
        at = pl.ds(pl.multiple_of(tab[WHO] * 2 * LANES + e * LANES, LANES), LANES)
        bias += [shifts[0:1, at], jnp.zeros((1, LANES), f32), shifts[1:2, at]]
    bias = jnp.concatenate(bias, axis=1)
    for k in range(count):

        @pl.when(pl.program_id(0) == k)
        def _():
            x = pieces[k]
            out_ref[...] = (mm(x[:rows, :depth], w0[...]) + mm(x[:rows, depth:], w1[...]) + bias).astype(bf16)
            keep_ref[...] = x[rows:, :rows].astype(f32).T[:, 0:1]


def middle_body(tab, r0, r1, tok, vec, *refs):
    pieces, (second_ref, mid_ref, norm_ref, std_ref, merged_ref, wo) = refs[:12], refs[12:]
    half = pieces[2].shape[0]

    @pl.when(pl.program_id(0) == 0)
    def _():
        for c in range(2):
            a0, a1, b00, b01, b10, b11 = pieces[6 * c : 6 * c + 6]
            for dx, a in enumerate((a0, a1)):
                wo[:, span(tab[COLS + 4 * c + dx], LANES)] = a[...]
            for dx, (top, bottom) in enumerate(((b00, b10), (b01, b11))):
                to = span(tab[COLS + 4 * c + 2 + dx], LANES)
                wo[:half, to] = top[...]
                wo[half:, to] = bottom[...]

    for p in range(8):
        a = tab[REL + p]
        source, odd = a // 2, lax.rem(a, 2)
        merged_ref[:, p * LANES : (p + 1) * LANES] = jnp.where(odd == 0, r0[source], r1[source])
    normed, inv_std = norm_of(mm(merged_ref[...], wo[...]) + vec[5:6, :])
    middle = tok[...].astype(f32) + (normed * vec[1:2, :] + vec[7:8, :])
    norm_ref[...] = normed
    std_ref[...] = inv_std
    mid_ref[...] = middle
    again, _ = norm_of(middle)
    second_ref[...] = (again * vec[2:3, :] + vec[8:9, :]).astype(bf16)


GELU = 0.7978845608028654
CUBE = 0.044715


def ffn_body(unit, tab, second, upstream, mid, hid, vec, *refs):
    ins, (hown, hsib, pown, psib, sg_ref, lo_ref, sums_ref, upv, dnv, act, slope, back, sems) = refs[:16], refs[16:]
    i = pl.program_id(0)
    depth = upv.shape[0] // 2
    ff = upv.shape[1]

    def copies(q, which):
        c, half, dx = q // 4, q // 2 % 2, q % 2
        held = (upv, dnv)[which]
        a0, a1, b0, b1 = ins[8 * which + 4 * c : 8 * which + 4 * c + 4]
        to, at = pl.ds(q * unit, unit), pl.ds(0, unit)
        if half == 0:
            pairs = [((a0, a1)[dx].at[:, at], held.at[:, to])]
        else:
            rows = pl.ds(dx * depth, depth)
            pairs = [(b0.at[rows, at], held.at[pl.ds(0, depth), to]), (b1.at[rows, at], held.at[pl.ds(depth, depth), to])]
        return [pltpu.make_async_copy(a, b, sems.at[which, q, k]) for k, (a, b) in enumerate(pairs)]

    @pl.when(i == 0)
    def _():
        sums_ref[...] = jnp.zeros_like(sums_ref)
        for q in range(8):
            for copy in copies(q, 0):
                copy.start()
        for q in range(8):
            for copy in copies(q, 1):
                copy.start()

    x = second[...]
    total = jnp.zeros((x.shape[0], 1), f32)
    for q in range(8):
        at = slice(q * unit, (q + 1) * unit)

        @pl.when(i == 0)
        def _():
            for copy in copies(q, 0):
                copy.wait()

        pre = mm(x, upv[:, at]) + hid[1:2, at]
        squared = pre * pre
        t = jnp.tanh(pre * (GELU + (GELU * CUBE) * squared))
        one = 0.5 + 0.5 * t
        value = pre * one
        act[:, at] = value
        slope[:, at] = one + 0.5 * pre * (1.0 - t * t) * (GELU + (3 * GELU * CUBE) * squared)
        total = total + jnp.sum(value, axis=1, keepdims=True)
    mean = total / ff
    total = jnp.zeros_like(mean)
    for q in range(8):
        at = slice(q * unit, (q + 1) * unit)
        centred = act[:, at] - mean
        total = total + jnp.sum(centred * centred, axis=1, keepdims=True)
    inv_std = lax.rsqrt(total / ff + EPSILON)
    u = upstream[...]
    m1, m2 = jnp.zeros_like(mean), jnp.zeros_like(mean)
    low = jnp.zeros(mid.shape, f32)
    for q in range(8):
        at = slice(q * unit, (q + 1) * unit)

        @pl.when(i == 0)
        def _():
            for copy in copies(q, 1):
                copy.wait()

        incoming = mm(u, dnv[:, at])
        normed = (act[:, at] - mean) * inv_std
        act[:, at] = normed
        gain = hid[0:1, at]
        held, to = ((hown, at) if q < 4 else (hsib, slice((q - 4) * unit, (q - 3) * unit)))
        hidden = (normed * gain + hid[2:3, at]).astype(bf16)
        held[:, to] = hidden
        low = low + mm_cols(hidden, dnv[:, at])
        along = incoming * normed
        sums_ref[0:1, at] += down_sum(along)
        sums_ref[2:3, at] += down_sum(incoming)
        m1 = m1 + jnp.sum(incoming * gain, axis=1, keepdims=True)
        m2 = m2 + jnp.sum(along * gain, axis=1, keepdims=True)
        back[:, at] = incoming
    m1, m2 = m1 / ff, m2 / ff
    second_grad = jnp.zeros(mid.shape, f32)
    for q in range(8):
        at = slice(q * unit, (q + 1) * unit)
        grad = inv_std * (back[:, at] * hid[0:1, at] - m1 - act[:, at] * m2)
        pre_grad = (grad * slope[:, at]).astype(bf16)
        held, to = ((pown, at) if q < 4 else (psib, slice((q - 4) * unit, (q - 3) * unit)))
        held[:, to] = pre_grad
        sums_ref[1:2, at] += down_sum(pre_grad.astype(f32))
        second_grad = second_grad + mm_cols(pre_grad, upv[:, at])
    sg_ref[...] = second_grad
    out = (mid[...] + low + vec[9:10, :]).astype(bf16)
    for p in range(8):
        lo_ref[:, span(tab[REL + p], LANES)] = out[:, p * LANES : (p + 1) * LANES]


def heads_body(tab, grad, mid, norm, std, up, vec, wo, mg_ref, own_ref, sib_ref, o0_ref, o1_ref, sums_ref, scr):
    @pl.when(pl.program_id(0) == 0)
    def _():
        sums_ref[...] = jnp.zeros_like(sums_ref)

    incoming = grad[...]
    again, inv_std = norm_of(mid[...])
    sums_ref[1:2, :] += down_sum(incoming * again)
    sums_ref[4:5, :] += down_sum(incoming)
    middle_grad = up[...].astype(f32) + norm_back(incoming, again, inv_std, vec[2:3, :])
    mg_ref[...] = middle_grad
    normed = norm[...]
    sums_ref[0:1, :] += down_sum(middle_grad * normed)
    sums_ref[3:4, :] += down_sum(middle_grad)
    low = norm_back(middle_grad, normed, std[...], vec[1:2, :]).astype(bf16)
    sums_ref[2:3, :] += down_sum(low.astype(f32))
    scr[...] = low
    for q in range(8):
        held = own_ref if q < 4 else sib_ref
        held[:, (q % 4) * LANES : (q % 4 + 1) * LANES] = scr[:, span(tab[COLS + q], LANES)]
    got = mm_cols(low, wo[...]).astype(bf16)
    for p in range(8):
        a = tab[REL + p]
        source, odd = a // 2, lax.rem(a, 2)
        for e, out in enumerate((o0_ref, o1_ref)):

            @pl.when(odd == e)
            def _():
                out[source] = got[:, p * LANES : (p + 1) * LANES]


def grads_body(sets, widths, tab, *refs):
    ins, (ak, asend, bk, bsend, xt) = refs[: 4 * sets], refs[4 * sets :]
    half = bk.shape[0]
    total = sum(widths)
    at = 0
    for n, wide in enumerate(widths):
        x0, x1, y0, y1 = ins[4 * n : 4 * n + 4]
        tokens = x0.shape[0]

        @pl.when(pl.program_id(0) == n)
        def _():
            xt[:, :tokens] = x0[...].T
            xt[:, tokens:] = x1[...].T
            for q in range(4):
                cols = slice(q * wide, (q + 1) * wide)
                g = mm(xt[...], jnp.concatenate([y0[:, cols], y1[:, cols]], axis=0)).astype(bf16)
                if q < 2:
                    (ak, asend)[q][:, at : at + wide] = g
                else:
                    to = slice((q - 2) * total + at, (q - 2) * total + at + wide)
                    bk[:, to] = g[:half]
                    bsend[:, to] = g[half:]

        at += wide


def fold_body(tab, ak, ra, bk, rb, a2k, a2s, b2k, b2s):
    rows, cols = b2k.shape
    a = ak[...].astype(f32) + ra[...].astype(f32)
    a2k[...] = a[:rows].astype(bf16)
    a2s[...] = a[rows:].astype(bf16)
    b = bk[...].astype(f32) + rb[...].astype(f32)
    b2k[...] = b[:, :cols].astype(bf16)
    b2s[...] = b[:, cols:].astype(bf16)


def spread_body(tab, ak, ra, bk, rb, keep, *sends):
    rows, cols = keep.shape[0], ak.shape[1]
    for side, (k, r) in enumerate(((ak, ra), (bk, rb))):
        total = k[...].astype(f32) + r[...].astype(f32)
        to = slice(side * cols, (side + 1) * cols)
        keep[:, to] = total[:rows]
        for n, send in enumerate(sends, 1):
            send[:, to] = total[n * rows : (n + 1) * rows].astype(bf16)


def gathered_body(widths, tab, keep, *refs):
    received, outs = refs[: len(refs) - len(widths)], refs[len(refs) - len(widths) :]
    total = keep[...]
    for r in received:
        total = total + r[...].astype(f32)
    half = keep.shape[1] // 2
    at = 0
    for out, wide in zip(outs, widths):
        out[:, :wide] = total[:, at : at + wide]
        out[:, wide:] = total[:, half + at : half + at + wide]
        at += wide


def scatter_weights(grid, tab, sets, widths, tag, deps=()):
    rows = sets[0][0].shape[1]
    total = sum(widths)
    args = [a for one in sets for a in one]
    outs = [((rows, total), bf16)] * 2 + [((rows // 2, 2 * total), bf16)] * 2
    tokens = sets[0][0].shape[0]
    ak, asend, bk, bsend = call(
        "grads_" + tag, functools.partial(grads_body, len(sets), widths), tab, args, outs, steps=len(sets),
        scratch=[pltpu.VMEM((rows, 2 * tokens), bf16)], vmem=56, flops=2 * rows * 4 * total * 2 * tokens, deps=deps,
    )
    ra, rb = swap(asend, "sp", 2), swap(bsend, "dp", 1)
    yield (ra, rb)
    quarter = [((rows // 2, total), bf16)] * 4
    a2k, a2s, b2k, b2s = call("fold_" + tag, fold_body, tab, [ak, ra, bk, rb], quarter, moved=8 << 20)
    ra, rb = swap(a2s, "dp", 1), swap(b2s, "sp", 2)
    yield (ra, rb)
    shard = (rows // 8, 2 * total)
    keep, *sends = call("spread_" + tag, spread_body, tab, [a2k, ra, b2k, rb], [(shard, f32)] + [(shard, bf16)] * 3)
    received = [swap(s, "dp", b) for s, b in zip(sends, grid.z_bits)]
    yield tuple(received)
    yield call(
        "sum_" + tag, functools.partial(gathered_body, widths), tab, [keep] + received,
        [((rows // 8, 2 * w), f32) for w in widths],
    )


def slabs_body(tab, *refs):
    pieces, (first, other) = refs[:-2], refs[-2:]
    rows, half = pieces[0].shape[0], first.shape[1]
    for k, piece in enumerate(pieces):
        to = slice(k * rows, (k + 1) * rows)
        first[to, :] = piece[:, :half]
        other[to, :] = piece[:, half:]


def stack_body(tab, a, b, out):
    rows = a.shape[0]
    out[:rows, :] = a[...]
    out[rows:, :] = b[...]


def stack(tab, a, b, tag):
    return call("stack_" + tag, stack_body, tab, [a, b], [((2 * a.shape[0], a.shape[1]), a.dtype)])[0]


def gather_weights(grid, tab, shard, tag, deps=()):
    if deps:
        shard = call("shard_" + tag, lambda tab, x, o: o.__setitem__(Ellipsis, x[...]), tab, [shard], [(shard.shape, bf16)], deps=deps)[0]
    pieces = [shard] + [swap(shard, "dp", b) for b in grid.z_bits]
    yield tuple(pieces[1:])
    rows, cols = shard.shape
    first, other = call("slabs_" + tag, slabs_body, tab, pieces, [((4 * rows, cols // 2), bf16)] * 2)
    ra, rb = swap(first, "dp", 1), swap(other, "sp", 2)
    yield (ra, rb)
    a0 = stack(tab, first, ra, tag)
    b0 = stack(tab, other, rb, tag)
    a1, b1 = swap(a0, "sp", 2), swap(b0, "dp", 1)
    own = [a0, a1, b0, b1]
    yield (a1, b1)
    sib = [swap(p, "sp", 1) for p in own]
    yield own + sib


def first_grad_body(tab, g0, g1, wy0, wy1, mine, cross, far):
    i = pl.program_id(0)
    half = 3 * LANES
    g = jnp.concatenate([g0[...], g1[...]], axis=1)
    got = jnp.concatenate([mm_cols(g, wy0[...]), mm_cols(g, wy1[...])], axis=1)
    rows = g0.shape[0]

    @pl.when(i == 0)
    def _():
        mine[...] = got

    @pl.when(i == 1)
    def _():
        cross[:rows] = got.astype(bf16)

    @pl.when(i == 2)
    def _():
        far[...] = got

    @pl.when(i == 3)
    def _():
        cross[rows:] = got.astype(bf16)


def relay_body(tab, far, theirs, out):
    out[...] = (far[...] + theirs[...].astype(f32)).astype(bf16)


def final_body(tab, mine, theirs, crossed, tok, mg, vec, s0, s1, out_ref, late_ref, acc):
    i = pl.program_id(0)
    width = tok.shape[1]

    @pl.when(i == 0)
    def _():
        acc[...] = jnp.zeros_like(acc)

    incoming = mine[...] + theirs[...].astype(f32) + crossed[...].astype(f32)
    normed, inv_std = norm_of(tok[...].astype(f32))
    acc[0:1, :] += down_sum(incoming * normed)
    acc[1:2, :] += down_sum(incoming)
    total = mg[...] + norm_back(incoming, normed, inv_std, vec[0:1, :])
    for p in range(8):
        out_ref[:, span(tab[REL + p], LANES)] = total[:, p * LANES : (p + 1) * LANES]

    @pl.when(i == pl.num_programs(0) - 1)
    def _():
        late_ref[...] = jnp.zeros_like(late_ref)
        for p in range(8):
            late_ref[0:2, span(tab[REL + p], LANES)] = acc[0:2, p * LANES : (p + 1) * LANES]
        lane = lax.broadcasted_iota(jnp.int32, (1, LANES), 1)
        for e, s in enumerate((s0, s1)):
            at = pl.ds(pl.multiple_of(tab[WHO] * 2 * LANES + e * LANES, LANES), LANES)
            late_ref[2:3, at] = s[0:1, :LANES]
            late_ref[3:4, at] = s[0:1, 2 * LANES :]
            for h in range(2):
                head = tab[WHO] * 4 + 2 * e + h
                late_ref[4:5, :LANES] += jnp.where(lane == head, jnp.sum(jnp.where(lane == h, s[1:2, :LANES], 0.0)), 0.0)


def pack_body(tab, sums, vec, hid, out_ref):
    width, unit = sums.shape[1], hid.shape[1] // 8
    out_ref[...] = jnp.zeros_like(out_ref)
    for p in range(8):
        to, at = span(tab[REL + p], LANES), slice(p * LANES, (p + 1) * LANES)
        out_ref[0:5, to] = sums[0:5, at]
        out_ref[5:6, to] = vec[10:11, at]
    for v in range(3):
        for q in range(8):
            unit_at = tab[HID + q]
            row, col = 6 + 4 * v + unit_at // 2, lax.rem(unit_at, 2)
            out_ref[pl.ds(row, 1), span(col, unit)] = hid[v : v + 1, q * unit : (q + 1) * unit]


def fast_layer(
    tokens,
    seq_spans,
    valid_mask,
    cotangent,
    w_qkv,
    w_out,
    w_up,
    w_down,
    model_gains,
    model_shifts,
    mid_gain,
    hidden_shifts,
    head_scale,
):
    dp, sp = lax.axis_size("dp"), lax.axis_size("sp")
    grid = Grid(dp, sp)
    rows, width = tokens.shape
    group = rows * sp
    heads = head_scale.shape[0]
    block = width // dp
    ff = mid_gain.shape[0]
    unit = ff // 8
    shard_lanes = 2 * LANES
    step = rows // 2

    rounds = matchings(sp)
    device = lax.axis_index("dp") * sp + lax.axis_index("sp")
    tab = lax.dynamic_slice_in_dim(jnp.asarray(tables(dp, sp, grid.ny, grid.nz, rounds)), device, 1, 0)[0]
    spans = seq_spans[0]
    forth = [[(s, rounds[m][s][2]) for s in range(sp)] for m in range(3)]
    back_to = [[(t, s) for s, t in pairs] for pairs in forth]
    carry = lambda x, pairs: x if all(a == b for a, b in pairs) else lax.ppermute(x, "sp", pairs)

    half_down, half_out = w_down.shape[1] // 2, w_out.shape[1] // 2
    shard = jnp.concatenate(
        [w_down[:, :half_down], w_out[:, :half_out], w_down[:, half_down:], w_out[:, half_out:]], axis=1
    )
    down_stages = gather_weights(grid, tab, shard, "down")
    arrived = next(down_stages)

    sent = call("part", part_body, tab, [w_qkv], [((block, shard_lanes), bf16)] * 3)
    moved = [carry(x, pairs) for x, pairs in zip(sent, forth)]
    wq_shard = call("join", join_body, tab, moved, [((block, 3 * shard_lanes), bf16)])[0]
    wq0 = grid.gather_z(wq_shard)
    wq1 = swap(wq0, "dp", 1)

    vcol = valid_mask.astype(f32)[:, None]
    vrow = jnp.pad(valid_mask.astype(bf16), (0, width - rows))[None]
    first, upstream, tokr, vec, hid = call(
        "prologue", prologue_body, tab,
        [tokens, cotangent, vcol, vrow, model_gains, model_shifts, mid_gain[None], hidden_shifts],
        [((rows + 16, width), bf16), ((rows, width), bf16), ((rows, width), bf16), ((16, width), f32), ((8, ff), f32)],
    )
    beyond = swap(first, "sp", 2)
    firsts = [first, swap(first, "sp", 1), beyond, swap(beyond, "sp", 1)]

    up_stages = gather_weights(grid, tab, w_up, "up", deps=arrived)
    next(up_stages)
    arrived = next(down_stages)

    pieces = firsts
    qkv, keep = call(
        "project", functools.partial(project_body, sp), tab, pieces + [wq0, wq1, model_shifts],
        [((group, 3 * shard_lanes), bf16), ((group, 1), f32)], steps=sp,
        out_specs=[by_rows(rows, 3 * shard_lanes), by_rows(rows, 1)], flops=2 * group * width * 3 * shard_lanes,
    )
    firsts_cat = jnp.concatenate([f[:rows] for f in firsts], axis=0)

    hds = [Heads(2, heads // sp, 2 * e, (3 * e, 3 * e + 1, 3 * e + 2), ORD, WHO, sp) for e in range(2)]
    attended = [attend_forward(hds[0], tab, spans, qkv, keep, head_scale, deps=arrived)]
    send_home = lambda x: lax.all_to_all(x.reshape(sp, rows, LANES), "sp", 0, 0, tiled=True)
    returned = [send_home(attended[0][0])]
    arrived_down = next(down_stages)
    arrived_up = next(up_stages)
    attended.append(attend_forward(hds[1], tab, spans, qkv, keep, head_scale, deps=arrived_up))
    returned.append(send_home(attended[1][0]))
    downs = next(down_stages)
    next(up_stages)
    ups = next(up_stages)

    out_at = half_down // LANES
    wo_args, wo_specs = [], []
    for c in range(2):
        a0, a1, b0, b1 = downs[4 * c : 4 * c + 4]
        wo_args += [a0, a1, b0, b0, b1, b1]
        wo_specs += [pl.BlockSpec((width, LANES), lambda *_: (0, out_at))] * 2
        for r in (0, 1, 0, 1):
            wo_specs.append(pl.BlockSpec((width // 2, LANES), lambda *_, r=r: (r, out_at)))
    ret_spec = pl.BlockSpec((sp, step, LANES), lambda i, *_: (0, i, 0))
    second, middle, attn_normed, attn_std, merged, wo = call(
        "to_middle", middle_body, tab, returned + [tokr, vec] + wo_args,
        [((rows, width), bf16), ((rows, width), f32), ((rows, width), f32), ((rows, 1), f32), ((rows, width), bf16), ((width, width), bf16)],
        steps=2,
        in_specs=[ret_spec, ret_spec, by_rows(step, width), whole(vec.shape)] + wo_specs,
        out_specs=[by_rows(step, width)] * 3 + [by_rows(step, 1), by_rows(step, width), whole((width, width))],
        flops=4 * rows * width * width,
    )

    anywhere = pl.BlockSpec(memory_space=pl.ANY)
    hid_own, hid_sib, pre_own, pre_sib, second_grad, layer_out, hidden_sums = call(
        "ffn", functools.partial(ffn_body, unit), tab, [second, upstream, middle, hid, vec] + ups + downs,
        [((rows, ff // 2), bf16)] * 4 + [((rows, width), f32), ((rows, width), bf16), ((8, ff), f32)],
        steps=2,
        in_specs=[by_rows(step, width)] * 3 + [whole(hid.shape), whole(vec.shape)] + [anywhere] * 16,
        out_specs=[by_rows(step, ff // 2)] * 4 + [by_rows(step, width)] * 2 + [whole((8, ff))],
        scratch=[pltpu.VMEM((width, ff), bf16)] * 2 + [pltpu.VMEM((step, ff), f32)] * 3 + [pltpu.SemaphoreType.DMA((2, 8, 2))],
        vmem=60, flops=20 * rows * width * ff, moved=40 << 20,
    )

    upstream_sib = swap(upstream, "sp", 1)
    down_sums = scatter_weights(grid, tab, [(upstream, upstream_sib, hid_own, swap(hid_sib, "sp", 1))], (unit,), "down")
    arrived = next(down_sums)

    middle_grad, attn_own, attn_sib, back0, back1, sums = call(
        "to_heads", heads_body, tab, [second_grad, middle, attn_normed, attn_std, upstream, vec, wo],
        [((rows, width), f32)] + [((rows, width // 2), bf16)] * 2 + [((sp, rows, LANES), bf16)] * 2 + [((8, width), f32)],
        steps=2,
        in_specs=[by_rows(step, width)] * 3 + [by_rows(step, 1), by_rows(step, width), whole(vec.shape), whole(wo.shape)],
        out_specs=[by_rows(step, width)] + [by_rows(step, width // 2)] * 2 + [ret_spec] * 2 + [whole((8, width))],
        scratch=[pltpu.VMEM((step, width), bf16)], flops=4 * rows * width * width,
    )
    fetch = lambda x: lax.all_to_all(x, "sp", 0, 0, tiled=True).reshape(group, LANES)
    grads_in = [fetch(back0), fetch(back1)]

    up_sums = scatter_weights(
        grid, tab,
        [(second, swap(second, "sp", 1), pre_own, swap(pre_sib, "sp", 1)), (merged, swap(merged, "sp", 1), attn_own, swap(attn_sib, "sp", 1))],
        (unit, LANES), "up",
    )
    early = grid.all_sum(call("pack", pack_body, tab, [sums, vec, hidden_sums], [((24, width), f32)])[0])

    first_up = next(up_sums)
    qkv_grads = [attend_backward(hds[0], tab, spans, qkv, keep, head_scale, grads_in[0], *attended[0][1:], deps=arrived)]
    arrived = next(down_sums)
    wide = 3 * LANES

    def qkv_scatter(e):
        g = mm_rows(firsts_cat, qkv_grads[e][0])
        sent = g[width // 2 :].astype(bf16)
        got = swap(sent, "dp", 1)
        yield (got,)
        total = g[: width // 2] + got.astype(f32)
        received = [swap(total[n * block : (n + 1) * block].astype(bf16), "dp", b) for n, b in enumerate(grid.z_bits, 1)]
        yield tuple(received)
        out = total[:block]
        for r in received:
            out = out + r.astype(f32)
        yield out

    qkv_sums = [qkv_scatter(0)]
    next(qkv_sums[0])
    qkv_grads.append(
        attend_backward(hds[1], tab, spans, qkv, keep, head_scale, grads_in[1], *attended[1][1:], deps=first_up + arrived)
    )
    (grad_w_down,) = (next(down_sums), next(down_sums))[1]
    next(up_sums)
    next(up_sums)
    grad_w_up, grad_w_out = next(up_sums)
    next(qkv_sums[0])

    by_token = lambda cols: pl.BlockSpec((rows, cols), lambda i, *_: (i, 0))
    mine, cross, far = call(
        "first_grad", first_grad_body, tab, [qkv_grads[0][0], qkv_grads[1][0], wq0, wq1],
        [((rows, width), f32), ((2 * rows, width), bf16), ((rows, width), f32)], steps=sp,
        in_specs=[by_token(wide), by_token(wide), whole(wq0.shape), whole(wq1.shape)], flops=2 * group * width * 2 * wide,
    )
    theirs = swap(cross, "sp", 1)
    relayed = call("relay", relay_body, tab, [far, theirs], [((rows, width), bf16)],
                   in_specs=[whole(far.shape), pl.BlockSpec((rows, width), lambda *_: (1, 0))])[0]
    crossed = swap(relayed, "sp", 2)

    qkv_sums.append(qkv_scatter(1))
    next(qkv_sums[1])
    next(qkv_sums[1])
    g_mine = [next(g) for g in qkv_sums]
    sent = call("unjoin", unjoin_body, tab, g_mine, [((block, shard_lanes), bf16)] * 3)
    got = [carry(x, pairs) for x, pairs in zip(sent, back_to)]
    grad_w_qkv = call("home", home_body, tab, got, [((block, 3 * shard_lanes), f32)])[0]

    grad_tokens, late = call(
        "to_tokens", final_body, tab, [mine, theirs, crossed, tokr, middle_grad, vec, qkv_grads[0][1], qkv_grads[1][1]],
        [((rows, width), f32), ((8, width), f32)], steps=2,
        in_specs=[by_rows(step, width)] * 5 + [whole(vec.shape), whole((8, wide)), whole((8, wide))],
        out_specs=[by_rows(step, width), whole((8, width))], scratch=[pltpu.VMEM((8, width), f32)],
    )
    late = grid.all_sum(late)
    grad_model_gains = jnp.stack([late[0], early[0], early[1]])
    grad_model_shifts = jnp.stack([late[2], late[3], early[2], late[1], early[3], early[4], early[5]])
    totals = early[6 : 6 + 3 * ff // width].reshape(3, ff)
    return (
        layer_out,
        grad_tokens,
        grad_w_qkv,
        grad_w_out,
        grad_w_up,
        grad_w_down,
        grad_model_gains,
        grad_model_shifts,
        totals[0],
        totals[1:3],
        late[4, :heads],
    )


def per_device(*arrays):
    dp, sp = lax.axis_size("dp"), lax.axis_size("sp")
    (rows, width), heads, ff = arrays[0].shape, arrays[12].shape[0], arrays[10].shape[0]
    if (dp, sp) == (8, 4) and width == 8 * LANES and heads * HEAD == width and ff == 4 * width and rows % BQ == 0:
        return fast_layer(*arrays)
    return general_layer(*arrays)


def solution(mesh):
    rows = P(("dp", "sp"), None)
    placed = (rows, P("dp", None), P(("dp", "sp")), rows) + (P("dp", "sp"),) * 4 + (P(),) * 5
    return jax.shard_map(
        per_device,
        mesh=mesh,
        in_specs=placed,
        out_specs=(rows, rows) + (P("dp", "sp"),) * 4 + (P(),) * 5,
        check_vma=False,
    )
```

time: 1290 us -> 545 us (0.42)
  waiting for transfers between devices: 735 us -> 175 us
  matrix products: 244 us -> 5.27 us
  Pallas kernels: 0 us -> 201 us
  starting transfers between devices: 16.5 us -> 92.6 us
  blocking collectives: 86.3 us -> 12.3 us
  other arithmetic: 77.3 us -> 3.89 us
  local copies, waits for them, and re-layouts: 95.6 us -> 43.3 us
  loops' own time: 14.7 us -> 0 us
  between operations: 15.2 us -> 2.16 us
    reduce_scatter x8 -> x0, waiting for transfers between devices: 421 us -> none  [the longest x1 74.1 us: per_device(): lax.psum_scatter(term_down.astype(jnp.bfloat16), 'sp', scatter_dimension=...]
    dot_general x40 -> x2, matrix products: 244 us -> 5.27 us  [mm_rows(): lax.dot_general(a, b, (((0,), (0,)), ((), ())), preferred_element_type=f32)]
    pallas_call x0 -> x32, Pallas kernels: none -> 201 us  [the longest x28 113 us: call(): pl.pallas_call(skipping(body, 1 + len(args), len(deps)), grid_spec=pltpu....]
    ppermute x0 -> x73, waiting for transfers between devices: none -> 166 us  [the longest x69 159 us: swap(): lax.ppermute(x, axis, [(i, i ^ bits) for i in range(lax.axis_size(axis))])]
    all_gather x7 -> x0, waiting for transfers between devices: 146 us -> none  [the longest x1 48.4 us: per_device(): lax.all_gather(w_qkv, 'dp', axis=0, tiled=True)]
    psum x1 -> x0, waiting for transfers between devices: 127 us -> none  [per_device(): lax.psum((gains_term, shifts_term, grad_mid, hidden_term, scale_term), ('...]
    ppermute x0 -> x73, starting transfers between devices: none -> 80.6 us  [the longest x69 78.1 us: swap(): lax.ppermute(x, axis, [(i, i ^ bits) for i in range(lax.axis_size(axis))])]
    all_to_all x1, blocking collectives: 51.9 us -> 12.3 us  [fast_layer(): lax.all_to_all(x.reshape(sp, rows, LANES), 'sp', 0, 0, tiled=True)]
  transfers between devices with their start and end apart: 20 -> 76, of which waited for: 16 -> 25; matrix products, arithmetic and copies ran while one was open for 27% -> 2% of each run, Pallas kernels for 0% -> 25%
where the time goes in v1:
time: 545 us; the launch traced here: 535 us
  Pallas kernels  201 us (37%)
  waiting for transfers between devices  175 us (32%)
  starting transfers between devices  92.6 us (17%)
  local copies, waits for them, and re-layouts  43.3 us (8%)
  blocking collectives  12.3 us (2%)
    ppermute x69, waiting for transfers between devices, swap(): lax.ppermute(x, axis, [(i, i ^ bits) for i in range(lax.axis_size(axis))])  159 us
    pallas_call x28, Pallas kernels, call(): pl.pallas_call(skipping(body, 1 + len(args), len(deps)), grid_spec=pltpu....  113 us
    ppermute x69, starting transfers between devices, swap(): lax.ppermute(x, axis, [(i, i ^ bits) for i in range(lax.axis_size(axis))])  78.1 us
    pallas_call x2, Pallas kernels, attend_backward(): pl.pallas_call(skipping(functools.partial(bwd_kernel, hd, bk), 10, len(de...  50.2 us
    pallas_call x2, Pallas kernels, attend_forward(): pl.pallas_call(skipping(functools.partial(fwd_kernel, hd, bk), 7, len(dep...  37.1 us
    unnamed x174, local copies, waits for them, and re-layouts  36.9 us
    all_to_all x1, blocking collectives, fast_layer(): lax.all_to_all(x.reshape(sp, rows, LANES), 'sp', 0, 0, tiled=True)  12.3 us
  transfers between devices with their start and end apart: 76, of which 25 were waited for; matrix products, arithmetic and copies ran while one was open for 2% of the time, Pallas kernels for 25%

profile of v1, /device:TPU:0, one launch (start us, length us, event | category | flops | bytes accessed | tf_op | source)
XLA Modules:
  0.0 535.4 jit_solution(1924089749685639119)
XLA Ops:
  2.6 4.1 collective-permute-start.10
  14.1 3.0 prologue.1
  20.4 8.9 %collective-permute-done.10.refs_3_ = bf16[128,1280]{1,0:T(8,128)(2,1)S(1)} collective-permute-done((bf16[128,1280]{1,0:T(8,128)(2,1)S(1)}, bf16[128,1280]{1,0:T(8,128)(2,1)S(1)}, u32[]{:S(2)}, u32[]{:S(2)}) %collective-permute-start.10) | collective-permute-done | bytes 327712 | tf_op jit(solution)/shard_map/ppermute | solution.py:295
  30.4 6.5 %collective-permute-start.14 = (bf16[128,1024]{1,0:T(8,128)(2,1)S(1)}, bf16[128,1024]{1,0:T(8,128)(2,1)S(1)}, u32[]{:S(2)}, u32[]{:S(2)}) collective-permute-start(bf16[128,1024]{1,0:T(8,128)(2,1)S(1)} %shard_up.1.refs_1_), channel_id=1, source_target_pairs={{0,8},{4,12},{8,0},{12,4},{16,24},{20,28},{24,16},{28,20},{1,9},{5... | collective-permute-start | bytes 786440 | tf_op jit(solution)/shard_map/ppermute | solution.py:295
  39.1 4.2 collective-permute-done.3.refs_2_
  44.9 1.6 collective-permute-start.5
  46.5 1.7 collective-permute-start.15
  48.1 5.2 collective-permute-done.5
  56.2 10.6 %collective-permute-done.15.refs_3_ = bf16[128,1024]{1,0:T(8,128)(2,1)S(1)} collective-permute-done((bf16[128,1024]{1,0:T(8,128)(2,1)S(1)}, bf16[128,1024]{1,0:T(8,128)(2,1)S(1)}, u32[]{:S(2)}, u32[]{:S(2)}) %collective-permute-start.15) | collective-permute-done | bytes 262176 | tf_op jit(solution)/shard_map/ppermute | solution.py:295
  66.8 4.1 collective-permute-start.7
  73.7 11.3 %collective-permute-done.6 = bf16[128,768]{1,0:T(8,128)(2,1)S(1)} collective-permute-done((bf16[128,768]{1,0:T(8,128)(2,1)S(1)}, bf16[128,768]{1,0:T(8,128)(2,1)S(1)}, u32[]{:S(2)}, u32[]{:S(2)}) %collective-permute-start.6) | collective-permute-done | bytes 196640 | tf_op jit(solution)/shard_map/ppermute | solution.py:295
  89.9 35.3 %collective-permute-done.18.refs_8_.refs_2_ = bf16[512,512]{1,0:T(8,128)(2,1)S(1)} collective-permute-done((bf16[512,512]{1,0:T(8,128)(2,1)S(1)}, bf16[512,512]{1,0:T(8,128)(2,1)S(1)}, u32[]{:S(2)}, u32[]{:S(2)}) %collective-permute-start.18) | collective-permute-done | bytes 524320 | tf_op jit(solution)/shard_map/ppermute | solution.py:295
  127.4 1.6 stack_up.3.refs_8_
  131.3 4.6 project.1
  135.9 1.7 copy-done.60
  137.6 7.4 %collective-permute-done.25.refs_7_ = bf16[1024,512]{1,0:T(8,128)(2,1)S(1)} collective-permute-done((bf16[1024,512]{1,0:T(8,128)(2,1)S(1)}, bf16[1024,512]{1,0:T(8,128)(2,1)S(1)}, u32[]{:S(2)}, u32[]{:S(2)}) %collective-permute-start.25) | collective-permute-done | bytes 1048608 | tf_op jit(solution)/shard_map/ppermute | solution.py:295
  146.6 18.5 %attend_forward.3 = (bf16[2048,128]{1,0:T(8,128)(2,1)S(1)}, f32[128,2048]{1,0:T(8,128)S(1)}, f32[8,2048]{1,0:T(8,128)S(1)}) custom-call(s32[128]{0:T(128)S(1)} %dynamic-slice_bitcast_fusion.refs_0_, s32[4]{0:T(128)S(1)} %bitcast.22, bf16[2048,768]{1,0:T(8,128)(2,1)} %copy-done.60, bf16[2048,768]{1,0:T(8,128)(2,1)} %copy-done.60, ...), custom_call_target="tpu_custom_call" | custom-call | flops 13958643712 | bytes 3145728 | tf_op jit(solution)/shard_map/attend_forward/pallas_call | solution.py:148
  167.5 3.5 all-to-all-start.1
  171.0 11.9 %collective-permute-done.26.refs_9_ = bf16[1024,512]{1,0:T(8,128)(2,1)} collective-permute-done((bf16[1024,512]{1,0:T(8,128)(2,1)}, bf16[1024,512]{1,0:T(8,128)(2,1)}, u32[]{:S(2)}, u32[]{:S(2)}) %collective-permute-start.26) | collective-permute-done | bytes 1048608 | tf_op jit(solution)/shard_map/ppermute | solution.py:295
  187.4 18.5 %attend_forward.2 = (bf16[2048,128]{1,0:T(8,128)(2,1)S(1)}, f32[128,2048]{1,0:T(8,128)S(1)}, f32[8,2048]{1,0:T(8,128)S(1)}) custom-call(s32[128]{0:T(128)S(1)} %dynamic-slice_bitcast_fusion.refs_0_, s32[4]{0:T(128)S(1)} %bitcast.23, bf16[2048,768]{1,0:T(8,128)(2,1)} %copy-done.60, bf16[2048,768]{1,0:T(8,128)(2,1)} %copy-done.60, ...), custom_call_target="tpu_custom_call" | custom-call | flops 13958643712 | bytes 3145728 | tf_op jit(solution)/shard_map/attend_forward/pallas_call | solution.py:148
  207.7 12.3 %all_to_all.20.refs_1_ = bf16[4,512,128]{2,1,0:T(8,128)(2,1)S(1)} all-to-all(bf16[4,512,128]{2,1,0:T(8,128)(2,1)} %bitcast.20), channel_id=1, replica_groups=mesh['dp'=8,'sp'=4] {'sp'}, dimensions={0} | all-to-all | bytes 1048576 | tf_op jit(solution)/shard_map/all_to_all | solution.py:1221
  221.3 7.6 %to_middle.1 = (bf16[512,1024]{1,0:T(8,128)(2,1)}, f32[512,1024]{1,0:T(8,128)}, f32[512,1024]{1,0:T(8,128)}, f32[512,1]{1,0:T(8,128)S(1)}, bf16[512,1024]{1,0:T(8,128)(2,1)}, /*index=5*/bf16[1024,1024]{1,0:T(8,128)(2,1)}) custom-call(s32[128]{0:T(128)S(1)} %dynamic-slice_bitcast_fusion.refs_0_, bf16[4,512,128]{2,1,0:T(8,128)(2,1)S(1)} %all_to_all.20.refs_1_, ...), custom_call_target="tpu_custom_call" | custom-call | flops 2147483648 | bytes 4194304 | tf_op jit(solution)/shard_map/to_middle/pallas_call | solution.py:708
  229.0 37.6 %ffn.1 = (bf16[512,2048]{1,0:T(8,128)(2,1)}, bf16[512,2048]{1,0:T(8,128)(2,1)}, bf16[512,2048]{1,0:T(8,128)(2,1)}, bf16[512,2048]{1,0:T(8,128)(2,1)}, f32[512,10...) custom-call(s32[128]{0:T(128)} %copy-done.43, bf16[512,1024]{1,0:T(8,128)(2,1)} %get-tuple-element.102.refs_1_, ...), custom_call_target="tpu_custom_call" | custom-call | flops 42949672960 | bytes 41943040 | tf_op jit(solution)/shard_map/ffn/pallas_call | solution.py:708
  267.2 1.6 copy-done.5
  268.8 1.6 copy-done.6
  270.4 1.6 copy-done.7
  273.6 6.1 %to_heads.1 = (f32[512,1024]{1,0:T(8,128)S(1)}, bf16[512,512]{1,0:T(8,128)(2,1)S(1)}, bf16[512,512]{1,0:T(8,128)(2,1)S(1)}, bf16[4,512,128]{2,1,0:T(8,128)(2,1)}...) custom-call(s32[128]{0:T(128)S(1)} %copy-done.44, f32[512,1024]{1,0:T(8,128)S(1)} %copy-done.8, ...), custom_call_target="tpu_custom_call" | custom-call | flops 2147483648 | bytes 4194304 | tf_op jit(solution)/shard_map/to_heads/pallas_call | solution.py:708
  283.6 9.3 %grads_down.1 = (bf16[1024,512]{1,0:T(8,128)(2,1)}, bf16[1024,512]{1,0:T(8,128)(2,1)}, bf16[512,1024]{1,0:T(8,128)(2,1)}, bf16[512,1024]{1,0:T(8,128)(2,1)}) custom-call(s32[128]{0:T(128)} %copy-done.43, bf16[512,1024]{1,0:T(8,128)(2,1)} %copy-done.13, bf16[512,1024]{1,0:T(8,128)(2,1)} %copy-done.84, bf16[512,2048]{1,0:T(8,128)(2,1)} %get-tuple-element.114.refs_3_, ...), custom_call_target="tpu_custom_call" | custom-call | flops 4294967296 | bytes 4194304 | tf_op jit(solution)/shard_map/grads_down/pallas_call | solution.py:708
  295.5 4.1 all-to-all-start.2
  300.7 13.9 %grads_up.1 = (bf16[1024,640]{1,0:T(8,128)(2,1)}, bf16[1024,640]{1,0:T(8,128)(2,1)}, bf16[512,1280]{1,0:T(8,128)(2,1)}, bf16[512,1280]{1,0:T(8,128)(2,1)}) custom-call(s32[128]{0:T(128)} %copy-done.43, bf16[512,1024]{1,0:T(8,128)(2,1)} %get-tuple-element.102.refs_1_, bf16[512,1024]{1,0:T(8,128)(2,1)} %collective-permute-done.35.refs_2_, ...), custom_call_target="tpu_custom_call" | custom-call | flops 5368709120 | bytes 4194304 | tf_op jit(solution)/shard_map/grads_up/pallas_call | solution.py:708
  314.6 2.0 collective-permute-start.39
  317.1 2.0 collective-permute-done.33.refs_10_.refs_2_
  319.5 3.2 fold_down.1
  324.3 2.4 collective-permute-start.41
  326.7 1.7 collective-permute-start.42
  328.4 4.3 all-to-all-start.3
  334.8 24.7 %attend_backward.2 = (bf16[2048,384]{1,0:T(8,128)(2,1)}, f32[8,384]{1,0:T(8,128)S(1)}) custom-call(s32[128]{0:T(128)S(1)} %copy-done.45, s32[4]{0:T(128)S(1)} %bitcast.24, bf16[2048,768]{1,0:T(8,128)(2,1)} %copy-done.60, bf16[2048,768]{1,0:T(8,128)(2,1)} %copy-done.60, bf16[2048,768]{1,0:T(8,128)(2,1)} %copy-done.60, f32[2048,1]{1,0:T(8,128)S(1)} %copy-done.66, ...), custom_call_target="tpu_custom_call" | custom-call | flops 22548578304 | bytes 5242880 | tf_op jit(solution)/shard_map/attend_backward/pallas_call | solution.py:255
  359.5 9.6 %all-to-all-done.3 = bf16[4,512,128]{2,1,0:T(8,128)(2,1)} async-done(((bf16[4,512,128]{2,1,0:T(8,128)(2,1)}), bf16[4,512,128]{2,1,0:T(8,128)(2,1)}, u32[]{:S(2)}, u32[]{:S(2)}) %all-to-all-start.3) | async-done | bytes 524320 | tf_op jit(solution)/shard_map/all_to_all | solution.py:1272
  371.0 25.5 %attend_backward.3 = (bf16[2048,384]{1,0:T(8,128)(2,1)}, f32[8,384]{1,0:T(8,128)S(1)}) custom-call(s32[128]{0:T(128)S(1)} %copy-done.45, s32[4]{0:T(128)S(1)} %bitcast.25, bf16[2048,768]{1,0:T(8,128)(2,1)} %copy-done.60, bf16[2048,768]{1,0:T(8,128)(2,1)} %copy-done.60, bf16[2048,768]{1,0:T(8,128)(2,1)} %copy-done.60, f32[2048,1]{1,0:T(8,128)} %copy-done.64, ...), custom_call_target="tpu_custom_call" | custom-call | flops 22548578304 | bytes 5242880 | tf_op jit(solution)/shard_map/attend_backward/pallas_call | solution.py:255
  398.0 5.1 first_grad.1
  404.3 3.1 collective-permute-done.68
  407.8 4.5 collective-permute-done.69
  413.9 3.1 collective-permute-done.70
  419.0 2.8 collective-permute-done.71
  423.8 2.6 fusion.1
  427.7 2.7 fold_up.1
  431.5 1.7 collective-permute-start.56
  433.2 2.6 fusion
  435.9 13.7 %collective-permute-done.44.refs_3_ = bf16[512,1024]{1,0:T(8,128)(2,1)S(1)} collective-permute-done((bf16[512,1024]{1,0:T(8,128)(2,1)S(1)}, bf16[512,1024]{1,0:T(8,128)(2,1)S(1)}, u32[]{:S(2)}, u32[]{:S(2)}) %collective-permute-start.44) | collective-permute-done | bytes 1048608 | tf_op jit(solution)/shard_map/ppermute | solution.py:295
  450.3 4.0 to_tokens.1
  456.0 2.0 spread_down.1
  459.0 2.0 collective-permute-start.47
  462.6 1.7 collective-permute-done.46
  464.3 3.9 collective-permute-done.47
  468.2 2.0 collective-permute-done.48
  471.3 2.7 collective-permute-start.50
  474.6 1.9 collective-permute-start.52
  478.2 2.0 collective-permute-start.62
  480.2 13.7 %collective-permute-done.61.refs_3_ = bf16[128,1024]{1,0:T(8,128)(2,1)S(1)} collective-permute-done((bf16[128,1024]{1,0:T(8,128)(2,1)S(1)}, bf16[128,1024]{1,0:T(8,128)(2,1)S(1)}, u32[]{:S(2)}, u32[]{:S(2)}) %collective-permute-start.61) | collective-permute-done | bytes 262176 | tf_op jit(solution)/shard_map/ppermute | solution.py:295
  493.8 3.2 collective-permute-start.58
  499.2 15.4 %collective-permute-done.66 = f32[8,1024]{1,0:T(8,128)S(1)} collective-permute-done((f32[8,1024]{1,0:T(8,128)S(1)}, f32[8,1024]{1,0:T(8,128)S(1)}, u32[]{:S(2)}, u32[]{:S(2)}) %collective-permute-start.66) | collective-permute-done | bytes 32800 | tf_op jit(solution)/shard_map/ppermute | solution.py:295
  515.3 2.0 collective-permute-start.54
  517.3 2.1 collective-permute-done.53.refs_2_
  519.5 4.1 collective-permute-start.67
  (339 shorter events, 93.3 us)
Async XLA Ops:
  2.6 26.7 %collective-permute-start.10 = (bf16[128,1280]{1,0:T(8,128)(2,1)S(1)}, bf16[128,1280]{1,0:T(8,128)(2,1)S(1)}, u32[]{:S(2)}, u32[]{:S(2)}) collective-permute-start(bf16[128,1280]{1,0:T(8,128)(2,1)S(1)} %pad_maximum_fusion.4.refs_1_), channel_id=1, source_target_pairs={{0,16},{4,20},{8,24},{12,28},{16,0},{20,4},{24,8},{28,12},{1,17},{... | collective-permute-start | bytes 983048 | tf_op jit(solution)/shard_map/ppermute | solution.py:295
  6.7 22.6 %collective-permute-start.11 = (bf16[128,1280]{1,0:T(8,128)(2,1)S(1)}, bf16[128,1280]{1,0:T(8,128)(2,1)S(1)}, u32[]{:S(2)}, u32[]{:S(2)}) collective-permute-start(bf16[128,1280]{1,0:T(8,128)(2,1)S(1)} %pad_maximum_fusion.4.refs_1_), channel_id=1, source_target_pairs={{0,24},{4,28},{8,16},{12,20},{16,8},{20,12},{24,0},{28,4},{1,25},{... | collective-permute-start | bytes 983048 | tf_op jit(solution)/shard_map/ppermute | solution.py:295
  8.0 21.8 %collective-permute-start.9 = (bf16[128,1280]{1,0:T(8,128)(2,1)S(1)}, bf16[128,1280]{1,0:T(8,128)(2,1)S(1)}, u32[]{:S(2)}, u32[]{:S(2)}) collective-permute-start(bf16[128,1280]{1,0:T(8,128)(2,1)S(1)} %pad_maximum_fusion.4.refs_1_), channel_id=1, source_target_pairs={{0,8},{4,12},{8,0},{12,4},{16,24},{20,28},{24,16},{28,20},{1,9},{5... | collective-permute-start | bytes 983048 | tf_op jit(solution)/shard_map/ppermute | solution.py:295
  17.8 69.3 %collective-permute-start.1 = (bf16[528,1024]{1,0:T(8,128)(2,1)S(1)}, bf16[528,1024]{1,0:T(8,128)(2,1)S(1)}, u32[]{:S(2)}, u32[]{:S(2)}) collective-permute-start(bf16[528,1024]{1,0:T(8,128)(2,1)S(1)} %get-tuple-element.88.refs_1_), channel_id=1, source_target_pairs={{0,2},{1,3},{2,0},{3,1},{4,6},{5,7},{6,4},{7,5},{8,10},{9,11},{10,... | collective-permute-start | bytes 3244040 | tf_op jit(solution)/shard_map/ppermute | solution.py:295
  19.9 23.4 %collective-permute-start.3 = (bf16[128,256]{1,0:T(8,128)(2,1)S(1)}, bf16[128,256]{1,0:T(8,128)(2,1)S(1)}, u32[]{:S(2)}, u32[]{:S(2)}) collective-permute-start(bf16[128,256]{1,0:T(8,128)(2,1)S(1)} %get-tuple-element.90), channel_id=1, source_target_pairs={{0,2},{1,0},{2,3},{3,1},{4,6},{5,4},{6,7},{7,5},{8,10},{9,8},{10,1... | collective-permute-start | bytes 196616 | tf_op jit(solution)/shard_map/ppermute | solution.py:1182
  29.3 15.0 %collective-permute-start.4 = (bf16[128,256]{1,0:T(8,128)(2,1)S(1)}, bf16[128,256]{1,0:T(8,128)(2,1)S(1)}, u32[]{:S(2)}, u32[]{:S(2)}) collective-permute-start(bf16[128,256]{1,0:T(8,128)(2,1)S(1)} %get-tuple-element.91), channel_id=1, source_target_pairs={{0,1},{1,3},{2,0},{3,2},{4,5},{5,7},{6,4},{7,6},{8,9},{9,11},{10,8... | collective-permute-start | bytes 196616 | tf_op jit(solution)/shard_map/ppermute | solution.py:1182
  30.4 24.4 %collective-permute-start.14 = (bf16[128,1024]{1,0:T(8,128)(2,1)S(1)}, bf16[128,1024]{1,0:T(8,128)(2,1)S(1)}, u32[]{:S(2)}, u32[]{:S(2)}) collective-permute-start(bf16[128,1024]{1,0:T(8,128)(2,1)S(1)} %shard_up.1.refs_1_), channel_id=1, source_target_pairs={{0,8},{4,12},{8,0},{12,4},{16,24},{20,28},{24,16},{28,20},{1,9},{5... | collective-permute-start | bytes 786440 | tf_op jit(solution)/shard_map/ppermute | solution.py:295
  37.5 34.0 %collective-permute-start.12 = (bf16[512,640]{1,0:T(8,128)(2,1)S(1)}, bf16[512,640]{1,0:T(8,128)(2,1)S(1)}, u32[]{:S(2)}, u32[]{:S(2)}) collective-permute-start(bf16[512,640]{1,0:T(8,128)(2,1)S(1)} %get-tuple-element.94.refs_1_), channel_id=1, source_target_pairs={{0,4},{4,0},{8,12},{12,8},{16,20},{20,16},{24,28},{28,24},{1,5},{5... | collective-permute-start | bytes 1966088 | tf_op jit(solution)/shard_map/ppermute | solution.py:295
  46.5 20.3 %collective-permute-start.15 = (bf16[128,1024]{1,0:T(8,128)(2,1)S(1)}, bf16[128,1024]{1,0:T(8,128)(2,1)S(1)}, u32[]{:S(2)}, u32[]{:S(2)}) collective-permute-start(bf16[128,1024]{1,0:T(8,128)(2,1)S(1)} %shard_up.1.refs_1_), channel_id=1, source_target_pairs={{0,16},{4,20},{8,24},{12,28},{16,0},{20,4},{24,8},{28,12},{1,17},{... | collective-permute-start | bytes 786440 | tf_op jit(solution)/shard_map/ppermute | solution.py:295
  53.3 33.7 %collective-permute-start.13 = (bf16[512,640]{1,0:T(8,128)(2,1)S(1)}, bf16[512,640]{1,0:T(8,128)(2,1)S(1)}, u32[]{:S(2)}, u32[]{:S(2)}) collective-permute-start(bf16[512,640]{1,0:T(8,128)(2,1)S(1)} %get-tuple-element.95.refs_1_), channel_id=1, source_target_pairs={{0,2},{1,3},{2,0},{3,1},{4,6},{5,7},{6,4},{7,5},{8,10},{9,11},{10,... | collective-permute-start | bytes 1966088 | tf_op jit(solution)/shard_map/ppermute | solution.py:295
  54.8 12.0 %collective-permute-start.16 = (bf16[128,1024]{1,0:T(8,128)(2,1)S(1)}, bf16[128,1024]{1,0:T(8,128)(2,1)S(1)}, u32[]{:S(2)}, u32[]{:S(2)}) collective-permute-start(bf16[128,1024]{1,0:T(8,128)(2,1)S(1)} %shard_up.1.refs_1_), channel_id=1, source_target_pairs={{0,24},{4,28},{8,16},{12,20},{16,8},{20,12},{24,0},{28,4},{1,25},{... | collective-permute-start | bytes 786440 | tf_op jit(solution)/shard_map/ppermute | solution.py:295
  66.8 18.3 %collective-permute-start.6 = (bf16[128,768]{1,0:T(8,128)(2,1)S(1)}, bf16[128,768]{1,0:T(8,128)(2,1)S(1)}, u32[]{:S(2)}, u32[]{:S(2)}) collective-permute-start(bf16[128,768]{1,0:T(8,128)(2,1)S(1)} %join.1), channel_id=1, source_target_pairs={{0,16},{4,20},{8,24},{12,28},{16,0},{20,4},{24,8},{28,12},{1,17},{... | collective-permute-start | bytes 589832 | tf_op jit(solution)/shard_map/ppermute | solution.py:295
  66.8 19.7 %collective-permute-start.7 = (bf16[128,768]{1,0:T(8,128)(2,1)S(1)}, bf16[128,768]{1,0:T(8,128)(2,1)S(1)}, u32[]{:S(2)}, u32[]{:S(2)}) collective-permute-start(bf16[128,768]{1,0:T(8,128)(2,1)S(1)} %join.1), channel_id=1, source_target_pairs={{0,24},{4,28},{8,16},{12,20},{16,8},{20,12},{24,0},{28,4},{1,25},{... | collective-permute-start | bytes 589832 | tf_op jit(solution)/shard_map/ppermute | solution.py:295
  71.5 16.2 %collective-permute-start.17 = (bf16[512,512]{1,0:T(8,128)(2,1)S(1)}, bf16[512,512]{1,0:T(8,128)(2,1)S(1)}, u32[]{:S(2)}, u32[]{:S(2)}) collective-permute-start(bf16[512,512]{1,0:T(8,128)(2,1)S(1)} %get-tuple-element.97.refs_1_), channel_id=1, source_target_pairs={{0,4},{4,0},{8,12},{12,8},{16,20},{20,16},{24,28},{28,24},{1,5},{5... | collective-permute-start | bytes 1572872 | tf_op jit(solution)/shard_map/ppermute | solution.py:295
  85.0 45.8 %collective-permute-start.19 = (bf16[1024,640]{1,0:T(8,128)(2,1)S(1)}, bf16[1024,640]{1,0:T(8,128)(2,1)}, u32[]{:S(2)}, u32[]{:S(2)}) collective-permute-start(bf16[1024,640]{1,0:T(8,128)(2,1)S(1)} %stack_down.2.refs_5_.refs_14_), channel_id=1, source_target_pairs={{0,2},{1,3},{2,0},{3,1},{4,6},{5,7},{6,4},{7,5},{8,10},{9,11},{10,... | collective-permute-start | bytes 3932168 | tf_op jit(solution)/shard_map/ppermute | solution.py:295
  86.5 38.7 %collective-permute-start.18 = (bf16[512,512]{1,0:T(8,128)(2,1)S(1)}, bf16[512,512]{1,0:T(8,128)(2,1)S(1)}, u32[]{:S(2)}, u32[]{:S(2)}) collective-permute-start(bf16[512,512]{1,0:T(8,128)(2,1)S(1)} %get-tuple-element.98.refs_1_), channel_id=1, source_target_pairs={{0,2},{1,3},{2,0},{3,1},{4,6},{5,7},{6,4},{7,5},{8,10},{9,11},{10,... | collective-permute-start | bytes 1572872 | tf_op jit(solution)/shard_map/ppermute | solution.py:295
  87.1 42.0 %collective-permute-start = (bf16[528,1024]{1,0:T(8,128)(2,1)S(1)}, bf16[528,1024]{1,0:T(8,128)(2,1)S(1)}, u32[]{:S(2)}, u32[]{:S(2)}) collective-permute-start(bf16[528,1024]{1,0:T(8,128)(2,1)S(1)} %get-tuple-element.88.refs_1_), channel_id=1, source_target_pairs={{0,1},{1,0},{2,3},{3,2},{4,5},{5,4},{6,7},{7,6},{8,9},{9,8},{10,11... | collective-permute-start | bytes 3244040 | tf_op jit(solution)/shard_map/ppermute | solution.py:295
  87.1 43.6 %collective-permute-start.2 = (bf16[528,1024]{1,0:T(8,128)(2,1)S(1)}, bf16[528,1024]{1,0:T(8,128)(2,1)S(1)}, u32[]{:S(2)}, u32[]{:S(2)}) collective-permute-start(bf16[528,1024]{1,0:T(8,128)(2,1)S(1)} %collective-permute-done.1.refs_3_), channel_id=1, source_target_pairs={{0,1},{1,0},{2,3},{3,2},{4,5},{5,4},{6,7},{7,6},{8,9},{9,8},{10,11... | collective-permute-start | bytes 3244040 | tf_op jit(solution)/shard_map/ppermute | solution.py:295
  87.7 41.3 %collective-permute-start.8 = (bf16[512,768]{1,0:T(8,128)(2,1)S(1)}, bf16[512,768]{1,0:T(8,128)(2,1)S(1)}, u32[]{:S(2)}, u32[]{:S(2)}) collective-permute-start(bf16[512,768]{1,0:T(8,128)(2,1)S(1)} %pad_maximum_fusion.1.refs_5_.refs_3_), channel_id=1, source_target_pairs={{0,4},{4,0},{8,12},{12,8},{16,20},{20,16},{24,28},{28,24},{1,5},{5... | collective-permute-start | bytes 2359304 | tf_op jit(solution)/shard_map/ppermute | solution.py:295
  125.2 19.8 %collective-permute-start.25 = (bf16[1024,512]{1,0:T(8,128)(2,1)S(1)}, bf16[1024,512]{1,0:T(8,128)(2,1)S(1)}, u32[]{:S(2)}, u32[]{:S(2)}) collective-permute-start(bf16[1024,512]{1,0:T(8,128)(2,1)S(1)} %stack_up.2.refs_6_), channel_id=1, source_target_pairs={{0,2},{1,3},{2,0},{3,1},{4,6},{5,7},{6,4},{7,5},{8,10},{9,11},{10,... | collective-permute-start | bytes 3145736 | tf_op jit(solution)/shard_map/ppermute | solution.py:295
  129.0 54.4 %collective-permute-start.21 = (bf16[1024,640]{1,0:T(8,128)(2,1)S(1)}, bf16[1024,640]{1,0:T(8,128)(2,1)}, u32[]{:S(2)}, u32[]{:S(2)}) collective-permute-start(bf16[1024,640]{1,0:T(8,128)(2,1)S(1)} %stack_down.2.refs_5_.refs_14_), channel_id=1, source_target_pairs={{0,1},{1,0},{2,3},{3,2},{4,5},{5,4},{6,7},{7,6},{8,9},{9,8},{10,11... | collective-permute-start | bytes 3932168 | tf_op jit(solution)/shard_map/ppermute | solution.py:295
  129.1 53.8 %collective-permute-start.20 = (bf16[1024,640]{1,0:T(8,128)(2,1)S(1)}, bf16[1024,640]{1,0:T(8,128)(2,1)}, u32[]{:S(2)}, u32[]{:S(2)}) collective-permute-start(bf16[1024,640]{1,0:T(8,128)(2,1)S(1)} %stack_down.3.refs_7_.refs_8_.refs_16_), channel_id=1, source_target_pairs={{0,4},{4,0},{8,12},{12,8},{16,20},{20,16},{24,28},{28,24},{1,5},{5... | collective-permute-start | bytes 3932168 | tf_op jit(solution)/shard_map/ppermute | solution.py:295
  130.7 52.8 %collective-permute-start.23 = (bf16[1024,640]{1,0:T(8,128)(2,1)S(1)}, bf16[1024,640]{1,0:T(8,128)(2,1)}, u32[]{:S(2)}, u32[]{:S(2)}) collective-permute-start(bf16[1024,640]{1,0:T(8,128)(2,1)S(1)} %stack_down.3.refs_7_.refs_8_.refs_16_), channel_id=1, source_target_pairs={{0,1},{1,0},{2,3},{3,2},{4,5},{5,4},{6,7},{7,6},{8,9},{9,8},{10,11... | collective-permute-start | bytes 3932168 | tf_op jit(solution)/shard_map/ppermute | solution.py:295
  130.9 53.0 %collective-permute-start.22 = (bf16[1024,640]{1,0:T(8,128)(2,1)}, bf16[1024,640]{1,0:T(8,128)(2,1)}, u32[]{:S(2)}, u32[]{:S(2)}) collective-permute-start(bf16[1024,640]{1,0:T(8,128)(2,1)} %collective-permute-done.19.refs_6_.refs_15_), channel_id=1, source_target_pairs={{0,1},{1,0},{2,3},{3,2},{4,5},{5,4},{6,7},{7,6},{8,9},{9,8},{10,11... | collective-permute-start | bytes 3932168 | tf_op jit(solution)/shard_map/ppermute | solution.py:295
  145.0 37.9 %collective-permute-start.26 = (bf16[1024,512]{1,0:T(8,128)(2,1)}, bf16[1024,512]{1,0:T(8,128)(2,1)}, u32[]{:S(2)}, u32[]{:S(2)}) collective-permute-start(bf16[1024,512]{1,0:T(8,128)(2,1)} %stack_up.3.refs_8_), channel_id=1, source_target_pairs={{0,4},{4,0},{8,12},{12,8},{16,20},{20,16},{24,28},{28,24},{1,5},{5... | collective-permute-start | bytes 3145736 | tf_op jit(solution)/shard_map/ppermute | solution.py:295
  167.5 40.2 %all-to-all-start.1 = ((bf16[4,512,128]{2,1,0:T(8,128)(2,1)}), bf16[4,512,128]{2,1,0:T(8,128)(2,1)S(1)}, u32[]{:S(2)}, u32[]{:S(2)}) async-start(bf16[4,512,128]{2,1,0:T(8,128)(2,1)} %bitcast.19), calls=%async_computation.1 | async-start | bytes 1048576 | tf_op jit(solution)/shard_map/all_to_all | solution.py:1221
  182.9 46.0 %collective-permute-start.27 = (bf16[1024,512]{1,0:T(8,128)(2,1)}, bf16[1024,512]{1,0:T(8,128)(2,1)}, u32[]{:S(2)}, u32[]{:S(2)}) collective-permute-start(bf16[1024,512]{1,0:T(8,128)(2,1)} %copy-done.17), channel_id=1, source_target_pairs={{0,1},{1,0},{2,3},{3,2},{4,5},{5,4},{6,7},{7,6},{8,9},{9,8},{10,11... | collective-permute-start | bytes 3145736 | tf_op jit(solution)/shard_map/ppermute | solution.py:295
  182.9 46.0 %collective-permute-start.29 = (bf16[1024,512]{1,0:T(8,128)(2,1)}, bf16[1024,512]{1,0:T(8,128)(2,1)}, u32[]{:S(2)}, u32[]{:S(2)}) collective-permute-start(bf16[1024,512]{1,0:T(8,128)(2,1)} %stack_up.3.refs_8_), channel_id=1, source_target_pairs={{0,1},{1,0},{2,3},{3,2},{4,5},{5,4},{6,7},{7,6},{8,9},{9,8},{10,11... | collective-permute-start | bytes 3145736 | tf_op jit(solution)/shard_map/ppermute | solution.py:295
  183.4 45.5 %collective-permute-start.28 = (bf16[1024,512]{1,0:T(8,128)(2,1)}, bf16[1024,512]{1,0:T(8,128)(2,1)}, u32[]{:S(2)}, u32[]{:S(2)}) collective-permute-start(bf16[1024,512]{1,0:T(8,128)(2,1)} %copy-done.82), channel_id=1, source_target_pairs={{0,1},{1,0},{2,3},{3,2},{4,5},{5,4},{6,7},{7,6},{8,9},{9,8},{10,11... | collective-permute-start | bytes 3145736 | tf_op jit(solution)/shard_map/ppermute | solution.py:295
  183.5 45.5 %collective-permute-start.30 = (bf16[1024,512]{1,0:T(8,128)(2,1)}, bf16[1024,512]{1,0:T(8,128)(2,1)}, u32[]{:S(2)}, u32[]{:S(2)}) collective-permute-start(bf16[1024,512]{1,0:T(8,128)(2,1)} %collective-permute-done.26.refs_9_), channel_id=1, source_target_pairs={{0,1},{1,0},{2,3},{3,2},{4,5},{5,4},{6,7},{7,6},{8,9},{9,8},{10,11... | collective-permute-start | bytes 3145736 | tf_op jit(solution)/shard_map/ppermute | solution.py:295
  183.9 36.1 %collective-permute-start.24 = (bf16[1024,640]{1,0:T(8,128)(2,1)}, bf16[1024,640]{1,0:T(8,128)(2,1)}, u32[]{:S(2)}, u32[]{:S(2)}) collective-permute-start(bf16[1024,640]{1,0:T(8,128)(2,1)} %collective-permute-done.20.refs_9_.refs_10_.refs_17_), channel_id=1, source_target_pairs={{0,1},{1,0},{2,3},{3,2},{4,5},{5,4},{6,7},{7,6},{8,9},{9,8},{10,11... | collective-permute-start | bytes 3932168 | tf_op jit(solution)/shard_map/ppermute | solution.py:295
  266.6 15.7 %collective-permute-start.32 = (bf16[512,2048]{1,0:T(8,128)(2,1)}, bf16[512,2048]{1,0:T(8,128)(2,1)S(1)}, u32[]{:S(2)}, u32[]{:S(2)}) collective-permute-start(bf16[512,2048]{1,0:T(8,128)(2,1)} %get-tuple-element.115), channel_id=1, source_target_pairs={{0,1},{1,0},{2,3},{3,2},{4,5},{5,4},{6,7},{7,6},{8,9},{9,8},{10,11... | collective-permute-start | bytes 6291464 | tf_op jit(solution)/shard_map/ppermute | solution.py:295
  266.6 15.2 %collective-permute-start.31 = (bf16[512,1024]{1,0:T(8,128)(2,1)S(1)}, bf16[512,1024]{1,0:T(8,128)(2,1)S(1)}, u32[]{:S(2)}, u32[]{:S(2)}) collective-permute-start(bf16[512,1024]{1,0:T(8,128)(2,1)S(1)} %copy-done.14), channel_id=1, source_target_pairs={{0,1},{1,0},{2,3},{3,2},{4,5},{5,4},{6,7},{7,6},{8,9},{9,8},{10,11... | collective-permute-start | bytes 3145736 | tf_op jit(solution)/shard_map/ppermute | solution.py:295
  267.1 32.6 %collective-permute-start.36 = (bf16[512,2048]{1,0:T(8,128)(2,1)}, bf16[512,2048]{1,0:T(8,128)(2,1)}, u32[]{:S(2)}, u32[]{:S(2)}) collective-permute-start(bf16[512,2048]{1,0:T(8,128)(2,1)} %get-tuple-element.123), channel_id=1, source_target_pairs={{0,1},{1,0},{2,3},{3,2},{4,5},{5,4},{6,7},{7,6},{8,9},{9,8},{10,11... | collective-permute-start | bytes 6291464 | tf_op jit(solution)/shard_map/ppermute | solution.py:295
  281.3 11.9 %collective-permute-start.38 = (bf16[512,512]{1,0:T(8,128)(2,1)S(1)}, bf16[512,512]{1,0:T(8,128)(2,1)S(1)}, u32[]{:S(2)}, u32[]{:S(2)}) collective-permute-start(bf16[512,512]{1,0:T(8,128)(2,1)S(1)} %get-tuple-element.126), channel_id=1, source_target_pairs={{0,1},{1,0},{2,3},{3,2},{4,5},{5,4},{6,7},{7,6},{8,9},{9,8},{10,11... | collective-permute-start | bytes 1572872 | tf_op jit(solution)/shard_map/ppermute | solution.py:295
  281.7 17.9 %collective-permute-start.35 = (bf16[512,1024]{1,0:T(8,128)(2,1)}, bf16[512,1024]{1,0:T(8,128)(2,1)}, u32[]{:S(2)}, u32[]{:S(2)}) collective-permute-start(bf16[512,1024]{1,0:T(8,128)(2,1)} %get-tuple-element.102.refs_1_), channel_id=1, source_target_pairs={{0,1},{1,0},{2,3},{3,2},{4,5},{5,4},{6,7},{7,6},{8,9},{9,8},{10,11... | collective-permute-start | bytes 3145736 | tf_op jit(solution)/shard_map/ppermute | solution.py:295
  281.8 17.9 %collective-permute-start.37 = (bf16[512,1024]{1,0:T(8,128)(2,1)}, bf16[512,1024]{1,0:T(8,128)(2,1)S(1)}, u32[]{:S(2)}, u32[]{:S(2)}) collective-permute-start(bf16[512,1024]{1,0:T(8,128)(2,1)} %get-tuple-element.124.refs_5_), channel_id=1, source_target_pairs={{0,1},{1,0},{2,3},{3,2},{4,5},{5,4},{6,7},{7,6},{8,9},{9,8},{10,11... | collective-permute-start | bytes 3145736 | tf_op jit(solution)/shard_map/ppermute | solution.py:295
  292.8 26.3 %collective-permute-start.33 = (bf16[1024,512]{1,0:T(8,128)(2,1)}, bf16[1024,512]{1,0:T(8,128)(2,1)}, u32[]{:S(2)}, u32[]{:S(2)}) collective-permute-start(bf16[1024,512]{1,0:T(8,128)(2,1)} %get-tuple-element.116), channel_id=1, source_target_pairs={{0,2},{1,3},{2,0},{3,1},{4,6},{5,7},{6,4},{7,5},{8,10},{9,11},{10,... | collective-permute-start | bytes 3145736 | tf_op jit(solution)/shard_map/ppermute | solution.py:295
  294.0 25.4 %collective-permute-start.34 = (bf16[512,1024]{1,0:T(8,128)(2,1)}, bf16[512,1024]{1,0:T(8,128)(2,1)}, u32[]{:S(2)}, u32[]{:S(2)}) collective-permute-start(bf16[512,1024]{1,0:T(8,128)(2,1)} %get-tuple-element.117), channel_id=1, source_target_pairs={{0,4},{4,0},{8,12},{12,8},{16,20},{20,16},{24,28},{28,24},{1,5},{5... | collective-permute-start | bytes 3145736 | tf_op jit(solution)/shard_map/ppermute | solution.py:295
  295.5 32.8 %all-to-all-start.2 = ((bf16[4,512,128]{2,1,0:T(8,128)(2,1)}), bf16[4,512,128]{2,1,0:T(8,128)(2,1)}, u32[]{:S(2)}, u32[]{:S(2)}) async-start(bf16[4,512,128]{2,1,0:T(8,128)(2,1)} %get-tuple-element.111), calls=%async_computation.2 | async-start | bytes 1048576 | tf_op jit(solution)/shard_map/all_to_all | solution.py:1272
  314.6 54.5 %collective-permute-start.39 = (bf16[1024,640]{1,0:T(8,128)(2,1)}, bf16[1024,640]{1,0:T(8,128)(2,1)S(1)}, u32[]{:S(2)}, u32[]{:S(2)}) collective-permute-start(bf16[1024,640]{1,0:T(8,128)(2,1)} %get-tuple-element.127), channel_id=1, source_target_pairs={{0,2},{1,3},{2,0},{3,1},{4,6},{5,7},{6,4},{7,5},{8,10},{9,11},{10,... | collective-permute-start | bytes 3932168 | tf_op jit(solution)/shard_map/ppermute | solution.py:295
  316.6 52.5 %collective-permute-start.40 = (bf16[512,1280]{1,0:T(8,128)(2,1)}, bf16[512,1280]{1,0:T(8,128)(2,1)}, u32[]{:S(2)}, u32[]{:S(2)}) collective-permute-start(bf16[512,1280]{1,0:T(8,128)(2,1)} %get-tuple-element.128), channel_id=1, source_target_pairs={{0,4},{4,0},{8,12},{12,8},{16,20},{20,16},{24,28},{28,24},{1,5},{5... | collective-permute-start | bytes 3932168 | tf_op jit(solution)/shard_map/ppermute | solution.py:295
  324.3 44.8 %collective-permute-start.41 = (bf16[512,512]{1,0:T(8,128)(2,1)}, bf16[512,512]{1,0:T(8,128)(2,1)}, u32[]{:S(2)}, u32[]{:S(2)}) collective-permute-start(bf16[512,512]{1,0:T(8,128)(2,1)} %get-tuple-element.131), channel_id=1, source_target_pairs={{0,4},{4,0},{8,12},{12,8},{16,20},{20,16},{24,28},{28,24},{1,5},{5... | collective-permute-start | bytes 1572872 | tf_op jit(solution)/shard_map/ppermute | solution.py:295
  326.7 42.4 %collective-permute-start.42 = (bf16[512,512]{1,0:T(8,128)(2,1)}, bf16[512,512]{1,0:T(8,128)(2,1)}, u32[]{:S(2)}, u32[]{:S(2)}) collective-permute-start(bf16[512,512]{1,0:T(8,128)(2,1)} %get-tuple-element.132), channel_id=1, source_target_pairs={{0,2},{1,3},{2,0},{3,1},{4,6},{5,7},{6,4},{7,5},{8,10},{9,11},{10,... | collective-permute-start | bytes 1572872 | tf_op jit(solution)/shard_map/ppermute | solution.py:295
  328.4 40.7 %all-to-all-start.3 = ((bf16[4,512,128]{2,1,0:T(8,128)(2,1)}), bf16[4,512,128]{2,1,0:T(8,128)(2,1)}, u32[]{:S(2)}, u32[]{:S(2)}) async-start(bf16[4,512,128]{2,1,0:T(8,128)(2,1)} %copy-done.40), calls=%async_computation.3 | async-start | bytes 1048576 | tf_op jit(solution)/shard_map/all_to_all | solution.py:1272
  403.0 19.6 %collective-permute-start.43 = (bf16[1024,1024]{1,0:T(8,128)(2,1)S(1)}, bf16[1024,1024]{1,0:T(8,128)(2,1)S(1)}, u32[]{:S(2)}, u32[]{:S(2)}) collective-permute-start(bf16[1024,1024]{1,0:T(8,128)(2,1)S(1)} %get-tuple-element.135), channel_id=1, source_target_pairs={{0,1},{1,0},{2,3},{3,2},{4,5},{5,4},{6,7},{7,6},{8,9},{9,8},{10,11... | collective-permute-start | bytes 6291464 | tf_op jit(solution)/shard_map/ppermute | solution.py:295
  421.7 36.2 %collective-permute-start.72 = (f32[24,1024]{1,0:T(8,128)S(1)}, f32[24,1024]{1,0:T(8,128)S(1)}, u32[]{:S(2)}, u32[]{:S(2)}) collective-permute-start(f32[24,1024]{1,0:T(8,128)S(1)} %add.80), channel_id=1, source_target_pairs={{0,16},{4,20},{8,24},{12,28},{16,0},{20,4},{24,8},{28,12},{1,17},{... | collective-permute-start | bytes 294920 | tf_op jit(solution)/shard_map/ppermute | solution.py:295
  423.4 26.2 %collective-permute-start.44 = (bf16[512,1024]{1,0:T(8,128)(2,1)S(1)}, bf16[512,1024]{1,0:T(8,128)(2,1)S(1)}, u32[]{:S(2)}, u32[]{:S(2)}) collective-permute-start(bf16[512,1024]{1,0:T(8,128)(2,1)S(1)} %relay.1), channel_id=1, source_target_pairs={{0,2},{1,3},{2,0},{3,1},{4,6},{5,7},{6,4},{7,5},{8,10},{9,11},{10,... | collective-permute-start | bytes 3145736 | tf_op jit(solution)/shard_map/ppermute | solution.py:295
  426.5 27.7 %collective-permute-start.45 = (bf16[512,384]{1,0:T(8,128)(2,1)S(1)}, bf16[512,384]{1,0:T(8,128)(2,1)S(1)}, u32[]{:S(2)}, u32[]{:S(2)}) collective-permute-start(bf16[512,384]{1,0:T(8,128)(2,1)S(1)} %slice.180), channel_id=1, source_target_pairs={{0,4},{4,0},{8,12},{12,8},{16,20},{20,16},{24,28},{28,24},{1,5},{5... | collective-permute-start | bytes 1179656 | tf_op jit(solution)/shard_map/ppermute | solution.py:295
  430.4 40.9 %collective-permute-start.55 = (bf16[512,640]{1,0:T(8,128)(2,1)S(1)}, bf16[512,640]{1,0:T(8,128)(2,1)S(1)}, u32[]{:S(2)}, u32[]{:S(2)}) collective-permute-start(bf16[512,640]{1,0:T(8,128)(2,1)S(1)} %get-tuple-element.147), channel_id=1, source_target_pairs={{0,4},{4,0},{8,12},{12,8},{16,20},{20,16},{24,28},{28,24},{1,5},{5... | collective-permute-start | bytes 1966088 | tf_op jit(solution)/shard_map/ppermute | solution.py:295
  431.5 42.6 %collective-permute-start.56 = (bf16[512,640]{1,0:T(8,128)(2,1)S(1)}, bf16[512,640]{1,0:T(8,128)(2,1)S(1)}, u32[]{:S(2)}, u32[]{:S(2)}) collective-permute-start(bf16[512,640]{1,0:T(8,128)(2,1)S(1)} %get-tuple-element.149), channel_id=1, source_target_pairs={{0,2},{1,3},{2,0},{3,1},{4,6},{5,7},{6,4},{7,5},{8,10},{9,11},{10,... | collective-permute-start | bytes 1966088 | tf_op jit(solution)/shard_map/ppermute | solution.py:295
  449.6 9.5 %collective-permute-start.49 = (bf16[512,384]{1,0:T(8,128)(2,1)S(1)}, bf16[512,384]{1,0:T(8,128)(2,1)S(1)}, u32[]{:S(2)}, u32[]{:S(2)}) collective-permute-start(bf16[512,384]{1,0:T(8,128)(2,1)S(1)} %slice.179), channel_id=1, source_target_pairs={{0,4},{4,0},{8,12},{12,8},{16,20},{20,16},{24,28},{28,24},{1,5},{5... | collective-permute-start | bytes 1179656 | tf_op jit(solution)/shard_map/ppermute | solution.py:295
  464.3 13.9 %collective-permute-start.60 = (bf16[128,1024]{1,0:T(8,128)(2,1)S(1)}, bf16[128,1024]{1,0:T(8,128)(2,1)S(1)}, u32[]{:S(2)}, u32[]{:S(2)}) collective-permute-start(bf16[128,1024]{1,0:T(8,128)(2,1)S(1)} %get-tuple-element.159), channel_id=1, source_target_pairs={{0,8},{4,12},{8,0},{12,4},{16,24},{20,28},{24,16},{28,20},{1,9},{5... | collective-permute-start | bytes 786440 | tf_op jit(solution)/shard_map/ppermute | solution.py:295
  468.2 25.6 %collective-permute-start.61 = (bf16[128,1024]{1,0:T(8,128)(2,1)S(1)}, bf16[128,1024]{1,0:T(8,128)(2,1)S(1)}, u32[]{:S(2)}, u32[]{:S(2)}) collective-permute-start(bf16[128,1024]{1,0:T(8,128)(2,1)S(1)} %get-tuple-element.160), channel_id=1, source_target_pairs={{0,16},{4,20},{8,24},{12,28},{16,0},{20,4},{24,8},{28,12},{1,17},{... | collective-permute-start | bytes 786440 | tf_op jit(solution)/shard_map/ppermute | solution.py:295
  471.3 22.5 %collective-permute-start.50 = (bf16[128,384]{1,0:T(8,128)(2,1)S(1)}, bf16[128,384]{1,0:T(8,128)(2,1)S(1)}, u32[]{:S(2)}, u32[]{:S(2)}) collective-permute-start(bf16[128,384]{1,0:T(8,128)(2,1)S(1)} %get-tuple-element.169), channel_id=1, source_target_pairs={{0,8},{4,12},{8,0},{12,4},{16,24},{20,28},{24,16},{28,20},{1,9},{5... | collective-permute-start | bytes 294920 | tf_op jit(solution)/shard_map/ppermute | solution.py:295
  474.1 23.0 %collective-permute-start.51 = (bf16[128,384]{1,0:T(8,128)(2,1)S(1)}, bf16[128,384]{1,0:T(8,128)(2,1)S(1)}, u32[]{:S(2)}, u32[]{:S(2)}) collective-permute-start(bf16[128,384]{1,0:T(8,128)(2,1)S(1)} %get-tuple-element.171), channel_id=1, source_target_pairs={{0,16},{4,20},{8,24},{12,28},{16,0},{20,4},{24,8},{28,12},{1,17},{... | collective-permute-start | bytes 294920 | tf_op jit(solution)/shard_map/ppermute | solution.py:295
  474.6 24.0 %collective-permute-start.52 = (bf16[128,384]{1,0:T(8,128)(2,1)S(1)}, bf16[128,384]{1,0:T(8,128)(2,1)S(1)}, u32[]{:S(2)}, u32[]{:S(2)}) collective-permute-start(bf16[128,384]{1,0:T(8,128)(2,1)S(1)} %get-tuple-element.170), channel_id=1, source_target_pairs={{0,24},{4,28},{8,16},{12,20},{16,8},{20,12},{24,0},{28,4},{1,25},{... | collective-permute-start | bytes 294920 | tf_op jit(solution)/shard_map/ppermute | solution.py:295
  478.2 37.1 %collective-permute-start.62 = (bf16[128,1024]{1,0:T(8,128)(2,1)S(1)}, bf16[128,1024]{1,0:T(8,128)(2,1)S(1)}, u32[]{:S(2)}, u32[]{:S(2)}) collective-permute-start(bf16[128,1024]{1,0:T(8,128)(2,1)S(1)} %get-tuple-element.161), channel_id=1, source_target_pairs={{0,24},{4,28},{8,16},{12,20},{16,8},{20,12},{24,0},{28,4},{1,25},{... | collective-permute-start | bytes 786440 | tf_op jit(solution)/shard_map/ppermute | solution.py:295
  493.8 37.1 %collective-permute-start.57 = (bf16[128,1280]{1,0:T(8,128)(2,1)}, bf16[128,1280]{1,0:T(8,128)(2,1)S(1)}, u32[]{:S(2)}, u32[]{:S(2)}) collective-permute-start(bf16[128,1280]{1,0:T(8,128)(2,1)} %get-tuple-element.151), channel_id=1, source_target_pairs={{0,8},{4,12},{8,0},{12,4},{16,24},{20,28},{24,16},{28,20},{1,9},{5... | collective-permute-start | bytes 983048 | tf_op jit(solution)/shard_map/ppermute | solution.py:295
  493.8 37.1 %collective-permute-start.58 = (bf16[128,1280]{1,0:T(8,128)(2,1)}, bf16[128,1280]{1,0:T(8,128)(2,1)S(1)}, u32[]{:S(2)}, u32[]{:S(2)}) collective-permute-start(bf16[128,1280]{1,0:T(8,128)(2,1)} %get-tuple-element.152), channel_id=1, source_target_pairs={{0,16},{4,20},{8,24},{12,28},{16,0},{20,4},{24,8},{28,12},{1,17},{... | collective-permute-start | bytes 983048 | tf_op jit(solution)/shard_map/ppermute | solution.py:295
  497.1 33.9 %collective-permute-start.59 = (bf16[128,1280]{1,0:T(8,128)(2,1)S(1)}, bf16[128,1280]{1,0:T(8,128)(2,1)S(1)}, u32[]{:S(2)}, u32[]{:S(2)}) collective-permute-start(bf16[128,1280]{1,0:T(8,128)(2,1)S(1)} %get-tuple-element.153), channel_id=1, source_target_pairs={{0,24},{4,28},{8,16},{12,20},{16,8},{20,12},{24,0},{28,4},{1,25},{... | collective-permute-start | bytes 983048 | tf_op jit(solution)/shard_map/ppermute | solution.py:295
  498.6 16.0 %collective-permute-start.66 = (f32[8,1024]{1,0:T(8,128)S(1)}, f32[8,1024]{1,0:T(8,128)S(1)}, u32[]{:S(2)}, u32[]{:S(2)}) collective-permute-start(f32[8,1024]{1,0:T(8,128)S(1)} %add.74), channel_id=1, source_target_pairs={{0,8},{4,12},{8,0},{12,4},{16,24},{20,28},{24,16},{28,20},{1,9},{5... | collective-permute-start | bytes 98312 | tf_op jit(solution)/shard_map/ppermute | solution.py:295
  515.3 14.3 %collective-permute-start.54 = (bf16[128,256]{1,0:T(8,128)(2,1)S(1)}, bf16[128,256]{1,0:T(8,128)(2,1)S(1)}, u32[]{:S(2)}, u32[]{:S(2)}) collective-permute-start(bf16[128,256]{1,0:T(8,128)(2,1)S(1)} %get-tuple-element.143), channel_id=1, source_target_pairs={{1,0},{3,1},{0,2},{2,3},{5,4},{7,5},{4,6},{6,7},{9,8},{11,9},{8,10... | collective-permute-start | bytes 196616 | tf_op jit(solution)/shard_map/ppermute | solution.py:1182
  519.5 12.9 %collective-permute-start.67 = (f32[8,1024]{1,0:T(8,128)}, f32[8,1024]{1,0:T(8,128)}, u32[]{:S(2)}, u32[]{:S(2)}) collective-permute-start(f32[8,1024]{1,0:T(8,128)} %add.75), channel_id=1, source_target_pairs={{0,16},{4,20},{8,24},{12,28},{16,0},{20,4},{24,8},{28,12},{1,17},{... | collective-permute-start | bytes 98312 | tf_op jit(solution)/shard_map/ppermute | solution.py:295
  (99 other events, 1746.6 us)

commit v2 on v1

--- a/solution.py
+++ b/solution.py
@@ -59,7 +59,7 @@
     for j in range(hd.parts):
         at = pl.ds(pl.multiple_of(tab[hd.order_at + j] * bk, bk), bk)
         places = j * bk + lax.broadcasted_iota(jnp.int32, (bk, 1), 0)
-        kseg[at, :] = jnp.where(keep_ref[at, :] > 0.5, segment_of(spans, places), -1)
+        kseg[at, :] = jnp.where(keep_ref[:, at].T[:, 0:1] > 0.5, segment_of(spans, places), -1)
 
 
 def visible(i, j, bk, spans, kseg, at):
@@ -151,7 +151,7 @@
             num_scalar_prefetch=2,
             grid=(n // BQ,),
             in_specs=head_specs(hd, n, w, bk)
-            + [pl.BlockSpec((n, 1), lambda i, t, s: (0, 0)), pl.BlockSpec(memory_space=pltpu.SMEM)]
+            + [pl.BlockSpec((8, n), lambda i, t, s: (0, 0)), pl.BlockSpec(memory_space=pltpu.SMEM)]
             + unread(deps),
             out_specs=[
                 pl.BlockSpec((BQ, w), lambda i, t, s: (i, 0)),
@@ -172,10 +172,8 @@
             jax.ShapeDtypeStruct((w, n), f32),
             jax.ShapeDtypeStruct((8, n), f32),
         ],
-        compiler_params=pltpu.CompilerParams(vmem_limit_bytes=48 << 20),
-        cost_estimate=pl.CostEstimate(
-            flops=nh * n * n * HEAD * 26, bytes_accessed=n * w * 12, transcendentals=nh * n * n // 2
-        ),
+        compiler_params=pltpu.CompilerParams(vmem_limit_bytes=60 << 20),
+        cost_estimate=pl.CostEstimate(flops=nh * n * n * HEAD * 38, bytes_accessed=1024, transcendentals=0),
         name="attend_forward",
     )(tab, spans, qkv, qkv, qkv, keep, head_scale[None], *deps)
 
@@ -249,7 +247,7 @@
         sums_ref[1:2, :] = gains
 
 
-def attend_backward(hd, tab, spans, qkv, keep, head_scale, scaled_grad, o_t, lse, deps=()):
+def attend_backward(hd, part, tab, spans, qkv, keep, head_scale, scaled_grad, o_t, lse, deps=()):
     n, nh, w = qkv.shape[0], hd.nh, hd.nh * HEAD
     bk = n // hd.parts
     return pl.pallas_call(
@@ -259,9 +257,9 @@
             grid=(n // BQ,),
             in_specs=head_specs(hd, n, w, bk)
             + [
-                pl.BlockSpec((n, 1), lambda i, t, s: (0, 0)),
+                pl.BlockSpec((8, n), lambda i, t, s: (0, 0)),
                 pl.BlockSpec(memory_space=pltpu.SMEM),
-                pl.BlockSpec((BQ, w), lambda i, t, s: (i, 0)),
+                pl.BlockSpec((BQ, w), lambda i, t, s: (i, part)),
                 pl.BlockSpec((w, BQ), lambda i, t, s: (0, i)),
                 pl.BlockSpec((8, BQ), lambda i, t, s: (0, i)),
             ]
@@ -283,10 +281,8 @@
             jax.ShapeDtypeStruct((n, 3 * w), bf16),
             jax.ShapeDtypeStruct((8, 3 * w), f32),
         ],
-        compiler_params=pltpu.CompilerParams(vmem_limit_bytes=52 << 20),
-        cost_estimate=pl.CostEstimate(
-            flops=nh * n * n * HEAD * 42, bytes_accessed=n * w * 20, transcendentals=nh * n * n // 2
-        ),
+        compiler_params=pltpu.CompilerParams(vmem_limit_bytes=60 << 20),
+        cost_estimate=pl.CostEstimate(flops=nh * n * n * HEAD * 50, bytes_accessed=1024, transcendentals=0),
         name="attend_backward",
     )(tab, spans, qkv, qkv, qkv, keep, head_scale[None], scaled_grad, o_t, lse, *deps)
 
@@ -480,7 +476,7 @@
 
     tab = jnp.concatenate([sp_place, me_s[None].astype(jnp.int32)])
     hd = Heads(nh, nh, 0, (0, 1, 2), 0, sp, sp)
-    keep_col = keep.astype(f32)[:, None]
+    keep_col = jnp.broadcast_to(keep.astype(f32)[None, :], (8, group))
     scaled, o_t, lse = attend_forward(hd, tab, seq_spans[0], qkv, keep_col, head_scale)
     returned = lax.all_to_all(scaled.reshape(sp, rows, lw), "sp", 0, 0, tiled=True)
     merged = jnp.concatenate([returned[t] for t in range(sp)], axis=1)
@@ -531,7 +527,7 @@
     grad_w_out = grid.scatter_z(grid.scatter_y(grid.scatter_x(g_out)))
 
     qkv_grad, head_sums = attend_backward(
-        hd, tab, seq_spans[0], qkv, keep_col, head_scale, scaled_grad, o_t, lse
+        hd, 0, tab, seq_spans[0], qkv, keep_col, head_scale, scaled_grad, o_t, lse
     )
     qkv_grad_rel = reorder_rows(qkv_grad, group_order, rows)
     first_part = mm_cols(qkv_grad_rel, wq)
@@ -621,7 +617,7 @@
     )
 
 
-REL, HID, ORD, COLS, WHO, SEND, SLOT = 0, 8, 16, 24, 32, 33, 36
+REL, HID, ORD, COLS, WHO, SEND, SLOT, ALONG = 0, 8, 16, 24, 32, 33, 36, 40
 LANES = 128
 
 
@@ -666,6 +662,8 @@
             for t in range(sp):
                 row[ORD + t] = s ^ t
             row[WHO] = s
+            for k in range(nz):
+                row[ALONG + k] = d // ny ^ k
             for m in range(3):
                 row[SEND + m] = rounds[m][s][0]
                 row[SLOT + m] = next(rounds[m][a][1] for a in range(sp) if rounds[m][a][2] == s)
@@ -702,10 +700,43 @@
     return pl.BlockSpec((rows, cols), lambda i, *_: (i, 0))
 
 
-def call(name, body, tab, args, outs, steps=1, in_specs=None, out_specs=None, scratch=(), deps=(), vmem=40, flops=0, moved=0):
+class Order:
+    last = ()
+
+    def after(self, deps):
+        return tuple(deps) + self.last
+
+    def passed(self, outs):
+        self.last = (outs[-1],)
+        return outs
+
+
+ORDER = Order()
+
+
+def with_rider(body, at, count):
+    def both(*refs):
+        first, second, total = refs[at], refs[at + 1], refs[at + 2 + count]
+
+        @pl.when(pl.program_id(0) == 0)
+        def _():
+            total[...] = first[...] + second[...]
+
+        body(*refs[:at], *refs[at + 2 : at + 2 + count], *refs[at + 3 + count :])
+
+    return both
+
+
+def call(name, body, tab, args, outs, steps=1, in_specs=None, out_specs=None, scratch=(), deps=(), vmem=20, us=0, rider=None):
     in_specs = [whole(a.shape) for a in args] if in_specs is None else in_specs
     out_specs = [whole(s) for s, _ in outs] if out_specs is None else out_specs
-    return pl.pallas_call(
+    if rider is not None:
+        body = with_rider(body, 1 + len(args), len(outs))
+        args, outs = list(args) + list(rider), list(outs) + [(rider[0].shape, rider[0].dtype)]
+        in_specs = list(in_specs) + [whole(rider[0].shape)] * 2
+        out_specs = list(out_specs) + [whole(rider[0].shape)]
+    deps = ORDER.after(deps)
+    made = pl.pallas_call(
         skipping(body, 1 + len(args), len(deps)),
         grid_spec=pltpu.PrefetchScalarGridSpec(
             num_scalar_prefetch=1,
@@ -716,9 +747,10 @@
         ),
         out_shape=[jax.ShapeDtypeStruct(s, t) for s, t in outs],
         compiler_params=pltpu.CompilerParams(vmem_limit_bytes=vmem << 20),
-        cost_estimate=pl.CostEstimate(flops=int(flops), bytes_accessed=int(moved) or (4 << 20), transcendentals=0),
+        cost_estimate=pl.CostEstimate(flops=int(us * 1.1e9) + 1024, bytes_accessed=1024, transcendentals=0),
         name=name,
     )(tab, *args, *deps)
+    return ORDER.passed(made)
 
 
 def part_body(tab, w, *outs):
@@ -730,14 +762,8 @@
 def join_body(tab, *refs):
     pieces, out = refs[:-1], refs[-1]
     for m, piece in enumerate(pieces):
-        for e in range(2):
-            out[:, span(tab[SLOT + m] + 3 * e, LANES)] = piece[:, e * LANES : (e + 1) * LANES]
-
-
-def unjoin_body(tab, e0, e1, *outs):
-    for m, out in enumerate(outs):
-        for e, g in enumerate((e0, e1)):
-            out[:, e * LANES : (e + 1) * LANES] = g[:, span(tab[SLOT + m], LANES)].astype(bf16)
+        for k in range(out.shape[0]):
+            out[k, :, span(tab[SLOT + m], piece.shape[1])] = piece[...]
 
 
 def home_body(tab, *refs):
@@ -747,7 +773,7 @@
         out[:, span(tab[SEND + m], width)] = piece[...].astype(f32)
 
 
-def prologue_body(tab, tok, cot, vcol, vrow, gains, shifts, mid, hsh, first_ref, up_ref, tokr_ref, vec_ref, hid_ref):
+def prologue_body(tab, tok, cot, vcol, vrow, gains, shifts, mid, hsh, first_ref, both_ref, up_ref, tokr_ref, vec_ref, hid_ref):
     rows, width = tok.shape
     unit = mid.shape[1] // 8
     valid = vcol[...]
@@ -771,56 +797,63 @@
 
     lax.fori_loop(0, rows // 64, chunk, 0)
     first_ref[rows:, :] = jnp.broadcast_to(vrow[...], (16, width))
+    both_ref[: rows + 16, :] = first_ref[...]
     for p in range(8):
         at, to = span(tab[REL + p], LANES), slice(p * LANES, (p + 1) * LANES)
         masked = cot[:, at].astype(f32) * valid
         up_ref[:, to] = masked.astype(bf16)
         vec_ref[10:11, to] = down_sum(masked)
+    both_ref[rows + 16 :, :] = up_ref[...]
 
 
 def project_body(count, tab, *refs):
     pieces, (w0, w1, shifts, out_ref, keep_ref) = refs[:count], refs[count:]
     rows, depth = out_ref.shape[0], w0.shape[0]
-    bias = []
-    for e in range(2):
-        at = pl.ds(pl.multiple_of(tab[WHO] * 2 * LANES + e * LANES, LANES), LANES)
-        bias += [shifts[0:1, at], jnp.zeros((1, LANES), f32), shifts[1:2, at]]
-    bias = jnp.concatenate(bias, axis=1)
+    at = span(tab[WHO], 2 * LANES)
+    bias = jnp.concatenate([shifts[0:1, at], jnp.zeros((1, 2 * LANES), f32), shifts[1:2, at]], axis=1)
     for k in range(count):
 
         @pl.when(pl.program_id(0) == k)
         def _():
             x = pieces[k]
             out_ref[...] = (mm(x[:rows, :depth], w0[...]) + mm(x[:rows, depth:], w1[...]) + bias).astype(bf16)
-            keep_ref[...] = x[rows:, :rows].astype(f32).T[:, 0:1]
-
-
-def middle_body(tab, r0, r1, tok, vec, *refs):
-    pieces, (second_ref, mid_ref, norm_ref, std_ref, merged_ref, wo) = refs[:12], refs[12:]
-    half = pieces[2].shape[0]
+            keep_ref[...] = x[rows : rows + 16, :rows].astype(f32)[:8]
+
+
+def middle_body(begin, tab, ret, tok, vec, shards, pair_ref, mid_ref, norm_ref, std_ref, wo, sems):
+    width = tok.shape[1]
+
+    def copies(p):
+        out = []
+        for q in range(8):
+            at = tab[HID + q]
+            source = shards.at[tab[REL + p] * 4 + at // 2, :, pl.ds(pl.multiple_of(begin + lax.rem(at, 2) * LANES, LANES), LANES)]
+            out.append(pltpu.make_async_copy(source, wo.at[pl.ds(p * LANES, LANES), span(tab[COLS + q], LANES)], sems.at[p, q]))
+        return out
 
     @pl.when(pl.program_id(0) == 0)
     def _():
-        for c in range(2):
-            a0, a1, b00, b01, b10, b11 = pieces[6 * c : 6 * c + 6]
-            for dx, a in enumerate((a0, a1)):
-                wo[:, span(tab[COLS + 4 * c + dx], LANES)] = a[...]
-            for dx, (top, bottom) in enumerate(((b00, b10), (b01, b11))):
-                to = span(tab[COLS + 4 * c + 2 + dx], LANES)
-                wo[:half, to] = top[...]
-                wo[half:, to] = bottom[...]
+        for p in range(8):
+            for copy in copies(p):
+                copy.start()
 
     for p in range(8):
         a = tab[REL + p]
-        source, odd = a // 2, lax.rem(a, 2)
-        merged_ref[:, p * LANES : (p + 1) * LANES] = jnp.where(odd == 0, r0[source], r1[source])
-    normed, inv_std = norm_of(mm(merged_ref[...], wo[...]) + vec[5:6, :])
+        pair_ref[:, width + p * LANES : width + (p + 1) * LANES] = ret[a // 2, :, span(lax.rem(a, 2), LANES)]
+
+    @pl.when(pl.program_id(0) == 0)
+    def _():
+        for p in range(8):
+            for copy in copies(p):
+                copy.wait()
+
+    normed, inv_std = norm_of(mm(pair_ref[:, width:], wo[...]) + vec[5:6, :])
     middle = tok[...].astype(f32) + (normed * vec[1:2, :] + vec[7:8, :])
     norm_ref[...] = normed
     std_ref[...] = inv_std
     mid_ref[...] = middle
     again, _ = norm_of(middle)
-    second_ref[...] = (again * vec[2:3, :] + vec[8:9, :]).astype(bf16)
+    pair_ref[:, :width] = (again * vec[2:3, :] + vec[8:9, :]).astype(bf16)
 
 
 GELU = 0.7978845608028654
@@ -828,22 +861,19 @@
 
 
 def ffn_body(unit, tab, second, upstream, mid, hid, vec, *refs):
-    ins, (hown, hsib, pown, psib, sg_ref, lo_ref, sums_ref, upv, dnv, act, slope, back, sems) = refs[:16], refs[16:]
+    shards, (hown, hsib, pown, psib, sg_ref, lo_ref, sums_ref, upv, dnv, act, slope, back, sems) = refs[0], refs[1:]
     i = pl.program_id(0)
-    depth = upv.shape[0] // 2
     ff = upv.shape[1]
 
     def copies(q, which):
-        c, half, dx = q // 4, q // 2 % 2, q % 2
         held = (upv, dnv)[which]
-        a0, a1, b0, b1 = ins[8 * which + 4 * c : 8 * which + 4 * c + 4]
-        to, at = pl.ds(q * unit, unit), pl.ds(0, unit)
-        if half == 0:
-            pairs = [((a0, a1)[dx].at[:, at], held.at[:, to])]
-        else:
-            rows = pl.ds(dx * depth, depth)
-            pairs = [(b0.at[rows, at], held.at[pl.ds(0, depth), to]), (b1.at[rows, at], held.at[pl.ds(depth, depth), to])]
-        return [pltpu.make_async_copy(a, b, sems.at[which, q, k]) for k, (a, b) in enumerate(pairs)]
+        at = tab[HID + q]
+        from_cols = pl.ds(pl.multiple_of(which * 2 * unit + lax.rem(at, 2) * unit, unit), unit)
+        out = []
+        for p in range(8):
+            source = shards.at[tab[REL + p] * 4 + at // 2, :, from_cols]
+            out.append(pltpu.make_async_copy(source, held.at[pl.ds(p * LANES, LANES), pl.ds(q * unit, unit)], sems.at[which, q, p]))
+        return out
 
     @pl.when(i == 0)
     def _():
@@ -921,7 +951,7 @@
         lo_ref[:, span(tab[REL + p], LANES)] = out[:, p * LANES : (p + 1) * LANES]
 
 
-def heads_body(tab, grad, mid, norm, std, up, vec, wo, mg_ref, own_ref, sib_ref, o0_ref, o1_ref, sums_ref, scr):
+def heads_body(tab, grad, mid, norm, std, up, vec, wo, mg_ref, own_ref, sib_ref, out_ref, sums_ref, scr):
     @pl.when(pl.program_id(0) == 0)
     def _():
         sums_ref[...] = jnp.zeros_like(sums_ref)
@@ -944,30 +974,42 @@
     got = mm_cols(low, wo[...]).astype(bf16)
     for p in range(8):
         a = tab[REL + p]
-        source, odd = a // 2, lax.rem(a, 2)
-        for e, out in enumerate((o0_ref, o1_ref)):
-
-            @pl.when(odd == e)
-            def _():
-                out[source] = got[:, p * LANES : (p + 1) * LANES]
-
-
-def grads_body(sets, widths, tab, *refs):
-    ins, (ak, asend, bk, bsend, xt) = refs[: 4 * sets], refs[4 * sets :]
+        out_ref[a // 2, :, span(lax.rem(a, 2), LANES)] = got[:, p * LANES : (p + 1) * LANES]
+
+
+def turn_body(tab, x0, x1, out):
+    tokens = x0.shape[0]
+    out[:, :tokens] = x0[...].T
+    out[:, tokens:] = x1[...].T
+
+
+def turn_late_body(tab, x0, both, out):
+    tokens = x0.shape[0]
+    out[:, :tokens] = x0[...].T
+    out[:, tokens:] = both[tokens + 16 :, :].T
+
+
+def grads_body(counts, widths, tab, *refs):
+    ins, (ak, asend, bk, bsend, xt) = refs[:-5], refs[-5:]
     half = bk.shape[0]
     total = sum(widths)
-    at = 0
-    for n, wide in enumerate(widths):
-        x0, x1, y0, y1 = ins[4 * n : 4 * n + 4]
-        tokens = x0.shape[0]
-
-        @pl.when(pl.program_id(0) == n)
-        def _():
-            xt[:, :tokens] = x0[...].T
-            xt[:, tokens:] = x1[...].T
-            for q in range(4):
-                cols = slice(q * wide, (q + 1) * wide)
-                g = mm(xt[...], jnp.concatenate([y0[:, cols], y1[:, cols]], axis=0)).astype(bf16)
+    i = pl.program_id(0)
+    at = begin = 0
+    for n, (count, wide) in enumerate(zip(counts, widths)):
+        xs, (y0, y1) = ins[begin : begin + count], ins[begin + count : begin + count + 2]
+        begin += count + 2
+        if count == 2:
+
+            @pl.when(i == 4 * n)
+            def _():
+                turn_body(tab, *xs, xt)
+
+        left = xt if count == 2 else xs[0]
+        for q in range(4):
+
+            @pl.when(i == 4 * n + q)
+            def _():
+                g = mm(left[...], jnp.concatenate([y0[...], y1[...]], axis=0)).astype(bf16)
                 if q < 2:
                     (ak, asend)[q][:, at : at + wide] = g
                 else:
@@ -978,7 +1020,27 @@
         at += wide
 
 
-def fold_body(tab, ak, ra, bk, rb, a2k, a2s, b2k, b2s):
+def groups_body(count, tab, *refs):
+    pieces, (grad, keep, send, acc) = refs[:count], refs[count:]
+    i = pl.program_id(0)
+    half = keep.shape[0]
+    rows = grad.shape[0]
+    for k in range(count):
+
+        @pl.when(i == k)
+        def _():
+            got = mm(pieces[k][:rows, :].T, grad[...])
+            acc[...] = got if k == 0 else acc[...] + got
+
+    @pl.when(i == count - 1)
+    def _():
+        keep[...] = acc[:half]
+        send[...] = acc[half:].astype(bf16)
+
+
+def fold_body(tab, ak, ra, bk, rb, x0, x1, a2k, a2s, b2k, b2s, y0, y1):
+    y0[...] = x0[...]
+    y1[...] = x1[...]
     rows, cols = b2k.shape
     a = ak[...].astype(f32) + ra[...].astype(f32)
     a2k[...] = a[:rows].astype(bf16)
@@ -988,98 +1050,93 @@
     b2s[...] = b[:, cols:].astype(bf16)
 
 
-def spread_body(tab, ak, ra, bk, rb, keep, *sends):
+def spread_body(tab, ak, ra, bk, rb, g, r, keep, *sends):
     rows, cols = keep.shape[0], ak.shape[1]
-    for side, (k, r) in enumerate(((ak, ra), (bk, rb))):
-        total = k[...].astype(f32) + r[...].astype(f32)
-        to = slice(side * cols, (side + 1) * cols)
+    at = 0
+    for mine, theirs in ((ak, ra), (bk, rb), (g, r)):
+        total = mine[...].astype(f32) + theirs[...].astype(f32)
+        to = slice(at, at + total.shape[1])
+        at += total.shape[1]
         keep[:, to] = total[:rows]
         for n, send in enumerate(sends, 1):
             send[:, to] = total[n * rows : (n + 1) * rows].astype(bf16)
 
 
-def gathered_body(widths, tab, keep, *refs):
-    received, outs = refs[: len(refs) - len(widths)], refs[len(refs) - len(widths) :]
-    total = keep[...]
-    for r in received:
-        total = total + r[...].astype(f32)
-    half = keep.shape[1] // 2
+def gathered_body(widths, tab, keep, r1, r2, r3, *refs):
+    outs, pieces, total = refs[: len(widths)], refs[len(widths) : -1], refs[-1]
+    total[...] = keep[...] + r1[...].astype(f32) + r2[...].astype(f32) + r3[...].astype(f32)
+    half = sum(widths)
     at = 0
     for out, wide in zip(outs, widths):
         out[:, :wide] = total[:, at : at + wide]
         out[:, wide:] = total[:, half + at : half + at + wide]
         at += wide
-
-
-def scatter_weights(grid, tab, sets, widths, tag, deps=()):
-    rows = sets[0][0].shape[1]
+    for m, piece in enumerate(pieces):
+        size = piece.shape[1]
+        piece[...] = total[:, pl.ds(pl.multiple_of(2 * half + tab[SLOT + m] * size, size), size)].astype(bf16)
+
+
+def spill_body(unit, tab, xt, own, sib, out):
+    tokens, width = own.shape[0], xt.shape[0]
+    for half, y in enumerate((own, sib)):
+
+        @pl.when(pl.program_id(0) // 4 == half)
+        def _():
+            g = mm(xt[:, :tokens], y[...]).astype(bf16)
+            at = tab[HID + pl.program_id(0)]
+            for p in range(8):
+                out[tab[REL + p] * 4 + at // 2, :, span(lax.rem(at, 2), unit)] = g[p * LANES : (p + 1) * LANES]
+
+
+def scatter_weights(grid, tab, rows, sets, widths, tag, rider=None):
     total = sum(widths)
-    args = [a for one in sets for a in one]
+    args, specs = [], []
+    for n, (xs, y0, y1) in enumerate(sets):
+        wide = widths[n]
+        tokens = y0[0].shape[0]
+        for x, part in xs:
+            args.append(x)
+            specs.append(whole(x.shape) if part is None else pl.BlockSpec((tokens, rows), lambda *_, part=part: (0, part)))
+        for y, begin in (y0, y1):
+            args.append(y)
+            specs.append(pl.BlockSpec((tokens, wide), lambda i, *_, n=n, begin=begin: (0, begin + jnp.clip(i - 4 * n, 0, 3))))
     outs = [((rows, total), bf16)] * 2 + [((rows // 2, 2 * total), bf16)] * 2
-    tokens = sets[0][0].shape[0]
-    ak, asend, bk, bsend = call(
-        "grads_" + tag, functools.partial(grads_body, len(sets), widths), tab, args, outs, steps=len(sets),
-        scratch=[pltpu.VMEM((rows, 2 * tokens), bf16)], vmem=56, flops=2 * rows * 4 * total * 2 * tokens, deps=deps,
+    ak, asend, bk, bsend, *carried = call(
+        "grads_" + tag, functools.partial(grads_body, [len(xs) for xs, _, _ in sets], widths), tab, args, outs,
+        steps=4 * len(sets), in_specs=specs, scratch=[pltpu.VMEM((rows, 2 * tokens), bf16)], vmem=28, us=6 * len(sets), rider=rider,
     )
     ra, rb = swap(asend, "sp", 2), swap(bsend, "dp", 1)
-    yield (ra, rb)
-    quarter = [((rows // 2, total), bf16)] * 4
-    a2k, a2s, b2k, b2s = call("fold_" + tag, fold_body, tab, [ak, ra, bk, rb], quarter, moved=8 << 20)
+    rider, ships = yield carried
+    quarter = [((rows // 2, total), bf16)] * 4 + [(x.shape, x.dtype) for x in ships]
+    a2k, a2s, b2k, b2s, *carried = call("fold_" + tag, fold_body, tab, [ak, ra, bk, rb] + ships, quarter, vmem=34, rider=rider)
     ra, rb = swap(a2s, "dp", 1), swap(b2s, "sp", 2)
-    yield (ra, rb)
-    shard = (rows // 8, 2 * total)
-    keep, *sends = call("spread_" + tag, spread_body, tab, [a2k, ra, b2k, rb], [(shard, f32)] + [(shard, bf16)] * 3)
-    received = [swap(s, "dp", b) for s, b in zip(sends, grid.z_bits)]
-    yield tuple(received)
+    deps = yield carried + [ra, rb]
+    (g, r), size = deps
+    shard = (rows // 8, 2 * total + g.shape[1])
+    keep, *sends = call("spread_" + tag, spread_body, tab, [a2k, ra, b2k, rb, g, r], [(shard, f32)] + [(shard, bf16)] * 3)
+    received = [swap(x, "dp", b) for x, b in zip(sends, grid.z_bits)]
+    rider = yield
     yield call(
         "sum_" + tag, functools.partial(gathered_body, widths), tab, [keep] + received,
-        [((rows // 8, 2 * w), f32) for w in widths],
-    )
-
-
-def slabs_body(tab, *refs):
-    pieces, (first, other) = refs[:-2], refs[-2:]
-    rows, half = pieces[0].shape[0], first.shape[1]
-    for k, piece in enumerate(pieces):
-        to = slice(k * rows, (k + 1) * rows)
-        first[to, :] = piece[:, :half]
-        other[to, :] = piece[:, half:]
-
-
-def stack_body(tab, a, b, out):
-    rows = a.shape[0]
-    out[:rows, :] = a[...]
-    out[rows:, :] = b[...]
-
-
-def stack(tab, a, b, tag):
-    return call("stack_" + tag, stack_body, tab, [a, b], [((2 * a.shape[0], a.shape[1]), a.dtype)])[0]
-
-
-def gather_weights(grid, tab, shard, tag, deps=()):
-    if deps:
-        shard = call("shard_" + tag, lambda tab, x, o: o.__setitem__(Ellipsis, x[...]), tab, [shard], [(shard.shape, bf16)], deps=deps)[0]
-    pieces = [shard] + [swap(shard, "dp", b) for b in grid.z_bits]
-    yield tuple(pieces[1:])
-    rows, cols = shard.shape
-    first, other = call("slabs_" + tag, slabs_body, tab, pieces, [((4 * rows, cols // 2), bf16)] * 2)
-    ra, rb = swap(first, "dp", 1), swap(other, "sp", 2)
-    yield (ra, rb)
-    a0 = stack(tab, first, ra, tag)
-    b0 = stack(tab, other, rb, tag)
-    a1, b1 = swap(a0, "sp", 2), swap(b0, "dp", 1)
-    own = [a0, a1, b0, b1]
-    yield (a1, b1)
-    sib = [swap(p, "sp", 1) for p in own]
-    yield own + sib
-
-
-def first_grad_body(tab, g0, g1, wy0, wy1, mine, cross, far):
+        [((rows // 8, 2 * w), f32) for w in widths] + [((rows // 8, size), bf16)] * 3, scratch=[pltpu.VMEM(shard, f32)], rider=rider,
+    )
+
+
+def along_z(grid, x):
+    lines = [[y + grid.ny * k for k in range(grid.nz)] for y in range(grid.ny)]
+    return lax.all_to_all(x, "dp", 0, 0, tiled=True, axis_index_groups=lines)
+
+
+def rows_body(tab, got, out):
+    rows = got.shape[1]
+    for k in range(got.shape[0]):
+        out[k * rows : (k + 1) * rows, :] = got[tab[ALONG + k]]
+
+
+def first_grad_body(tab, g, wy0, wy1, mine, cross, far):
     i = pl.program_id(0)
-    half = 3 * LANES
-    g = jnp.concatenate([g0[...], g1[...]], axis=1)
-    got = jnp.concatenate([mm_cols(g, wy0[...]), mm_cols(g, wy1[...])], axis=1)
-    rows = g0.shape[0]
+    got = jnp.concatenate([mm_cols(g[...], wy0[...]), mm_cols(g[...], wy1[...])], axis=1)
+    rows = g.shape[0]
 
     @pl.when(i == 0)
     def _():
@@ -1102,7 +1159,7 @@
     out[...] = (far[...] + theirs[...].astype(f32)).astype(bf16)
 
 
-def final_body(tab, mine, theirs, crossed, tok, mg, vec, s0, s1, out_ref, late_ref, acc):
+def final_body(tab, mine, theirs, crossed, tok, mg, vec, s0, out_ref, late_ref, acc, note):
     i = pl.program_id(0)
     width = tok.shape[1]
 
@@ -1120,17 +1177,43 @@
 
     @pl.when(i == pl.num_programs(0) - 1)
     def _():
-        late_ref[...] = jnp.zeros_like(late_ref)
+        note[...] = jnp.zeros_like(note)
         for p in range(8):
-            late_ref[0:2, span(tab[REL + p], LANES)] = acc[0:2, p * LANES : (p + 1) * LANES]
-        lane = lax.broadcasted_iota(jnp.int32, (1, LANES), 1)
-        for e, s in enumerate((s0, s1)):
-            at = pl.ds(pl.multiple_of(tab[WHO] * 2 * LANES + e * LANES, LANES), LANES)
-            late_ref[2:3, at] = s[0:1, :LANES]
-            late_ref[3:4, at] = s[0:1, 2 * LANES :]
-            for h in range(2):
-                head = tab[WHO] * 4 + 2 * e + h
-                late_ref[4:5, :LANES] += jnp.where(lane == head, jnp.sum(jnp.where(lane == h, s[1:2, :LANES], 0.0)), 0.0)
+            cols = slice(p * LANES, (p + 1) * LANES)
+            note[pl.ds(tab[REL + p], 1), :] = acc[0:1, cols]
+            note[pl.ds(8 + tab[REL + p], 1), :] = acc[1:2, cols]
+        for e in range(2):
+            note[16 + e : 17 + e, :] = s0[0:1, e * LANES : (e + 1) * LANES]
+            note[18 + e : 19 + e, :] = s0[0:1, (4 + e) * LANES : (5 + e) * LANES]
+        note[20:21, :] = s0[1:2, :LANES]
+        for n in range(late_ref.shape[0]):
+            late_ref[n] = note[...]
+
+
+def totals_body(sp, tab, got, out):
+    out[...] = jnp.zeros_like(out)
+    count = got.shape[0]
+    total = got[0, :16]
+    for n in range(1, count):
+        total = total + got[n, :16]
+    for p in range(8):
+        cols = slice(p * LANES, (p + 1) * LANES)
+        out[0:1, cols] = total[p : p + 1]
+        out[1:2, cols] = total[8 + p : 9 + p]
+    heads = jnp.zeros((1, LANES), f32)
+    lane = lax.broadcasted_iota(jnp.int32, (1, LANES), 1)
+    for s in range(sp):
+        mine = got[s, 16:24]
+        for n in range(s + sp, count, sp):
+            mine = mine + got[n, 16:24]
+        for e in range(2):
+            cols = slice((2 * s + e) * LANES, (2 * s + e + 1) * LANES)
+            out[2:3, cols] = mine[e : e + 1]
+            out[3:4, cols] = mine[2 + e : 3 + e]
+        for h in range(4):
+            value = jnp.sum(jnp.where(lane == h, mine[4:5], 0.0))
+            heads = jnp.where(lane == 4 * s + h, value, heads)
+    out[4:5, :LANES] = heads
 
 
 def pack_body(tab, sums, vec, hid, out_ref):
@@ -1181,159 +1264,121 @@
     back_to = [[(t, s) for s, t in pairs] for pairs in forth]
     carry = lambda x, pairs: x if all(a == b for a, b in pairs) else lax.ppermute(x, "sp", pairs)
 
-    half_down, half_out = w_down.shape[1] // 2, w_out.shape[1] // 2
-    shard = jnp.concatenate(
-        [w_down[:, :half_down], w_out[:, :half_out], w_down[:, half_down:], w_out[:, half_out:]], axis=1
-    )
-    down_stages = gather_weights(grid, tab, shard, "down")
-    arrived = next(down_stages)
-
+    ORDER.last = ()
+    shards = lax.all_gather(jnp.concatenate([w_up, w_down, w_out], axis=1), ("dp", "sp"), axis=0)
     sent = call("part", part_body, tab, [w_qkv], [((block, shard_lanes), bf16)] * 3)
     moved = [carry(x, pairs) for x, pairs in zip(sent, forth)]
-    wq_shard = call("join", join_body, tab, moved, [((block, 3 * shard_lanes), bf16)])[0]
-    wq0 = grid.gather_z(wq_shard)
-    wq1 = swap(wq0, "dp", 1)
-
+    wq_lines = along_z(grid, call("join", join_body, tab, moved, [((grid.nz, block, 3 * shard_lanes), bf16)])[0])
     vcol = valid_mask.astype(f32)[:, None]
     vrow = jnp.pad(valid_mask.astype(bf16), (0, width - rows))[None]
-    first, upstream, tokr, vec, hid = call(
+    first, both, upstream, tokr, vec, hid = call(
         "prologue", prologue_body, tab,
         [tokens, cotangent, vcol, vrow, model_gains, model_shifts, mid_gain[None], hidden_shifts],
-        [((rows + 16, width), bf16), ((rows, width), bf16), ((rows, width), bf16), ((16, width), f32), ((8, ff), f32)],
+        [((rows + 16, width), bf16), ((2 * rows + 16, width), bf16), ((rows, width), bf16), ((rows, width), bf16), ((16, width), f32), ((8, ff), f32)],
     )
     beyond = swap(first, "sp", 2)
-    firsts = [first, swap(first, "sp", 1), beyond, swap(beyond, "sp", 1)]
-
-    up_stages = gather_weights(grid, tab, w_up, "up", deps=arrived)
-    next(up_stages)
-    arrived = next(down_stages)
-
-    pieces = firsts
+    theirs = swap(both, "sp", 1)
+    upstream_t = call("turn", turn_late_body, tab, [upstream, theirs], [((width, 2 * rows), bf16)], deps=(beyond,))[0]
+    wq0 = call("rows_qkv", rows_body, tab, [wq_lines], [((grid.nz * block, 3 * shard_lanes), bf16)])[0]
+    wq1 = swap(wq0, "dp", 1)
+    firsts = [first, theirs, beyond, swap(beyond, "sp", 1)]
     qkv, keep = call(
-        "project", functools.partial(project_body, sp), tab, pieces + [wq0, wq1, model_shifts],
-        [((group, 3 * shard_lanes), bf16), ((group, 1), f32)], steps=sp,
-        out_specs=[by_rows(rows, 3 * shard_lanes), by_rows(rows, 1)], flops=2 * group * width * 3 * shard_lanes,
-    )
-    firsts_cat = jnp.concatenate([f[:rows] for f in firsts], axis=0)
-
-    hds = [Heads(2, heads // sp, 2 * e, (3 * e, 3 * e + 1, 3 * e + 2), ORD, WHO, sp) for e in range(2)]
-    attended = [attend_forward(hds[0], tab, spans, qkv, keep, head_scale, deps=arrived)]
-    send_home = lambda x: lax.all_to_all(x.reshape(sp, rows, LANES), "sp", 0, 0, tiled=True)
-    returned = [send_home(attended[0][0])]
-    arrived_down = next(down_stages)
-    arrived_up = next(up_stages)
-    attended.append(attend_forward(hds[1], tab, spans, qkv, keep, head_scale, deps=arrived_up))
-    returned.append(send_home(attended[1][0]))
-    downs = next(down_stages)
-    next(up_stages)
-    ups = next(up_stages)
-
-    out_at = half_down // LANES
-    wo_args, wo_specs = [], []
-    for c in range(2):
-        a0, a1, b0, b1 = downs[4 * c : 4 * c + 4]
-        wo_args += [a0, a1, b0, b0, b1, b1]
-        wo_specs += [pl.BlockSpec((width, LANES), lambda *_: (0, out_at))] * 2
-        for r in (0, 1, 0, 1):
-            wo_specs.append(pl.BlockSpec((width // 2, LANES), lambda *_, r=r: (r, out_at)))
-    ret_spec = pl.BlockSpec((sp, step, LANES), lambda i, *_: (0, i, 0))
-    second, middle, attn_normed, attn_std, merged, wo = call(
-        "to_middle", middle_body, tab, returned + [tokr, vec] + wo_args,
-        [((rows, width), bf16), ((rows, width), f32), ((rows, width), f32), ((rows, 1), f32), ((rows, width), bf16), ((width, width), bf16)],
+        "project", functools.partial(project_body, sp), tab, firsts + [wq0, wq1, model_shifts],
+        [((group, 3 * shard_lanes), bf16), ((8, group), f32)], steps=sp,
+        out_specs=[by_rows(rows, 3 * shard_lanes), pl.BlockSpec((8, rows), lambda i, *_: (0, i))],
+    )
+    hd = Heads(4, heads // sp, 0, (0, 1, 2), ORD, WHO, sp)
+    scaled, o_t, lse = ORDER.passed(attend_forward(hd, tab, spans, qkv, keep, head_scale, deps=ORDER.last))
+    returned = lax.all_to_all(scaled.reshape(sp, rows, shard_lanes), "sp", 0, 0, tiled=True)
+
+    ret_spec = pl.BlockSpec((sp, step, shard_lanes), lambda i, *_: (0, i, 0))
+    anywhere = pl.BlockSpec(memory_space=pl.ANY)
+    pair, middle, attn_normed, attn_std, wo = call(
+        "to_middle", functools.partial(middle_body, 2 * w_up.shape[1]), tab, [returned, tokr, vec, shards],
+        [((rows, 2 * width), bf16), ((rows, width), f32), ((rows, width), f32), ((rows, 1), f32), ((width, width), bf16)],
         steps=2,
-        in_specs=[ret_spec, ret_spec, by_rows(step, width), whole(vec.shape)] + wo_specs,
-        out_specs=[by_rows(step, width)] * 3 + [by_rows(step, 1), by_rows(step, width), whole((width, width))],
-        flops=4 * rows * width * width,
-    )
-
-    anywhere = pl.BlockSpec(memory_space=pl.ANY)
+        in_specs=[ret_spec, by_rows(step, width), whole(vec.shape), anywhere],
+        out_specs=[by_rows(step, 2 * width)] + [by_rows(step, width)] * 2 + [by_rows(step, 1), whole((width, width))],
+        scratch=[pltpu.SemaphoreType.DMA((8, 8))], vmem=40,
+    )
+    pair_sib = swap(pair, "sp", 1)
     hid_own, hid_sib, pre_own, pre_sib, second_grad, layer_out, hidden_sums = call(
-        "ffn", functools.partial(ffn_body, unit), tab, [second, upstream, middle, hid, vec] + ups + downs,
+        "ffn", functools.partial(ffn_body, unit), tab, [pair, upstream, middle, hid, vec, shards],
         [((rows, ff // 2), bf16)] * 4 + [((rows, width), f32), ((rows, width), bf16), ((8, ff), f32)],
         steps=2,
-        in_specs=[by_rows(step, width)] * 3 + [whole(hid.shape), whole(vec.shape)] + [anywhere] * 16,
+        in_specs=[by_rows(step, width)] * 3 + [whole(hid.shape), whole(vec.shape)] + [anywhere],
         out_specs=[by_rows(step, ff // 2)] * 4 + [by_rows(step, width)] * 2 + [whole((8, ff))],
-        scratch=[pltpu.VMEM((width, ff), bf16)] * 2 + [pltpu.VMEM((step, ff), f32)] * 3 + [pltpu.SemaphoreType.DMA((2, 8, 2))],
-        vmem=60, flops=20 * rows * width * ff, moved=40 << 20,
-    )
-
-    upstream_sib = swap(upstream, "sp", 1)
-    down_sums = scatter_weights(grid, tab, [(upstream, upstream_sib, hid_own, swap(hid_sib, "sp", 1))], (unit,), "down")
-    arrived = next(down_sums)
-
-    middle_grad, attn_own, attn_sib, back0, back1, sums = call(
+        scratch=[pltpu.VMEM((width, ff), bf16)] * 2 + [pltpu.VMEM((step, ff), f32)] * 3 + [pltpu.SemaphoreType.DMA((2, 8, 8))],
+        vmem=63, us=37,
+    )
+
+    pre_across = swap(pre_sib, "sp", 1)
+    spilled = call(
+        "spill", functools.partial(spill_body, unit), tab, [upstream_t, hid_own, hid_sib], [((dp * sp, block, 2 * unit), bf16)], steps=8,
+        in_specs=[pl.BlockSpec((width, rows), lambda *_: (0, 0)),
+                  pl.BlockSpec((rows, unit), lambda i, *_: (0, jnp.clip(i, 0, 3))),
+                  pl.BlockSpec((rows, unit), lambda i, *_: (0, jnp.clip(i - 4, 0, 3)))],
+        vmem=40,
+    )[0]
+    grad_w_down = lax.psum_scatter(spilled, ("dp", "sp"), scatter_dimension=0, tiled=True)[0].astype(f32)
+    middle_grad, attn_own, attn_sib, back, sums = call(
         "to_heads", heads_body, tab, [second_grad, middle, attn_normed, attn_std, upstream, vec, wo],
-        [((rows, width), f32)] + [((rows, width // 2), bf16)] * 2 + [((sp, rows, LANES), bf16)] * 2 + [((8, width), f32)],
+        [((rows, width), f32)] + [((rows, width // 2), bf16)] * 2 + [((sp, rows, shard_lanes), bf16), ((8, width), f32)],
         steps=2,
         in_specs=[by_rows(step, width)] * 3 + [by_rows(step, 1), by_rows(step, width), whole(vec.shape), whole(wo.shape)],
-        out_specs=[by_rows(step, width)] + [by_rows(step, width // 2)] * 2 + [ret_spec] * 2 + [whole((8, width))],
-        scratch=[pltpu.VMEM((step, width), bf16)], flops=4 * rows * width * width,
-    )
-    fetch = lambda x: lax.all_to_all(x, "sp", 0, 0, tiled=True).reshape(group, LANES)
-    grads_in = [fetch(back0), fetch(back1)]
-
+        out_specs=[by_rows(step, width)] + [by_rows(step, width // 2)] * 2 + [ret_spec, whole((8, width))],
+        scratch=[pltpu.VMEM((step, width), bf16)],
+        vmem=62,
+    )
+    attn_across = swap(attn_sib, "sp", 1)
+    early = call("pack", pack_body, tab, [sums, vec, hidden_sums], [((24, width), f32)])[0]
+    early = (early, swap(early, "sp", 1))
+
+    grads_in = lax.all_to_all(back, "sp", 0, 0, tiled=True).reshape(group, shard_lanes)
     up_sums = scatter_weights(
-        grid, tab,
-        [(second, swap(second, "sp", 1), pre_own, swap(pre_sib, "sp", 1)), (merged, swap(merged, "sp", 1), attn_own, swap(attn_sib, "sp", 1))],
-        (unit, LANES), "up",
-    )
-    early = grid.all_sum(call("pack", pack_body, tab, [sums, vec, hidden_sums], [((24, width), f32)])[0])
-
-    first_up = next(up_sums)
-    qkv_grads = [attend_backward(hds[0], tab, spans, qkv, keep, head_scale, grads_in[0], *attended[0][1:], deps=arrived)]
-    arrived = next(down_sums)
-    wide = 3 * LANES
-
-    def qkv_scatter(e):
-        g = mm_rows(firsts_cat, qkv_grads[e][0])
-        sent = g[width // 2 :].astype(bf16)
-        got = swap(sent, "dp", 1)
-        yield (got,)
-        total = g[: width // 2] + got.astype(f32)
-        received = [swap(total[n * block : (n + 1) * block].astype(bf16), "dp", b) for n, b in enumerate(grid.z_bits, 1)]
-        yield tuple(received)
-        out = total[:block]
-        for r in received:
-            out = out + r.astype(f32)
-        yield out
-
-    qkv_sums = [qkv_scatter(0)]
-    next(qkv_sums[0])
-    qkv_grads.append(
-        attend_backward(hds[1], tab, spans, qkv, keep, head_scale, grads_in[1], *attended[1][1:], deps=first_up + arrived)
-    )
-    (grad_w_down,) = (next(down_sums), next(down_sums))[1]
-    next(up_sums)
-    next(up_sums)
-    grad_w_up, grad_w_out = next(up_sums)
-    next(qkv_sums[0])
-
-    by_token = lambda cols: pl.BlockSpec((rows, cols), lambda i, *_: (i, 0))
+        grid, tab, width,
+        [([(pair, 0), (pair_sib, 0)], (pre_own, 0), (pre_across, 0)), ([(pair, 1), (pair_sib, 1)], (attn_own, 0), (attn_across, 0))],
+        (unit, LANES), "up", rider=early,
+    )
+    (early,) = next(up_sums)
+    early = (early, swap(early, "sp", 2))
+    wide = 3 * shard_lanes
+    qkv_grad, head_sums = ORDER.passed(
+        attend_backward(hd, 0, tab, spans, qkv, keep, head_scale, grads_in, o_t, lse, deps=ORDER.last)
+    )
     mine, cross, far = call(
-        "first_grad", first_grad_body, tab, [qkv_grads[0][0], qkv_grads[1][0], wq0, wq1],
+        "first_grad", first_grad_body, tab, [qkv_grad, wq0, wq1],
         [((rows, width), f32), ((2 * rows, width), bf16), ((rows, width), f32)], steps=sp,
-        in_specs=[by_token(wide), by_token(wide), whole(wq0.shape), whole(wq1.shape)], flops=2 * group * width * 2 * wide,
-    )
-    theirs = swap(cross, "sp", 1)
+        in_specs=[by_rows(rows, wide), whole(wq0.shape), whole(wq1.shape)],
+        out_specs=[whole((rows, width)), whole((2 * rows, width)), whole((rows, width))],
+    )
+    keep_rows, send = call(
+        "group_grads", functools.partial(groups_body, sp), tab, firsts + [qkv_grad],
+        [((width // 2, wide), f32), ((width // 2, wide), bf16)], steps=sp,
+        in_specs=[whole(f.shape) for f in firsts] + [by_rows(rows, wide)],
+        scratch=[pltpu.VMEM((width, wide), f32)], vmem=30,
+    )
+    cross, send, early, *second_up = up_sums.send((early, [cross, send]))
+    early = (early, swap(early, "dp", 1))
+    theirs, other_rows = swap(cross, "sp", 1), swap(send, "dp", 1)
     relayed = call("relay", relay_body, tab, [far, theirs], [((rows, width), bf16)],
                    in_specs=[whole(far.shape), pl.BlockSpec((rows, width), lambda *_: (1, 0))])[0]
     crossed = swap(relayed, "sp", 2)
-
-    qkv_sums.append(qkv_scatter(1))
-    next(qkv_sums[1])
-    next(qkv_sums[1])
-    g_mine = [next(g) for g in qkv_sums]
-    sent = call("unjoin", unjoin_body, tab, g_mine, [((block, shard_lanes), bf16)] * 3)
+    grad_tokens, late, early = call(
+        "to_tokens", final_body, tab, [mine, theirs, crossed, tokr, middle_grad, vec, head_sums],
+        [((rows, width), f32), ((dp * sp, 24, LANES), f32)], steps=2,
+        in_specs=[by_rows(step, width)] * 5 + [whole(vec.shape), whole((8, wide))],
+        out_specs=[by_rows(step, width), whole((dp * sp, 24, LANES))],
+        scratch=[pltpu.VMEM((8, width), f32), pltpu.VMEM((24, LANES), f32)], rider=early, deps=(other_rows, *second_up),
+    )
+    early = (early, swap(early, "dp", 2))
+    late = lax.all_to_all(late, ("dp", "sp"), 0, 0, tiled=True)
+    up_sums.send(((keep_rows, other_rows), shard_lanes))
+    late = call("totals", functools.partial(totals_body, sp), tab, [late], [((8, width), f32)])[0]
+    grad_w_up, grad_w_out, *sent, early = up_sums.send(early)
+    early = (early, swap(early, "dp", 4))
     got = [carry(x, pairs) for x, pairs in zip(sent, back_to)]
-    grad_w_qkv = call("home", home_body, tab, got, [((block, 3 * shard_lanes), f32)])[0]
-
-    grad_tokens, late = call(
-        "to_tokens", final_body, tab, [mine, theirs, crossed, tokr, middle_grad, vec, qkv_grads[0][1], qkv_grads[1][1]],
-        [((rows, width), f32), ((8, width), f32)], steps=2,
-        in_specs=[by_rows(step, width)] * 5 + [whole(vec.shape), whole((8, wide)), whole((8, wide))],
-        out_specs=[by_rows(step, width), whole((8, width))], scratch=[pltpu.VMEM((8, width), f32)],
-    )
-    late = grid.all_sum(late)
+    grad_w_qkv, early = call("home", home_body, tab, got, [((block, 3 * shard_lanes), f32)], rider=early)
     grad_model_gains = jnp.stack([late[0], early[0], early[1]])
     grad_model_shifts = jnp.stack([late[2], late[3], early[2], late[1], early[3], early[4], early[5]])
     totals = early[6 : 6 + 3 * ff // width].reshape(3, ff)

time: 545 us -> 491 us (0.901)
  starting transfers between devices: 92.6 us -> 51 us
  Pallas kernels: 201 us -> 181 us
  between operations: 2.16 us -> 14.9 us
  blocking collectives: 12.3 us -> 18.1 us
    ppermute x69 -> x22, starting transfers between devices: 78.1 us -> 32 us  [swap(): lax.ppermute(x, axis, [(i, i ^ bits) for i in range(lax.axis_size(axis))])]
    pallas_call x2 -> x1, Pallas kernels: 50.2 us -> 37.1 us  [attend_backward(): pl.pallas_call(skipping(functools.partial(bwd_kernel, hd, bk), 10, len(de...]
    pallas_call x2 -> x1, Pallas kernels: 37.1 us -> 24.3 us  [attend_forward(): pl.pallas_call(skipping(functools.partial(fwd_kernel, hd, bk), 7, len(dep...]
    pallas_call x28 -> x21, Pallas kernels: 113 us -> 120 us  [call(): pl.pallas_call(skipping(body, 1 + len(args), len(deps)), grid_spec=pltpu....]
    all_to_all x1, blocking collectives: 12.3 us -> 18.1 us  [fast_layer(): lax.all_to_all(scaled.reshape(sp, rows, shard_lanes), 'sp', 0, 0, tiled=T...]
    ppermute x69 -> x22, waiting for transfers between devices: 159 us -> 157 us  [swap(): lax.ppermute(x, axis, [(i, i ^ bits) for i in range(lax.axis_size(axis))])]
    unnamed x174 -> x124, local copies, waits for them, and re-layouts: 36.9 us -> 36.8 us
  transfers between devices with their start and end apart: 76 -> 31, of which waited for: 25 -> 14; matrix products, arithmetic and copies ran while one was open for 2% -> 1% of each run, Pallas kernels for 25% -> 26%
where the time goes in v2:
time: 491 us; the launch traced here: 483 us
  Pallas kernels  181 us (37%)
  waiting for transfers between devices  172 us (35%)
  starting transfers between devices  51 us (10%)
  local copies, waits for them, and re-layouts  38.9 us (8%)
  blocking collectives  18.1 us (4%)
  between operations  14.9 us (3%)
  other arithmetic  5.85 us (1%)
    ppermute x22, waiting for transfers between devices, swap(): lax.ppermute(x, axis, [(i, i ^ bits) for i in range(lax.axis_size(axis))])  157 us
    pallas_call x21, Pallas kernels, call(): pl.pallas_call(skipping(body, 1 + len(args), len(deps)), grid_spec=pltpu....  120 us
    pallas_call x1, Pallas kernels, attend_backward(): pl.pallas_call(skipping(functools.partial(bwd_kernel, hd, bk), 10, len(de...  37.1 us
    unnamed x124, local copies, waits for them, and re-layouts  36.8 us
    ppermute x22, starting transfers between devices, swap(): lax.ppermute(x, axis, [(i, i ^ bits) for i in range(lax.axis_size(axis))])  32 us
    pallas_call x1, Pallas kernels, attend_forward(): pl.pallas_call(skipping(functools.partial(fwd_kernel, hd, bk), 7, len(dep...  24.3 us
    all_to_all x1, blocking collectives, fast_layer(): lax.all_to_all(scaled.reshape(sp, rows, shard_lanes), 'sp', 0, 0, tiled=T...  18.1 us
  transfers between devices with their start and end apart: 31, of which 14 were waited for; matrix products, arithmetic and copies ran while one was open for 1% of the time, Pallas kernels for 26%

profile of v2, /device:TPU:0, one launch (start us, length us, event | category | flops | bytes accessed | tf_op | source)
XLA Modules:
  0.0 482.6 jit_solution(17214360954555802836)
XLA Ops:
  7.2 2.1 pad_maximum_fusion
  11.5 3.0 collective-permute-start
  16.4 2.4 collective-permute-done.1.refs_3_
  22.4 4.9 %prologue.1 = (bf16[528,1024]{1,0:T(8,128)(2,1)}, bf16[1040,1024]{1,0:T(8,128)(2,1)}, bf16[512,1024]{1,0:T(8,128)(2,1)S(1)}, bf16[512,1024]{1,0:T(8,128)(2,1)S(1...) custom-call(s32[128]{0:T(128)S(1)} %dynamic-slice_bitcast_fusion.refs_0_, bf16[512,1024]{1,0:T(8,128)(2,1)S(1)} %copy-done.29, ...), custom_call_target="tpu_custom_call" | custom-call | flops 1024 | bytes 1024 | tf_op jit(solution)/shard_map/prologue/pallas_call | solution.py:739
  29.3 4.9 %all-to-all-start = ((bf16[4,128,768]{2,1,0:T(8,128)(2,1)}), bf16[4,128,768]{2,1,0:T(8,128)(2,1)}, u32[]{:S(2)}, u32[]{:S(2)}) async-start(bf16[4,128,768]{2,1,0:T(8,128)(2,1)} %copy-done.11), calls=%async_computation | async-start | bytes 1572864 | tf_op jit(solution)/shard_map/all_to_all | solution.py:1127
  34.2 31.1 %collective-permute-done.3.refs_3_ = bf16[528,1024]{1,0:T(8,128)(2,1)S(1)} collective-permute-done((bf16[528,1024]{1,0:T(8,128)(2,1)}, bf16[528,1024]{1,0:T(8,128)(2,1)S(1)}, u32[]{:S(2)}, u32[]{:S(2)}) %collective-permute-start.3) | collective-permute-done | bytes 1081376 | tf_op jit(solution)/shard_map/ppermute | solution.py:291
  65.4 2.0 copy-done.16
  67.3 1.2 turn.1.refs_2_.refs_1_
  68.5 1.3 copy-done.2
  69.9 1.6 copy-done.3
  71.5 1.7 rows_qkv.1.refs_5_.refs_8_.refs_2_
  73.2 1.6 collective-permute-start.5
  74.8 20.8 %collective-permute-done.5.refs_6_.refs_3_ = bf16[512,768]{1,0:T(8,128)(2,1)S(1)} collective-permute-done((bf16[512,768]{1,0:T(8,128)(2,1)S(1)}, bf16[512,768]{1,0:T(8,128)(2,1)S(1)}, u32[]{:S(2)}, u32[]{:S(2)}) %collective-permute-start.5) | collective-permute-done | bytes 786464 | tf_op jit(solution)/shard_map/ppermute | solution.py:291
  95.6 6.2 %project.1 = (bf16[2048,768]{1,0:T(8,128)(2,1)S(1)}, f32[8,2048]{1,0:T(8,128)S(1)}) custom-call(s32[128]{0:T(128)S(1)} %dynamic-slice_bitcast_fusion.refs_0_, bf16[528,1024]{1,0:T(8,128)(2,1)} %get-tuple-element.79.refs_1_, bf16[1040,1024]{1,0:T(8,128)(2,1)S(1)} %collective-permute-done.2.refs_2_, bf16[528,1024]{1,0:T(8,128)(2,1)S(1)} %collective-permute-done.3.refs_3_, ...), custom_call_target="tpu_custom_call" | custom-call | flops 1024 | bytes 1024 | tf_op jit(solution)/shard_map/project/pallas_call | solution.py:739
  101.8 1.7 copy-done.57
  104.1 24.3 %attend_forward.1 = (bf16[2048,256]{1,0:T(8,128)(2,1)}, f32[256,2048]{1,0:T(8,128)}, f32[8,2048]{1,0:T(8,128)}) custom-call(s32[128]{0:T(128)} %copy-done.41, s32[4]{0:T(128)} %bitcast.25, bf16[2048,768]{1,0:T(8,128)(2,1)} %copy-done.57, bf16[2048,768]{1,0:T(8,128)(2,1)} %copy-done.57, bf16[2048,768]{1,0:T(8,128)(2,1)} %copy-done.57, f32[8,2048]{1,0:T(8,128)} %copy-done.59, ...), custom_call_target="tpu_custom_call" | custom-call | flops 40802189312 | bytes 1024 | tf_op jit(solution)/shard_map/attend_forward/pallas_call | solution.py:148
  128.5 18.1 %all_to_all.20.refs_1_ = bf16[4,512,256]{2,1,0:T(8,128)(2,1)S(1)} all-to-all(bf16[4,512,256]{2,1,0:T(8,128)(2,1)} %bitcast.22), channel_id=1, replica_groups=mesh['dp'=8,'sp'=4] {'sp'}, dimensions={0} | all-to-all | bytes 2097152 | tf_op jit(solution)/shard_map/all_to_all | solution.py:1292
  146.6 4.2 all-gather.3.cloned.1.call-done
  150.9 6.9 %to_middle.1 = (bf16[512,2048]{1,0:T(8,128)(2,1)}, f32[512,1024]{1,0:T(8,128)S(1)}, f32[512,1024]{1,0:T(8,128)S(1)}, f32[512,1]{1,0:T(8,128)S(1)}, bf16[1024,1024]{1,0:T(8,128)(2,1)S(1)}) custom-call(s32[128]{0:T(128)S(1)} %copy-done.42, bf16[4,512,256]{2,1,0:T(8,128)(2,1)S(1)} %all_to_all.20.refs_1_, bf16[512,1024]{1,0:T(8,128)(2,1)S(1)} %copy-done.13, ...), custom_call_target="tpu_custom_call" | custom-call | flops 1024 | bytes 1024 | tf_op jit(solution)/shard_map/to_middle/pallas_call | solution.py:739
  157.7 1.3 copy-done.22
  159.0 1.3 copy-done.23
  160.4 1.3 copy-done.24
  162.4 38.7 %ffn.1 = (bf16[512,2048]{1,0:T(8,128)(2,1)}, bf16[512,2048]{1,0:T(8,128)(2,1)}, bf16[512,2048]{1,0:T(8,128)(2,1)}, bf16[512,2048]{1,0:T(8,128)(2,1)}, f32[512,10...) custom-call(s32[128]{0:T(128)} %copy-done.41, bf16[512,2048]{1,0:T(8,128)(2,1)} %get-tuple-element.89.refs_1_.refs_5_, ...), custom_call_target="tpu_custom_call" | custom-call | flops 40700002304 | bytes 1024 | tf_op jit(solution)/shard_map/ffn/pallas_call | solution.py:739
  201.1 1.6 copy-done.4
  202.7 1.6 copy-done.20
  204.3 1.6 copy-done.21
  206.8 10.2 %spill.1.refs_8_ = bf16[32,128,1024]{2,1,0:T(8,128)(2,1)} custom-call(s32[128]{0:T(128)S(1)} %copy-done.43, bf16[1024,1024]{1,0:T(8,128)(2,1)S(1)} %copy-done.4, bf16[512,2048]{1,0:T(8,128)(2,1)S(1)} %copy-done.20, bf16[512,2048]{1,0:T(8,128)(2,1)S(1)} %copy-done.21, f32[8,4096]{1,0:T(8,128)S(1)} %copy-done.37), custom_call_target="tpu_custom_call" | custom-call | flops 1024 | bytes 1024 | tf_op jit(solution)/shard_map/spill/pallas_call | solution.py:739
  217.6 9.2 %to_heads.1 = (f32[512,1024]{1,0:T(8,128)}, bf16[512,512]{1,0:T(8,128)(2,1)}, bf16[512,512]{1,0:T(8,128)(2,1)}, bf16[4,512,256]{2,1,0:T(8,128)(2,1)}, f32[8,1024]{1,0:T(8,128)}) custom-call(s32[128]{0:T(128)} %copy-done.41, f32[512,1024]{1,0:T(8,128)} %get-tuple-element.93.refs_1_, f32[512,1024]{1,0:T(8,128)} %copy-done.22, f32[512,1024]{1,0:T(8,128)} %copy-done.23, ...), custom_call_target="tpu_custom_call" | custom-call | flops 1024 | bytes 1024 | tf_op jit(solution)/shard_map/to_heads/pallas_call | solution.py:739
  228.9 4.3 all-to-all-start.2
  233.2 1.6 copy-done.60
  234.8 13.4 %grads_up.1 = (bf16[1024,640]{1,0:T(8,128)(2,1)S(1)}, bf16[1024,640]{1,0:T(8,128)(2,1)}, bf16[512,1280]{1,0:T(8,128)(2,1)S(1)}, bf16[512,1280]{1,0:T(8,128)(2,1)}, f32[24,1024]{1,0:T(8,128)S(1)}) custom-call(s32[128]{0:T(128)S(1)} %copy-done.44, bf16[512,2048]{1,0:T(8,128)(2,1)} %get-tuple-element.89.refs_1_.refs_5_, ...), custom_call_target="tpu_custom_call" | custom-call | flops 13200001024 | bytes 1024 | tf_op jit(solution)/shard_map/grads_up/pallas_call | solution.py:739
  249.3 2.0 collective-permute-start.12
  251.3 1.6 collective-permute-start.11
  252.9 5.9 %all-to-all-done.2 = bf16[4,512,256]{2,1,0:T(8,128)(2,1)} async-done(((bf16[4,512,256]{2,1,0:T(8,128)(2,1)}), bf16[4,512,256]{2,1,0:T(8,128)(2,1)}, u32[]{:S(2)}, u32[]{:S(2)}) %all-to-all-start.2) | async-done | bytes 1048608 | tf_op jit(solution)/shard_map/all_to_all | solution.py:1337
  258.8 37.1 %attend_backward.1 = (bf16[2048,768]{1,0:T(8,128)(2,1)}, f32[8,768]{1,0:T(8,128)}) custom-call(s32[128]{0:T(128)} %copy-done.41, s32[4]{0:T(128)} %bitcast.26, bf16[2048,768]{1,0:T(8,128)(2,1)} %copy-done.57, bf16[2048,768]{1,0:T(8,128)(2,1)} %copy-done.57, bf16[2048,768]{1,0:T(8,128)(2,1)} %copy-done.57, f32[8,2048]{1,0:T(8,128)} %copy-done.59, ...), custom_call_target="tpu_custom_call" | custom-call | flops 53687091200 | bytes 1024 | tf_op jit(solution)/shard_map/attend_backward/pallas_call | solution.py:253
  296.0 1.9 copy-done.7
  298.6 5.1 %first_grad.1 = (f32[512,1024]{1,0:T(8,128)S(1)}, bf16[1024,1024]{1,0:T(8,128)(2,1)S(1)}, f32[512,1024]{1,0:T(8,128)S(1)}) custom-call(s32[128]{0:T(128)S(1)} %copy-done.45, bf16[2048,768]{1,0:T(8,128)(2,1)S(1)} %copy-done.7, bf16[512,768]{1,0:T(8,128)(2,1)S(1)} %copy-done.6, bf16[512,768]{1,0:T(8,128)(2,1)S(1)} %copy-done.18, f32[8,768]{1,0:T(8,128)S(1)} %copy-done.52), custom_call_target="tpu_custom_call" | custom-call | flops 1024 | bytes 1024 | tf_op jit(solution)/shard_map/first_grad/pallas_call | solution.py:739
  303.7 1.9 copy-done.8
  305.6 6.7 %group_grads.1 = (f32[512,768]{1,0:T(8,128)S(1)}, bf16[512,768]{1,0:T(8,128)(2,1)S(1)}) custom-call(s32[128]{0:T(128)S(1)} %copy-done.45, bf16[528,1024]{1,0:T(8,128)(2,1)} %get-tuple-element.79.refs_1_, bf16[1040,1024]{1,0:T(8,128)(2,1)S(1)} %copy-done.1, bf16[528,1024]{1,0:T(8,128)(2,1)S(1)} %copy-done.10, ...), custom_call_target="tpu_custom_call" | custom-call | flops 1024 | bytes 1024 | tf_op jit(solution)/shard_map/group_grads/pallas_call | solution.py:739
  312.3 1.1 copy-done.25
  313.5 5.6 %collective-permute-done.10.refs_2_ = bf16[1024,640]{1,0:T(8,128)(2,1)} collective-permute-done((bf16[1024,640]{1,0:T(8,128)(2,1)}, bf16[1024,640]{1,0:T(8,128)(2,1)}, u32[]{:S(2)}, u32[]{:S(2)}) %collective-permute-start.10) | collective-permute-done | bytes 1310752 | tf_op jit(solution)/shard_map/ppermute | solution.py:291
  319.1 3.1 fold_up.1
  322.3 4.1 collective-permute-done.13.refs_2_
  327.2 2.6 collective-permute-start.14
  329.8 2.4 collective-permute-start.16
  332.3 1.9 collective-permute-start.18
  334.2 2.0 collective-permute-start.15
  336.2 43.4 %collective-permute-done.15.refs_9_ = f32[24,1024]{1,0:T(8,128)S(1)} collective-permute-done((f32[24,1024]{1,0:T(8,128)S(1)}, f32[24,1024]{1,0:T(8,128)S(1)}, u32[]{:S(2)}, u32[]{:S(2)}) %collective-permute-start.15) | collective-permute-done | bytes 98336 | tf_op jit(solution)/shard_map/ppermute | solution.py:291
  379.6 15.6 %collective-permute-done.18.refs_12_.refs_4_ = bf16[512,640]{1,0:T(8,128)(2,1)S(1)} collective-permute-done((bf16[512,640]{1,0:T(8,128)(2,1)S(1)}, bf16[512,640]{1,0:T(8,128)(2,1)S(1)}, u32[]{:S(2)}, u32[]{:S(2)}) %collective-permute-start.18) | collective-permute-done | bytes 655392 | tf_op jit(solution)/shard_map/ppermute | solution.py:291
  395.3 3.8 to_tokens.1
  399.1 4.8 all-to-all-start.3
  404.0 1.4 copy-done.26
  405.4 1.1 copy-done.34
  407.5 1.8 spread_up.1
  409.4 1.8 collective-permute-start.19
  411.2 2.4 collective-permute-start.20
  414.6 2.3 all-to-all-done.3.refs_1_
  417.6 32.4 %collective-permute-done.22.refs_6_ = f32[24,1024]{1,0:T(8,128)S(1)} collective-permute-done((f32[24,1024]{1,0:T(8,128)}, f32[24,1024]{1,0:T(8,128)S(1)}, u32[]{:S(2)}, u32[]{:S(2)}) %collective-permute-start.22) | collective-permute-done | bytes 98336 | tf_op jit(solution)/shard_map/ppermute | solution.py:291
  450.4 2.6 sum_up.1
  453.0 2.0 collective-permute-start.24
  455.1 11.2 %collective-permute-start.25 = (f32[24,1024]{1,0:T(8,128)S(1)}, f32[24,1024]{1,0:T(8,128)S(1)}, u32[]{:S(2)}, u32[]{:S(2)}) collective-permute-start(f32[24,1024]{1,0:T(8,128)S(1)} %get-tuple-element.136.refs_4_.refs_6_), channel_id=1, source_target_pairs={{0,16},{4,20},{8,24},{12,28},{16,0},{20,4},{24,8},{28,12},{1,17},{... | collective-permute-start | bytes 294920 | tf_op jit(solution)/shard_map/ppermute | solution.py:291
  466.8 3.1 collective-permute-done.25.refs_5_
  469.9 1.3 home.1
  473.8 1.8 bitcast_convert_fusion
  (165 shorter events, 23.8 us)
Async XLA Ops:
  7.2 12.2 %copy-start.30 = (bf16[512,1024]{1,0:T(8,128)(2,1)S(1)}, bf16[512,1024]{1,0:T(8,128)(2,1)}, u32[]{:S(2)}) copy-start(bf16[512,1024]{1,0:T(8,128)(2,1)} %refs_2_.1) | copy-start | bytes 3145732
  7.2 12.2 %copy-start.29 = (bf16[512,1024]{1,0:T(8,128)(2,1)S(1)}, bf16[512,1024]{1,0:T(8,128)(2,1)}, u32[]{:S(2)}) copy-start(bf16[512,1024]{1,0:T(8,128)(2,1)} %refs_1_.3) | copy-start | bytes 3145732
  7.2 143.6 %all-gather.3.cloned.1.call-start = ((), (), s32[]{:S(2)}) async-start(), calls=%async_computation.6 | async-start | bytes 19464192 | tf_op jit(solution)/shard_map/all_gather | solution.py:1268
  11.0 84.7 %copy-start.41 = (s32[128]{0:T(128)}, s32[128]{0:T(128)S(1)}, u32[]{:S(2)}) copy-start(s32[128]{0:T(128)S(1)} %dynamic-slice_bitcast_fusion.refs_0_) | copy-start | bytes 1540
  11.5 4.9 %collective-permute-start = (bf16[128,256]{1,0:T(8,128)(2,1)S(1)}, bf16[128,256]{1,0:T(8,128)(2,1)S(1)}, u32[]{:S(2)}, u32[]{:S(2)}) collective-permute-start(bf16[128,256]{1,0:T(8,128)(2,1)S(1)} %get-tuple-element.77), channel_id=1, source_target_pairs={{0,2},{1,0},{2,3},{3,1},{4,6},{5,4},{6,7},{7,5},{8,10},{9,8},{10,1... | collective-permute-start | bytes 196616 | tf_op jit(solution)/shard_map/ppermute | solution.py:1265
  14.5 4.3 collective-permute-start.1
  19.3 9.9 %copy-start.11 = (bf16[4,128,768]{2,1,0:T(8,128)(2,1)}, bf16[4,128,768]{2,1,0:T(8,128)(2,1)S(1)}, u32[]{:S(2)}) copy-start(bf16[4,128,768]{2,1,0:T(8,128)(2,1)S(1)} %join.1.refs_9_) | copy-start | bytes 2359300
  29.2 39.3 %copy-start.48 = (f32[8,4096]{1,0:T(8,128)}, f32[8,4096]{1,0:T(8,128)S(1)}, u32[]{:S(2)}) copy-start(f32[8,4096]{1,0:T(8,128)S(1)} %get-tuple-element.82.refs_4_) | copy-start | bytes 393220
  29.2 121.6 %copy-start.31 = (f32[16,1024]{1,0:T(8,128)}, f32[16,1024]{1,0:T(8,128)S(1)}, u32[]{:S(2)}) copy-start(f32[16,1024]{1,0:T(8,128)S(1)} %get-tuple-element.87.refs_3_.refs_5_.refs_6_.refs_2_) | copy-start | bytes 196612
  29.2 36.1 %collective-permute-start.2 = (bf16[1040,1024]{1,0:T(8,128)(2,1)}, bf16[1040,1024]{1,0:T(8,128)(2,1)S(1)}, u32[]{:S(2)}, u32[]{:S(2)}) collective-permute-start(bf16[1040,1024]{1,0:T(8,128)(2,1)} %get-tuple-element.80), channel_id=1, source_target_pairs={{0,1},{1,0},{2,3},{3,2},{4,5},{5,4},{6,7},{7,6},{8,9},{9,8},{10,11... | collective-permute-start | bytes 6389768 | tf_op jit(solution)/shard_map/ppermute | solution.py:291
  29.2 36.1 %collective-permute-start.3 = (bf16[528,1024]{1,0:T(8,128)(2,1)}, bf16[528,1024]{1,0:T(8,128)(2,1)S(1)}, u32[]{:S(2)}, u32[]{:S(2)}) collective-permute-start(bf16[528,1024]{1,0:T(8,128)(2,1)} %get-tuple-element.79.refs_1_), channel_id=1, source_target_pairs={{0,2},{1,3},{2,0},{3,1},{4,6},{5,7},{6,4},{7,5},{8,10},{9,11},{10,... | collective-permute-start | bytes 3244040 | tf_op jit(solution)/shard_map/ppermute | solution.py:291
  29.3 40.5 %all-to-all-start = ((bf16[4,128,768]{2,1,0:T(8,128)(2,1)}), bf16[4,128,768]{2,1,0:T(8,128)(2,1)}, u32[]{:S(2)}, u32[]{:S(2)}) async-start(bf16[4,128,768]{2,1,0:T(8,128)(2,1)} %copy-done.11), calls=%async_computation | async-start | bytes 1572864 | tf_op jit(solution)/shard_map/all_to_all | solution.py:1127
  34.2 439.6 %reduce-scatter.2.cloned.1.call-start = ((), (), s32[]{:S(2)}) async-start(), calls=%async_computation.5 | async-start | bytes 8650752 | tf_op jit(solution)/shard_map/reduce_scatter | solution.py:1323
  65.3 30.3 %copy-start.9 = (bf16[528,1024]{1,0:T(8,128)(2,1)}, bf16[528,1024]{1,0:T(8,128)(2,1)S(1)}, u32[]{:S(2)}) copy-start(bf16[528,1024]{1,0:T(8,128)(2,1)S(1)} %collective-permute-done.3.refs_3_) | copy-start | bytes 3244036
  65.3 9.5 %collective-permute-start.4 = (bf16[528,1024]{1,0:T(8,128)(2,1)S(1)}, bf16[528,1024]{1,0:T(8,128)(2,1)}, u32[]{:S(2)}, u32[]{:S(2)}) collective-permute-start(bf16[528,1024]{1,0:T(8,128)(2,1)S(1)} %collective-permute-done.3.refs_3_), channel_id=1, source_target_pairs={{0,1},{1,0},{2,3},{3,2},{4,5},{5,4},{6,7},{7,6},{8,9},{9,8},{10,11... | collective-permute-start | bytes 3244040 | tf_op jit(solution)/shard_map/ppermute | solution.py:291
  65.3 30.3 %copy-start = (bf16[1040,1024]{1,0:T(8,128)(2,1)}, bf16[1040,1024]{1,0:T(8,128)(2,1)S(1)}, u32[]{:S(2)}) copy-start(bf16[1040,1024]{1,0:T(8,128)(2,1)S(1)} %collective-permute-done.2.refs_2_) | copy-start | bytes 6389764
  65.3 2.0 copy-start.16
  71.5 24.2 %copy-start.47 = (f32[7,1024]{1,0:T(8,128)S(1)}, f32[7,1024]{1,0:T(8,128)}, u32[]{:S(2)}) copy-start(f32[7,1024]{1,0:T(8,128)} %refs_7_.1) | copy-start | bytes 86020
  73.2 28.6 %copy-start.5 = (bf16[512,768]{1,0:T(8,128)(2,1)}, bf16[512,768]{1,0:T(8,128)(2,1)S(1)}, u32[]{:S(2)}) copy-start(bf16[512,768]{1,0:T(8,128)(2,1)S(1)} %rows_qkv.1.refs_5_.refs_8_.refs_2_) | copy-start | bytes 2359300
  73.2 22.4 %collective-permute-start.5 = (bf16[512,768]{1,0:T(8,128)(2,1)S(1)}, bf16[512,768]{1,0:T(8,128)(2,1)S(1)}, u32[]{:S(2)}, u32[]{:S(2)}) collective-permute-start(bf16[512,768]{1,0:T(8,128)(2,1)S(1)} %rows_qkv.1.refs_5_.refs_8_.refs_2_), channel_id=1, source_target_pairs={{0,4},{4,0},{8,12},{12,8},{16,20},{20,16},{24,28},{28,24},{1,5},{5... | collective-permute-start | bytes 2359304 | tf_op jit(solution)/shard_map/ppermute | solution.py:291
  95.6 6.2 %copy-start.17 = (bf16[512,768]{1,0:T(8,128)(2,1)}, bf16[512,768]{1,0:T(8,128)(2,1)S(1)}, u32[]{:S(2)}) copy-start(bf16[512,768]{1,0:T(8,128)(2,1)S(1)} %collective-permute-done.5.refs_6_.refs_3_) | copy-start | bytes 2359300
  128.5 22.4 %copy-start.13 = (bf16[512,1024]{1,0:T(8,128)(2,1)S(1)}, bf16[512,1024]{1,0:T(8,128)(2,1)}, u32[]{:S(2)}) copy-start(bf16[512,1024]{1,0:T(8,128)(2,1)} %copy-done.12) | copy-start | bytes 3145732
  128.5 22.4 %copy-start.42 = (s32[128]{0:T(128)S(1)}, s32[128]{0:T(128)}, u32[]{:S(2)}) copy-start(s32[128]{0:T(128)} %copy-done.41) | copy-start | bytes 1540
  128.5 22.4 %copy-start.53 = (f32[8,2048]{1,0:T(8,128)S(1)}, f32[8,2048]{1,0:T(8,128)}, u32[]{:S(2)}) copy-start(f32[8,2048]{1,0:T(8,128)} %get-tuple-element.88.refs_5_.refs_9_) | copy-start | bytes 196612
  162.4 38.7 %copy-start.43 = (s32[128]{0:T(128)S(1)}, s32[128]{0:T(128)}, u32[]{:S(2)}) copy-start(s32[128]{0:T(128)} %copy-done.41) | copy-start | bytes 1540
  217.0 16.2 %collective-permute-start.7 = (bf16[512,2048]{1,0:T(8,128)(2,1)}, bf16[512,2048]{1,0:T(8,128)(2,1)}, u32[]{:S(2)}, u32[]{:S(2)}) collective-permute-start(bf16[512,2048]{1,0:T(8,128)(2,1)} %get-tuple-element.102), channel_id=1, source_target_pairs={{0,1},{1,0},{2,3},{3,2},{4,5},{5,4},{6,7},{7,6},{8,9},{9,8},{10,11... | collective-permute-start | bytes 6291464 | tf_op jit(solution)/shard_map/ppermute | solution.py:291
  217.3 15.8 %collective-permute-start.6 = (bf16[512,2048]{1,0:T(8,128)(2,1)}, bf16[512,2048]{1,0:T(8,128)(2,1)}, u32[]{:S(2)}, u32[]{:S(2)}) collective-permute-start(bf16[512,2048]{1,0:T(8,128)(2,1)} %get-tuple-element.89.refs_1_.refs_5_), channel_id=1, source_target_pairs={{0,1},{1,0},{2,3},{3,2},{4,5},{5,4},{6,7},{7,6},{8,9},{9,8},{10,11... | collective-permute-start | bytes 6291464 | tf_op jit(solution)/shard_map/ppermute | solution.py:291
  217.6 9.5 %copy-start.32 = (f32[16,1024]{1,0:T(8,128)S(1)}, f32[16,1024]{1,0:T(8,128)}, u32[]{:S(2)}) copy-start(f32[16,1024]{1,0:T(8,128)} %copy-done.31) | copy-start | bytes 196612
  217.6 9.5 %copy-start.38 = (f32[8,4096]{1,0:T(8,128)S(1)}, f32[8,4096]{1,0:T(8,128)}, u32[]{:S(2)}) copy-start(f32[8,4096]{1,0:T(8,128)} %get-tuple-element.98.refs_4_.refs_3_) | copy-start | bytes 393220
  217.6 9.5 %copy-start.44 = (s32[128]{0:T(128)S(1)}, s32[128]{0:T(128)}, u32[]{:S(2)}) copy-start(s32[128]{0:T(128)} %copy-done.41) | copy-start | bytes 1540
  226.8 6.4 %collective-permute-start.8 = (bf16[512,512]{1,0:T(8,128)(2,1)}, bf16[512,512]{1,0:T(8,128)(2,1)S(1)}, u32[]{:S(2)}, u32[]{:S(2)}) collective-permute-start(bf16[512,512]{1,0:T(8,128)(2,1)} %get-tuple-element.104), channel_id=1, source_target_pairs={{0,1},{1,0},{2,3},{3,2},{4,5},{5,4},{6,7},{7,6},{8,9},{9,8},{10,11... | collective-permute-start | bytes 1572872 | tf_op jit(solution)/shard_map/ppermute | solution.py:291
  227.9 5.3 %copy-start.58 = (bf16[512,512]{1,0:T(8,128)(2,1)S(1)}, bf16[512,512]{1,0:T(8,128)(2,1)}, u32[]{:S(2)}) copy-start(bf16[512,512]{1,0:T(8,128)(2,1)} %get-tuple-element.103.refs_7_) | copy-start | bytes 1572868
  228.6 4.6 collective-permute-start.9
  228.9 29.9 %all-to-all-start.2 = ((bf16[4,512,256]{2,1,0:T(8,128)(2,1)}), bf16[4,512,256]{2,1,0:T(8,128)(2,1)}, u32[]{:S(2)}, u32[]{:S(2)}) async-start(bf16[4,512,256]{2,1,0:T(8,128)(2,1)} %get-tuple-element.99), calls=%async_computation.2 | async-start | bytes 2097152 | tf_op jit(solution)/shard_map/all_to_all | solution.py:1337
  249.3 9.6 %copy-start.50 = (f32[24,1024]{1,0:T(8,128)}, f32[24,1024]{1,0:T(8,128)S(1)}, u32[]{:S(2)}) copy-start(f32[24,1024]{1,0:T(8,128)S(1)} %get-tuple-element.106.refs_10_.refs_7_) | copy-start | bytes 294916
  249.3 64.2 %collective-permute-start.12 = (f32[24,1024]{1,0:T(8,128)S(1)}, f32[24,1024]{1,0:T(8,128)S(1)}, u32[]{:S(2)}, u32[]{:S(2)}) collective-permute-start(f32[24,1024]{1,0:T(8,128)S(1)} %get-tuple-element.106.refs_10_.refs_7_), channel_id=1, source_target_pairs={{0,2},{1,3},{2,0},{3,1},{4,6},{5,7},{6,4},{7,5},{8,10},{9,11},{10,... | collective-permute-start | bytes 294920 | tf_op jit(solution)/shard_map/ppermute | solution.py:291
  251.3 67.8 %collective-permute-start.10 = (bf16[1024,640]{1,0:T(8,128)(2,1)}, bf16[1024,640]{1,0:T(8,128)(2,1)}, u32[]{:S(2)}, u32[]{:S(2)}) collective-permute-start(bf16[1024,640]{1,0:T(8,128)(2,1)} %get-tuple-element.111), channel_id=1, source_target_pairs={{0,2},{1,3},{2,0},{3,1},{4,6},{5,7},{6,4},{7,5},{8,10},{9,11},{10,... | collective-permute-start | bytes 3932168 | tf_op jit(solution)/shard_map/ppermute | solution.py:291
  251.3 67.8 %collective-permute-start.11 = (bf16[512,1280]{1,0:T(8,128)(2,1)}, bf16[512,1280]{1,0:T(8,128)(2,1)}, u32[]{:S(2)}, u32[]{:S(2)}) collective-permute-start(bf16[512,1280]{1,0:T(8,128)(2,1)} %get-tuple-element.113), channel_id=1, source_target_pairs={{0,4},{4,0},{8,12},{12,8},{16,20},{20,16},{24,28},{28,24},{1,5},{5... | collective-permute-start | bytes 3932168 | tf_op jit(solution)/shard_map/ppermute | solution.py:291
  258.8 37.1 %copy-start.6 = (bf16[512,768]{1,0:T(8,128)(2,1)S(1)}, bf16[512,768]{1,0:T(8,128)(2,1)}, u32[]{:S(2)}) copy-start(bf16[512,768]{1,0:T(8,128)(2,1)} %copy-done.5) | copy-start | bytes 2359300
  258.8 37.1 %copy-start.18 = (bf16[512,768]{1,0:T(8,128)(2,1)S(1)}, bf16[512,768]{1,0:T(8,128)(2,1)}, u32[]{:S(2)}) copy-start(bf16[512,768]{1,0:T(8,128)(2,1)} %copy-done.17) | copy-start | bytes 2359300
  258.8 37.1 %copy-start.45 = (s32[128]{0:T(128)S(1)}, s32[128]{0:T(128)}, u32[]{:S(2)}) copy-start(s32[128]{0:T(128)} %copy-done.41) | copy-start | bytes 1540
  296.0 1.9 copy-start.7
  298.6 5.1 %copy-start.1 = (bf16[1040,1024]{1,0:T(8,128)(2,1)S(1)}, bf16[1040,1024]{1,0:T(8,128)(2,1)}, u32[]{:S(2)}) copy-start(bf16[1040,1024]{1,0:T(8,128)(2,1)} %copy-done) | copy-start | bytes 6389764
  298.6 5.1 %copy-start.10 = (bf16[528,1024]{1,0:T(8,128)(2,1)S(1)}, bf16[528,1024]{1,0:T(8,128)(2,1)}, u32[]{:S(2)}) copy-start(bf16[528,1024]{1,0:T(8,128)(2,1)} %copy-done.9) | copy-start | bytes 3244036
  305.6 13.5 %copy-start.28 = (bf16[512,1280]{1,0:T(8,128)(2,1)S(1)}, bf16[512,1280]{1,0:T(8,128)(2,1)}, u32[]{:S(2)}) copy-start(bf16[512,1280]{1,0:T(8,128)(2,1)} %copy-done.27) | copy-start | bytes 3932164
  305.6 13.5 %copy-start.51 = (f32[24,1024]{1,0:T(8,128)S(1)}, f32[24,1024]{1,0:T(8,128)}, u32[]{:S(2)}) copy-start(f32[24,1024]{1,0:T(8,128)} %copy-done.50) | copy-start | bytes 294916
  322.2 5.0 %copy-start.33 = (bf16[512,640]{1,0:T(8,128)(2,1)}, bf16[512,640]{1,0:T(8,128)(2,1)S(1)}, u32[]{:S(2)}) copy-start(bf16[512,640]{1,0:T(8,128)(2,1)S(1)} %get-tuple-element.124.refs_1_) | copy-start | bytes 1966084
  322.2 5.0 %copy-start.35 = (bf16[512,640]{1,0:T(8,128)(2,1)}, bf16[512,640]{1,0:T(8,128)(2,1)S(1)}, u32[]{:S(2)}) copy-start(bf16[512,640]{1,0:T(8,128)(2,1)S(1)} %get-tuple-element.125.refs_3_) | copy-start | bytes 1966084
  322.3 4.2 collective-permute-start.13
  326.5 68.8 %copy-start.14 = (bf16[512,1024]{1,0:T(8,128)(2,1)S(1)}, bf16[512,1024]{1,0:T(8,128)(2,1)}, u32[]{:S(2)}) copy-start(bf16[512,1024]{1,0:T(8,128)(2,1)} %copy-done.12) | copy-start | bytes 3145732
  326.5 68.8 %copy-start.19 = (f32[512,1024]{1,0:T(8,128)S(1)}, f32[512,1024]{1,0:T(8,128)}, u32[]{:S(2)}) copy-start(f32[512,1024]{1,0:T(8,128)} %get-tuple-element.119.refs_5_) | copy-start | bytes 6291460
  327.2 68.0 %collective-permute-start.14 = (bf16[512,1024]{1,0:T(8,128)(2,1)S(1)}, bf16[512,1024]{1,0:T(8,128)(2,1)S(1)}, u32[]{:S(2)}, u32[]{:S(2)}) collective-permute-start(bf16[512,1024]{1,0:T(8,128)(2,1)S(1)} %relay.1.refs_13_), channel_id=1, source_target_pairs={{0,2},{1,3},{2,0},{3,1},{4,6},{5,7},{6,4},{7,5},{8,10},{9,11},{10,... | collective-permute-start | bytes 3145736 | tf_op jit(solution)/shard_map/ppermute | solution.py:291
  329.8 65.4 %collective-permute-start.16 = (bf16[512,768]{1,0:T(8,128)(2,1)S(1)}, bf16[512,768]{1,0:T(8,128)(2,1)S(1)}, u32[]{:S(2)}, u32[]{:S(2)}) collective-permute-start(bf16[512,768]{1,0:T(8,128)(2,1)S(1)} %get-tuple-element.120), channel_id=1, source_target_pairs={{0,4},{4,0},{8,12},{12,8},{16,20},{20,16},{24,28},{28,24},{1,5},{5... | collective-permute-start | bytes 2359304 | tf_op jit(solution)/shard_map/ppermute | solution.py:291
  332.2 47.4 %collective-permute-start.17 = (bf16[512,640]{1,0:T(8,128)(2,1)S(1)}, bf16[512,640]{1,0:T(8,128)(2,1)S(1)}, u32[]{:S(2)}, u32[]{:S(2)}) collective-permute-start(bf16[512,640]{1,0:T(8,128)(2,1)S(1)} %get-tuple-element.121), channel_id=1, source_target_pairs={{0,4},{4,0},{8,12},{12,8},{16,20},{20,16},{24,28},{28,24},{1,5},{5... | collective-permute-start | bytes 1966088 | tf_op jit(solution)/shard_map/ppermute | solution.py:291
  332.3 62.9 %collective-permute-start.18 = (bf16[512,640]{1,0:T(8,128)(2,1)S(1)}, bf16[512,640]{1,0:T(8,128)(2,1)S(1)}, u32[]{:S(2)}, u32[]{:S(2)}) collective-permute-start(bf16[512,640]{1,0:T(8,128)(2,1)S(1)} %get-tuple-element.122), channel_id=1, source_target_pairs={{0,2},{1,3},{2,0},{3,1},{4,6},{5,7},{6,4},{7,5},{8,10},{9,11},{10,... | collective-permute-start | bytes 1966088 | tf_op jit(solution)/shard_map/ppermute | solution.py:291
  334.2 45.4 %collective-permute-start.15 = (f32[24,1024]{1,0:T(8,128)S(1)}, f32[24,1024]{1,0:T(8,128)S(1)}, u32[]{:S(2)}, u32[]{:S(2)}) collective-permute-start(f32[24,1024]{1,0:T(8,128)S(1)} %get-tuple-element.118.refs_3_.refs_8_), channel_id=1, source_target_pairs={{0,4},{4,0},{8,12},{12,8},{16,20},{20,16},{24,28},{28,24},{1,5},{5... | collective-permute-start | bytes 294920 | tf_op jit(solution)/shard_map/ppermute | solution.py:291
  399.1 17.8 %all-to-all-start.3 = ((f32[32,24,128]{2,1,0:T(8,128)}), f32[32,24,128]{2,1,0:T(8,128)S(1)}, u32[]{:S(2)}, u32[]{:S(2)}) async-start(f32[32,24,128]{2,1,0:T(8,128)} %get-tuple-element.132), calls=%async_computation.3 | async-start | bytes 786432 | tf_op jit(solution)/shard_map/all_to_all | solution.py:1375
  409.4 40.7 %collective-permute-start.19 = (bf16[128,2048]{1,0:T(8,128)(2,1)}, bf16[128,2048]{1,0:T(8,128)(2,1)S(1)}, u32[]{:S(2)}, u32[]{:S(2)}) collective-permute-start(bf16[128,2048]{1,0:T(8,128)(2,1)} %get-tuple-element.129), channel_id=1, source_target_pairs={{0,8},{4,12},{8,0},{12,4},{16,24},{20,28},{24,16},{28,20},{1,9},{5... | collective-permute-start | bytes 1572872 | tf_op jit(solution)/shard_map/ppermute | solution.py:291
  411.2 39.2 %collective-permute-start.20 = (bf16[128,2048]{1,0:T(8,128)(2,1)}, bf16[128,2048]{1,0:T(8,128)(2,1)S(1)}, u32[]{:S(2)}, u32[]{:S(2)}) collective-permute-start(bf16[128,2048]{1,0:T(8,128)(2,1)} %get-tuple-element.130), channel_id=1, source_target_pairs={{0,16},{4,20},{8,24},{12,28},{16,0},{20,4},{24,8},{28,12},{1,17},{... | collective-permute-start | bytes 1572872 | tf_op jit(solution)/shard_map/ppermute | solution.py:291
  413.6 36.8 %collective-permute-start.21 = (bf16[128,2048]{1,0:T(8,128)(2,1)}, bf16[128,2048]{1,0:T(8,128)(2,1)S(1)}, u32[]{:S(2)}, u32[]{:S(2)}) collective-permute-start(bf16[128,2048]{1,0:T(8,128)(2,1)} %get-tuple-element.131.refs_2_), channel_id=1, source_target_pairs={{0,24},{4,28},{8,16},{12,20},{16,8},{20,12},{24,0},{28,4},{1,25},{... | collective-permute-start | bytes 1572872 | tf_op jit(solution)/shard_map/ppermute | solution.py:291
  413.8 36.3 %collective-permute-start.22 = (f32[24,1024]{1,0:T(8,128)}, f32[24,1024]{1,0:T(8,128)S(1)}, u32[]{:S(2)}, u32[]{:S(2)}) collective-permute-start(f32[24,1024]{1,0:T(8,128)} %get-tuple-element.127.refs_7_.refs_5_), channel_id=1, source_target_pairs={{0,8},{4,12},{8,0},{12,4},{16,24},{20,28},{24,16},{28,20},{1,9},{5... | collective-permute-start | bytes 294920 | tf_op jit(solution)/shard_map/ppermute | solution.py:291
  453.0 13.7 %collective-permute-start.23 = (bf16[128,256]{1,0:T(8,128)(2,1)S(1)}, bf16[128,256]{1,0:T(8,128)(2,1)S(1)}, u32[]{:S(2)}, u32[]{:S(2)}) collective-permute-start(bf16[128,256]{1,0:T(8,128)(2,1)S(1)} %get-tuple-element.134), channel_id=1, source_target_pairs={{2,0},{0,1},{3,2},{1,3},{6,4},{4,5},{7,6},{5,7},{10,8},{8,9},{11,1... | collective-permute-start | bytes 196616 | tf_op jit(solution)/shard_map/ppermute | solution.py:1265
  453.0 13.7 %collective-permute-start.24 = (bf16[128,256]{1,0:T(8,128)(2,1)S(1)}, bf16[128,256]{1,0:T(8,128)(2,1)S(1)}, u32[]{:S(2)}, u32[]{:S(2)}) collective-permute-start(bf16[128,256]{1,0:T(8,128)(2,1)S(1)} %get-tuple-element.135), channel_id=1, source_target_pairs={{1,0},{3,1},{0,2},{2,3},{5,4},{7,5},{4,6},{6,7},{9,8},{11,9},{8,10... | collective-permute-start | bytes 196616 | tf_op jit(solution)/shard_map/ppermute | solution.py:1265
  455.1 14.8 %collective-permute-start.25 = (f32[24,1024]{1,0:T(8,128)S(1)}, f32[24,1024]{1,0:T(8,128)S(1)}, u32[]{:S(2)}, u32[]{:S(2)}) collective-permute-start(f32[24,1024]{1,0:T(8,128)S(1)} %get-tuple-element.136.refs_4_.refs_6_), channel_id=1, source_target_pairs={{0,16},{4,20},{8,24},{12,28},{16,0},{20,4},{24,8},{28,12},{1,17},{... | collective-permute-start | bytes 294920 | tf_op jit(solution)/shard_map/ppermute | solution.py:291
  (28 other events, 32.3 us)
Sparse Core Ops, SparseCore 0:
  10.9 139.8 all-gather.2
  217.1 166.2 reduce-scatter.1

commit v3 on v2

--- a/solution.py
+++ b/solution.py
@@ -11,7 +11,6 @@
 EPSILON = 1e-05
 MASKED = -1e30
 HEAD = 64
-BQ = 256
 bf16 = jnp.bfloat16
 f32 = jnp.float32
 
@@ -50,46 +49,52 @@
 
 
 class Heads:
-    def __init__(self, nh, local, first, blocks, order_at, who_at, parts):
+    def __init__(self, nh, local, first, blocks, order_at, who_at, parts, rows):
         self.nh, self.local, self.first, self.blocks = nh, local, first, blocks
-        self.order_at, self.who_at, self.parts = order_at, who_at, parts
-
-
-def keys_of(hd, tab, spans, keep_ref, kseg, bk):
+        self.order_at, self.who_at, self.parts, self.rows = order_at, who_at, parts, rows
+        self.bq, self.bk = min(512, rows), min(256, rows)
+
+    def place(self, tab, row):
+        return tab[self.order_at + row // self.rows] * self.rows + row % self.rows
+
+
+def keys_of(hd, tab, spans, keep_ref, kseg):
     for j in range(hd.parts):
-        at = pl.ds(pl.multiple_of(tab[hd.order_at + j] * bk, bk), bk)
-        places = j * bk + lax.broadcasted_iota(jnp.int32, (bk, 1), 0)
+        at = pl.ds(pl.multiple_of(tab[hd.order_at + j] * hd.rows, hd.rows), hd.rows)
+        places = j * hd.rows + lax.broadcasted_iota(jnp.int32, (hd.rows, 1), 0)
         kseg[at, :] = jnp.where(keep_ref[:, at].T[:, 0:1] > 0.5, segment_of(spans, places), -1)
 
 
-def visible(i, j, bk, spans, kseg, at):
-    kpos = j * bk + lax.broadcasted_iota(jnp.int32, (bk, BQ), 0)
-    qpos = i * BQ + lax.broadcasted_iota(jnp.int32, (bk, BQ), 1)
-    qseg = segment_of(spans, i * BQ + lax.broadcasted_iota(jnp.int32, (1, BQ), 1))
+def visible(hd, i, j, spans, kseg, at):
+    bq, bk = hd.bq, hd.bk
+    kpos = j * bk + lax.broadcasted_iota(jnp.int32, (bk, bq), 0)
+    qpos = i * bq + lax.broadcasted_iota(jnp.int32, (bk, bq), 1)
+    qseg = segment_of(spans, i * bq + lax.broadcasted_iota(jnp.int32, (1, bq), 1))
     return (kseg[at, :] == qseg) & (kpos <= qpos)
 
 
-def each_block(hd, tab, spans, i, bk, body):
-    first = segment_of(spans, i * BQ)
+def each_block(hd, tab, spans, i, body):
+    bq, bk = hd.bq, hd.bk
+    first = segment_of(spans, i * bq)
 
     def step(j, carry):
-        at = pl.ds(pl.multiple_of(tab[hd.order_at + j] * bk, bk), bk)
+        at = pl.ds(pl.multiple_of(hd.place(tab, j * bk), bk), bk)
         pl.when(first <= segment_of(spans, (j + 1) * bk - 1))(lambda: body(j, at))
         return carry
 
-    lax.fori_loop(0, (i * BQ) // bk + 1, step, 0)
-
-
-def fwd_kernel(hd, bk, tab, spans, q_ref, k_ref, v_ref, keep_ref, hs_ref, scaled_ref, o_ref, lse_ref,
+    lax.fori_loop(0, ((i + 1) * bq - 1) // bk + 1, step, 0)
+
+
+def fwd_kernel(hd, tab, spans, q_ref, k_ref, v_ref, keep_ref, hs_ref, scaled_ref, o_ref, lse_ref,
                kseg, vms, sscr, mpart, lpart, acc):
-    nh = hd.nh
+    nh, bq, bk = hd.nh, hd.bq, hd.bk
     i = pl.program_id(0)
 
     @pl.when(i == 0)
     def _():
         for h in range(nh):
             vms[h] = lanes_of(v_ref[...], h)
-        keys_of(hd, tab, spans, keep_ref, kseg, bk)
+        keys_of(hd, tab, spans, keep_ref, kseg)
 
     qs = q_ref[...] * bf16(0.125)
     qm = [lanes_of(qs, h) for h in range(nh)]
@@ -99,27 +104,27 @@
 
     def one(j, at):
         kb = k_ref[at, :]
-        mask = visible(i, j, bk, spans, kseg, at)
+        mask = visible(hd, i, j, spans, kseg, at)
         for h in range(nh):
             s = jnp.where(mask, mm_cols(kb, qm[h]), MASKED)
             sscr[h, at, :] = s
-            mpart[h] = jnp.maximum(mpart[h], jnp.max(s.reshape(bk // 8, 8, BQ), axis=0))
-
-    each_block(hd, tab, spans, i, bk, one)
+            mpart[h] = jnp.maximum(mpart[h], jnp.max(s.reshape(bk // 8, 8, bq), axis=0))
+
+    each_block(hd, tab, spans, i, one)
     ms = [jnp.max(mpart[h], axis=0, keepdims=True) for h in range(nh)]
 
     def two(j, at):
         pts = []
         for h in range(nh):
             p = jnp.exp(sscr[h, at, :] - ms[h])
-            lpart[h] += jnp.sum(p.reshape(bk // 8, 8, BQ), axis=0)
+            lpart[h] += jnp.sum(p.reshape(bk // 8, 8, bq), axis=0)
             pts.append(p.astype(bf16).T)
         acc[...] += mm(
             jnp.concatenate(pts, axis=1),
             jnp.concatenate([vms[h, at, :] for h in range(nh)], axis=0),
         )
 
-    each_block(hd, tab, spans, i, bk, two)
+    each_block(hd, tab, spans, i, two)
     out_t = acc[...].T
     parts = []
     for h in range(nh):
@@ -132,11 +137,11 @@
     scaled_ref[...] = jnp.concatenate(parts, axis=0).T.astype(bf16)
 
 
-def head_specs(hd, n, w, bk):
+def head_specs(hd, n, w):
     q, k, v = hd.blocks
-    ratio = bk // BQ
+    bq = hd.bq
     return [
-        pl.BlockSpec((BQ, w), lambda i, t, s: (t[hd.order_at + (i * BQ) // bk] * ratio + i % ratio, q)),
+        pl.BlockSpec((bq, w), lambda i, t, s: (hd.place(t, i * bq) // bq, q)),
         pl.BlockSpec((n, w), lambda i, t, s: (0, k)),
         pl.BlockSpec((n, w), lambda i, t, s: (0, v)),
     ]
@@ -144,27 +149,27 @@
 
 def attend_forward(hd, tab, spans, qkv, keep, head_scale, deps=()):
     n, nh, w = qkv.shape[0], hd.nh, hd.nh * HEAD
-    bk = n // hd.parts
+    bq = hd.bq
     return pl.pallas_call(
-        skipping(functools.partial(fwd_kernel, hd, bk), 7, len(deps)),
+        skipping(functools.partial(fwd_kernel, hd), 7, len(deps)),
         grid_spec=pltpu.PrefetchScalarGridSpec(
             num_scalar_prefetch=2,
-            grid=(n // BQ,),
-            in_specs=head_specs(hd, n, w, bk)
+            grid=(n // bq,),
+            in_specs=head_specs(hd, n, w)
             + [pl.BlockSpec((8, n), lambda i, t, s: (0, 0)), pl.BlockSpec(memory_space=pltpu.SMEM)]
             + unread(deps),
             out_specs=[
-                pl.BlockSpec((BQ, w), lambda i, t, s: (i, 0)),
-                pl.BlockSpec((w, BQ), lambda i, t, s: (0, i)),
-                pl.BlockSpec((8, BQ), lambda i, t, s: (0, i)),
+                pl.BlockSpec((bq, w), lambda i, t, s: (i, 0)),
+                pl.BlockSpec((w, bq), lambda i, t, s: (0, i)),
+                pl.BlockSpec((8, bq), lambda i, t, s: (0, i)),
             ],
             scratch_shapes=[
                 pltpu.VMEM((n, 1), jnp.int32),
                 pltpu.VMEM((nh, n, w), bf16),
-                pltpu.VMEM((nh, n, BQ), f32),
-                pltpu.VMEM((nh, 8, BQ), f32),
-                pltpu.VMEM((nh, 8, BQ), f32),
-                pltpu.VMEM((BQ, w), f32),
+                pltpu.VMEM((nh, n, bq), f32),
+                pltpu.VMEM((nh, 8, bq), f32),
+                pltpu.VMEM((nh, 8, bq), f32),
+                pltpu.VMEM((bq, w), f32),
             ],
         ),
         out_shape=[
@@ -178,9 +183,9 @@
     )(tab, spans, qkv, qkv, qkv, keep, head_scale[None], *deps)
 
 
-def bwd_kernel(hd, bk, tab, spans, q_ref, k_ref, v_ref, keep_ref, hs_ref, sg_ref, o_ref, lse_ref,
+def bwd_kernel(hd, tab, spans, q_ref, k_ref, v_ref, keep_ref, hs_ref, sg_ref, o_ref, lse_ref,
                grad_ref, sums_ref, kseg, dk, dv, dq, gacc, kms):
-    nh = hd.nh
+    nh, bq, bk = hd.nh, hd.bq, hd.bk
     i = pl.program_id(0)
     n, w = k_ref.shape[0], nh * HEAD
 
@@ -191,7 +196,7 @@
         gacc[...] = jnp.zeros_like(gacc)
         for h in range(nh):
             kms[h] = lanes_of(k_ref[...], h)
-        keys_of(hd, tab, spans, keep_ref, kseg, bk)
+        keys_of(hd, tab, spans, keep_ref, kseg)
 
     qs = q_ref[...] * bf16(0.125)
     qm = [lanes_of(qs, h) for h in range(nh)]
@@ -215,7 +220,7 @@
     def block(j, at):
         kb = k_ref[at, :]
         vb = v_ref[at, :]
-        mask = visible(i, j, bk, spans, kseg, at)
+        mask = visible(hd, i, j, spans, kseg, at)
         ps, dss, dsts = [], [], []
         for h in range(nh):
             p = jnp.where(mask, jnp.exp(mm_cols(kb, qm[h]) - lse[h]), 0.0)
@@ -230,11 +235,11 @@
             jnp.concatenate([kms[h, at, :] for h in range(nh)], axis=0),
         )
 
-    each_block(hd, tab, spans, i, bk, block)
-    mine = tab[hd.order_at + (i * BQ) // bk] * bk + (i * BQ) % bk
-    grad_ref[pl.ds(pl.multiple_of(mine, BQ), BQ), 0:w] = (dq[...] * 0.125).astype(bf16)
-
-    @pl.when(i == n // BQ - 1)
+    each_block(hd, tab, spans, i, block)
+    mine = hd.place(tab, i * bq)
+    grad_ref[pl.ds(pl.multiple_of(mine, bq), bq), 0:w] = (dq[...] * 0.125).astype(bf16)
+
+    @pl.when(i == n // bq - 1)
     def _():
         grad_ref[:, w : 2 * w] = dk[...].astype(bf16)
         grad_ref[:, 2 * w : 3 * w] = dv[...].astype(bf16)
@@ -249,19 +254,19 @@
 
 def attend_backward(hd, part, tab, spans, qkv, keep, head_scale, scaled_grad, o_t, lse, deps=()):
     n, nh, w = qkv.shape[0], hd.nh, hd.nh * HEAD
-    bk = n // hd.parts
+    bq = hd.bq
     return pl.pallas_call(
-        skipping(functools.partial(bwd_kernel, hd, bk), 10, len(deps)),
+        skipping(functools.partial(bwd_kernel, hd), 10, len(deps)),
         grid_spec=pltpu.PrefetchScalarGridSpec(
             num_scalar_prefetch=2,
-            grid=(n // BQ,),
-            in_specs=head_specs(hd, n, w, bk)
+            grid=(n // bq,),
+            in_specs=head_specs(hd, n, w)
             + [
                 pl.BlockSpec((8, n), lambda i, t, s: (0, 0)),
                 pl.BlockSpec(memory_space=pltpu.SMEM),
-                pl.BlockSpec((BQ, w), lambda i, t, s: (i, part)),
-                pl.BlockSpec((w, BQ), lambda i, t, s: (0, i)),
-                pl.BlockSpec((8, BQ), lambda i, t, s: (0, i)),
+                pl.BlockSpec((bq, w), lambda i, t, s: (i, part)),
+                pl.BlockSpec((w, bq), lambda i, t, s: (0, i)),
+                pl.BlockSpec((8, bq), lambda i, t, s: (0, i)),
             ]
             + unread(deps),
             out_specs=[
@@ -272,8 +277,8 @@
                 pltpu.VMEM((n, 1), jnp.int32),
                 pltpu.VMEM((n, w), f32),
                 pltpu.VMEM((n, w), f32),
-                pltpu.VMEM((BQ, w), f32),
-                pltpu.VMEM((w, BQ), f32),
+                pltpu.VMEM((bq, w), f32),
+                pltpu.VMEM((w, bq), f32),
                 pltpu.VMEM((nh, n, w), bf16),
             ],
         ),
@@ -475,7 +480,7 @@
     wo = reorder(reorder_rows(wos, to_abs, block), sp_abs, oc)
 
     tab = jnp.concatenate([sp_place, me_s[None].astype(jnp.int32)])
-    hd = Heads(nh, nh, 0, (0, 1, 2), 0, sp, sp)
+    hd = Heads(nh, nh, 0, (0, 1, 2), 0, sp, sp, rows)
     keep_col = jnp.broadcast_to(keep.astype(f32)[None, :], (8, group))
     scaled, o_t, lse = attend_forward(hd, tab, seq_spans[0], qkv, keep_col, head_scale)
     returned = lax.all_to_all(scaled.reshape(sp, rows, lw), "sp", 0, 0, tiled=True)
@@ -766,11 +771,20 @@
             out[k, :, span(tab[SLOT + m], piece.shape[1])] = piece[...]
 
 
-def home_body(tab, *refs):
-    pieces, out = refs[:-1], refs[-1]
-    width = pieces[0].shape[1]
-    for m, piece in enumerate(pieces):
-        out[:, span(tab[SEND + m], width)] = piece[...].astype(f32)
+def home_body(tab, p0, p1, p2, late, early, out, gains, shifts, mid, hid, scale):
+    size, width = p0.shape[1], late.shape[1]
+    for m, piece in enumerate((p0, p1, p2)):
+        out[:, span(tab[SEND + m], size)] = piece[...].astype(f32)
+    for row, source in enumerate((late[0:1], early[0:1], early[1:2])):
+        gains[row : row + 1, :] = source
+    for row, source in enumerate((late[2:3], late[3:4], early[2:3], late[1:2], early[3:4], early[4:5], early[5:6])):
+        shifts[row : row + 1, :] = source
+    for k in range(mid.shape[1] // width):
+        to = slice(k * width, (k + 1) * width)
+        mid[:, to] = early[6 + k : 7 + k, :]
+        hid[0:1, to] = early[10 + k : 11 + k, :]
+        hid[1:2, to] = early[14 + k : 15 + k, :]
+    scale[...] = late[4:5, : scale.shape[1]]
 
 
 def prologue_body(tab, tok, cot, vcol, vrow, gains, shifts, mid, hsh, first_ref, both_ref, up_ref, tokr_ref, vec_ref, hid_ref):
@@ -1038,9 +1052,8 @@
         send[...] = acc[half:].astype(bf16)
 
 
-def fold_body(tab, ak, ra, bk, rb, x0, x1, a2k, a2s, b2k, b2s, y0, y1):
+def fold_body(tab, ak, ra, bk, rb, x0, a2k, a2s, b2k, b2s, y0):
     y0[...] = x0[...]
-    y1[...] = x1[...]
     rows, cols = b2k.shape
     a = ak[...].astype(f32) + ra[...].astype(f32)
     a2k[...] = a[:rows].astype(bf16)
@@ -1062,8 +1075,9 @@
             send[:, to] = total[n * rows : (n + 1) * rows].astype(bf16)
 
 
-def gathered_body(widths, tab, keep, r1, r2, r3, *refs):
-    outs, pieces, total = refs[: len(widths)], refs[len(widths) : -1], refs[-1]
+def gathered_body(widths, tab, keep, r1, r2, r3, low, *refs):
+    outs, pieces, (wide_low, total) = refs[: len(widths)], refs[len(widths) : -2], refs[-2:]
+    wide_low[...] = low[...].astype(f32)
     total[...] = keep[...] + r1[...].astype(f32) + r2[...].astype(f32) + r3[...].astype(f32)
     half = sum(widths)
     at = 0
@@ -1111,14 +1125,17 @@
     a2k, a2s, b2k, b2s, *carried = call("fold_" + tag, fold_body, tab, [ak, ra, bk, rb] + ships, quarter, vmem=34, rider=rider)
     ra, rb = swap(a2s, "dp", 1), swap(b2s, "sp", 2)
     deps = yield carried + [ra, rb]
-    (g, r), size = deps
+    (g, r), size, rider = deps
     shard = (rows // 8, 2 * total + g.shape[1])
-    keep, *sends = call("spread_" + tag, spread_body, tab, [a2k, ra, b2k, rb, g, r], [(shard, f32)] + [(shard, bf16)] * 3)
+    keep, *sends, carried = call(
+        "spread_" + tag, spread_body, tab, [a2k, ra, b2k, rb, g, r], [(shard, f32)] + [(shard, bf16)] * 3, rider=rider
+    )
     received = [swap(x, "dp", b) for x, b in zip(sends, grid.z_bits)]
-    rider = yield
+    low = yield carried
     yield call(
-        "sum_" + tag, functools.partial(gathered_body, widths), tab, [keep] + received,
-        [((rows // 8, 2 * w), f32) for w in widths] + [((rows // 8, size), bf16)] * 3, scratch=[pltpu.VMEM(shard, f32)], rider=rider,
+        "sum_" + tag, functools.partial(gathered_body, widths), tab, [keep] + received + [low],
+        [((rows // 8, 2 * w), f32) for w in widths] + [((rows // 8, size), bf16)] * 3 + [(low.shape, f32)],
+        scratch=[pltpu.VMEM(shard, f32)],
     )
 
 
@@ -1155,7 +1172,8 @@
         cross[rows:] = got.astype(bf16)
 
 
-def relay_body(tab, far, theirs, out):
+def relay_body(tab, far, theirs, send, out, sent):
+    sent[...] = send[...]
     out[...] = (far[...] + theirs[...].astype(f32)).astype(bf16)
 
 
@@ -1287,7 +1305,7 @@
         [((group, 3 * shard_lanes), bf16), ((8, group), f32)], steps=sp,
         out_specs=[by_rows(rows, 3 * shard_lanes), pl.BlockSpec((8, rows), lambda i, *_: (0, i))],
     )
-    hd = Heads(4, heads // sp, 0, (0, 1, 2), ORD, WHO, sp)
+    hd = Heads(4, heads // sp, 0, (0, 1, 2), ORD, WHO, sp, rows)
     scaled, o_t, lse = ORDER.passed(attend_forward(hd, tab, spans, qkv, keep, head_scale, deps=ORDER.last))
     returned = lax.all_to_all(scaled.reshape(sp, rows, shard_lanes), "sp", 0, 0, tiled=True)
 
@@ -1299,7 +1317,7 @@
         steps=2,
         in_specs=[ret_spec, by_rows(step, width), whole(vec.shape), anywhere],
         out_specs=[by_rows(step, 2 * width)] + [by_rows(step, width)] * 2 + [by_rows(step, 1), whole((width, width))],
-        scratch=[pltpu.SemaphoreType.DMA((8, 8))], vmem=40,
+        scratch=[pltpu.SemaphoreType.DMA((8, 8))], vmem=62,
     )
     pair_sib = swap(pair, "sp", 1)
     hid_own, hid_sib, pre_own, pre_sib, second_grad, layer_out, hidden_sums = call(
@@ -1318,9 +1336,9 @@
         in_specs=[pl.BlockSpec((width, rows), lambda *_: (0, 0)),
                   pl.BlockSpec((rows, unit), lambda i, *_: (0, jnp.clip(i, 0, 3))),
                   pl.BlockSpec((rows, unit), lambda i, *_: (0, jnp.clip(i - 4, 0, 3)))],
-        vmem=40,
+        vmem=62,
     )[0]
-    grad_w_down = lax.psum_scatter(spilled, ("dp", "sp"), scatter_dimension=0, tiled=True)[0].astype(f32)
+    down_part = lax.psum_scatter(spilled, ("dp", "sp"), scatter_dimension=0, tiled=True)[0]
     middle_grad, attn_own, attn_sib, back, sums = call(
         "to_heads", heads_body, tab, [second_grad, middle, attn_normed, attn_std, upstream, vec, wo],
         [((rows, width), f32)] + [((rows, width // 2), bf16)] * 2 + [((sp, rows, shard_lanes), bf16), ((8, width), f32)],
@@ -1352,18 +1370,21 @@
         in_specs=[by_rows(rows, wide), whole(wq0.shape), whole(wq1.shape)],
         out_specs=[whole((rows, width)), whole((2 * rows, width)), whole((rows, width))],
     )
+    cross, early, *second_up = up_sums.send((early, [cross]))
+    theirs = swap(cross, "sp", 1)
+    early = (early, swap(early, "dp", 1))
     keep_rows, send = call(
         "group_grads", functools.partial(groups_body, sp), tab, firsts + [qkv_grad],
         [((width // 2, wide), f32), ((width // 2, wide), bf16)], steps=sp,
         in_specs=[whole(f.shape) for f in firsts] + [by_rows(rows, wide)],
         scratch=[pltpu.VMEM((width, wide), f32)], vmem=30,
     )
-    cross, send, early, *second_up = up_sums.send((early, [cross, send]))
-    early = (early, swap(early, "dp", 1))
-    theirs, other_rows = swap(cross, "sp", 1), swap(send, "dp", 1)
-    relayed = call("relay", relay_body, tab, [far, theirs], [((rows, width), bf16)],
-                   in_specs=[whole(far.shape), pl.BlockSpec((rows, width), lambda *_: (1, 0))])[0]
-    crossed = swap(relayed, "sp", 2)
+    relayed, send, early = call(
+        "relay", relay_body, tab, [far, theirs, send], [((rows, width), bf16), (send.shape, bf16)],
+        in_specs=[whole(far.shape), pl.BlockSpec((rows, width), lambda *_: (1, 0)), whole(send.shape)], rider=early,
+    )
+    crossed, other_rows = swap(relayed, "sp", 2), swap(send, "dp", 1)
+    early = (early, swap(early, "dp", 2))
     grad_tokens, late, early = call(
         "to_tokens", final_body, tab, [mine, theirs, crossed, tokr, middle_grad, vec, head_sums],
         [((rows, width), f32), ((dp * sp, 24, LANES), f32)], steps=2,
@@ -1371,17 +1392,16 @@
         out_specs=[by_rows(step, width), whole((dp * sp, 24, LANES))],
         scratch=[pltpu.VMEM((8, width), f32), pltpu.VMEM((24, LANES), f32)], rider=early, deps=(other_rows, *second_up),
     )
-    early = (early, swap(early, "dp", 2))
+    early = (early, swap(early, "dp", 4))
     late = lax.all_to_all(late, ("dp", "sp"), 0, 0, tiled=True)
-    up_sums.send(((keep_rows, other_rows), shard_lanes))
+    early = up_sums.send(((keep_rows, other_rows), shard_lanes, early))
     late = call("totals", functools.partial(totals_body, sp), tab, [late], [((8, width), f32)])[0]
-    grad_w_up, grad_w_out, *sent, early = up_sums.send(early)
-    early = (early, swap(early, "dp", 4))
+    grad_w_up, grad_w_out, *sent, grad_w_down = up_sums.send(down_part)
     got = [carry(x, pairs) for x, pairs in zip(sent, back_to)]
-    grad_w_qkv, early = call("home", home_body, tab, got, [((block, 3 * shard_lanes), f32)], rider=early)
-    grad_model_gains = jnp.stack([late[0], early[0], early[1]])
-    grad_model_shifts = jnp.stack([late[2], late[3], early[2], late[1], early[3], early[4], early[5]])
-    totals = early[6 : 6 + 3 * ff // width].reshape(3, ff)
+    grad_w_qkv, gain_sums, shift_sums, mid_sums, hid_sums, scale_sums = call(
+        "home", home_body, tab, got + [late, early],
+        [((block, 3 * shard_lanes), f32), ((3, width), f32), ((7, width), f32), ((1, ff), f32), ((2, ff), f32), ((1, heads), f32)],
+    )
     return (
         layer_out,
         grad_tokens,
@@ -1389,18 +1409,18 @@
         grad_w_out,
         grad_w_up,
         grad_w_down,
-        grad_model_gains,
-        grad_model_shifts,
-        totals[0],
-        totals[1:3],
-        late[4, :heads],
+        gain_sums,
+        shift_sums,
+        mid_sums[0],
+        hid_sums,
+        scale_sums[0],
     )
 
 
 def per_device(*arrays):
     dp, sp = lax.axis_size("dp"), lax.axis_size("sp")
     (rows, width), heads, ff = arrays[0].shape, arrays[12].shape[0], arrays[10].shape[0]
-    if (dp, sp) == (8, 4) and width == 8 * LANES and heads * HEAD == width and ff == 4 * width and rows % BQ == 0:
+    if (dp, sp) == (8, 4) and width == 8 * LANES and heads * HEAD == width and ff == 4 * width and rows == 512:
         return fast_layer(*arrays)
     return general_layer(*arrays)
 

time: 491 us -> 498 us (1.014)
  the two profiles are of different devices: /device:TPU:0 before, /device:TPU:10 now
where the time goes in v3:
time: 498 us; the launch traced here: 489 us
  Pallas kernels  195 us (39%)
  waiting for transfers between devices  181 us (36%)
  starting transfers between devices  45.4 us (9%)
  local copies, waits for them, and re-layouts  29.8 us (6%)
  blocking collectives  21 us (4%)
  between operations  14.8 us (3%)
    ppermute x22, waiting for transfers between devices, swap(): lax.ppermute(x, axis, [(i, i ^ bits) for i in range(lax.axis_size(axis))])  169 us
    pallas_call x21, Pallas kernels, call(): pl.pallas_call(skipping(body, 1 + len(args), len(deps)), grid_spec=pltpu....  124 us
    pallas_call x1, Pallas kernels, attend_backward(): pl.pallas_call(skipping(functools.partial(bwd_kernel, hd), 10, len(deps))...  42.8 us
    unnamed x112, local copies, waits for them, and re-layouts  29 us
    pallas_call x1, Pallas kernels, attend_forward(): pl.pallas_call(skipping(functools.partial(fwd_kernel, hd), 7, len(deps)),...  28.1 us
    ppermute x22, starting transfers between devices, swap(): lax.ppermute(x, axis, [(i, i ^ bits) for i in range(lax.axis_size(axis))])  24.4 us
    all_to_all x1, blocking collectives, fast_layer(): lax.all_to_all(scaled.reshape(sp, rows, shard_lanes), 'sp', 0, 0, tiled=T...  21 us
  transfers between devices with their start and end apart: 31, of which 13 were waited for; matrix products, arithmetic and copies ran while one was open for 0% of the time, Pallas kernels for 27%

profile of v3, /device:TPU:10, one launch (start us, length us, event | category | flops | bytes accessed | tf_op | source)
XLA Modules:
  0.0 489.2 jit_solution(12380841607956355116)
XLA Ops:
  7.2 2.1 pad_maximum_fusion
  10.0 0.9 copy-done.38
  11.6 2.0 collective-permute-start.1
  14.5 1.3 collective-permute-done.refs_2_
  19.4 4.9 prologue.1
  24.3 1.0 copy-done.11
  25.3 1.0 copy-done.13
  26.9 2.1 collective-permute-start.3
  29.0 5.3 %all-to-all-start = ((bf16[4,128,768]{2,1,0:T(8,128)(2,1)}), bf16[4,128,768]{2,1,0:T(8,128)(2,1)}, u32[]{:S(2)}, u32[]{:S(2)}) async-start(bf16[4,128,768]{2,1,0:T(8,128)(2,1)} %copy-done.10), calls=%async_computation | async-start | bytes 1572864 | tf_op jit(solution)/shard_map/all_to_all | solution.py:1144
  34.3 29.1 %collective-permute-done.3.refs_3_ = bf16[528,1024]{1,0:T(8,128)(2,1)S(1)} collective-permute-done((bf16[528,1024]{1,0:T(8,128)(2,1)}, bf16[528,1024]{1,0:T(8,128)(2,1)S(1)}, u32[]{:S(2)}, u32[]{:S(2)}) %collective-permute-start.3) | collective-permute-done | bytes 1081376 | tf_op jit(solution)/shard_map/ppermute | solution.py:296
  63.4 2.0 copy-done.14
  65.4 1.2 turn.1.refs_2_.refs_1_
  66.6 1.3 copy-done.2
  67.9 1.6 copy-done.3
  69.5 1.7 rows_qkv.1.refs_5_.refs_8_.refs_2_
  71.2 1.6 collective-permute-start.5
  72.9 19.6 %collective-permute-done.5.refs_6_.refs_3_ = bf16[512,768]{1,0:T(8,128)(2,1)S(1)} collective-permute-done((bf16[512,768]{1,0:T(8,128)(2,1)S(1)}, bf16[512,768]{1,0:T(8,128)(2,1)S(1)}, u32[]{:S(2)}, u32[]{:S(2)}) %collective-permute-start.5) | collective-permute-done | bytes 786464 | tf_op jit(solution)/shard_map/ppermute | solution.py:296
  92.5 6.2 %project.1 = (bf16[2048,768]{1,0:T(8,128)(2,1)S(1)}, f32[8,2048]{1,0:T(8,128)S(1)}) custom-call(s32[128]{0:T(128)S(1)} %dynamic-slice_bitcast_fusion.refs_0_, bf16[528,1024]{1,0:T(8,128)(2,1)} %get-tuple-element.86.refs_1_, bf16[1040,1024]{1,0:T(8,128)(2,1)S(1)} %collective-permute-done.2.refs_2_, bf16[528,1024]{1,0:T(8,128)(2,1)S(1)} %collective-permute-done.3.refs_3_, ...), custom_call_target="tpu_custom_call" | custom-call | flops 1024 | bytes 1024 | tf_op jit(solution)/shard_map/project/pallas_call | solution.py:744
  98.7 1.7 copy-done.52
  101.0 28.1 %attend_forward.1 = (bf16[2048,256]{1,0:T(8,128)(2,1)}, f32[256,2048]{1,0:T(8,128)}, f32[8,2048]{1,0:T(8,128)}) custom-call(s32[128]{0:T(128)} %copy-done.39, s32[4]{0:T(128)} %bitcast.19, bf16[2048,768]{1,0:T(8,128)(2,1)} %copy-done.52, bf16[2048,768]{1,0:T(8,128)(2,1)} %copy-done.52, bf16[2048,768]{1,0:T(8,128)(2,1)} %copy-done.52, f32[8,2048]{1,0:T(8,128)} %copy-done.54, ...), custom_call_target="tpu_custom_call" | custom-call | flops 40802189312 | bytes 1024 | tf_op jit(solution)/shard_map/attend_forward/pallas_call | solution.py:153
  129.1 21.0 %all_to_all.20.refs_1_ = bf16[4,512,256]{2,1,0:T(8,128)(2,1)} all-to-all(bf16[4,512,256]{2,1,0:T(8,128)(2,1)} %bitcast.16), channel_id=1, replica_groups=mesh['dp'=8,'sp'=4] {'sp'}, dimensions={0} | all-to-all | bytes 2097152 | tf_op jit(solution)/shard_map/all_to_all | solution.py:1310
  150.1 9.1 %to_middle.1 = (bf16[512,2048]{1,0:T(8,128)(2,1)}, f32[512,1024]{1,0:T(8,128)}, f32[512,1024]{1,0:T(8,128)}, f32[512,1]{1,0:T(8,128)}, bf16[1024,1024]{1,0:T(8,128)(2,1)}) custom-call(s32[128]{0:T(128)} %copy-done.39, bf16[4,512,256]{2,1,0:T(8,128)(2,1)} %all_to_all.20.refs_1_, bf16[512,1024]{1,0:T(8,128)(2,1)} %copy-done.11, f32[16,1024]{1,0:T(8,128)} %copy-done.22, ...), custom_call_target="tpu_custom_call" | custom-call | flops 1024 | bytes 1024 | tf_op jit(solution)/shard_map/to_middle/pallas_call | solution.py:744
  159.2 38.6 %ffn.1 = (bf16[512,2048]{1,0:T(8,128)(2,1)}, bf16[512,2048]{1,0:T(8,128)(2,1)}, bf16[512,2048]{1,0:T(8,128)(2,1)}, bf16[512,2048]{1,0:T(8,128)(2,1)}, f32[512,10...) custom-call(s32[128]{0:T(128)} %copy-done.39, bf16[512,2048]{1,0:T(8,128)(2,1)} %get-tuple-element.96.refs_1_.refs_5_, ...), custom_call_target="tpu_custom_call" | custom-call | flops 40700002304 | bytes 1024 | tf_op jit(solution)/shard_map/ffn/pallas_call | solution.py:744
  197.8 12.4 %spill.1.refs_8_ = bf16[32,128,1024]{2,1,0:T(8,128)(2,1)} custom-call(s32[128]{0:T(128)} %copy-done.39, bf16[1024,1024]{1,0:T(8,128)(2,1)} %copy-done.2, bf16[512,2048]{1,0:T(8,128)(2,1)} %get-tuple-element.103.refs_2_, bf16[512,2048]{1,0:T(8,128)(2,1)} %get-tuple-element.104.refs_3_, f32[8,4096]{1,0:T(8,128)} %get-tuple-element.105.refs_4_.refs_3_), custom_call_target="tpu_custom_call" | custom-call | flops 1024 | bytes 1024 | tf_op jit(solution)/shard_map/spill/pallas_call | solution.py:744
  210.8 9.2 %to_heads.1 = (f32[512,1024]{1,0:T(8,128)}, bf16[512,512]{1,0:T(8,128)(2,1)}, bf16[512,512]{1,0:T(8,128)(2,1)}, bf16[4,512,256]{2,1,0:T(8,128)(2,1)}, f32[8,1024]{1,0:T(8,128)}) custom-call(s32[128]{0:T(128)} %copy-done.39, f32[512,1024]{1,0:T(8,128)} %get-tuple-element.100.refs_1_, f32[512,1024]{1,0:T(8,128)} %get-tuple-element.97.refs_3_.refs_2_, ...), custom_call_target="tpu_custom_call" | custom-call | flops 1024 | bytes 1024 | tf_op jit(solution)/shard_map/to_heads/pallas_call | solution.py:744
  222.1 5.9 %all-to-all-start.2 = ((bf16[4,512,256]{2,1,0:T(8,128)(2,1)}), bf16[4,512,256]{2,1,0:T(8,128)(2,1)}, u32[]{:S(2)}, u32[]{:S(2)}) async-start(bf16[4,512,256]{2,1,0:T(8,128)(2,1)} %get-tuple-element.106), calls=%async_computation.2 | async-start | bytes 2097152 | tf_op jit(solution)/shard_map/all_to_all | solution.py:1355
  228.0 1.6 copy-done.55
  229.6 13.4 %grads_up.1 = (bf16[1024,640]{1,0:T(8,128)(2,1)S(1)}, bf16[1024,640]{1,0:T(8,128)(2,1)}, bf16[512,1280]{1,0:T(8,128)(2,1)S(1)}, bf16[512,1280]{1,0:T(8,128)(2,1)}, f32[24,1024]{1,0:T(8,128)S(1)}) custom-call(s32[128]{0:T(128)S(1)} %copy-done.40, bf16[512,2048]{1,0:T(8,128)(2,1)} %get-tuple-element.96.refs_1_.refs_5_, ...), custom_call_target="tpu_custom_call" | custom-call | flops 13200001024 | bytes 1024 | tf_op jit(solution)/shard_map/grads_up/pallas_call | solution.py:744
  243.0 1.1 copy-done.20
  244.2 1.9 collective-permute-start.10
  246.1 2.4 collective-permute-start.11
  248.5 5.8 %all-to-all-done.2 = bf16[4,512,256]{2,1,0:T(8,128)(2,1)} async-done(((bf16[4,512,256]{2,1,0:T(8,128)(2,1)}), bf16[4,512,256]{2,1,0:T(8,128)(2,1)}, u32[]{:S(2)}, u32[]{:S(2)}) %all-to-all-start.2) | async-done | bytes 1048608 | tf_op jit(solution)/shard_map/all_to_all | solution.py:1355
  254.3 42.8 %attend_backward.1 = (bf16[2048,768]{1,0:T(8,128)(2,1)}, f32[8,768]{1,0:T(8,128)}) custom-call(s32[128]{0:T(128)} %copy-done.39, s32[4]{0:T(128)} %bitcast.20, bf16[2048,768]{1,0:T(8,128)(2,1)} %copy-done.52, bf16[2048,768]{1,0:T(8,128)(2,1)} %copy-done.52, bf16[2048,768]{1,0:T(8,128)(2,1)} %copy-done.52, f32[8,2048]{1,0:T(8,128)} %copy-done.54, ...), custom_call_target="tpu_custom_call" | custom-call | flops 53687091200 | bytes 1024 | tf_op jit(solution)/shard_map/attend_backward/pallas_call | solution.py:258
  297.1 1.9 copy-done.4
  299.8 5.1 %first_grad.1 = (f32[512,1024]{1,0:T(8,128)S(1)}, bf16[1024,1024]{1,0:T(8,128)(2,1)S(1)}, f32[512,1024]{1,0:T(8,128)S(1)}) custom-call(s32[128]{0:T(128)S(1)} %copy-done.41, bf16[2048,768]{1,0:T(8,128)(2,1)S(1)} %copy-done.4, bf16[512,768]{1,0:T(8,128)(2,1)S(1)} %copy-done.7, bf16[512,768]{1,0:T(8,128)(2,1)S(1)} %copy-done.16, f32[8,768]{1,0:T(8,128)S(1)} %copy-done.48), custom_call_target="tpu_custom_call" | custom-call | flops 1024 | bytes 1024 | tf_op jit(solution)/shard_map/first_grad/pallas_call | solution.py:744
  304.8 9.9 %collective-permute-done.10.refs_2_ = bf16[1024,640]{1,0:T(8,128)(2,1)} collective-permute-done((bf16[1024,640]{1,0:T(8,128)(2,1)}, bf16[1024,640]{1,0:T(8,128)(2,1)}, u32[]{:S(2)}, u32[]{:S(2)}) %collective-permute-start.10) | collective-permute-done | bytes 1310752 | tf_op jit(solution)/shard_map/ppermute | solution.py:296
  314.7 3.4 fold_up.1
  318.3 1.3 collective-permute-start.14
  319.5 6.7 %group_grads.1 = (f32[512,768]{1,0:T(8,128)S(1)}, bf16[512,768]{1,0:T(8,128)(2,1)S(1)}) custom-call(s32[128]{0:T(128)S(1)} %copy-done.41, bf16[528,1024]{1,0:T(8,128)(2,1)} %get-tuple-element.86.refs_1_, bf16[1040,1024]{1,0:T(8,128)(2,1)S(1)} %copy-done.1, bf16[528,1024]{1,0:T(8,128)(2,1)S(1)} %copy-done.9, ...), custom_call_target="tpu_custom_call" | custom-call | flops 1024 | bytes 1024 | tf_op jit(solution)/shard_map/group_grads/pallas_call | solution.py:744
  326.3 1.1 copy-done.18
  328.2 2.4 collective-permute-start.15
  330.7 2.0 collective-permute-start.18
  332.8 1.7 collective-permute-start.16
  334.5 39.9 %collective-permute-done.18.refs_11_.refs_2_ = bf16[512,640]{1,0:T(8,128)(2,1)S(1)} collective-permute-done((bf16[512,640]{1,0:T(8,128)(2,1)S(1)}, bf16[512,640]{1,0:T(8,128)(2,1)S(1)}, u32[]{:S(2)}, u32[]{:S(2)}) %collective-permute-start.18) | collective-permute-done | bytes 655392 | tf_op jit(solution)/shard_map/ppermute | solution.py:296
  374.4 16.2 %collective-permute-done.19.refs_12_.refs_4_ = bf16[512,640]{1,0:T(8,128)(2,1)S(1)} collective-permute-done((bf16[512,640]{1,0:T(8,128)(2,1)S(1)}, bf16[512,640]{1,0:T(8,128)(2,1)S(1)}, u32[]{:S(2)}, u32[]{:S(2)}) %collective-permute-start.19) | collective-permute-done | bytes 655392 | tf_op jit(solution)/shard_map/ppermute | solution.py:296
  390.6 3.8 to_tokens.1
  394.5 7.2 %all-to-all-start.3 = ((f32[32,24,128]{2,1,0:T(8,128)}), f32[32,24,128]{2,1,0:T(8,128)S(1)}, u32[]{:S(2)}, u32[]{:S(2)}) async-start(f32[32,24,128]{2,1,0:T(8,128)} %get-tuple-element.141), calls=%async_computation.4 | async-start | bytes 786432 | tf_op jit(solution)/shard_map/all_to_all | solution.py:1396
  401.7 2.5 collective-permute-start.20
  404.2 10.8 %collective-permute-done.20.refs_8_ = f32[24,1024]{1,0:T(8,128)S(1)} collective-permute-done((f32[24,1024]{1,0:T(8,128)S(1)}, f32[24,1024]{1,0:T(8,128)S(1)}, u32[]{:S(2)}, u32[]{:S(2)}) %collective-permute-start.20) | collective-permute-done | bytes 98336 | tf_op jit(solution)/shard_map/ppermute | solution.py:296
  415.0 1.4 copy-done.19
  416.4 1.1 copy-done.27
  417.5 1.1 copy-done.29
  419.4 1.9 spread_up.1
  421.9 3.4 collective-permute-start.21
  425.3 1.5 collective-permute-start.23
  428.4 18.4 %collective-permute-done.21.refs_2_ = bf16[128,2048]{1,0:T(8,128)(2,1)S(1)} collective-permute-done((bf16[128,2048]{1,0:T(8,128)(2,1)}, bf16[128,2048]{1,0:T(8,128)(2,1)S(1)}, u32[]{:S(2)}, u32[]{:S(2)}) %collective-permute-start.21) | collective-permute-done | bytes 524320 | tf_op jit(solution)/shard_map/ppermute | solution.py:296
  446.7 13.7 %collective-permute-done.22.refs_3_ = bf16[128,2048]{1,0:T(8,128)(2,1)S(1)} collective-permute-done((bf16[128,2048]{1,0:T(8,128)(2,1)}, bf16[128,2048]{1,0:T(8,128)(2,1)S(1)}, u32[]{:S(2)}, u32[]{:S(2)}) %collective-permute-start.22) | collective-permute-done | bytes 524320 | tf_op jit(solution)/shard_map/ppermute | solution.py:296
  460.4 11.7 %collective-permute-done.23.refs_4_ = bf16[128,2048]{1,0:T(8,128)(2,1)S(1)} collective-permute-done((bf16[128,2048]{1,0:T(8,128)(2,1)}, bf16[128,2048]{1,0:T(8,128)(2,1)S(1)}, u32[]{:S(2)}, u32[]{:S(2)}) %collective-permute-start.23) | collective-permute-done | bytes 524320 | tf_op jit(solution)/shard_map/ppermute | solution.py:296
  472.2 0.9 copy-done.37
  473.1 1.7 sum_up.1
  475.5 1.9 collective-permute-done.24.refs_2_
  477.4 2.4 collective-permute-done.25.refs_3_
  479.7 1.0 copy-done.31
  480.8 1.3 home.1
  (142 shorter events, 15.5 us)
Async XLA Ops:
  7.2 9.2 %copy-start.25 = (bf16[512,1024]{1,0:T(8,128)(2,1)S(1)}, bf16[512,1024]{1,0:T(8,128)(2,1)}, u32[]{:S(2)}) copy-start(bf16[512,1024]{1,0:T(8,128)(2,1)} %refs_2_.1) | copy-start | bytes 3145732
  7.2 9.2 %copy-start.24 = (bf16[512,1024]{1,0:T(8,128)(2,1)S(1)}, bf16[512,1024]{1,0:T(8,128)(2,1)}, u32[]{:S(2)}) copy-start(bf16[512,1024]{1,0:T(8,128)(2,1)} %refs_1_.3) | copy-start | bytes 3145732
  7.2 142.9 %all-gather.3.cloned.1.call-start = ((), (), s32[]{:S(2)}) async-start(), calls=%async_computation.6 | async-start | bytes 19464192 | tf_op jit(solution)/shard_map/all_gather | solution.py:1286
  11.0 81.5 %copy-start.39 = (s32[128]{0:T(128)}, s32[128]{0:T(128)S(1)}, u32[]{:S(2)}) copy-start(s32[128]{0:T(128)S(1)} %dynamic-slice_bitcast_fusion.refs_0_) | copy-start | bytes 1540
  11.5 4.3 collective-permute-start
  11.6 4.3 collective-permute-start.1
  16.4 10.5 %copy-start.10 = (bf16[4,128,768]{2,1,0:T(8,128)(2,1)}, bf16[4,128,768]{2,1,0:T(8,128)(2,1)S(1)}, u32[]{:S(2)}) copy-start(bf16[4,128,768]{2,1,0:T(8,128)(2,1)S(1)} %join.1.refs_9_) | copy-start | bytes 2359300
  26.9 39.7 %copy-start.44 = (f32[8,4096]{1,0:T(8,128)}, f32[8,4096]{1,0:T(8,128)S(1)}, u32[]{:S(2)}) copy-start(f32[8,4096]{1,0:T(8,128)S(1)} %get-tuple-element.89.refs_4_) | copy-start | bytes 393220
  26.9 36.5 %collective-permute-start.2 = (bf16[1040,1024]{1,0:T(8,128)(2,1)}, bf16[1040,1024]{1,0:T(8,128)(2,1)S(1)}, u32[]{:S(2)}, u32[]{:S(2)}) collective-permute-start(bf16[1040,1024]{1,0:T(8,128)(2,1)} %get-tuple-element.87), channel_id=1, source_target_pairs={{0,1},{1,0},{2,3},{3,2},{4,5},{5,4},{6,7},{7,6},{8,9},{9,8},{10,11... | collective-permute-start | bytes 6389768 | tf_op jit(solution)/shard_map/ppermute | solution.py:296
  26.9 36.5 %collective-permute-start.3 = (bf16[528,1024]{1,0:T(8,128)(2,1)}, bf16[528,1024]{1,0:T(8,128)(2,1)S(1)}, u32[]{:S(2)}, u32[]{:S(2)}) collective-permute-start(bf16[528,1024]{1,0:T(8,128)(2,1)} %get-tuple-element.86.refs_1_), channel_id=1, source_target_pairs={{0,2},{1,3},{2,0},{3,1},{4,6},{5,7},{6,4},{7,5},{8,10},{9,11},{10,... | collective-permute-start | bytes 3244040 | tf_op jit(solution)/shard_map/ppermute | solution.py:296
  29.0 38.9 %all-to-all-start = ((bf16[4,128,768]{2,1,0:T(8,128)(2,1)}), bf16[4,128,768]{2,1,0:T(8,128)(2,1)}, u32[]{:S(2)}, u32[]{:S(2)}) async-start(bf16[4,128,768]{2,1,0:T(8,128)(2,1)} %copy-done.10), calls=%async_computation | async-start | bytes 1572864 | tf_op jit(solution)/shard_map/all_to_all | solution.py:1144
  34.3 437.9 %reduce-scatter.2.cloned.1.call-start = ((), (), s32[]{:S(2)}) async-start(), calls=%async_computation.5 | async-start | bytes 8650752 | tf_op jit(solution)/shard_map/reduce_scatter | solution.py:1341
  63.4 29.1 %copy-start.8 = (bf16[528,1024]{1,0:T(8,128)(2,1)}, bf16[528,1024]{1,0:T(8,128)(2,1)S(1)}, u32[]{:S(2)}) copy-start(bf16[528,1024]{1,0:T(8,128)(2,1)S(1)} %collective-permute-done.3.refs_3_) | copy-start | bytes 3244036
  63.4 9.5 %collective-permute-start.4 = (bf16[528,1024]{1,0:T(8,128)(2,1)S(1)}, bf16[528,1024]{1,0:T(8,128)(2,1)}, u32[]{:S(2)}, u32[]{:S(2)}) collective-permute-start(bf16[528,1024]{1,0:T(8,128)(2,1)S(1)} %collective-permute-done.3.refs_3_), channel_id=1, source_target_pairs={{0,1},{1,0},{2,3},{3,2},{4,5},{5,4},{6,7},{7,6},{8,9},{9,8},{10,11... | collective-permute-start | bytes 3244040 | tf_op jit(solution)/shard_map/ppermute | solution.py:296
  63.4 29.1 %copy-start = (bf16[1040,1024]{1,0:T(8,128)(2,1)}, bf16[1040,1024]{1,0:T(8,128)(2,1)S(1)}, u32[]{:S(2)}) copy-start(bf16[1040,1024]{1,0:T(8,128)(2,1)S(1)} %collective-permute-done.2.refs_2_) | copy-start | bytes 6389764
  63.4 2.0 copy-start.14
  69.5 23.0 %copy-start.43 = (f32[7,1024]{1,0:T(8,128)S(1)}, f32[7,1024]{1,0:T(8,128)}, u32[]{:S(2)}) copy-start(f32[7,1024]{1,0:T(8,128)} %refs_7_.1) | copy-start | bytes 86020
  71.2 27.4 %copy-start.6 = (bf16[512,768]{1,0:T(8,128)(2,1)}, bf16[512,768]{1,0:T(8,128)(2,1)S(1)}, u32[]{:S(2)}) copy-start(bf16[512,768]{1,0:T(8,128)(2,1)S(1)} %rows_qkv.1.refs_5_.refs_8_.refs_2_) | copy-start | bytes 2359300
  71.2 21.2 %collective-permute-start.5 = (bf16[512,768]{1,0:T(8,128)(2,1)S(1)}, bf16[512,768]{1,0:T(8,128)(2,1)S(1)}, u32[]{:S(2)}, u32[]{:S(2)}) collective-permute-start(bf16[512,768]{1,0:T(8,128)(2,1)S(1)} %rows_qkv.1.refs_5_.refs_8_.refs_2_), channel_id=1, source_target_pairs={{0,4},{4,0},{8,12},{12,8},{16,20},{20,16},{24,28},{28,24},{1,5},{5... | collective-permute-start | bytes 2359304 | tf_op jit(solution)/shard_map/ppermute | solution.py:296
  92.5 6.2 %copy-start.15 = (bf16[512,768]{1,0:T(8,128)(2,1)}, bf16[512,768]{1,0:T(8,128)(2,1)S(1)}, u32[]{:S(2)}) copy-start(bf16[512,768]{1,0:T(8,128)(2,1)S(1)} %collective-permute-done.5.refs_6_.refs_3_) | copy-start | bytes 2359300
  98.7 1.7 copy-start.52
  210.2 17.8 %collective-permute-start.7 = (bf16[512,2048]{1,0:T(8,128)(2,1)}, bf16[512,2048]{1,0:T(8,128)(2,1)}, u32[]{:S(2)}, u32[]{:S(2)}) collective-permute-start(bf16[512,2048]{1,0:T(8,128)(2,1)} %get-tuple-element.109), channel_id=1, source_target_pairs={{0,1},{1,0},{2,3},{3,2},{4,5},{5,4},{6,7},{7,6},{8,9},{9,8},{10,11... | collective-permute-start | bytes 6291464 | tf_op jit(solution)/shard_map/ppermute | solution.py:296
  210.3 17.7 %collective-permute-start.6 = (bf16[512,2048]{1,0:T(8,128)(2,1)}, bf16[512,2048]{1,0:T(8,128)(2,1)}, u32[]{:S(2)}, u32[]{:S(2)}) collective-permute-start(bf16[512,2048]{1,0:T(8,128)(2,1)} %get-tuple-element.96.refs_1_.refs_5_), channel_id=1, source_target_pairs={{0,1},{1,0},{2,3},{3,2},{4,5},{5,4},{6,7},{7,6},{8,9},{9,8},{10,11... | collective-permute-start | bytes 6291464 | tf_op jit(solution)/shard_map/ppermute | solution.py:296
  210.8 9.4 %copy-start.23 = (f32[16,1024]{1,0:T(8,128)S(1)}, f32[16,1024]{1,0:T(8,128)}, u32[]{:S(2)}) copy-start(f32[16,1024]{1,0:T(8,128)} %copy-done.22) | copy-start | bytes 196612
  210.8 9.4 %copy-start.30 = (f32[8,4096]{1,0:T(8,128)S(1)}, f32[8,4096]{1,0:T(8,128)}, u32[]{:S(2)}) copy-start(f32[8,4096]{1,0:T(8,128)} %get-tuple-element.105.refs_4_.refs_3_) | copy-start | bytes 393220
  210.8 9.4 %copy-start.40 = (s32[128]{0:T(128)S(1)}, s32[128]{0:T(128)}, u32[]{:S(2)}) copy-start(s32[128]{0:T(128)} %copy-done.39) | copy-start | bytes 1540
  220.0 7.9 %collective-permute-start.8 = (bf16[512,512]{1,0:T(8,128)(2,1)}, bf16[512,512]{1,0:T(8,128)(2,1)S(1)}, u32[]{:S(2)}, u32[]{:S(2)}) collective-permute-start(bf16[512,512]{1,0:T(8,128)(2,1)} %get-tuple-element.111), channel_id=1, source_target_pairs={{0,1},{1,0},{2,3},{3,2},{4,5},{5,4},{6,7},{7,6},{8,9},{9,8},{10,11... | collective-permute-start | bytes 1572872 | tf_op jit(solution)/shard_map/ppermute | solution.py:296
  220.9 7.0 %copy-start.53 = (bf16[512,512]{1,0:T(8,128)(2,1)S(1)}, bf16[512,512]{1,0:T(8,128)(2,1)}, u32[]{:S(2)}) copy-start(bf16[512,512]{1,0:T(8,128)(2,1)} %get-tuple-element.110.refs_7_) | copy-start | bytes 1572868
  221.6 6.4 %collective-permute-start.9 = (f32[24,1024]{1,0:T(8,128)S(1)}, f32[24,1024]{1,0:T(8,128)S(1)}, u32[]{:S(2)}, u32[]{:S(2)}) collective-permute-start(f32[24,1024]{1,0:T(8,128)S(1)} %pack.1.refs_9_.refs_11_), channel_id=1, source_target_pairs={{0,1},{1,0},{2,3},{3,2},{4,5},{5,4},{6,7},{7,6},{8,9},{9,8},{10,11... | collective-permute-start | bytes 294920 | tf_op jit(solution)/shard_map/ppermute | solution.py:296
  222.1 32.2 %all-to-all-start.2 = ((bf16[4,512,256]{2,1,0:T(8,128)(2,1)}), bf16[4,512,256]{2,1,0:T(8,128)(2,1)}, u32[]{:S(2)}, u32[]{:S(2)}) async-start(bf16[4,512,256]{2,1,0:T(8,128)(2,1)} %get-tuple-element.106), calls=%async_computation.2 | async-start | bytes 2097152 | tf_op jit(solution)/shard_map/all_to_all | solution.py:1355
  228.0 1.6 copy-start.55
  244.1 10.2 %copy-start.46 = (f32[24,1024]{1,0:T(8,128)}, f32[24,1024]{1,0:T(8,128)S(1)}, u32[]{:S(2)}) copy-start(f32[24,1024]{1,0:T(8,128)S(1)} %get-tuple-element.113.refs_10_.refs_6_) | copy-start | bytes 294916
  244.1 60.8 %collective-permute-start.12 = (f32[24,1024]{1,0:T(8,128)S(1)}, f32[24,1024]{1,0:T(8,128)S(1)}, u32[]{:S(2)}, u32[]{:S(2)}) collective-permute-start(f32[24,1024]{1,0:T(8,128)S(1)} %get-tuple-element.113.refs_10_.refs_6_), channel_id=1, source_target_pairs={{0,2},{1,3},{2,0},{3,1},{4,6},{5,7},{6,4},{7,5},{8,10},{9,11},{10,... | collective-permute-start | bytes 294920 | tf_op jit(solution)/shard_map/ppermute | solution.py:296
  244.2 70.5 %collective-permute-start.10 = (bf16[1024,640]{1,0:T(8,128)(2,1)}, bf16[1024,640]{1,0:T(8,128)(2,1)}, u32[]{:S(2)}, u32[]{:S(2)}) collective-permute-start(bf16[1024,640]{1,0:T(8,128)(2,1)} %get-tuple-element.118), channel_id=1, source_target_pairs={{0,2},{1,3},{2,0},{3,1},{4,6},{5,7},{6,4},{7,5},{8,10},{9,11},{10,... | collective-permute-start | bytes 3932168 | tf_op jit(solution)/shard_map/ppermute | solution.py:296
  246.1 68.6 %collective-permute-start.11 = (bf16[512,1280]{1,0:T(8,128)(2,1)}, bf16[512,1280]{1,0:T(8,128)(2,1)}, u32[]{:S(2)}, u32[]{:S(2)}) collective-permute-start(bf16[512,1280]{1,0:T(8,128)(2,1)} %get-tuple-element.120), channel_id=1, source_target_pairs={{0,4},{4,0},{8,12},{12,8},{16,20},{20,16},{24,28},{28,24},{1,5},{5... | collective-permute-start | bytes 3932168 | tf_op jit(solution)/shard_map/ppermute | solution.py:296
  254.3 42.8 %copy-start.7 = (bf16[512,768]{1,0:T(8,128)(2,1)S(1)}, bf16[512,768]{1,0:T(8,128)(2,1)}, u32[]{:S(2)}) copy-start(bf16[512,768]{1,0:T(8,128)(2,1)} %copy-done.6) | copy-start | bytes 2359300
  254.3 42.8 %copy-start.16 = (bf16[512,768]{1,0:T(8,128)(2,1)S(1)}, bf16[512,768]{1,0:T(8,128)(2,1)}, u32[]{:S(2)}) copy-start(bf16[512,768]{1,0:T(8,128)(2,1)} %copy-done.15) | copy-start | bytes 2359300
  254.3 42.8 %copy-start.41 = (s32[128]{0:T(128)S(1)}, s32[128]{0:T(128)}, u32[]{:S(2)}) copy-start(s32[128]{0:T(128)} %copy-done.39) | copy-start | bytes 1540
  297.1 1.9 copy-start.4
  299.8 14.9 %copy-start.21 = (bf16[512,1280]{1,0:T(8,128)(2,1)S(1)}, bf16[512,1280]{1,0:T(8,128)(2,1)}, u32[]{:S(2)}) copy-start(bf16[512,1280]{1,0:T(8,128)(2,1)} %copy-done.20) | copy-start | bytes 3932164
  299.8 14.9 %copy-start.47 = (f32[24,1024]{1,0:T(8,128)S(1)}, f32[24,1024]{1,0:T(8,128)}, u32[]{:S(2)}) copy-start(f32[24,1024]{1,0:T(8,128)} %copy-done.46) | copy-start | bytes 294916
  314.7 4.8 copy-start.1
  314.7 4.8 copy-start.5
  314.7 4.8 copy-start.9
  318.1 8.2 %copy-start.26 = (bf16[512,640]{1,0:T(8,128)(2,1)}, bf16[512,640]{1,0:T(8,128)(2,1)S(1)}, u32[]{:S(2)}) copy-start(bf16[512,640]{1,0:T(8,128)(2,1)S(1)} %get-tuple-element.133.refs_1_) | copy-start | bytes 1966084
  318.1 8.2 %copy-start.28 = (bf16[512,640]{1,0:T(8,128)(2,1)}, bf16[512,640]{1,0:T(8,128)(2,1)S(1)}, u32[]{:S(2)}) copy-start(bf16[512,640]{1,0:T(8,128)(2,1)S(1)} %get-tuple-element.134.refs_3_) | copy-start | bytes 1966084
  318.1 9.3 %collective-permute-start.13 = (bf16[1024,1024]{1,0:T(8,128)(2,1)S(1)}, bf16[1024,1024]{1,0:T(8,128)(2,1)S(1)}, u32[]{:S(2)}, u32[]{:S(2)}) collective-permute-start(bf16[1024,1024]{1,0:T(8,128)(2,1)S(1)} %get-tuple-element.123), channel_id=1, source_target_pairs={{0,1},{1,0},{2,3},{3,2},{4,5},{5,4},{6,7},{7,6},{8,9},{9,8},{10,11... | collective-permute-start | bytes 6291464 | tf_op jit(solution)/shard_map/ppermute | solution.py:296
  318.3 9.2 %collective-permute-start.14 = (f32[24,1024]{1,0:T(8,128)S(1)}, f32[24,1024]{1,0:T(8,128)S(1)}, u32[]{:S(2)}, u32[]{:S(2)}) collective-permute-start(f32[24,1024]{1,0:T(8,128)S(1)} %get-tuple-element.124.refs_6_.refs_4_), channel_id=1, source_target_pairs={{0,4},{4,0},{8,12},{12,8},{16,20},{20,16},{24,28},{28,24},{1,5},{5... | collective-permute-start | bytes 294920 | tf_op jit(solution)/shard_map/ppermute | solution.py:296
  327.4 63.2 %copy-start.12 = (bf16[512,1024]{1,0:T(8,128)(2,1)S(1)}, bf16[512,1024]{1,0:T(8,128)(2,1)}, u32[]{:S(2)}) copy-start(bf16[512,1024]{1,0:T(8,128)(2,1)} %copy-done.11) | copy-start | bytes 3145732
  327.4 63.2 %copy-start.17 = (f32[512,1024]{1,0:T(8,128)S(1)}, f32[512,1024]{1,0:T(8,128)}, u32[]{:S(2)}) copy-start(f32[512,1024]{1,0:T(8,128)} %get-tuple-element.127.refs_5_) | copy-start | bytes 6291460
  328.2 62.4 %collective-permute-start.15 = (bf16[512,1024]{1,0:T(8,128)(2,1)S(1)}, bf16[512,1024]{1,0:T(8,128)(2,1)S(1)}, u32[]{:S(2)}, u32[]{:S(2)}) collective-permute-start(bf16[512,1024]{1,0:T(8,128)(2,1)S(1)} %get-tuple-element.126), channel_id=1, source_target_pairs={{0,2},{1,3},{2,0},{3,1},{4,6},{5,7},{6,4},{7,5},{8,10},{9,11},{10,... | collective-permute-start | bytes 3145736 | tf_op jit(solution)/shard_map/ppermute | solution.py:296
  330.7 59.9 %collective-permute-start.17 = (bf16[512,768]{1,0:T(8,128)(2,1)S(1)}, bf16[512,768]{1,0:T(8,128)(2,1)S(1)}, u32[]{:S(2)}, u32[]{:S(2)}) collective-permute-start(bf16[512,768]{1,0:T(8,128)(2,1)S(1)} %get-tuple-element.129), channel_id=1, source_target_pairs={{0,4},{4,0},{8,12},{12,8},{16,20},{20,16},{24,28},{28,24},{1,5},{5... | collective-permute-start | bytes 2359304 | tf_op jit(solution)/shard_map/ppermute | solution.py:296
  330.7 43.6 %collective-permute-start.18 = (bf16[512,640]{1,0:T(8,128)(2,1)S(1)}, bf16[512,640]{1,0:T(8,128)(2,1)S(1)}, u32[]{:S(2)}, u32[]{:S(2)}) collective-permute-start(bf16[512,640]{1,0:T(8,128)(2,1)S(1)} %get-tuple-element.130), channel_id=1, source_target_pairs={{0,4},{4,0},{8,12},{12,8},{16,20},{20,16},{24,28},{28,24},{1,5},{5... | collective-permute-start | bytes 1966088 | tf_op jit(solution)/shard_map/ppermute | solution.py:296
  332.7 57.9 %collective-permute-start.19 = (bf16[512,640]{1,0:T(8,128)(2,1)S(1)}, bf16[512,640]{1,0:T(8,128)(2,1)S(1)}, u32[]{:S(2)}, u32[]{:S(2)}) collective-permute-start(bf16[512,640]{1,0:T(8,128)(2,1)S(1)} %get-tuple-element.131), channel_id=1, source_target_pairs={{0,2},{1,3},{2,0},{3,1},{4,6},{5,7},{6,4},{7,5},{8,10},{9,11},{10,... | collective-permute-start | bytes 1966088 | tf_op jit(solution)/shard_map/ppermute | solution.py:296
  332.8 57.8 %collective-permute-start.16 = (f32[24,1024]{1,0:T(8,128)S(1)}, f32[24,1024]{1,0:T(8,128)S(1)}, u32[]{:S(2)}, u32[]{:S(2)}) collective-permute-start(f32[24,1024]{1,0:T(8,128)S(1)} %get-tuple-element.128.refs_8_.refs_13_), channel_id=1, source_target_pairs={{0,8},{4,12},{8,0},{12,4},{16,24},{20,28},{24,16},{28,20},{1,9},{5... | collective-permute-start | bytes 294920 | tf_op jit(solution)/shard_map/ppermute | solution.py:296
  394.5 20.5 %copy-start.35 = (f32[24,1024]{1,0:T(8,128)}, f32[24,1024]{1,0:T(8,128)S(1)}, u32[]{:S(2)}) copy-start(f32[24,1024]{1,0:T(8,128)S(1)} %get-tuple-element.136.refs_7_.refs_9_) | copy-start | bytes 294916
  394.5 32.3 %all-to-all-start.3 = ((f32[32,24,128]{2,1,0:T(8,128)}), f32[32,24,128]{2,1,0:T(8,128)S(1)}, u32[]{:S(2)}, u32[]{:S(2)}) async-start(f32[32,24,128]{2,1,0:T(8,128)} %get-tuple-element.141), calls=%async_computation.4 | async-start | bytes 786432 | tf_op jit(solution)/shard_map/all_to_all | solution.py:1396
  401.7 13.3 %collective-permute-start.20 = (f32[24,1024]{1,0:T(8,128)S(1)}, f32[24,1024]{1,0:T(8,128)S(1)}, u32[]{:S(2)}, u32[]{:S(2)}) collective-permute-start(f32[24,1024]{1,0:T(8,128)S(1)} %get-tuple-element.136.refs_7_.refs_9_), channel_id=1, source_target_pairs={{0,16},{4,20},{8,24},{12,28},{16,0},{20,4},{24,8},{28,12},{1,17},{... | collective-permute-start | bytes 294920 | tf_op jit(solution)/shard_map/ppermute | solution.py:296
  421.9 24.8 %collective-permute-start.21 = (bf16[128,2048]{1,0:T(8,128)(2,1)}, bf16[128,2048]{1,0:T(8,128)(2,1)S(1)}, u32[]{:S(2)}, u32[]{:S(2)}) collective-permute-start(bf16[128,2048]{1,0:T(8,128)(2,1)} %get-tuple-element.138), channel_id=1, source_target_pairs={{0,8},{4,12},{8,0},{12,4},{16,24},{20,28},{24,16},{28,20},{1,9},{5... | collective-permute-start | bytes 1572872 | tf_op jit(solution)/shard_map/ppermute | solution.py:296
  425.3 35.1 %collective-permute-start.22 = (bf16[128,2048]{1,0:T(8,128)(2,1)}, bf16[128,2048]{1,0:T(8,128)(2,1)S(1)}, u32[]{:S(2)}, u32[]{:S(2)}) collective-permute-start(bf16[128,2048]{1,0:T(8,128)(2,1)} %get-tuple-element.139), channel_id=1, source_target_pairs={{0,16},{4,20},{8,24},{12,28},{16,0},{20,4},{24,8},{28,12},{1,17},{... | collective-permute-start | bytes 1572872 | tf_op jit(solution)/shard_map/ppermute | solution.py:296
  425.3 46.9 %collective-permute-start.23 = (bf16[128,2048]{1,0:T(8,128)(2,1)}, bf16[128,2048]{1,0:T(8,128)(2,1)S(1)}, u32[]{:S(2)}, u32[]{:S(2)}) collective-permute-start(bf16[128,2048]{1,0:T(8,128)(2,1)} %get-tuple-element.140), channel_id=1, source_target_pairs={{0,24},{4,28},{8,16},{12,20},{16,8},{20,12},{24,0},{28,4},{1,25},{... | collective-permute-start | bytes 1572872 | tf_op jit(solution)/shard_map/ppermute | solution.py:296
  427.7 52.0 %copy-start.34 = (f32[24,1024]{1,0:T(8,128)S(1)}, f32[24,1024]{1,0:T(8,128)}, u32[]{:S(2)}) copy-start(f32[24,1024]{1,0:T(8,128)} %copy-done.32) | copy-start | bytes 294916
  474.9 2.5 collective-permute-start.24
  475.4 4.3 collective-permute-start.25
  (23 other events, 21.7 us)
Sparse Core Ops, SparseCore 0:
  10.9 136.3 all-gather.2
  210.3 167.5 reduce-scatter.1

commit v4 on v3

--- a/solution.py
+++ b/solution.py
@@ -771,8 +771,9 @@
             out[k, :, span(tab[SLOT + m], piece.shape[1])] = piece[...]
 
 
-def home_body(tab, p0, p1, p2, late, early, out, gains, shifts, mid, hid, scale):
+def home_body(tab, p0, p1, p2, late, e0, e1, out, gains, shifts, mid, hid, scale):
     size, width = p0.shape[1], late.shape[1]
+    early = e0[...] + e1[...]
     for m, piece in enumerate((p0, p1, p2)):
         out[:, span(tab[SEND + m], size)] = piece[...].astype(f32)
     for row, source in enumerate((late[0:1], early[0:1], early[1:2])):
@@ -1125,17 +1126,15 @@
     a2k, a2s, b2k, b2s, *carried = call("fold_" + tag, fold_body, tab, [ak, ra, bk, rb] + ships, quarter, vmem=34, rider=rider)
     ra, rb = swap(a2s, "dp", 1), swap(b2s, "sp", 2)
     deps = yield carried + [ra, rb]
-    (g, r), size, rider = deps
+    (g, r), size = deps
     shard = (rows // 8, 2 * total + g.shape[1])
-    keep, *sends, carried = call(
-        "spread_" + tag, spread_body, tab, [a2k, ra, b2k, rb, g, r], [(shard, f32)] + [(shard, bf16)] * 3, rider=rider
-    )
+    keep, *sends = call("spread_" + tag, spread_body, tab, [a2k, ra, b2k, rb, g, r], [(shard, f32)] + [(shard, bf16)] * 3)
     received = [swap(x, "dp", b) for x, b in zip(sends, grid.z_bits)]
-    low = yield carried
+    rider, low = yield
     yield call(
         "sum_" + tag, functools.partial(gathered_body, widths), tab, [keep] + received + [low],
         [((rows // 8, 2 * w), f32) for w in widths] + [((rows // 8, size), bf16)] * 3 + [(low.shape, f32)],
-        scratch=[pltpu.VMEM(shard, f32)],
+        scratch=[pltpu.VMEM(shard, f32)], rider=rider,
     )
 
 
@@ -1372,19 +1371,18 @@
     )
     cross, early, *second_up = up_sums.send((early, [cross]))
     theirs = swap(cross, "sp", 1)
-    early = (early, swap(early, "dp", 1))
     keep_rows, send = call(
         "group_grads", functools.partial(groups_body, sp), tab, firsts + [qkv_grad],
         [((width // 2, wide), f32), ((width // 2, wide), bf16)], steps=sp,
         in_specs=[whole(f.shape) for f in firsts] + [by_rows(rows, wide)],
         scratch=[pltpu.VMEM((width, wide), f32)], vmem=30,
     )
-    relayed, send, early = call(
+    relayed, send = call(
         "relay", relay_body, tab, [far, theirs, send], [((rows, width), bf16), (send.shape, bf16)],
-        in_specs=[whole(far.shape), pl.BlockSpec((rows, width), lambda *_: (1, 0)), whole(send.shape)], rider=early,
+        in_specs=[whole(far.shape), pl.BlockSpec((rows, width), lambda *_: (1, 0)), whole(send.shape)],
     )
     crossed, other_rows = swap(relayed, "sp", 2), swap(send, "dp", 1)
-    early = (early, swap(early, "dp", 2))
+    early = (early, swap(early, "dp", 1))
     grad_tokens, late, early = call(
         "to_tokens", final_body, tab, [mine, theirs, crossed, tokr, middle_grad, vec, head_sums],
         [((rows, width), f32), ((dp * sp, 24, LANES), f32)], steps=2,
@@ -1392,14 +1390,15 @@
         out_specs=[by_rows(step, width), whole((dp * sp, 24, LANES))],
         scratch=[pltpu.VMEM((8, width), f32), pltpu.VMEM((24, LANES), f32)], rider=early, deps=(other_rows, *second_up),
     )
-    early = (early, swap(early, "dp", 4))
+    early = (early, swap(early, "dp", 2))
     late = lax.all_to_all(late, ("dp", "sp"), 0, 0, tiled=True)
-    early = up_sums.send(((keep_rows, other_rows), shard_lanes, early))
+    up_sums.send(((keep_rows, other_rows), shard_lanes))
     late = call("totals", functools.partial(totals_body, sp), tab, [late], [((8, width), f32)])[0]
-    grad_w_up, grad_w_out, *sent, grad_w_down = up_sums.send(down_part)
+    grad_w_up, grad_w_out, *sent, grad_w_down, early = up_sums.send((early, down_part))
+    along = swap(early, "dp", 4)
     got = [carry(x, pairs) for x, pairs in zip(sent, back_to)]
     grad_w_qkv, gain_sums, shift_sums, mid_sums, hid_sums, scale_sums = call(
-        "home", home_body, tab, got + [late, early],
+        "home", home_body, tab, got + [late, early, along],
         [((block, 3 * shard_lanes), f32), ((3, width), f32), ((7, width), f32), ((1, ff), f32), ((2, ff), f32), ((1, heads), f32)],
     )
     return (

time: 498 us -> 490 us (0.984)
  the two profiles are of different devices: /device:TPU:10 before, /device:TPU:0 now
where the time goes in v4:
time: 490 us; the launch traced here: 487 us
  Pallas kernels  206 us (42%)
  waiting for transfers between devices  164 us (33%)
  starting transfers between devices  53.9 us (11%)
  local copies, waits for them, and re-layouts  26.6 us (5%)
  blocking collectives  18.8 us (4%)
  between operations  14.8 us (3%)
    ppermute x22, waiting for transfers between devices, swap(): lax.ppermute(x, axis, [(i, i ^ bits) for i in range(lax.axis_size(axis))])  151 us
    pallas_call x21, Pallas kernels, call(): pl.pallas_call(skipping(body, 1 + len(args), len(deps)), grid_spec=pltpu....  135 us
    pallas_call x1, Pallas kernels, attend_backward(): pl.pallas_call(skipping(functools.partial(bwd_kernel, hd), 10, len(deps))...  42.8 us
    ppermute x22, starting transfers between devices, swap(): lax.ppermute(x, axis, [(i, i ^ bits) for i in range(lax.axis_size(axis))])  33.9 us
    pallas_call x1, Pallas kernels, attend_forward(): pl.pallas_call(skipping(functools.partial(fwd_kernel, hd), 7, len(deps)),...  28.1 us
    unnamed x100, local copies, waits for them, and re-layouts  25.7 us
    all_to_all x1, blocking collectives, fast_layer(): lax.all_to_all(scaled.reshape(sp, rows, shard_lanes), 'sp', 0, 0, tiled=T...  18.8 us
  transfers between devices with their start and end apart: 31, of which 12 were waited for; matrix products, arithmetic and copies ran while one was open for 0% of the time, Pallas kernels for 27%

profile of v4, /device:TPU:0, one launch (start us, length us, event | category | flops | bytes accessed | tf_op | source)
XLA Modules:
  0.0 487.0 jit_solution(15467376084963653110)
XLA Ops:
  7.2 2.1 pad_maximum_fusion
  10.0 0.9 copy-done.32
  11.5 3.0 collective-permute-start
  15.4 1.0 collective-permute-done.refs_2_
  16.4 2.4 collective-permute-done.1.refs_3_
  19.4 0.8 copy-done.36
  22.4 4.9 %prologue.1 = (bf16[528,1024]{1,0:T(8,128)(2,1)}, bf16[1040,1024]{1,0:T(8,128)(2,1)}, bf16[512,1024]{1,0:T(8,128)(2,1)S(1)}, bf16[512,1024]{1,0:T(8,128)(2,1)S(1...) custom-call(s32[128]{0:T(128)S(1)} %dynamic-slice_bitcast_fusion.refs_0_, bf16[512,1024]{1,0:T(8,128)(2,1)S(1)} %copy-done.24, ...), custom_call_target="tpu_custom_call" | custom-call | flops 1024 | bytes 1024 | tf_op jit(solution)/shard_map/prologue/pallas_call | solution.py:744
  27.3 1.0 copy-done.11
  28.3 1.0 copy-done.13
  29.9 4.9 all-to-all-start
  34.8 31.7 %collective-permute-done.3.refs_3_ = bf16[528,1024]{1,0:T(8,128)(2,1)S(1)} collective-permute-done((bf16[528,1024]{1,0:T(8,128)(2,1)}, bf16[528,1024]{1,0:T(8,128)(2,1)S(1)}, u32[]{:S(2)}, u32[]{:S(2)}) %collective-permute-start.3) | collective-permute-done | bytes 1081376 | tf_op jit(solution)/shard_map/ppermute | solution.py:296
  66.5 2.0 copy-done.14
  68.5 1.2 turn.1.refs_2_.refs_1_
  69.7 1.3 copy-done.2
  71.1 1.6 copy-done.3
  72.6 1.7 rows_qkv.1.refs_5_.refs_8_.refs_2_
  74.4 1.6 collective-permute-start.5
  76.0 21.4 %collective-permute-done.5.refs_6_.refs_3_ = bf16[512,768]{1,0:T(8,128)(2,1)S(1)} collective-permute-done((bf16[512,768]{1,0:T(8,128)(2,1)S(1)}, bf16[512,768]{1,0:T(8,128)(2,1)S(1)}, u32[]{:S(2)}, u32[]{:S(2)}) %collective-permute-start.5) | collective-permute-done | bytes 786464 | tf_op jit(solution)/shard_map/ppermute | solution.py:296
  97.5 6.2 %project.1 = (bf16[2048,768]{1,0:T(8,128)(2,1)S(1)}, f32[8,2048]{1,0:T(8,128)S(1)}) custom-call(s32[128]{0:T(128)S(1)} %dynamic-slice_bitcast_fusion.refs_0_, bf16[528,1024]{1,0:T(8,128)(2,1)} %get-tuple-element.85.refs_1_, bf16[1040,1024]{1,0:T(8,128)(2,1)S(1)} %collective-permute-done.2.refs_2_, bf16[528,1024]{1,0:T(8,128)(2,1)S(1)} %collective-permute-done.3.refs_3_, ...), custom_call_target="tpu_custom_call" | custom-call | flops 1024 | bytes 1024 | tf_op jit(solution)/shard_map/project/pallas_call | solution.py:744
  103.7 1.7 copy-done.46
  106.0 28.1 %attend_forward.1 = (bf16[2048,256]{1,0:T(8,128)(2,1)}, f32[256,2048]{1,0:T(8,128)}, f32[8,2048]{1,0:T(8,128)}) custom-call(s32[128]{0:T(128)} %copy-done.33, s32[4]{0:T(128)} %bitcast.19, bf16[2048,768]{1,0:T(8,128)(2,1)} %copy-done.46, bf16[2048,768]{1,0:T(8,128)(2,1)} %copy-done.46, bf16[2048,768]{1,0:T(8,128)(2,1)} %copy-done.46, f32[8,2048]{1,0:T(8,128)} %copy-done.48, ...), custom_call_target="tpu_custom_call" | custom-call | flops 40802189312 | bytes 1024 | tf_op jit(solution)/shard_map/attend_forward/pallas_call | solution.py:153
  134.1 18.8 %all_to_all.20.refs_1_ = bf16[4,512,256]{2,1,0:T(8,128)(2,1)} all-to-all(bf16[4,512,256]{2,1,0:T(8,128)(2,1)} %bitcast.16), channel_id=1, replica_groups=mesh['dp'=8,'sp'=4] {'sp'}, dimensions={0} | all-to-all | bytes 2097152 | tf_op jit(solution)/shard_map/all_to_all | solution.py:1309
  152.8 9.1 %to_middle.1 = (bf16[512,2048]{1,0:T(8,128)(2,1)}, f32[512,1024]{1,0:T(8,128)}, f32[512,1024]{1,0:T(8,128)}, f32[512,1]{1,0:T(8,128)}, bf16[1024,1024]{1,0:T(8,128)(2,1)}) custom-call(s32[128]{0:T(128)} %copy-done.33, bf16[4,512,256]{2,1,0:T(8,128)(2,1)} %all_to_all.20.refs_1_, bf16[512,1024]{1,0:T(8,128)(2,1)} %copy-done.11, f32[16,1024]{1,0:T(8,128)} %copy-done.22, ...), custom_call_target="tpu_custom_call" | custom-call | flops 1024 | bytes 1024 | tf_op jit(solution)/shard_map/to_middle/pallas_call | solution.py:744
  161.9 49.0 %ffn.1 = (bf16[512,2048]{1,0:T(8,128)(2,1)}, bf16[512,2048]{1,0:T(8,128)(2,1)}, bf16[512,2048]{1,0:T(8,128)(2,1)}, bf16[512,2048]{1,0:T(8,128)(2,1)}, f32[512,10...) custom-call(s32[128]{0:T(128)} %copy-done.33, bf16[512,2048]{1,0:T(8,128)(2,1)} %get-tuple-element.95.refs_1_.refs_5_, ...), custom_call_target="tpu_custom_call" | custom-call | flops 40700002304 | bytes 1024 | tf_op jit(solution)/shard_map/ffn/pallas_call | solution.py:744
  210.9 12.4 %spill.1.refs_8_ = bf16[32,128,1024]{2,1,0:T(8,128)(2,1)} custom-call(s32[128]{0:T(128)} %copy-done.33, bf16[1024,1024]{1,0:T(8,128)(2,1)} %copy-done.2, bf16[512,2048]{1,0:T(8,128)(2,1)} %get-tuple-element.102.refs_2_, bf16[512,2048]{1,0:T(8,128)(2,1)} %get-tuple-element.103.refs_3_, f32[8,4096]{1,0:T(8,128)} %get-tuple-element.104.refs_4_.refs_3_), custom_call_target="tpu_custom_call" | custom-call | flops 1024 | bytes 1024 | tf_op jit(solution)/shard_map/spill/pallas_call | solution.py:744
  223.9 9.2 %to_heads.1 = (f32[512,1024]{1,0:T(8,128)}, bf16[512,512]{1,0:T(8,128)(2,1)}, bf16[512,512]{1,0:T(8,128)(2,1)}, bf16[4,512,256]{2,1,0:T(8,128)(2,1)}, f32[8,1024]{1,0:T(8,128)}) custom-call(s32[128]{0:T(128)} %copy-done.33, f32[512,1024]{1,0:T(8,128)} %get-tuple-element.99.refs_1_, f32[512,1024]{1,0:T(8,128)} %get-tuple-element.96.refs_3_.refs_2_, ...), custom_call_target="tpu_custom_call" | custom-call | flops 1024 | bytes 1024 | tf_op jit(solution)/shard_map/to_heads/pallas_call | solution.py:744
  235.2 4.3 all-to-all-start.2
  239.5 1.6 copy-done.49
  241.1 13.4 %grads_up.1 = (bf16[1024,640]{1,0:T(8,128)(2,1)S(1)}, bf16[1024,640]{1,0:T(8,128)(2,1)}, bf16[512,1280]{1,0:T(8,128)(2,1)S(1)}, bf16[512,1280]{1,0:T(8,128)(2,1)}, f32[24,1024]{1,0:T(8,128)S(1)}) custom-call(s32[128]{0:T(128)S(1)} %copy-done.34, bf16[512,2048]{1,0:T(8,128)(2,1)} %get-tuple-element.95.refs_1_.refs_5_, ...), custom_call_target="tpu_custom_call" | custom-call | flops 13200001024 | bytes 1024 | tf_op jit(solution)/shard_map/grads_up/pallas_call | solution.py:744
  254.5 1.1 copy-done.20
  255.6 2.0 collective-permute-start.12
  257.6 2.5 collective-permute-start.11
  260.1 4.9 %all-to-all-done.2 = bf16[4,512,256]{2,1,0:T(8,128)(2,1)} async-done(((bf16[4,512,256]{2,1,0:T(8,128)(2,1)}), bf16[4,512,256]{2,1,0:T(8,128)(2,1)}, u32[]{:S(2)}, u32[]{:S(2)}) %all-to-all-start.2) | async-done | bytes 1048608 | tf_op jit(solution)/shard_map/all_to_all | solution.py:1354
  265.0 42.8 %attend_backward.1 = (bf16[2048,768]{1,0:T(8,128)(2,1)}, f32[8,768]{1,0:T(8,128)}) custom-call(s32[128]{0:T(128)} %copy-done.33, s32[4]{0:T(128)} %bitcast.20, bf16[2048,768]{1,0:T(8,128)(2,1)} %copy-done.46, bf16[2048,768]{1,0:T(8,128)(2,1)} %copy-done.46, bf16[2048,768]{1,0:T(8,128)(2,1)} %copy-done.46, f32[8,2048]{1,0:T(8,128)} %copy-done.48, ...), custom_call_target="tpu_custom_call" | custom-call | flops 53687091200 | bytes 1024 | tf_op jit(solution)/shard_map/attend_backward/pallas_call | solution.py:258
  307.8 1.9 copy-done.4
  310.4 5.1 %first_grad.1 = (f32[512,1024]{1,0:T(8,128)S(1)}, bf16[1024,1024]{1,0:T(8,128)(2,1)S(1)}, f32[512,1024]{1,0:T(8,128)S(1)}) custom-call(s32[128]{0:T(128)S(1)} %copy-done.35, bf16[2048,768]{1,0:T(8,128)(2,1)S(1)} %copy-done.4, bf16[512,768]{1,0:T(8,128)(2,1)S(1)} %copy-done.7, bf16[512,768]{1,0:T(8,128)(2,1)S(1)} %copy-done.16, f32[8,768]{1,0:T(8,128)S(1)} %copy-done.42), custom_call_target="tpu_custom_call" | custom-call | flops 1024 | bytes 1024 | tf_op jit(solution)/shard_map/first_grad/pallas_call | solution.py:744
  315.5 9.6 %collective-permute-done.10.refs_2_ = bf16[1024,640]{1,0:T(8,128)(2,1)} collective-permute-done((bf16[1024,640]{1,0:T(8,128)(2,1)}, bf16[1024,640]{1,0:T(8,128)(2,1)}, u32[]{:S(2)}, u32[]{:S(2)}) %collective-permute-start.10) | collective-permute-done | bytes 1310752 | tf_op jit(solution)/shard_map/ppermute | solution.py:296
  325.2 3.3 fold_up.1
  328.8 6.7 %group_grads.1 = (f32[512,768]{1,0:T(8,128)S(1)}, bf16[512,768]{1,0:T(8,128)(2,1)S(1)}) custom-call(s32[128]{0:T(128)S(1)} %copy-done.35, bf16[528,1024]{1,0:T(8,128)(2,1)} %get-tuple-element.85.refs_1_, bf16[1040,1024]{1,0:T(8,128)(2,1)S(1)} %copy-done.1, bf16[528,1024]{1,0:T(8,128)(2,1)S(1)} %copy-done.9, ...), custom_call_target="tpu_custom_call" | custom-call | flops 1024 | bytes 1024 | tf_op jit(solution)/shard_map/group_grads/pallas_call | solution.py:744
  335.6 1.1 copy-done.18
  336.7 0.8 relay.1
  337.5 2.4 collective-permute-start.14
  339.9 3.5 collective-permute-start.16
  343.5 1.9 collective-permute-start.18
  345.4 2.0 collective-permute-start.15
  347.4 42.4 %collective-permute-done.15.refs_9_ = f32[24,1024]{1,0:T(8,128)S(1)} collective-permute-done((f32[24,1024]{1,0:T(8,128)S(1)}, f32[24,1024]{1,0:T(8,128)S(1)}, u32[]{:S(2)}, u32[]{:S(2)}) %collective-permute-start.15) | collective-permute-done | bytes 98336 | tf_op jit(solution)/shard_map/ppermute | solution.py:296
  389.9 13.3 %collective-permute-done.18.refs_12_.refs_4_ = bf16[512,640]{1,0:T(8,128)(2,1)S(1)} collective-permute-done((bf16[512,640]{1,0:T(8,128)(2,1)S(1)}, bf16[512,640]{1,0:T(8,128)(2,1)S(1)}, u32[]{:S(2)}, u32[]{:S(2)}) %collective-permute-start.18) | collective-permute-done | bytes 655392 | tf_op jit(solution)/shard_map/ppermute | solution.py:296
  403.2 3.8 to_tokens.1
  407.0 5.9 %all-to-all-start.3 = ((f32[32,24,128]{2,1,0:T(8,128)}), f32[32,24,128]{2,1,0:T(8,128)S(1)}, u32[]{:S(2)}, u32[]{:S(2)}) async-start(f32[32,24,128]{2,1,0:T(8,128)} %get-tuple-element.139), calls=%async_computation.4 | async-start | bytes 786432 | tf_op jit(solution)/shard_map/all_to_all | solution.py:1394
  412.9 1.4 copy-done.19
  414.3 1.1 copy-done.27
  415.4 1.1 copy-done.29
  416.5 1.8 spread_up.1
  418.3 1.8 collective-permute-start.19
  420.1 2.4 collective-permute-start.20
  422.7 0.9 collective-permute-start.22
  423.5 2.3 all-to-all-done.3.refs_1_
  426.6 32.4 %collective-permute-done.22.refs_7_ = f32[24,1024]{1,0:T(8,128)S(1)} collective-permute-done((f32[24,1024]{1,0:T(8,128)}, f32[24,1024]{1,0:T(8,128)S(1)}, u32[]{:S(2)}, u32[]{:S(2)}) %collective-permute-start.22) | collective-permute-done | bytes 98336 | tf_op jit(solution)/shard_map/ppermute | solution.py:296
  459.3 0.9 copy-done.31
  460.3 2.6 sum_up.1
  462.9 11.2 %collective-permute-start.25 = (f32[24,1024]{1,0:T(8,128)S(1)}, f32[24,1024]{1,0:T(8,128)S(1)}, u32[]{:S(2)}, u32[]{:S(2)}) collective-permute-start(f32[24,1024]{1,0:T(8,128)S(1)} %get-tuple-element.143.refs_5_.refs_7_), channel_id=1, source_target_pairs={{0,16},{4,20},{8,24},{12,28},{16,0},{20,4},{24,8},{28,12},{1,17},{... | collective-permute-start | bytes 294920 | tf_op jit(solution)/shard_map/ppermute | solution.py:296
  474.1 2.0 collective-permute-start.24
  476.1 2.5 collective-permute-done.23.refs_2_
  478.6 1.3 home.1
  (130 shorter events, 11.5 us)
Async XLA Ops:
  7.2 12.2 %copy-start.25 = (bf16[512,1024]{1,0:T(8,128)(2,1)S(1)}, bf16[512,1024]{1,0:T(8,128)(2,1)}, u32[]{:S(2)}) copy-start(bf16[512,1024]{1,0:T(8,128)(2,1)} %refs_2_.1) | copy-start | bytes 3145732
  7.2 12.2 %copy-start.24 = (bf16[512,1024]{1,0:T(8,128)(2,1)S(1)}, bf16[512,1024]{1,0:T(8,128)(2,1)}, u32[]{:S(2)}) copy-start(bf16[512,1024]{1,0:T(8,128)(2,1)} %refs_1_.3) | copy-start | bytes 3145732
  7.2 145.7 %all-gather.3.cloned.1.call-start = ((), (), s32[]{:S(2)}) async-start(), calls=%async_computation.6 | async-start | bytes 19464192 | tf_op jit(solution)/shard_map/all_gather | solution.py:1285
  11.0 86.5 %copy-start.33 = (s32[128]{0:T(128)}, s32[128]{0:T(128)S(1)}, u32[]{:S(2)}) copy-start(s32[128]{0:T(128)S(1)} %dynamic-slice_bitcast_fusion.refs_0_) | copy-start | bytes 1540
  11.5 4.9 collective-permute-start
  14.5 4.3 collective-permute-start.1
  19.3 10.5 %copy-start.10 = (bf16[4,128,768]{2,1,0:T(8,128)(2,1)}, bf16[4,128,768]{2,1,0:T(8,128)(2,1)S(1)}, u32[]{:S(2)}) copy-start(bf16[4,128,768]{2,1,0:T(8,128)(2,1)S(1)} %join.1.refs_9_) | copy-start | bytes 2359300
  29.9 39.9 %copy-start.38 = (f32[8,4096]{1,0:T(8,128)}, f32[8,4096]{1,0:T(8,128)S(1)}, u32[]{:S(2)}) copy-start(f32[8,4096]{1,0:T(8,128)S(1)} %get-tuple-element.88.refs_4_) | copy-start | bytes 393220
  29.9 36.7 %collective-permute-start.2 = (bf16[1040,1024]{1,0:T(8,128)(2,1)}, bf16[1040,1024]{1,0:T(8,128)(2,1)S(1)}, u32[]{:S(2)}, u32[]{:S(2)}) collective-permute-start(bf16[1040,1024]{1,0:T(8,128)(2,1)} %get-tuple-element.86), channel_id=1, source_target_pairs={{0,1},{1,0},{2,3},{3,2},{4,5},{5,4},{6,7},{7,6},{8,9},{9,8},{10,11... | collective-permute-start | bytes 6389768 | tf_op jit(solution)/shard_map/ppermute | solution.py:296
  29.9 36.6 %collective-permute-start.3 = (bf16[528,1024]{1,0:T(8,128)(2,1)}, bf16[528,1024]{1,0:T(8,128)(2,1)S(1)}, u32[]{:S(2)}, u32[]{:S(2)}) collective-permute-start(bf16[528,1024]{1,0:T(8,128)(2,1)} %get-tuple-element.85.refs_1_), channel_id=1, source_target_pairs={{0,2},{1,3},{2,0},{3,1},{4,6},{5,7},{6,4},{7,5},{8,10},{9,11},{10,... | collective-permute-start | bytes 3244040 | tf_op jit(solution)/shard_map/ppermute | solution.py:296
  29.9 41.1 %all-to-all-start = ((bf16[4,128,768]{2,1,0:T(8,128)(2,1)}), bf16[4,128,768]{2,1,0:T(8,128)(2,1)}, u32[]{:S(2)}, u32[]{:S(2)}) async-start(bf16[4,128,768]{2,1,0:T(8,128)(2,1)} %copy-done.10), calls=%async_computation | async-start | bytes 1572864 | tf_op jit(solution)/shard_map/all_to_all | solution.py:1143
  34.8 424.5 %reduce-scatter.2.cloned.1.call-start = ((), (), s32[]{:S(2)}) async-start(), calls=%async_computation.5 | async-start | bytes 8650752 | tf_op jit(solution)/shard_map/reduce_scatter | solution.py:1340
  66.5 30.9 %copy-start.8 = (bf16[528,1024]{1,0:T(8,128)(2,1)}, bf16[528,1024]{1,0:T(8,128)(2,1)S(1)}, u32[]{:S(2)}) copy-start(bf16[528,1024]{1,0:T(8,128)(2,1)S(1)} %collective-permute-done.3.refs_3_) | copy-start | bytes 3244036
  66.5 9.5 %collective-permute-start.4 = (bf16[528,1024]{1,0:T(8,128)(2,1)S(1)}, bf16[528,1024]{1,0:T(8,128)(2,1)}, u32[]{:S(2)}, u32[]{:S(2)}) collective-permute-start(bf16[528,1024]{1,0:T(8,128)(2,1)S(1)} %collective-permute-done.3.refs_3_), channel_id=1, source_target_pairs={{0,1},{1,0},{2,3},{3,2},{4,5},{5,4},{6,7},{7,6},{8,9},{9,8},{10,11... | collective-permute-start | bytes 3244040 | tf_op jit(solution)/shard_map/ppermute | solution.py:296
  66.5 30.9 %copy-start = (bf16[1040,1024]{1,0:T(8,128)(2,1)}, bf16[1040,1024]{1,0:T(8,128)(2,1)S(1)}, u32[]{:S(2)}) copy-start(bf16[1040,1024]{1,0:T(8,128)(2,1)S(1)} %collective-permute-done.2.refs_2_) | copy-start | bytes 6389764
  66.5 2.0 copy-start.14
  71.1 1.6 copy-start.3
  72.6 24.8 %copy-start.37 = (f32[7,1024]{1,0:T(8,128)S(1)}, f32[7,1024]{1,0:T(8,128)}, u32[]{:S(2)}) copy-start(f32[7,1024]{1,0:T(8,128)} %refs_7_.1) | copy-start | bytes 86020
  74.4 29.3 %copy-start.6 = (bf16[512,768]{1,0:T(8,128)(2,1)}, bf16[512,768]{1,0:T(8,128)(2,1)S(1)}, u32[]{:S(2)}) copy-start(bf16[512,768]{1,0:T(8,128)(2,1)S(1)} %rows_qkv.1.refs_5_.refs_8_.refs_2_) | copy-start | bytes 2359300
  74.4 23.1 %collective-permute-start.5 = (bf16[512,768]{1,0:T(8,128)(2,1)S(1)}, bf16[512,768]{1,0:T(8,128)(2,1)S(1)}, u32[]{:S(2)}, u32[]{:S(2)}) collective-permute-start(bf16[512,768]{1,0:T(8,128)(2,1)S(1)} %rows_qkv.1.refs_5_.refs_8_.refs_2_), channel_id=1, source_target_pairs={{0,4},{4,0},{8,12},{12,8},{16,20},{20,16},{24,28},{28,24},{1,5},{5... | collective-permute-start | bytes 2359304 | tf_op jit(solution)/shard_map/ppermute | solution.py:296
  97.4 6.2 %copy-start.15 = (bf16[512,768]{1,0:T(8,128)(2,1)}, bf16[512,768]{1,0:T(8,128)(2,1)S(1)}, u32[]{:S(2)}) copy-start(bf16[512,768]{1,0:T(8,128)(2,1)S(1)} %collective-permute-done.5.refs_6_.refs_3_) | copy-start | bytes 2359300
  103.7 1.7 copy-start.46
  223.3 16.1 %collective-permute-start.7 = (bf16[512,2048]{1,0:T(8,128)(2,1)}, bf16[512,2048]{1,0:T(8,128)(2,1)}, u32[]{:S(2)}, u32[]{:S(2)}) collective-permute-start(bf16[512,2048]{1,0:T(8,128)(2,1)} %get-tuple-element.108), channel_id=1, source_target_pairs={{0,1},{1,0},{2,3},{3,2},{4,5},{5,4},{6,7},{7,6},{8,9},{9,8},{10,11... | collective-permute-start | bytes 6291464 | tf_op jit(solution)/shard_map/ppermute | solution.py:296
  223.4 16.1 %collective-permute-start.6 = (bf16[512,2048]{1,0:T(8,128)(2,1)}, bf16[512,2048]{1,0:T(8,128)(2,1)}, u32[]{:S(2)}, u32[]{:S(2)}) collective-permute-start(bf16[512,2048]{1,0:T(8,128)(2,1)} %get-tuple-element.95.refs_1_.refs_5_), channel_id=1, source_target_pairs={{0,1},{1,0},{2,3},{3,2},{4,5},{5,4},{6,7},{7,6},{8,9},{9,8},{10,11... | collective-permute-start | bytes 6291464 | tf_op jit(solution)/shard_map/ppermute | solution.py:296
  223.9 9.4 %copy-start.23 = (f32[16,1024]{1,0:T(8,128)S(1)}, f32[16,1024]{1,0:T(8,128)}, u32[]{:S(2)}) copy-start(f32[16,1024]{1,0:T(8,128)} %copy-done.22) | copy-start | bytes 196612
  223.9 9.4 %copy-start.30 = (f32[8,4096]{1,0:T(8,128)S(1)}, f32[8,4096]{1,0:T(8,128)}, u32[]{:S(2)}) copy-start(f32[8,4096]{1,0:T(8,128)} %get-tuple-element.104.refs_4_.refs_3_) | copy-start | bytes 393220
  223.9 9.4 %copy-start.34 = (s32[128]{0:T(128)S(1)}, s32[128]{0:T(128)}, u32[]{:S(2)}) copy-start(s32[128]{0:T(128)} %copy-done.33) | copy-start | bytes 1540
  233.1 6.4 %collective-permute-start.8 = (bf16[512,512]{1,0:T(8,128)(2,1)}, bf16[512,512]{1,0:T(8,128)(2,1)S(1)}, u32[]{:S(2)}, u32[]{:S(2)}) collective-permute-start(bf16[512,512]{1,0:T(8,128)(2,1)} %get-tuple-element.110), channel_id=1, source_target_pairs={{0,1},{1,0},{2,3},{3,2},{4,5},{5,4},{6,7},{7,6},{8,9},{9,8},{10,11... | collective-permute-start | bytes 1572872 | tf_op jit(solution)/shard_map/ppermute | solution.py:296
  234.0 5.5 %copy-start.47 = (bf16[512,512]{1,0:T(8,128)(2,1)S(1)}, bf16[512,512]{1,0:T(8,128)(2,1)}, u32[]{:S(2)}) copy-start(bf16[512,512]{1,0:T(8,128)(2,1)} %get-tuple-element.109.refs_7_) | copy-start | bytes 1572868
  234.7 4.8 collective-permute-start.9
  235.2 29.8 %all-to-all-start.2 = ((bf16[4,512,256]{2,1,0:T(8,128)(2,1)}), bf16[4,512,256]{2,1,0:T(8,128)(2,1)}, u32[]{:S(2)}, u32[]{:S(2)}) async-start(bf16[4,512,256]{2,1,0:T(8,128)(2,1)} %get-tuple-element.105), calls=%async_computation.2 | async-start | bytes 2097152 | tf_op jit(solution)/shard_map/all_to_all | solution.py:1354
  239.5 1.6 copy-start.49
  255.6 9.4 %copy-start.40 = (f32[24,1024]{1,0:T(8,128)}, f32[24,1024]{1,0:T(8,128)S(1)}, u32[]{:S(2)}) copy-start(f32[24,1024]{1,0:T(8,128)S(1)} %get-tuple-element.112.refs_10_.refs_6_) | copy-start | bytes 294916
  255.6 59.9 %collective-permute-start.12 = (f32[24,1024]{1,0:T(8,128)S(1)}, f32[24,1024]{1,0:T(8,128)S(1)}, u32[]{:S(2)}, u32[]{:S(2)}) collective-permute-start(f32[24,1024]{1,0:T(8,128)S(1)} %get-tuple-element.112.refs_10_.refs_6_), channel_id=1, source_target_pairs={{0,2},{1,3},{2,0},{3,1},{4,6},{5,7},{6,4},{7,5},{8,10},{9,11},{10,... | collective-permute-start | bytes 294920 | tf_op jit(solution)/shard_map/ppermute | solution.py:296
  257.5 67.6 %collective-permute-start.10 = (bf16[1024,640]{1,0:T(8,128)(2,1)}, bf16[1024,640]{1,0:T(8,128)(2,1)}, u32[]{:S(2)}, u32[]{:S(2)}) collective-permute-start(bf16[1024,640]{1,0:T(8,128)(2,1)} %get-tuple-element.117), channel_id=1, source_target_pairs={{0,2},{1,3},{2,0},{3,1},{4,6},{5,7},{6,4},{7,5},{8,10},{9,11},{10,... | collective-permute-start | bytes 3932168 | tf_op jit(solution)/shard_map/ppermute | solution.py:296
  257.6 67.5 %collective-permute-start.11 = (bf16[512,1280]{1,0:T(8,128)(2,1)}, bf16[512,1280]{1,0:T(8,128)(2,1)}, u32[]{:S(2)}, u32[]{:S(2)}) collective-permute-start(bf16[512,1280]{1,0:T(8,128)(2,1)} %get-tuple-element.119), channel_id=1, source_target_pairs={{0,4},{4,0},{8,12},{12,8},{16,20},{20,16},{24,28},{28,24},{1,5},{5... | collective-permute-start | bytes 3932168 | tf_op jit(solution)/shard_map/ppermute | solution.py:296
  264.9 42.8 %copy-start.7 = (bf16[512,768]{1,0:T(8,128)(2,1)S(1)}, bf16[512,768]{1,0:T(8,128)(2,1)}, u32[]{:S(2)}) copy-start(bf16[512,768]{1,0:T(8,128)(2,1)} %copy-done.6) | copy-start | bytes 2359300
  264.9 42.8 %copy-start.16 = (bf16[512,768]{1,0:T(8,128)(2,1)S(1)}, bf16[512,768]{1,0:T(8,128)(2,1)}, u32[]{:S(2)}) copy-start(bf16[512,768]{1,0:T(8,128)(2,1)} %copy-done.15) | copy-start | bytes 2359300
  265.0 42.8 %copy-start.35 = (s32[128]{0:T(128)S(1)}, s32[128]{0:T(128)}, u32[]{:S(2)}) copy-start(s32[128]{0:T(128)} %copy-done.33) | copy-start | bytes 1540
  307.8 1.9 copy-start.4
  310.4 14.7 %copy-start.21 = (bf16[512,1280]{1,0:T(8,128)(2,1)S(1)}, bf16[512,1280]{1,0:T(8,128)(2,1)}, u32[]{:S(2)}) copy-start(bf16[512,1280]{1,0:T(8,128)(2,1)} %copy-done.20) | copy-start | bytes 3932164
  310.4 14.7 %copy-start.41 = (f32[24,1024]{1,0:T(8,128)S(1)}, f32[24,1024]{1,0:T(8,128)}, u32[]{:S(2)}) copy-start(f32[24,1024]{1,0:T(8,128)} %copy-done.40) | copy-start | bytes 294916
  325.1 3.5 copy-start.1
  325.2 3.5 copy-start.5
  325.2 3.6 copy-start.9
  328.5 7.0 %copy-start.26 = (bf16[512,640]{1,0:T(8,128)(2,1)}, bf16[512,640]{1,0:T(8,128)(2,1)S(1)}, u32[]{:S(2)}) copy-start(bf16[512,640]{1,0:T(8,128)(2,1)S(1)} %get-tuple-element.131.refs_1_) | copy-start | bytes 1966084
  328.5 7.0 %copy-start.28 = (bf16[512,640]{1,0:T(8,128)(2,1)}, bf16[512,640]{1,0:T(8,128)(2,1)S(1)}, u32[]{:S(2)}) copy-start(bf16[512,640]{1,0:T(8,128)(2,1)S(1)} %get-tuple-element.132.refs_3_) | copy-start | bytes 1966084
  328.5 8.2 %collective-permute-start.13 = (bf16[1024,1024]{1,0:T(8,128)(2,1)S(1)}, bf16[1024,1024]{1,0:T(8,128)(2,1)S(1)}, u32[]{:S(2)}, u32[]{:S(2)}) collective-permute-start(bf16[1024,1024]{1,0:T(8,128)(2,1)S(1)} %get-tuple-element.122), channel_id=1, source_target_pairs={{0,1},{1,0},{2,3},{3,2},{4,5},{5,4},{6,7},{7,6},{8,9},{9,8},{10,11... | collective-permute-start | bytes 6291464 | tf_op jit(solution)/shard_map/ppermute | solution.py:296
  336.7 66.5 %copy-start.12 = (bf16[512,1024]{1,0:T(8,128)(2,1)S(1)}, bf16[512,1024]{1,0:T(8,128)(2,1)}, u32[]{:S(2)}) copy-start(bf16[512,1024]{1,0:T(8,128)(2,1)} %copy-done.11) | copy-start | bytes 3145732
  336.7 66.5 %copy-start.17 = (f32[512,1024]{1,0:T(8,128)S(1)}, f32[512,1024]{1,0:T(8,128)}, u32[]{:S(2)}) copy-start(f32[512,1024]{1,0:T(8,128)} %get-tuple-element.126.refs_5_) | copy-start | bytes 6291460
  337.5 65.7 %collective-permute-start.14 = (bf16[512,1024]{1,0:T(8,128)(2,1)S(1)}, bf16[512,1024]{1,0:T(8,128)(2,1)S(1)}, u32[]{:S(2)}, u32[]{:S(2)}) collective-permute-start(bf16[512,1024]{1,0:T(8,128)(2,1)S(1)} %get-tuple-element.125), channel_id=1, source_target_pairs={{0,2},{1,3},{2,0},{3,1},{4,6},{5,7},{6,4},{7,5},{8,10},{9,11},{10,... | collective-permute-start | bytes 3145736 | tf_op jit(solution)/shard_map/ppermute | solution.py:296
  339.9 63.3 %collective-permute-start.16 = (bf16[512,768]{1,0:T(8,128)(2,1)S(1)}, bf16[512,768]{1,0:T(8,128)(2,1)S(1)}, u32[]{:S(2)}, u32[]{:S(2)}) collective-permute-start(bf16[512,768]{1,0:T(8,128)(2,1)S(1)} %get-tuple-element.127.refs_13_), channel_id=1, source_target_pairs={{0,4},{4,0},{8,12},{12,8},{16,20},{20,16},{24,28},{28,24},{1,5},{5... | collective-permute-start | bytes 2359304 | tf_op jit(solution)/shard_map/ppermute | solution.py:296
  343.4 46.4 %collective-permute-start.17 = (bf16[512,640]{1,0:T(8,128)(2,1)S(1)}, bf16[512,640]{1,0:T(8,128)(2,1)S(1)}, u32[]{:S(2)}, u32[]{:S(2)}) collective-permute-start(bf16[512,640]{1,0:T(8,128)(2,1)S(1)} %get-tuple-element.128), channel_id=1, source_target_pairs={{0,4},{4,0},{8,12},{12,8},{16,20},{20,16},{24,28},{28,24},{1,5},{5... | collective-permute-start | bytes 1966088 | tf_op jit(solution)/shard_map/ppermute | solution.py:296
  343.5 59.6 %collective-permute-start.18 = (bf16[512,640]{1,0:T(8,128)(2,1)S(1)}, bf16[512,640]{1,0:T(8,128)(2,1)S(1)}, u32[]{:S(2)}, u32[]{:S(2)}) collective-permute-start(bf16[512,640]{1,0:T(8,128)(2,1)S(1)} %get-tuple-element.129), channel_id=1, source_target_pairs={{0,2},{1,3},{2,0},{3,1},{4,6},{5,7},{6,4},{7,5},{8,10},{9,11},{10,... | collective-permute-start | bytes 1966088 | tf_op jit(solution)/shard_map/ppermute | solution.py:296
  345.4 44.4 %collective-permute-start.15 = (f32[24,1024]{1,0:T(8,128)S(1)}, f32[24,1024]{1,0:T(8,128)S(1)}, u32[]{:S(2)}, u32[]{:S(2)}) collective-permute-start(f32[24,1024]{1,0:T(8,128)S(1)} %get-tuple-element.123.refs_6_.refs_8_), channel_id=1, source_target_pairs={{0,4},{4,0},{8,12},{12,8},{16,20},{20,16},{24,28},{28,24},{1,5},{5... | collective-permute-start | bytes 294920 | tf_op jit(solution)/shard_map/ppermute | solution.py:296
  407.0 18.9 %all-to-all-start.3 = ((f32[32,24,128]{2,1,0:T(8,128)}), f32[32,24,128]{2,1,0:T(8,128)S(1)}, u32[]{:S(2)}, u32[]{:S(2)}) async-start(f32[32,24,128]{2,1,0:T(8,128)} %get-tuple-element.139), calls=%async_computation.4 | async-start | bytes 786432 | tf_op jit(solution)/shard_map/all_to_all | solution.py:1394
  412.9 1.4 copy-start.19
  418.3 40.7 %collective-permute-start.19 = (bf16[128,2048]{1,0:T(8,128)(2,1)}, bf16[128,2048]{1,0:T(8,128)(2,1)S(1)}, u32[]{:S(2)}, u32[]{:S(2)}) collective-permute-start(bf16[128,2048]{1,0:T(8,128)(2,1)} %get-tuple-element.136), channel_id=1, source_target_pairs={{0,8},{4,12},{8,0},{12,4},{16,24},{20,28},{24,16},{28,20},{1,9},{5... | collective-permute-start | bytes 1572872 | tf_op jit(solution)/shard_map/ppermute | solution.py:296
  420.1 39.3 %collective-permute-start.20 = (bf16[128,2048]{1,0:T(8,128)(2,1)}, bf16[128,2048]{1,0:T(8,128)(2,1)S(1)}, u32[]{:S(2)}, u32[]{:S(2)}) collective-permute-start(bf16[128,2048]{1,0:T(8,128)(2,1)} %get-tuple-element.137), channel_id=1, source_target_pairs={{0,16},{4,20},{8,24},{12,28},{16,0},{20,4},{24,8},{28,12},{1,17},{... | collective-permute-start | bytes 1572872 | tf_op jit(solution)/shard_map/ppermute | solution.py:296
  422.5 36.8 %collective-permute-start.21 = (bf16[128,2048]{1,0:T(8,128)(2,1)}, bf16[128,2048]{1,0:T(8,128)(2,1)S(1)}, u32[]{:S(2)}, u32[]{:S(2)}) collective-permute-start(bf16[128,2048]{1,0:T(8,128)(2,1)} %get-tuple-element.138.refs_2_), channel_id=1, source_target_pairs={{0,24},{4,28},{8,16},{12,20},{16,8},{20,12},{24,0},{28,4},{1,25},{... | collective-permute-start | bytes 1572872 | tf_op jit(solution)/shard_map/ppermute | solution.py:296
  422.7 36.3 %collective-permute-start.22 = (f32[24,1024]{1,0:T(8,128)}, f32[24,1024]{1,0:T(8,128)S(1)}, u32[]{:S(2)}, u32[]{:S(2)}) collective-permute-start(f32[24,1024]{1,0:T(8,128)} %get-tuple-element.134.refs_7_.refs_6_), channel_id=1, source_target_pairs={{0,8},{4,12},{8,0},{12,4},{16,24},{20,28},{24,16},{28,20},{1,9},{5... | collective-permute-start | bytes 294920 | tf_op jit(solution)/shard_map/ppermute | solution.py:296
  462.9 15.7 %collective-permute-start.25 = (f32[24,1024]{1,0:T(8,128)S(1)}, f32[24,1024]{1,0:T(8,128)S(1)}, u32[]{:S(2)}, u32[]{:S(2)}) collective-permute-start(f32[24,1024]{1,0:T(8,128)S(1)} %get-tuple-element.143.refs_5_.refs_7_), channel_id=1, source_target_pairs={{0,16},{4,20},{8,24},{12,28},{16,0},{20,4},{24,8},{28,12},{1,17},{... | collective-permute-start | bytes 294920 | tf_op jit(solution)/shard_map/ppermute | solution.py:296
  474.1 4.5 collective-permute-start.23
  474.1 4.5 collective-permute-start.24
  (17 other events, 15.3 us)
Sparse Core Ops, SparseCore 0:
  10.9 141.0 all-gather.2
  223.4 166.2 reduce-scatter.1

commit v5 on v4

--- a/solution.py
+++ b/solution.py
@@ -1369,14 +1369,14 @@
         in_specs=[by_rows(rows, wide), whole(wq0.shape), whole(wq1.shape)],
         out_specs=[whole((rows, width)), whole((2 * rows, width)), whole((rows, width))],
     )
-    cross, early, *second_up = up_sums.send((early, [cross]))
-    theirs = swap(cross, "sp", 1)
     keep_rows, send = call(
         "group_grads", functools.partial(groups_body, sp), tab, firsts + [qkv_grad],
         [((width // 2, wide), f32), ((width // 2, wide), bf16)], steps=sp,
         in_specs=[whole(f.shape) for f in firsts] + [by_rows(rows, wide)],
         scratch=[pltpu.VMEM((width, wide), f32)], vmem=30,
     )
+    cross, early, *second_up = up_sums.send((early, [cross]))
+    theirs = swap(cross, "sp", 1)
     relayed, send = call(
         "relay", relay_body, tab, [far, theirs, send], [((rows, width), bf16), (send.shape, bf16)],
         in_specs=[whole(far.shape), pl.BlockSpec((rows, width), lambda *_: (1, 0)), whole(send.shape)],

time: 490 us -> 489 us (level)
  waiting for transfers between devices: 164 us -> 175 us
  Pallas kernels: 206 us -> 197 us
  starting transfers between devices: 53.9 us -> 48.9 us
    ppermute x22, waiting for transfers between devices: 151 us -> 158 us  [swap(): lax.ppermute(x, axis, [(i, i ^ bits) for i in range(lax.axis_size(axis))])]
    pallas_call x1, Pallas kernels: 42.8 us -> 37.7 us  [attend_backward(): pl.pallas_call(skipping(functools.partial(bwd_kernel, hd), 10, len(deps))...]
  transfers between devices with their start and end apart: 31 -> 31, of which waited for: 12 -> 14; matrix products, arithmetic and copies ran while one was open for 0% -> 0% of each run, Pallas kernels for 27% -> 25%
where the time goes in v5:
time: 489 us; the launch traced here: 485 us
  Pallas kernels  197 us (40%)
  waiting for transfers between devices  175 us (36%)
  starting transfers between devices  48.9 us (10%)
  local copies, waits for them, and re-layouts  28.3 us (6%)
  blocking collectives  18.8 us (4%)
  between operations  14.8 us (3%)
    ppermute x22, waiting for transfers between devices, swap(): lax.ppermute(x, axis, [(i, i ^ bits) for i in range(lax.axis_size(axis))])  158 us
    pallas_call x21, Pallas kernels, call(): pl.pallas_call(skipping(body, 1 + len(args), len(deps)), grid_spec=pltpu....  134 us
    pallas_call x1, Pallas kernels, attend_backward(): pl.pallas_call(skipping(functools.partial(bwd_kernel, hd), 10, len(deps))...  37.7 us
    ppermute x22, starting transfers between devices, swap(): lax.ppermute(x, axis, [(i, i ^ bits) for i in range(lax.axis_size(axis))])  29.4 us
    unnamed x100, local copies, waits for them, and re-layouts  27.4 us
    pallas_call x1, Pallas kernels, attend_forward(): pl.pallas_call(skipping(functools.partial(fwd_kernel, hd), 7, len(deps)),...  24.9 us
    all_to_all x1, blocking collectives, fast_layer(): lax.all_to_all(scaled.reshape(sp, rows, shard_lanes), 'sp', 0, 0, tiled=T...  18.8 us
  transfers between devices with their start and end apart: 31, of which 14 were waited for; matrix products, arithmetic and copies ran while one was open for 0% of the time, Pallas kernels for 25%

profile of v5, /device:TPU:0, one launch (start us, length us, event | category | flops | bytes accessed | tf_op | source)
XLA Modules:
  0.0 485.4 jit_solution(2467975169724779483)
XLA Ops:
  7.2 2.1 pad_maximum_fusion
  10.0 0.9 copy-done.32
  11.5 3.0 collective-permute-start
  15.4 1.0 collective-permute-done.refs_2_
  16.4 2.4 collective-permute-done.1.refs_3_
  22.4 4.9 %prologue.1 = (bf16[528,1024]{1,0:T(8,128)(2,1)}, bf16[1040,1024]{1,0:T(8,128)(2,1)}, bf16[512,1024]{1,0:T(8,128)(2,1)S(1)}, bf16[512,1024]{1,0:T(8,128)(2,1)S(1...) custom-call(s32[128]{0:T(128)S(1)} %dynamic-slice_bitcast_fusion.refs_0_, bf16[512,1024]{1,0:T(8,128)(2,1)S(1)} %copy-done.24, ...), custom_call_target="tpu_custom_call" | custom-call | flops 1024 | bytes 1024 | tf_op jit(solution)/shard_map/prologue/pallas_call | solution.py:744
  27.3 1.0 copy-done.11
  28.3 1.0 copy-done.13
  29.9 4.9 %all-to-all-start = ((bf16[4,128,768]{2,1,0:T(8,128)(2,1)}), bf16[4,128,768]{2,1,0:T(8,128)(2,1)}, u32[]{:S(2)}, u32[]{:S(2)}) async-start(bf16[4,128,768]{2,1,0:T(8,128)(2,1)} %copy-done.10), calls=%async_computation | async-start | bytes 1572864 | tf_op jit(solution)/shard_map/all_to_all | solution.py:1143
  34.8 31.7 %collective-permute-done.3.refs_3_ = bf16[528,1024]{1,0:T(8,128)(2,1)S(1)} collective-permute-done((bf16[528,1024]{1,0:T(8,128)(2,1)}, bf16[528,1024]{1,0:T(8,128)(2,1)S(1)}, u32[]{:S(2)}, u32[]{:S(2)}) %collective-permute-start.3) | collective-permute-done | bytes 1081376 | tf_op jit(solution)/shard_map/ppermute | solution.py:296
  66.5 2.0 copy-done.14
  68.5 1.2 turn.1.refs_2_.refs_1_
  69.7 1.3 copy-done.2
  71.1 1.6 copy-done.3
  72.6 1.7 rows_qkv.1.refs_5_.refs_8_.refs_2_
  74.4 1.6 collective-permute-start.5
  76.0 21.4 %collective-permute-done.5.refs_6_.refs_3_ = bf16[512,768]{1,0:T(8,128)(2,1)S(1)} collective-permute-done((bf16[512,768]{1,0:T(8,128)(2,1)S(1)}, bf16[512,768]{1,0:T(8,128)(2,1)S(1)}, u32[]{:S(2)}, u32[]{:S(2)}) %collective-permute-start.5) | collective-permute-done | bytes 786464 | tf_op jit(solution)/shard_map/ppermute | solution.py:296
  97.5 6.2 %project.1 = (bf16[2048,768]{1,0:T(8,128)(2,1)S(1)}, f32[8,2048]{1,0:T(8,128)S(1)}) custom-call(s32[128]{0:T(128)S(1)} %dynamic-slice_bitcast_fusion.refs_0_, bf16[528,1024]{1,0:T(8,128)(2,1)} %get-tuple-element.85.refs_1_, bf16[1040,1024]{1,0:T(8,128)(2,1)S(1)} %collective-permute-done.2.refs_2_, bf16[528,1024]{1,0:T(8,128)(2,1)S(1)} %collective-permute-done.3.refs_3_, ...), custom_call_target="tpu_custom_call" | custom-call | flops 1024 | bytes 1024 | tf_op jit(solution)/shard_map/project/pallas_call | solution.py:744
  103.7 1.7 copy-done.46
  106.0 24.9 %attend_forward.1 = (bf16[2048,256]{1,0:T(8,128)(2,1)}, f32[256,2048]{1,0:T(8,128)}, f32[8,2048]{1,0:T(8,128)}) custom-call(s32[128]{0:T(128)} %copy-done.33, s32[4]{0:T(128)} %bitcast.19, bf16[2048,768]{1,0:T(8,128)(2,1)} %copy-done.46, bf16[2048,768]{1,0:T(8,128)(2,1)} %copy-done.46, bf16[2048,768]{1,0:T(8,128)(2,1)} %copy-done.46, f32[8,2048]{1,0:T(8,128)} %copy-done.48, ...), custom_call_target="tpu_custom_call" | custom-call | flops 40802189312 | bytes 1024 | tf_op jit(solution)/shard_map/attend_forward/pallas_call | solution.py:153
  130.9 18.8 %all_to_all.20.refs_1_ = bf16[4,512,256]{2,1,0:T(8,128)(2,1)} all-to-all(bf16[4,512,256]{2,1,0:T(8,128)(2,1)} %bitcast.16), channel_id=1, replica_groups=mesh['dp'=8,'sp'=4] {'sp'}, dimensions={0} | all-to-all | bytes 2097152 | tf_op jit(solution)/shard_map/all_to_all | solution.py:1309
  149.7 2.4 all-gather.3.cloned.1.call-done
  152.1 9.1 %to_middle.1 = (bf16[512,2048]{1,0:T(8,128)(2,1)}, f32[512,1024]{1,0:T(8,128)}, f32[512,1024]{1,0:T(8,128)}, f32[512,1]{1,0:T(8,128)}, bf16[1024,1024]{1,0:T(8,128)(2,1)}) custom-call(s32[128]{0:T(128)} %copy-done.33, bf16[4,512,256]{2,1,0:T(8,128)(2,1)} %all_to_all.20.refs_1_, bf16[512,1024]{1,0:T(8,128)(2,1)} %copy-done.11, f32[16,1024]{1,0:T(8,128)} %copy-done.22, ...), custom_call_target="tpu_custom_call" | custom-call | flops 1024 | bytes 1024 | tf_op jit(solution)/shard_map/to_middle/pallas_call | solution.py:744
  161.1 48.4 %ffn.1 = (bf16[512,2048]{1,0:T(8,128)(2,1)}, bf16[512,2048]{1,0:T(8,128)(2,1)}, bf16[512,2048]{1,0:T(8,128)(2,1)}, bf16[512,2048]{1,0:T(8,128)(2,1)}, f32[512,10...) custom-call(s32[128]{0:T(128)} %copy-done.33, bf16[512,2048]{1,0:T(8,128)(2,1)} %get-tuple-element.95.refs_1_.refs_5_, ...), custom_call_target="tpu_custom_call" | custom-call | flops 40700002304 | bytes 1024 | tf_op jit(solution)/shard_map/ffn/pallas_call | solution.py:744
  209.5 12.4 %spill.1.refs_8_ = bf16[32,128,1024]{2,1,0:T(8,128)(2,1)} custom-call(s32[128]{0:T(128)} %copy-done.33, bf16[1024,1024]{1,0:T(8,128)(2,1)} %copy-done.2, bf16[512,2048]{1,0:T(8,128)(2,1)} %get-tuple-element.102.refs_2_, bf16[512,2048]{1,0:T(8,128)(2,1)} %get-tuple-element.103.refs_3_, f32[8,4096]{1,0:T(8,128)} %get-tuple-element.104.refs_4_.refs_3_), custom_call_target="tpu_custom_call" | custom-call | flops 1024 | bytes 1024 | tf_op jit(solution)/shard_map/spill/pallas_call | solution.py:744
  222.5 9.2 %to_heads.1 = (f32[512,1024]{1,0:T(8,128)}, bf16[512,512]{1,0:T(8,128)(2,1)}, bf16[512,512]{1,0:T(8,128)(2,1)}, bf16[4,512,256]{2,1,0:T(8,128)(2,1)}, f32[8,1024]{1,0:T(8,128)}) custom-call(s32[128]{0:T(128)} %copy-done.33, f32[512,1024]{1,0:T(8,128)} %get-tuple-element.99.refs_1_, f32[512,1024]{1,0:T(8,128)} %get-tuple-element.96.refs_3_.refs_2_, ...), custom_call_target="tpu_custom_call" | custom-call | flops 1024 | bytes 1024 | tf_op jit(solution)/shard_map/to_heads/pallas_call | solution.py:744
  233.8 4.3 all-to-all-start.2
  238.1 1.6 copy-done.49
  239.7 13.4 %grads_up.1 = (bf16[1024,640]{1,0:T(8,128)(2,1)S(1)}, bf16[1024,640]{1,0:T(8,128)(2,1)}, bf16[512,1280]{1,0:T(8,128)(2,1)S(1)}, bf16[512,1280]{1,0:T(8,128)(2,1)}, f32[24,1024]{1,0:T(8,128)S(1)}) custom-call(s32[128]{0:T(128)S(1)} %copy-done.34, bf16[512,2048]{1,0:T(8,128)(2,1)} %get-tuple-element.95.refs_1_.refs_5_, ...), custom_call_target="tpu_custom_call" | custom-call | flops 13200001024 | bytes 1024 | tf_op jit(solution)/shard_map/grads_up/pallas_call | solution.py:744
  253.1 1.1 copy-done.20
  254.2 1.9 collective-permute-start.12
  256.2 1.6 collective-permute-start.11
  257.9 6.8 %all-to-all-done.2 = bf16[4,512,256]{2,1,0:T(8,128)(2,1)} async-done(((bf16[4,512,256]{2,1,0:T(8,128)(2,1)}), bf16[4,512,256]{2,1,0:T(8,128)(2,1)}, u32[]{:S(2)}, u32[]{:S(2)}) %all-to-all-start.2) | async-done | bytes 1048608 | tf_op jit(solution)/shard_map/all_to_all | solution.py:1354
  264.7 37.7 %attend_backward.1 = (bf16[2048,768]{1,0:T(8,128)(2,1)}, f32[8,768]{1,0:T(8,128)}) custom-call(s32[128]{0:T(128)} %copy-done.33, s32[4]{0:T(128)} %bitcast.20, bf16[2048,768]{1,0:T(8,128)(2,1)} %copy-done.46, bf16[2048,768]{1,0:T(8,128)(2,1)} %copy-done.46, bf16[2048,768]{1,0:T(8,128)(2,1)} %copy-done.46, f32[8,2048]{1,0:T(8,128)} %copy-done.48, ...), custom_call_target="tpu_custom_call" | custom-call | flops 53687091200 | bytes 1024 | tf_op jit(solution)/shard_map/attend_backward/pallas_call | solution.py:258
  302.4 1.9 copy-done.6
  305.1 5.1 %first_grad.1 = (f32[512,1024]{1,0:T(8,128)S(1)}, bf16[1024,1024]{1,0:T(8,128)(2,1)S(1)}, f32[512,1024]{1,0:T(8,128)S(1)}) custom-call(s32[128]{0:T(128)S(1)} %copy-done.35, bf16[2048,768]{1,0:T(8,128)(2,1)S(1)} %copy-done.6, bf16[512,768]{1,0:T(8,128)(2,1)S(1)} %copy-done.5, bf16[512,768]{1,0:T(8,128)(2,1)S(1)} %copy-done.16, f32[8,768]{1,0:T(8,128)S(1)} %copy-done.42), custom_call_target="tpu_custom_call" | custom-call | flops 1024 | bytes 1024 | tf_op jit(solution)/shard_map/first_grad/pallas_call | solution.py:744
  310.2 1.9 copy-done.7
  312.1 6.7 %group_grads.1 = (f32[512,768]{1,0:T(8,128)S(1)}, bf16[512,768]{1,0:T(8,128)(2,1)S(1)}) custom-call(s32[128]{0:T(128)S(1)} %copy-done.35, bf16[528,1024]{1,0:T(8,128)(2,1)} %get-tuple-element.85.refs_1_, bf16[1040,1024]{1,0:T(8,128)(2,1)S(1)} %copy-done.1, bf16[528,1024]{1,0:T(8,128)(2,1)S(1)} %copy-done.9, ...), custom_call_target="tpu_custom_call" | custom-call | flops 1024 | bytes 1024 | tf_op jit(solution)/shard_map/group_grads/pallas_call | solution.py:744
  318.8 1.1 copy-done.18
  319.9 4.9 %collective-permute-done.10.refs_2_ = bf16[1024,640]{1,0:T(8,128)(2,1)} collective-permute-done((bf16[1024,640]{1,0:T(8,128)(2,1)}, bf16[1024,640]{1,0:T(8,128)(2,1)}, u32[]{:S(2)}, u32[]{:S(2)}) %collective-permute-start.10) | collective-permute-done | bytes 1310752 | tf_op jit(solution)/shard_map/ppermute | solution.py:296
  324.8 3.1 fold_up.1
  328.0 4.1 collective-permute-done.13.refs_2_
  333.0 2.7 collective-permute-start.14
  335.7 2.0 collective-permute-start.17
  337.8 1.5 collective-permute-start.15
  339.3 45.2 %collective-permute-done.15.refs_9_ = f32[24,1024]{1,0:T(8,128)S(1)} collective-permute-done((f32[24,1024]{1,0:T(8,128)S(1)}, f32[24,1024]{1,0:T(8,128)S(1)}, u32[]{:S(2)}, u32[]{:S(2)}) %collective-permute-start.15) | collective-permute-done | bytes 98336 | tf_op jit(solution)/shard_map/ppermute | solution.py:296
  384.5 17.6 %collective-permute-done.18.refs_12_.refs_4_ = bf16[512,640]{1,0:T(8,128)(2,1)S(1)} collective-permute-done((bf16[512,640]{1,0:T(8,128)(2,1)S(1)}, bf16[512,640]{1,0:T(8,128)(2,1)S(1)}, u32[]{:S(2)}, u32[]{:S(2)}) %collective-permute-start.18) | collective-permute-done | bytes 655392 | tf_op jit(solution)/shard_map/ppermute | solution.py:296
  402.1 3.8 to_tokens.1
  405.9 5.4 %all-to-all-start.3 = ((f32[32,24,128]{2,1,0:T(8,128)}), f32[32,24,128]{2,1,0:T(8,128)S(1)}, u32[]{:S(2)}, u32[]{:S(2)}) async-start(f32[32,24,128]{2,1,0:T(8,128)} %get-tuple-element.139), calls=%async_computation.4 | async-start | bytes 786432 | tf_op jit(solution)/shard_map/all_to_all | solution.py:1394
  411.3 1.4 copy-done.19
  412.7 1.1 copy-done.27
  413.8 1.1 copy-done.29
  414.9 1.8 spread_up.1
  416.7 1.8 collective-permute-start.19
  418.5 2.4 collective-permute-start.20
  421.1 0.9 collective-permute-start.22
  422.0 2.3 all-to-all-done.3.refs_1_
  425.0 32.4 %collective-permute-done.22.refs_7_ = f32[24,1024]{1,0:T(8,128)S(1)} collective-permute-done((f32[24,1024]{1,0:T(8,128)}, f32[24,1024]{1,0:T(8,128)S(1)}, u32[]{:S(2)}, u32[]{:S(2)}) %collective-permute-start.22) | collective-permute-done | bytes 98336 | tf_op jit(solution)/shard_map/ppermute | solution.py:296
  457.7 0.9 copy-done.31
  458.7 2.6 sum_up.1
  461.3 11.2 %collective-permute-start.25 = (f32[24,1024]{1,0:T(8,128)S(1)}, f32[24,1024]{1,0:T(8,128)S(1)}, u32[]{:S(2)}, u32[]{:S(2)}) collective-permute-start(f32[24,1024]{1,0:T(8,128)S(1)} %get-tuple-element.143.refs_5_.refs_7_), channel_id=1, source_target_pairs={{0,16},{4,20},{8,24},{12,28},{16,0},{20,4},{24,8},{28,12},{1,17},{... | collective-permute-start | bytes 294920 | tf_op jit(solution)/shard_map/ppermute | solution.py:296
  472.5 2.0 collective-permute-start.24
  474.5 2.5 collective-permute-done.23.refs_2_
  477.0 1.3 home.1
  (130 shorter events, 12.9 us)
Async XLA Ops:
  7.2 12.2 %copy-start.25 = (bf16[512,1024]{1,0:T(8,128)(2,1)S(1)}, bf16[512,1024]{1,0:T(8,128)(2,1)}, u32[]{:S(2)}) copy-start(bf16[512,1024]{1,0:T(8,128)(2,1)} %refs_2_.1) | copy-start | bytes 3145732
  7.2 12.2 %copy-start.24 = (bf16[512,1024]{1,0:T(8,128)(2,1)S(1)}, bf16[512,1024]{1,0:T(8,128)(2,1)}, u32[]{:S(2)}) copy-start(bf16[512,1024]{1,0:T(8,128)(2,1)} %refs_1_.3) | copy-start | bytes 3145732
  7.2 144.9 %all-gather.3.cloned.1.call-start = ((), (), s32[]{:S(2)}) async-start(), calls=%async_computation.6 | async-start | bytes 19464192 | tf_op jit(solution)/shard_map/all_gather | solution.py:1285
  11.0 86.5 %copy-start.33 = (s32[128]{0:T(128)}, s32[128]{0:T(128)S(1)}, u32[]{:S(2)}) copy-start(s32[128]{0:T(128)S(1)} %dynamic-slice_bitcast_fusion.refs_0_) | copy-start | bytes 1540
  11.5 4.9 %collective-permute-start = (bf16[128,256]{1,0:T(8,128)(2,1)S(1)}, bf16[128,256]{1,0:T(8,128)(2,1)S(1)}, u32[]{:S(2)}, u32[]{:S(2)}) collective-permute-start(bf16[128,256]{1,0:T(8,128)(2,1)S(1)} %get-tuple-element.83), channel_id=1, source_target_pairs={{0,2},{1,0},{2,3},{3,1},{4,6},{5,4},{6,7},{7,5},{8,10},{9,8},{10,1... | collective-permute-start | bytes 196616 | tf_op jit(solution)/shard_map/ppermute | solution.py:1282
  14.5 4.3 collective-permute-start.1
  19.3 10.5 %copy-start.10 = (bf16[4,128,768]{2,1,0:T(8,128)(2,1)}, bf16[4,128,768]{2,1,0:T(8,128)(2,1)S(1)}, u32[]{:S(2)}) copy-start(bf16[4,128,768]{2,1,0:T(8,128)(2,1)S(1)} %join.1.refs_9_) | copy-start | bytes 2359300
  29.9 39.9 %copy-start.38 = (f32[8,4096]{1,0:T(8,128)}, f32[8,4096]{1,0:T(8,128)S(1)}, u32[]{:S(2)}) copy-start(f32[8,4096]{1,0:T(8,128)S(1)} %get-tuple-element.88.refs_4_) | copy-start | bytes 393220
  29.9 36.7 %collective-permute-start.2 = (bf16[1040,1024]{1,0:T(8,128)(2,1)}, bf16[1040,1024]{1,0:T(8,128)(2,1)S(1)}, u32[]{:S(2)}, u32[]{:S(2)}) collective-permute-start(bf16[1040,1024]{1,0:T(8,128)(2,1)} %get-tuple-element.86), channel_id=1, source_target_pairs={{0,1},{1,0},{2,3},{3,2},{4,5},{5,4},{6,7},{7,6},{8,9},{9,8},{10,11... | collective-permute-start | bytes 6389768 | tf_op jit(solution)/shard_map/ppermute | solution.py:296
  29.9 36.6 %collective-permute-start.3 = (bf16[528,1024]{1,0:T(8,128)(2,1)}, bf16[528,1024]{1,0:T(8,128)(2,1)S(1)}, u32[]{:S(2)}, u32[]{:S(2)}) collective-permute-start(bf16[528,1024]{1,0:T(8,128)(2,1)} %get-tuple-element.85.refs_1_), channel_id=1, source_target_pairs={{0,2},{1,3},{2,0},{3,1},{4,6},{5,7},{6,4},{7,5},{8,10},{9,11},{10,... | collective-permute-start | bytes 3244040 | tf_op jit(solution)/shard_map/ppermute | solution.py:296
  29.9 41.1 %all-to-all-start = ((bf16[4,128,768]{2,1,0:T(8,128)(2,1)}), bf16[4,128,768]{2,1,0:T(8,128)(2,1)}, u32[]{:S(2)}, u32[]{:S(2)}) async-start(bf16[4,128,768]{2,1,0:T(8,128)(2,1)} %copy-done.10), calls=%async_computation | async-start | bytes 1572864 | tf_op jit(solution)/shard_map/all_to_all | solution.py:1143
  34.8 422.9 %reduce-scatter.2.cloned.1.call-start = ((), (), s32[]{:S(2)}) async-start(), calls=%async_computation.5 | async-start | bytes 8650752 | tf_op jit(solution)/shard_map/reduce_scatter | solution.py:1340
  66.5 30.9 %copy-start.8 = (bf16[528,1024]{1,0:T(8,128)(2,1)}, bf16[528,1024]{1,0:T(8,128)(2,1)S(1)}, u32[]{:S(2)}) copy-start(bf16[528,1024]{1,0:T(8,128)(2,1)S(1)} %collective-permute-done.3.refs_3_) | copy-start | bytes 3244036
  66.5 9.5 %collective-permute-start.4 = (bf16[528,1024]{1,0:T(8,128)(2,1)S(1)}, bf16[528,1024]{1,0:T(8,128)(2,1)}, u32[]{:S(2)}, u32[]{:S(2)}) collective-permute-start(bf16[528,1024]{1,0:T(8,128)(2,1)S(1)} %collective-permute-done.3.refs_3_), channel_id=1, source_target_pairs={{0,1},{1,0},{2,3},{3,2},{4,5},{5,4},{6,7},{7,6},{8,9},{9,8},{10,11... | collective-permute-start | bytes 3244040 | tf_op jit(solution)/shard_map/ppermute | solution.py:296
  66.5 30.9 %copy-start = (bf16[1040,1024]{1,0:T(8,128)(2,1)}, bf16[1040,1024]{1,0:T(8,128)(2,1)S(1)}, u32[]{:S(2)}) copy-start(bf16[1040,1024]{1,0:T(8,128)(2,1)S(1)} %collective-permute-done.2.refs_2_) | copy-start | bytes 6389764
  66.5 2.0 copy-start.14
  71.1 1.6 copy-start.3
  72.6 24.8 %copy-start.37 = (f32[7,1024]{1,0:T(8,128)S(1)}, f32[7,1024]{1,0:T(8,128)}, u32[]{:S(2)}) copy-start(f32[7,1024]{1,0:T(8,128)} %refs_7_.1) | copy-start | bytes 86020
  74.4 29.3 %copy-start.4 = (bf16[512,768]{1,0:T(8,128)(2,1)}, bf16[512,768]{1,0:T(8,128)(2,1)S(1)}, u32[]{:S(2)}) copy-start(bf16[512,768]{1,0:T(8,128)(2,1)S(1)} %rows_qkv.1.refs_5_.refs_8_.refs_2_) | copy-start | bytes 2359300
  74.4 23.1 %collective-permute-start.5 = (bf16[512,768]{1,0:T(8,128)(2,1)S(1)}, bf16[512,768]{1,0:T(8,128)(2,1)S(1)}, u32[]{:S(2)}, u32[]{:S(2)}) collective-permute-start(bf16[512,768]{1,0:T(8,128)(2,1)S(1)} %rows_qkv.1.refs_5_.refs_8_.refs_2_), channel_id=1, source_target_pairs={{0,4},{4,0},{8,12},{12,8},{16,20},{20,16},{24,28},{28,24},{1,5},{5... | collective-permute-start | bytes 2359304 | tf_op jit(solution)/shard_map/ppermute | solution.py:296
  97.4 6.2 %copy-start.15 = (bf16[512,768]{1,0:T(8,128)(2,1)}, bf16[512,768]{1,0:T(8,128)(2,1)S(1)}, u32[]{:S(2)}) copy-start(bf16[512,768]{1,0:T(8,128)(2,1)S(1)} %collective-permute-done.5.refs_6_.refs_3_) | copy-start | bytes 2359300
  103.7 1.7 copy-start.46
  221.9 16.1 %collective-permute-start.7 = (bf16[512,2048]{1,0:T(8,128)(2,1)}, bf16[512,2048]{1,0:T(8,128)(2,1)}, u32[]{:S(2)}, u32[]{:S(2)}) collective-permute-start(bf16[512,2048]{1,0:T(8,128)(2,1)} %get-tuple-element.108), channel_id=1, source_target_pairs={{0,1},{1,0},{2,3},{3,2},{4,5},{5,4},{6,7},{7,6},{8,9},{9,8},{10,11... | collective-permute-start | bytes 6291464 | tf_op jit(solution)/shard_map/ppermute | solution.py:296
  222.3 15.8 %collective-permute-start.6 = (bf16[512,2048]{1,0:T(8,128)(2,1)}, bf16[512,2048]{1,0:T(8,128)(2,1)}, u32[]{:S(2)}, u32[]{:S(2)}) collective-permute-start(bf16[512,2048]{1,0:T(8,128)(2,1)} %get-tuple-element.95.refs_1_.refs_5_), channel_id=1, source_target_pairs={{0,1},{1,0},{2,3},{3,2},{4,5},{5,4},{6,7},{7,6},{8,9},{9,8},{10,11... | collective-permute-start | bytes 6291464 | tf_op jit(solution)/shard_map/ppermute | solution.py:296
  222.5 9.6 %copy-start.23 = (f32[16,1024]{1,0:T(8,128)S(1)}, f32[16,1024]{1,0:T(8,128)}, u32[]{:S(2)}) copy-start(f32[16,1024]{1,0:T(8,128)} %copy-done.22) | copy-start | bytes 196612
  222.5 9.6 %copy-start.30 = (f32[8,4096]{1,0:T(8,128)S(1)}, f32[8,4096]{1,0:T(8,128)}, u32[]{:S(2)}) copy-start(f32[8,4096]{1,0:T(8,128)} %get-tuple-element.104.refs_4_.refs_3_) | copy-start | bytes 393220
  222.5 9.6 %copy-start.34 = (s32[128]{0:T(128)S(1)}, s32[128]{0:T(128)}, u32[]{:S(2)}) copy-start(s32[128]{0:T(128)} %copy-done.33) | copy-start | bytes 1540
  231.7 6.4 %collective-permute-start.8 = (bf16[512,512]{1,0:T(8,128)(2,1)}, bf16[512,512]{1,0:T(8,128)(2,1)S(1)}, u32[]{:S(2)}, u32[]{:S(2)}) collective-permute-start(bf16[512,512]{1,0:T(8,128)(2,1)} %get-tuple-element.110), channel_id=1, source_target_pairs={{0,1},{1,0},{2,3},{3,2},{4,5},{5,4},{6,7},{7,6},{8,9},{9,8},{10,11... | collective-permute-start | bytes 1572872 | tf_op jit(solution)/shard_map/ppermute | solution.py:296
  232.8 5.3 %copy-start.47 = (bf16[512,512]{1,0:T(8,128)(2,1)S(1)}, bf16[512,512]{1,0:T(8,128)(2,1)}, u32[]{:S(2)}) copy-start(bf16[512,512]{1,0:T(8,128)(2,1)} %get-tuple-element.109.refs_7_) | copy-start | bytes 1572868
  233.5 4.6 collective-permute-start.9
  233.8 30.9 %all-to-all-start.2 = ((bf16[4,512,256]{2,1,0:T(8,128)(2,1)}), bf16[4,512,256]{2,1,0:T(8,128)(2,1)}, u32[]{:S(2)}, u32[]{:S(2)}) async-start(bf16[4,512,256]{2,1,0:T(8,128)(2,1)} %get-tuple-element.105), calls=%async_computation.2 | async-start | bytes 2097152 | tf_op jit(solution)/shard_map/all_to_all | solution.py:1354
  238.1 1.6 copy-start.49
  254.2 10.5 %copy-start.40 = (f32[24,1024]{1,0:T(8,128)}, f32[24,1024]{1,0:T(8,128)S(1)}, u32[]{:S(2)}) copy-start(f32[24,1024]{1,0:T(8,128)S(1)} %get-tuple-element.112.refs_10_.refs_6_) | copy-start | bytes 294916
  254.2 65.7 %collective-permute-start.12 = (f32[24,1024]{1,0:T(8,128)S(1)}, f32[24,1024]{1,0:T(8,128)S(1)}, u32[]{:S(2)}, u32[]{:S(2)}) collective-permute-start(f32[24,1024]{1,0:T(8,128)S(1)} %get-tuple-element.112.refs_10_.refs_6_), channel_id=1, source_target_pairs={{0,2},{1,3},{2,0},{3,1},{4,6},{5,7},{6,4},{7,5},{8,10},{9,11},{10,... | collective-permute-start | bytes 294920 | tf_op jit(solution)/shard_map/ppermute | solution.py:296
  256.1 68.7 %collective-permute-start.10 = (bf16[1024,640]{1,0:T(8,128)(2,1)}, bf16[1024,640]{1,0:T(8,128)(2,1)}, u32[]{:S(2)}, u32[]{:S(2)}) collective-permute-start(bf16[1024,640]{1,0:T(8,128)(2,1)} %get-tuple-element.117), channel_id=1, source_target_pairs={{0,2},{1,3},{2,0},{3,1},{4,6},{5,7},{6,4},{7,5},{8,10},{9,11},{10,... | collective-permute-start | bytes 3932168 | tf_op jit(solution)/shard_map/ppermute | solution.py:296
  256.2 68.6 %collective-permute-start.11 = (bf16[512,1280]{1,0:T(8,128)(2,1)}, bf16[512,1280]{1,0:T(8,128)(2,1)}, u32[]{:S(2)}, u32[]{:S(2)}) collective-permute-start(bf16[512,1280]{1,0:T(8,128)(2,1)} %get-tuple-element.119), channel_id=1, source_target_pairs={{0,4},{4,0},{8,12},{12,8},{16,20},{20,16},{24,28},{28,24},{1,5},{5... | collective-permute-start | bytes 3932168 | tf_op jit(solution)/shard_map/ppermute | solution.py:296
  264.7 37.7 %copy-start.5 = (bf16[512,768]{1,0:T(8,128)(2,1)S(1)}, bf16[512,768]{1,0:T(8,128)(2,1)}, u32[]{:S(2)}) copy-start(bf16[512,768]{1,0:T(8,128)(2,1)} %copy-done.4) | copy-start | bytes 2359300
  264.7 37.7 %copy-start.16 = (bf16[512,768]{1,0:T(8,128)(2,1)S(1)}, bf16[512,768]{1,0:T(8,128)(2,1)}, u32[]{:S(2)}) copy-start(bf16[512,768]{1,0:T(8,128)(2,1)} %copy-done.15) | copy-start | bytes 2359300
  264.7 37.7 %copy-start.35 = (s32[128]{0:T(128)S(1)}, s32[128]{0:T(128)}, u32[]{:S(2)}) copy-start(s32[128]{0:T(128)} %copy-done.33) | copy-start | bytes 1540
  302.4 1.9 copy-start.6
  305.1 5.1 %copy-start.1 = (bf16[1040,1024]{1,0:T(8,128)(2,1)S(1)}, bf16[1040,1024]{1,0:T(8,128)(2,1)}, u32[]{:S(2)}) copy-start(bf16[1040,1024]{1,0:T(8,128)(2,1)} %copy-done) | copy-start | bytes 6389764
  305.1 5.1 %copy-start.9 = (bf16[528,1024]{1,0:T(8,128)(2,1)S(1)}, bf16[528,1024]{1,0:T(8,128)(2,1)}, u32[]{:S(2)}) copy-start(bf16[528,1024]{1,0:T(8,128)(2,1)} %copy-done.8) | copy-start | bytes 3244036
  310.2 1.9 copy-start.7
  312.1 12.8 %copy-start.21 = (bf16[512,1280]{1,0:T(8,128)(2,1)S(1)}, bf16[512,1280]{1,0:T(8,128)(2,1)}, u32[]{:S(2)}) copy-start(bf16[512,1280]{1,0:T(8,128)(2,1)} %copy-done.20) | copy-start | bytes 3932164
  312.1 12.8 %copy-start.41 = (f32[24,1024]{1,0:T(8,128)S(1)}, f32[24,1024]{1,0:T(8,128)}, u32[]{:S(2)}) copy-start(f32[24,1024]{1,0:T(8,128)} %copy-done.40) | copy-start | bytes 294916
  327.9 5.0 %copy-start.26 = (bf16[512,640]{1,0:T(8,128)(2,1)}, bf16[512,640]{1,0:T(8,128)(2,1)S(1)}, u32[]{:S(2)}) copy-start(bf16[512,640]{1,0:T(8,128)(2,1)S(1)} %get-tuple-element.131.refs_1_) | copy-start | bytes 1966084
  327.9 5.0 %copy-start.28 = (bf16[512,640]{1,0:T(8,128)(2,1)}, bf16[512,640]{1,0:T(8,128)(2,1)S(1)}, u32[]{:S(2)}) copy-start(bf16[512,640]{1,0:T(8,128)(2,1)S(1)} %get-tuple-element.132.refs_3_) | copy-start | bytes 1966084
  327.9 4.2 collective-permute-start.13
  332.2 69.9 %copy-start.12 = (bf16[512,1024]{1,0:T(8,128)(2,1)S(1)}, bf16[512,1024]{1,0:T(8,128)(2,1)}, u32[]{:S(2)}) copy-start(bf16[512,1024]{1,0:T(8,128)(2,1)} %copy-done.11) | copy-start | bytes 3145732
  332.2 69.9 %copy-start.17 = (f32[512,1024]{1,0:T(8,128)S(1)}, f32[512,1024]{1,0:T(8,128)}, u32[]{:S(2)}) copy-start(f32[512,1024]{1,0:T(8,128)} %get-tuple-element.126.refs_5_) | copy-start | bytes 6291460
  333.0 69.1 %collective-permute-start.14 = (bf16[512,1024]{1,0:T(8,128)(2,1)S(1)}, bf16[512,1024]{1,0:T(8,128)(2,1)S(1)}, u32[]{:S(2)}, u32[]{:S(2)}) collective-permute-start(bf16[512,1024]{1,0:T(8,128)(2,1)S(1)} %get-tuple-element.125), channel_id=1, source_target_pairs={{0,2},{1,3},{2,0},{3,1},{4,6},{5,7},{6,4},{7,5},{8,10},{9,11},{10,... | collective-permute-start | bytes 3145736 | tf_op jit(solution)/shard_map/ppermute | solution.py:296
  335.7 66.4 %collective-permute-start.16 = (bf16[512,768]{1,0:T(8,128)(2,1)S(1)}, bf16[512,768]{1,0:T(8,128)(2,1)S(1)}, u32[]{:S(2)}, u32[]{:S(2)}) collective-permute-start(bf16[512,768]{1,0:T(8,128)(2,1)S(1)} %get-tuple-element.127.refs_13_), channel_id=1, source_target_pairs={{0,4},{4,0},{8,12},{12,8},{16,20},{20,16},{24,28},{28,24},{1,5},{5... | collective-permute-start | bytes 2359304 | tf_op jit(solution)/shard_map/ppermute | solution.py:296
  335.7 48.8 %collective-permute-start.17 = (bf16[512,640]{1,0:T(8,128)(2,1)S(1)}, bf16[512,640]{1,0:T(8,128)(2,1)S(1)}, u32[]{:S(2)}, u32[]{:S(2)}) collective-permute-start(bf16[512,640]{1,0:T(8,128)(2,1)S(1)} %get-tuple-element.128), channel_id=1, source_target_pairs={{0,4},{4,0},{8,12},{12,8},{16,20},{20,16},{24,28},{28,24},{1,5},{5... | collective-permute-start | bytes 1966088 | tf_op jit(solution)/shard_map/ppermute | solution.py:296
  337.7 64.4 %collective-permute-start.18 = (bf16[512,640]{1,0:T(8,128)(2,1)S(1)}, bf16[512,640]{1,0:T(8,128)(2,1)S(1)}, u32[]{:S(2)}, u32[]{:S(2)}) collective-permute-start(bf16[512,640]{1,0:T(8,128)(2,1)S(1)} %get-tuple-element.129), channel_id=1, source_target_pairs={{0,2},{1,3},{2,0},{3,1},{4,6},{5,7},{6,4},{7,5},{8,10},{9,11},{10,... | collective-permute-start | bytes 1966088 | tf_op jit(solution)/shard_map/ppermute | solution.py:296
  337.8 46.7 %collective-permute-start.15 = (f32[24,1024]{1,0:T(8,128)S(1)}, f32[24,1024]{1,0:T(8,128)S(1)}, u32[]{:S(2)}, u32[]{:S(2)}) collective-permute-start(f32[24,1024]{1,0:T(8,128)S(1)} %get-tuple-element.124.refs_4_.refs_8_), channel_id=1, source_target_pairs={{0,4},{4,0},{8,12},{12,8},{16,20},{20,16},{24,28},{28,24},{1,5},{5... | collective-permute-start | bytes 294920 | tf_op jit(solution)/shard_map/ppermute | solution.py:296
  405.9 18.4 %all-to-all-start.3 = ((f32[32,24,128]{2,1,0:T(8,128)}), f32[32,24,128]{2,1,0:T(8,128)S(1)}, u32[]{:S(2)}, u32[]{:S(2)}) async-start(f32[32,24,128]{2,1,0:T(8,128)} %get-tuple-element.139), calls=%async_computation.4 | async-start | bytes 786432 | tf_op jit(solution)/shard_map/all_to_all | solution.py:1394
  411.3 1.4 copy-start.19
  416.7 40.7 %collective-permute-start.19 = (bf16[128,2048]{1,0:T(8,128)(2,1)}, bf16[128,2048]{1,0:T(8,128)(2,1)S(1)}, u32[]{:S(2)}, u32[]{:S(2)}) collective-permute-start(bf16[128,2048]{1,0:T(8,128)(2,1)} %get-tuple-element.136), channel_id=1, source_target_pairs={{0,8},{4,12},{8,0},{12,4},{16,24},{20,28},{24,16},{28,20},{1,9},{5... | collective-permute-start | bytes 1572872 | tf_op jit(solution)/shard_map/ppermute | solution.py:296
  418.5 39.3 %collective-permute-start.20 = (bf16[128,2048]{1,0:T(8,128)(2,1)}, bf16[128,2048]{1,0:T(8,128)(2,1)S(1)}, u32[]{:S(2)}, u32[]{:S(2)}) collective-permute-start(bf16[128,2048]{1,0:T(8,128)(2,1)} %get-tuple-element.137), channel_id=1, source_target_pairs={{0,16},{4,20},{8,24},{12,28},{16,0},{20,4},{24,8},{28,12},{1,17},{... | collective-permute-start | bytes 1572872 | tf_op jit(solution)/shard_map/ppermute | solution.py:296
  420.9 36.8 %collective-permute-start.21 = (bf16[128,2048]{1,0:T(8,128)(2,1)}, bf16[128,2048]{1,0:T(8,128)(2,1)S(1)}, u32[]{:S(2)}, u32[]{:S(2)}) collective-permute-start(bf16[128,2048]{1,0:T(8,128)(2,1)} %get-tuple-element.138.refs_2_), channel_id=1, source_target_pairs={{0,24},{4,28},{8,16},{12,20},{16,8},{20,12},{24,0},{28,4},{1,25},{... | collective-permute-start | bytes 1572872 | tf_op jit(solution)/shard_map/ppermute | solution.py:296
  421.1 36.3 %collective-permute-start.22 = (f32[24,1024]{1,0:T(8,128)}, f32[24,1024]{1,0:T(8,128)S(1)}, u32[]{:S(2)}, u32[]{:S(2)}) collective-permute-start(f32[24,1024]{1,0:T(8,128)} %get-tuple-element.134.refs_7_.refs_6_), channel_id=1, source_target_pairs={{0,8},{4,12},{8,0},{12,4},{16,24},{20,28},{24,16},{28,20},{1,9},{5... | collective-permute-start | bytes 294920 | tf_op jit(solution)/shard_map/ppermute | solution.py:296
  461.3 15.7 %collective-permute-start.25 = (f32[24,1024]{1,0:T(8,128)S(1)}, f32[24,1024]{1,0:T(8,128)S(1)}, u32[]{:S(2)}, u32[]{:S(2)}) collective-permute-start(f32[24,1024]{1,0:T(8,128)S(1)} %get-tuple-element.143.refs_5_.refs_7_), channel_id=1, source_target_pairs={{0,16},{4,20},{8,24},{12,28},{16,0},{20,4},{24,8},{28,12},{1,17},{... | collective-permute-start | bytes 294920 | tf_op jit(solution)/shard_map/ppermute | solution.py:296
  472.5 4.5 collective-permute-start.23
  472.5 4.5 collective-permute-start.24
  (17 other events, 15.3 us)
Sparse Core Ops, SparseCore 0:
  10.9 141.0 all-gather.2
  222.0 169.9 reduce-scatter.1
